TPU v7x, 32 devices: a whole 2x2x4 slice. The times are simulated.
32 devices in a mesh: dp: 8 (over z, x), tensor: 4 (over y, core).
Axes of the slice: x: 2, y: 2, z: 4, core: 2. Of those that a mesh axis runs over, the one named last changes fastest.
Arguments:
- latent: bfloat16 [8192, 1408], P(('dp', 'tensor')), may hold values from -6 to 6
- skip_states: bfloat16 [8192, 1408], P(('dp', 'tensor')), may hold values from -6 to 6
- text_states: bfloat16 [8, 333, 1024], P('dp'), may hold values from -6 to 6
- condition: bfloat16 [8, 1408], P('dp'), may hold values from -3 to 3
- teacher: bfloat16 [8192, 1408], P(('dp', 'tensor')), may hold values from -9 to 9
- loss_mask: int32 [8192], P(('dp', 'tensor')), may hold values 0 or 1
- true_counts: int32 [8], P('dp'), may hold values from 341 to 1024, as said below
- positions: int32 [2, 8192], P(None, 'dp'), may hold values from 0 to 63, as said below
- skip_proj: bfloat16 [2816, 1408], P('dp', 'tensor'), may hold values from -0.109375 to 0.109375
- shift_proj: bfloat16 [1408, 1408], P('dp'), may hold values from -0.15625 to 0.15625
- self_project: bfloat16 [1408, 3, 1408], P('dp', None, 'tensor'), may hold values from -0.15625 to 0.15625
- self_output: bfloat16 [1408, 1408], P('tensor', 'dp'), may hold values from -0.21875 to 0.21875
- cross_query: bfloat16 [1408, 1408], P('dp', 'tensor'), may hold values from -0.15625 to 0.15625
- cross_keyval: bfloat16 [1024, 2, 1408], P('dp', None, 'tensor'), may hold values from -0.1875 to 0.1875
- cross_output: bfloat16 [1408, 1408], P('tensor', 'dp'), may hold values from -0.21875 to 0.21875
- hidden_up: bfloat16 [1408, 6144], P('dp', 'tensor'), may hold values from -0.15625 to 0.15625
- hidden_down: bfloat16 [6144, 1408], P('tensor', 'dp'), may hold values from -0.078125 to 0.078125
- norm_gain: float32 [4, 1408], replicated, may hold values from 0.5 to 1.5
- norm_bias: float32 [4, 1408], replicated, may hold values from -1.8 to 1.8
- head_gain: float32 [4, 88], replicated, may hold values from 1 to 2
- head_bias: float32 [4, 88], replicated, may hold values from -1.8 to 1.8
- column_bias: float32 [5, 1408], replicated, may hold values from -0.9 to 0.9
- hidden_bias: float32 [6144], replicated, may hold values from -1.8 to 1.8
- row_bias: float32 [4, 1408], replicated, may hold values from -0.9 to 0.9
Outputs:
- block_out: bfloat16 [8192, 1408], P(('dp', 'tensor'))
- grad_latent: float32 [8192, 1408], P(('dp', 'tensor'))
- grad_skip: float32 [8192, 1408], P(('dp', 'tensor'))
- grad_text: float32 [8, 333, 1024], P('dp')
- grad_skip_proj: float32 [2816, 1408], P('dp', 'tensor')
- grad_shift_proj: float32 [1408, 1408], P('dp')
- grad_self_project: float32 [1408, 3, 1408], P('dp', None, 'tensor')
- grad_self_output: float32 [1408, 1408], P('tensor', 'dp')
- grad_cross_query: float32 [1408, 1408], P('dp', 'tensor')
- grad_cross_keyval: float32 [1024, 2, 1408], P('dp', None, 'tensor')
- grad_cross_output: float32 [1408, 1408], P('tensor', 'dp')
- grad_hidden_up: float32 [1408, 6144], P('dp', 'tensor')
- grad_hidden_down: float32 [6144, 1408], P('tensor', 'dp')
- grad_norm_gain: float32 [4, 1408], replicated
- grad_norm_bias: float32 [4, 1408], replicated
- grad_head_gain: float32 [4, 88], replicated
- grad_head_bias: float32 [4, 88], replicated
- grad_column_bias: float32 [5, 1408], replicated
- grad_hidden_bias: float32 [6144], replicated
- grad_row_bias: float32 [4, 1408], replicated
Inputs may be any that keep to these rules, and one draw needn't show every extreme that they name: The loss counts the first true_counts tokens of each latent; the first latent counts 1024 // 3 of them and the last all 1024. positions[0] is a token's grid row and positions[1] its grid column, the grid of each latent being filled row by row; its width may differ between latents.
All inputs are finite; a program needn't handle non-finite values. No bound on the sum of `loss_mask` on one device may be relied on, other than what follows from the above.
Results may differ from a plain program's by a relative error of at most 0.024.
Values may be sent and summed in bfloat16 or wider, within the bound.
A program may use at most 256 MiB of HBM per device.

v0:
```python
import jax
import jax.numpy as jnp
from jax import lax
from jax.sharding import PartitionSpec as P

EPSILON = 1e-06


def layer_norm(values, gain_vector, offset):
    centred = values - jnp.mean(values, axis=-1, keepdims=True)
    spread = jnp.mean(centred * centred, axis=-1, keepdims=True)
    return centred * lax.rsqrt(spread + EPSILON) * gain_vector + offset


def rotary_tables(positions, head_size):
    quarter = head_size // 4
    frequency = 10000.0 ** (-jnp.arange(quarter, dtype=jnp.float32) / quarter)
    angles = positions.astype(jnp.float32)[:, :, None] * frequency[None, None, :]
    angles = jnp.repeat(angles, 2, axis=2)
    angles = jnp.concatenate([angles[0], angles[1]], axis=1)
    return (jnp.cos(angles), jnp.sin(angles))


def rotate(values, cosine_table, sine_table):
    value_pairs = values.reshape(values.shape[:-1] + (values.shape[-1] // 2, 2))
    turned = jnp.stack([-value_pairs[..., 1], value_pairs[..., 0]], axis=-1).reshape(values.shape)
    return values * cosine_table[:, None, :] + turned * sine_table[:, None, :]


def contract_rows(left_side, right_side):
    return lax.dot_general(
        left_side, right_side, (((0,), (0,)), ((), ())), preferred_element_type=jnp.float32
    )


def contract_cols(left_side, right_side):
    return lax.dot_general(
        left_side, right_side, (((1,), (1,)), ((), ())), preferred_element_type=jnp.float32
    )


def spread_rows(values):
    return lax.all_gather(values, "tensor", axis=0, tiled=True)


def collect_rows(row_fn, local_rows):
    return lax.psum_scatter(
        row_fn(jnp.int32(0), local_rows * lax.axis_size("tensor")).astype(jnp.bfloat16),
        "tensor",
        scatter_dimension=0,
        tiled=True,
    ).astype(jnp.float32)


def row_term(left_side, right_side, transposed):

    def partial_rows(row_start, row_count):
        if transposed:
            return contract_cols(left_side, right_side)
        return jnp.dot(left_side, right_side, preferred_element_type=jnp.float32)

    return partial_rows


def attend_block(query_block, key_rows, value_rows, score_scale):
    scores = (
        jnp.einsum("qhd,khd->hqk", query_block, key_rows, preferred_element_type=jnp.float32)
        * score_scale
    )
    highest = jnp.max(scores, axis=-1, keepdims=True)
    exponent = jnp.exp(scores - highest)
    denominator = jnp.sum(exponent, axis=-1, keepdims=True)
    prob_low = (exponent / denominator).astype(jnp.bfloat16)
    outputs = jnp.einsum("hqk,khd->qhd", prob_low, value_rows, preferred_element_type=jnp.float32)
    return (outputs, (highest + jnp.log(denominator))[..., 0])


def attention_forward(query_rows, key_rows, value_rows, score_scale, block_rows):
    latent_count, sequence_len = (query_rows.shape[0], query_rows.shape[1])
    blocked = query_rows.reshape(
        (latent_count, sequence_len // block_rows, block_rows) + query_rows.shape[2:]
    )

    def per_latent(operands):
        query_blocks, keys_one, values_one = operands
        return lax.map(
            lambda query_block: attend_block(query_block, keys_one, values_one, score_scale),
            query_blocks,
        )

    outputs, log_sums = lax.map(per_latent, (blocked, key_rows, value_rows))
    return (outputs.reshape(query_rows.shape), log_sums)


def attend_back(query_block, key_rows, value_rows, sum_block, grad_block, score_scale):
    scores = (
        jnp.einsum("qhd,khd->hqk", query_block, key_rows, preferred_element_type=jnp.float32)
        * score_scale
    )
    recomputed = jnp.exp(scores - sum_block[..., None])
    grad_probs = jnp.einsum(
        "qhd,khd->hqk", grad_block, value_rows, preferred_element_type=jnp.float32
    )
    inner_sum = jnp.sum(recomputed * grad_probs, axis=-1, keepdims=True)
    grad_scores = (recomputed * (grad_probs - inner_sum)).astype(jnp.bfloat16)
    grad_query = (
        jnp.einsum("hqk,khd->qhd", grad_scores, key_rows, preferred_element_type=jnp.float32)
        * score_scale
    )
    grad_keys = (
        jnp.einsum("hqk,qhd->khd", grad_scores, query_block, preferred_element_type=jnp.float32)
        * score_scale
    )
    grad_values = jnp.einsum(
        "hqk,qhd->khd",
        recomputed.astype(jnp.bfloat16),
        grad_block,
        preferred_element_type=jnp.float32,
    )
    return (grad_query, grad_keys, grad_values)


def attention_backward(
    query_rows, key_rows, value_rows, log_sums, grad_rows, score_scale, block_rows
):
    latent_count, sequence_len = (query_rows.shape[0], query_rows.shape[1])
    block_shape = (latent_count, sequence_len // block_rows, block_rows) + query_rows.shape[2:]

    def per_latent(operands):
        query_blocks, keys_one, values_one, sums_one, grads_one = operands

        def per_block(running, block_operands):
            query_block, sum_block, grad_block = block_operands
            grad_query, grad_keys, grad_values = attend_back(
                query_block, keys_one, values_one, sum_block, grad_block, score_scale
            )
            return ((running[0] + grad_keys, running[1] + grad_values), grad_query)

        zero_keys = jnp.zeros(keys_one.shape, jnp.float32)
        (grad_keys, grad_values), grad_queries = lax.scan(
            per_block, (zero_keys, zero_keys), (query_blocks, sums_one, grads_one)
        )
        return (grad_queries, grad_keys, grad_values)

    grad_queries, grad_keys, grad_values = lax.map(
        per_latent,
        (
            query_rows.reshape(block_shape),
            key_rows,
            value_rows,
            log_sums,
            grad_rows.reshape(block_shape),
        ),
    )
    return (grad_queries.reshape(query_rows.shape), grad_keys, grad_values)


def body(
    latent,
    skip_states,
    text_states,
    condition,
    teacher,
    loss_mask,
    true_counts,
    positions,
    skip_proj,
    shift_proj,
    self_project,
    self_output,
    cross_query,
    cross_keyval,
    cross_output,
    hidden_up,
    hidden_down,
    norm_gain,
    norm_bias,
    head_gain,
    head_bias,
    column_bias,
    hidden_bias,
    row_bias,
):
    tensor_index = lax.axis_index("tensor")
    tensor_size = lax.axis_size("tensor")
    local_rows, model_width = latent.shape
    group_rows = local_rows * tensor_size
    latent_count = condition.shape[0]
    sequence_len = group_rows // latent_count
    head_size = head_gain.shape[1]
    local_cols = self_project.shape[2]
    head_count = local_cols // head_size
    hidden_cols = hidden_up.shape[1]
    text_len = text_states.shape[1]
    score_scale = head_size ** (-0.5)
    block_rows = min(512, sequence_len)
    by_row = (group_rows, head_count, head_size)
    by_latent = (latent_count, sequence_len, head_count, head_size)
    text_shape = (latent_count, text_len, head_count, head_size)
    counted_total = lax.psum(jnp.sum(true_counts), "dp").astype(jnp.float32)
    loss_scale = latent_count * lax.axis_size("dp") * sequence_len / counted_total
    gathered = (
        lax.all_gather(skip_proj, "dp", axis=0, tiled=True),
        lax.all_gather(shift_proj, "dp", axis=0, tiled=True),
        lax.all_gather(self_project, "dp", axis=0, tiled=True),
        lax.all_gather(self_output, "dp", axis=1, tiled=True),
        lax.all_gather(cross_query, "dp", axis=0, tiled=True),
        lax.all_gather(cross_keyval, "dp", axis=0, tiled=True),
        lax.all_gather(cross_output, "dp", axis=1, tiled=True),
        lax.all_gather(hidden_up, "dp", axis=0, tiled=True),
        lax.all_gather(hidden_down, "dp", axis=1, tiled=True),
    )
    (
        skip_full,
        shift_full,
        project_full,
        output_full,
        query_full,
        keyval_full,
        cross_out_full,
        up_full,
        down_full,
    ) = gathered
    bias_cols = lax.dynamic_slice_in_dim(column_bias, tensor_index * local_cols, local_cols, 1)
    zero_cols = jnp.zeros((local_cols,), jnp.float32)
    hidden_cols_bias = lax.dynamic_slice_in_dim(
        hidden_bias, tensor_index * hidden_cols, hidden_cols, 0
    )
    cosine_table, sine_table = rotary_tables(positions, head_size)
    row_ids = tensor_index * local_rows + jnp.arange(local_rows)
    select = row_ids[:, None] // sequence_len == jnp.arange(latent_count)[None, :]
    select_rows = select.astype(jnp.float32)
    joined = jnp.concatenate([latent, skip_states], axis=1)
    joined_all = spread_rows(joined)
    skip_pre = jnp.dot(joined_all, skip_full, preferred_element_type=jnp.float32) + bias_cols[4]
    skipped = lax.all_to_all(
        skip_pre.astype(jnp.bfloat16), "tensor", split_axis=0, concat_axis=1, tiled=True
    ).astype(jnp.float32)
    residual, pull_skip = jax.vjp(layer_norm, skipped, norm_gain[0], norm_bias[0])
    silu_cond = jax.nn.silu(condition.astype(jnp.float32)).astype(jnp.bfloat16)
    shift_term = jnp.dot(silu_cond, shift_full, preferred_element_type=jnp.float32) + row_bias[3]
    shift_rows = jnp.dot(select_rows, shift_term, precision=lax.Precision.HIGHEST)

    def first_norm(values, gain_vector, offset, shift_values):
        return layer_norm(values, gain_vector, offset) + shift_values

    normed_first, pull_first = jax.vjp(first_norm, residual, norm_gain[1], norm_bias[1], shift_rows)
    first_all = spread_rows(normed_first.astype(jnp.bfloat16))
    self_bias = jnp.stack([bias_cols[0], zero_cols, bias_cols[1]])
    projected = (
        jnp.einsum("nd,dce->nce", first_all, project_full, preferred_element_type=jnp.float32)
        + self_bias[None]
    )

    def self_heads(query_pre, key_pre, gain_pair, offset_pair):
        query_rows = rotate(
            layer_norm(query_pre.reshape(by_row), gain_pair[0], offset_pair[0]),
            cosine_table,
            sine_table,
        )
        key_rows = rotate(
            layer_norm(key_pre.reshape(by_row), gain_pair[1], offset_pair[1]),
            cosine_table,
            sine_table,
        )
        return (query_rows, key_rows)

    (query_rows, key_rows), pull_heads = jax.vjp(
        self_heads, projected[:, 0], projected[:, 1], head_gain[0:2], head_bias[0:2]
    )
    query_low = query_rows.astype(jnp.bfloat16).reshape(by_latent)
    key_low = key_rows.astype(jnp.bfloat16).reshape(by_latent)
    value_low = projected[:, 2].astype(jnp.bfloat16).reshape(by_latent)
    mixed_heads, self_sums = attention_forward(
        query_low, key_low, value_low, score_scale, block_rows
    )
    mixed_low = mixed_heads.reshape(group_rows, local_cols).astype(jnp.bfloat16)
    attn_out = collect_rows(row_term(mixed_low, output_full, False), local_rows) + row_bias[0]
    second = residual + attn_out
    normed_third, pull_third = jax.vjp(layer_norm, second, norm_gain[2], norm_bias[2])
    third_all = spread_rows(normed_third.astype(jnp.bfloat16))
    cross_pre = jnp.dot(third_all, query_full, preferred_element_type=jnp.float32) + bias_cols[2]

    def cross_heads(query_pre, gain_vector, offset):
        return rotate(
            layer_norm(query_pre.reshape(by_row), gain_vector, offset), cosine_table, sine_table
        )

    cross_rows, pull_cross = jax.vjp(cross_heads, cross_pre, head_gain[2], head_bias[2])
    text_bias = jnp.stack([zero_cols, bias_cols[3]])
    text_proj = (
        jnp.einsum("ltd,dce->ltce", text_states, keyval_full, preferred_element_type=jnp.float32)
        + text_bias[None, None]
    )

    def text_heads(key_pre, gain_vector, offset):
        return layer_norm(key_pre.reshape(text_shape), gain_vector, offset)

    text_keys, pull_text = jax.vjp(text_heads, text_proj[:, :, 0], head_gain[3], head_bias[3])
    text_key_low = text_keys.astype(jnp.bfloat16)
    text_value_low = text_proj[:, :, 1].reshape(text_shape).astype(jnp.bfloat16)
    cross_low = cross_rows.astype(jnp.bfloat16).reshape(by_latent)
    cross_mixed, cross_sums = attention_forward(
        cross_low, text_key_low, text_value_low, score_scale, block_rows
    )
    cross_mixed_low = cross_mixed.reshape(group_rows, local_cols).astype(jnp.bfloat16)
    cross_out = (
        collect_rows(row_term(cross_mixed_low, cross_out_full, False), local_rows) + row_bias[1]
    )
    third_sum = second + cross_out
    normed_fourth, pull_fourth = jax.vjp(layer_norm, third_sum, norm_gain[3], norm_bias[3])
    fourth_all = spread_rows(normed_fourth.astype(jnp.bfloat16))
    upper_pre = jnp.dot(fourth_all, up_full, preferred_element_type=jnp.float32) + hidden_cols_bias
    active, pull_gelu = jax.vjp(
        lambda upper_values: jax.nn.gelu(upper_values, approximate=True), upper_pre
    )
    active_low = active.astype(jnp.bfloat16)
    mlp_out = collect_rows(row_term(active_low, down_full, False), local_rows) + row_bias[2]
    final_rows = third_sum + mlp_out
    block_out = final_rows.astype(jnp.bfloat16)
    count_rows = jnp.sum(jnp.where(select, true_counts[None, :], 0), axis=1)
    place_in = row_ids % sequence_len
    loss_weight = loss_mask.astype(jnp.float32) * (place_in < count_rows).astype(jnp.float32)
    grad_final = loss_scale * loss_weight[:, None] * (final_rows - teacher.astype(jnp.float32))
    (
        skip_back,
        project_back,
        output_back,
        query_back,
        keyval_back,
        cross_out_back,
        up_back,
        down_back,
    ) = (
        lax.all_gather(skip_proj, "dp", axis=0, tiled=True),
        lax.all_gather(self_project, "dp", axis=0, tiled=True),
        lax.all_gather(self_output, "dp", axis=1, tiled=True),
        lax.all_gather(cross_query, "dp", axis=0, tiled=True),
        lax.all_gather(cross_keyval, "dp", axis=0, tiled=True),
        lax.all_gather(cross_output, "dp", axis=1, tiled=True),
        lax.all_gather(hidden_up, "dp", axis=0, tiled=True),
        lax.all_gather(hidden_down, "dp", axis=1, tiled=True),
    )
    grad_mlp_low = grad_final.astype(jnp.bfloat16)
    bias_mlp = jnp.sum(grad_mlp_low.astype(jnp.float32), axis=0)
    grad_mlp_all = spread_rows(grad_mlp_low)
    grad_down = contract_rows(active_low, grad_mlp_all)
    grad_active = contract_cols(grad_mlp_all, down_back)
    (grad_upper,) = pull_gelu(grad_active)
    grad_upper_low = grad_upper.astype(jnp.bfloat16)
    bias_hidden = jnp.sum(grad_upper_low.astype(jnp.float32), axis=0)
    grad_up = contract_rows(fourth_all, grad_upper_low)
    grad_normed_fourth = collect_rows(row_term(grad_upper_low, up_back, True), local_rows)
    grad_third_norm, gain_fourth, offset_fourth = pull_fourth(grad_normed_fourth)
    grad_third = grad_final + grad_third_norm
    grad_cross_low = grad_third.astype(jnp.bfloat16)
    bias_cross_out = jnp.sum(grad_cross_low.astype(jnp.float32), axis=0)
    grad_cross_all = spread_rows(grad_cross_low)
    grad_cross_output = contract_rows(cross_mixed_low, grad_cross_all)
    grad_cross_mixed = (
        contract_cols(grad_cross_all, cross_out_back).astype(jnp.bfloat16).reshape(by_latent)
    )
    grad_cross_rows, grad_text_keys, grad_text_values = attention_backward(
        cross_low,
        text_key_low,
        text_value_low,
        cross_sums,
        grad_cross_mixed,
        score_scale,
        block_rows,
    )
    grad_cross_pre, gain_cross, offset_cross = pull_cross(grad_cross_rows.reshape(by_row))
    grad_cross_pre_low = grad_cross_pre.astype(jnp.bfloat16)
    grad_key_text, gain_text, offset_text = pull_text(grad_text_keys)
    grad_keyval_low = jnp.stack(
        [grad_key_text, grad_text_values.reshape(latent_count, text_len, local_cols)], axis=2
    ).astype(jnp.bfloat16)
    grad_keyval = jnp.einsum(
        "ltd,ltce->dce", text_states, grad_keyval_low, preferred_element_type=jnp.float32
    )
    text_part = jnp.einsum(
        "ltce,dce->ltd", grad_keyval_low, keyval_back, preferred_element_type=jnp.float32
    )
    bias_text_value = jnp.sum(grad_keyval_low[:, :, 1].astype(jnp.float32), axis=(0, 1))
    bias_cross_query = jnp.sum(grad_cross_pre_low.astype(jnp.float32), axis=0)
    grad_query = contract_rows(third_all, grad_cross_pre_low)
    grad_normed_third = collect_rows(row_term(grad_cross_pre_low, query_back, True), local_rows)
    grad_second_norm, gain_third, offset_third = pull_third(grad_normed_third)
    grad_second = grad_third + grad_second_norm
    grad_attn_low = grad_second.astype(jnp.bfloat16)
    bias_attn = jnp.sum(grad_attn_low.astype(jnp.float32), axis=0)
    grad_attn_all = spread_rows(grad_attn_low)
    grad_self_output = contract_rows(mixed_low, grad_attn_all)
    grad_mixed = contract_cols(grad_attn_all, output_back).astype(jnp.bfloat16).reshape(by_latent)
    grad_query_rows, grad_key_rows, grad_value_rows = attention_backward(
        query_low, key_low, value_low, self_sums, grad_mixed, score_scale, block_rows
    )
    grad_query_pre, grad_key_pre, gain_pair, offset_pair = pull_heads(
        (grad_query_rows.reshape(by_row), grad_key_rows.reshape(by_row))
    )
    grad_projected_low = jnp.stack(
        [grad_query_pre, grad_key_pre, grad_value_rows.reshape(group_rows, local_cols)], axis=1
    ).astype(jnp.bfloat16)
    bias_query = jnp.sum(grad_projected_low[:, 0].astype(jnp.float32), axis=0)
    bias_value = jnp.sum(grad_projected_low[:, 2].astype(jnp.float32), axis=0)
    grad_project = jnp.einsum(
        "nd,nce->dce", first_all, grad_projected_low, preferred_element_type=jnp.float32
    )
    grad_normed_first = collect_rows(
        row_term(
            grad_projected_low.reshape(group_rows, 3 * local_cols),
            project_back.reshape(model_width, 3 * local_cols),
            True,
        ),
        local_rows,
    )
    grad_resid_norm, gain_first, offset_first, grad_shift_rows = pull_first(grad_normed_first)
    grad_residual = grad_second + grad_resid_norm
    shift_part = jnp.dot(select_rows.T, grad_shift_rows, precision=lax.Precision.HIGHEST)
    grad_shift_total, grad_text = (
        lax.psum(shift_part.astype(jnp.bfloat16), "tensor").astype(jnp.float32),
        lax.psum(text_part.astype(jnp.bfloat16), "tensor").astype(jnp.float32),
    )
    grad_shift_low = grad_shift_total.astype(jnp.bfloat16)
    grad_shift_proj = contract_rows(silu_cond, grad_shift_low)
    bias_shift = jnp.sum(grad_shift_low.astype(jnp.float32), axis=0) * (tensor_index == 0).astype(
        jnp.float32
    )
    grad_skipped, gain_skip, offset_skip = pull_skip(grad_residual)
    grad_skip_pre = lax.all_to_all(
        grad_skipped.astype(jnp.bfloat16), "tensor", split_axis=1, concat_axis=0, tiled=True
    )
    bias_skip = jnp.sum(grad_skip_pre.astype(jnp.float32), axis=0)
    grad_skip_proj = contract_rows(joined_all, grad_skip_pre)
    grad_joined = collect_rows(row_term(grad_skip_pre, skip_back, True), local_rows)
    grad_latent = grad_joined[:, :model_width]
    grad_skip = grad_joined[:, model_width:]
    scattered = (
        lax.psum_scatter(grad_skip_proj, "dp", scatter_dimension=0, tiled=True),
        lax.psum_scatter(grad_shift_proj, "dp", scatter_dimension=0, tiled=True),
        lax.psum_scatter(grad_project, "dp", scatter_dimension=0, tiled=True),
        lax.psum_scatter(grad_self_output, "dp", scatter_dimension=1, tiled=True),
        lax.psum_scatter(grad_query, "dp", scatter_dimension=0, tiled=True),
        lax.psum_scatter(grad_keyval, "dp", scatter_dimension=0, tiled=True),
        lax.psum_scatter(grad_cross_output, "dp", scatter_dimension=1, tiled=True),
        lax.psum_scatter(grad_up, "dp", scatter_dimension=0, tiled=True),
        lax.psum_scatter(grad_down, "dp", scatter_dimension=1, tiled=True),
    )
    norm_gain_part = jnp.stack([gain_skip, gain_first, gain_third, gain_fourth])
    norm_bias_part = jnp.stack([offset_skip, offset_first, offset_third, offset_fourth])
    head_gain_part = jnp.concatenate([gain_pair, gain_cross[None], gain_text[None]], axis=0)
    head_bias_part = jnp.concatenate([offset_pair, offset_cross[None], offset_text[None]], axis=0)
    column_rows = jnp.stack([bias_query, bias_value, bias_cross_query, bias_text_value, bias_skip])
    column_part = lax.dynamic_update_slice_in_dim(
        jnp.zeros(column_bias.shape, jnp.float32), column_rows, tensor_index * local_cols, 1
    )
    hidden_part = lax.dynamic_update_slice_in_dim(
        jnp.zeros(hidden_bias.shape, jnp.float32), bias_hidden, tensor_index * hidden_cols, 0
    )
    row_part = jnp.stack([bias_attn, bias_cross_out, bias_mlp, bias_shift])
    small_sums = lax.psum(
        (
            norm_gain_part,
            norm_bias_part,
            head_gain_part,
            head_bias_part,
            column_part,
            hidden_part,
            row_part,
        ),
        ("dp", "tensor"),
    )
    return (
        block_out,
        grad_latent,
        grad_skip,
        grad_text,
        scattered[0],
        scattered[1],
        scattered[2],
        scattered[3],
        scattered[4],
        scattered[5],
        scattered[6],
        scattered[7],
        scattered[8],
        small_sums[0],
        small_sums[1],
        small_sums[2],
        small_sums[3],
        small_sums[4],
        small_sums[5],
        small_sums[6],
    )


def solution(mesh):
    return jax.shard_map(
        body,
        mesh=mesh,
        in_specs=(
            P(("dp", "tensor"), None),
            P(("dp", "tensor"), None),
            P("dp", None, None),
            P("dp", None),
            P(("dp", "tensor"), None),
            P(("dp", "tensor")),
            P("dp"),
            P(None, "dp"),
            P("dp", "tensor"),
            P("dp", None),
            P("dp", None, "tensor"),
            P("tensor", "dp"),
            P("dp", "tensor"),
            P("dp", None, "tensor"),
            P("tensor", "dp"),
            P("dp", "tensor"),
            P("tensor", "dp"),
            P(),
            P(),
            P(),
            P(),
            P(),
            P(),
            P(),
        ),
        out_specs=(
            P(("dp", "tensor"), None),
            P(("dp", "tensor"), None),
            P(("dp", "tensor"), None),
            P("dp", None, None),
            P("dp", "tensor"),
            P("dp", None),
            P("dp", None, "tensor"),
            P("tensor", "dp"),
            P("dp", "tensor"),
            P("dp", None, "tensor"),
            P("tensor", "dp"),
            P("dp", "tensor"),
            P("tensor", "dp"),
            P(),
            P(),
            P(),
            P(),
            P(),
            P(),
            P(),
        ),
        check_vma=False,
    )
```

profile of v0, /device:TPU:0, one launch (start us, length us, event | category | flops | bytes accessed | tf_op | source)
XLA Modules:
  0.0 2452.5 jit_solution(15133617630600758071)
XLA Ops:
  12.9 50.0 %all-gather.16.cloned.1.call-done = bf16[2816,352]{1,0:T(8,128)(2,1)} async-done(((bf16[352,352]{1,0:T(8,128)(2,1)}), bf16[2816,352]{1,0:T(8,128)(2,1)}) %all-gather.16.cloned.1.call-update) | async-done | bytes 1982480 | tf_op jit(solution)/shard_map/all_gather | solution.py:203
  62.9 44.1 %all-gather.14.cloned.1.call-done = bf16[1024,2816]{1,0:T(8,128)(2,1)} async-done(((bf16[256,2816]{1,0:T(8,128)(2,1)}), bf16[1024,2816]{1,0:T(8,128)(2,1)}) %all-gather.14.cloned.1.call-update) | async-done | bytes 5767184 | tf_op jit(solution)/shard_map/all_gather | solution.py:43
  118.5 61.2 %all-gather.18.cloned.1.call-done = bf16[1408,1408]{1,0:T(8,128)(2,1)} async-done(((bf16[176,1408]{1,0:T(8,128)(2,1)}), bf16[1408,1408]{1,0:T(8,128)(2,1)}) %all-gather.18.cloned.1.call-update) | async-done | bytes 3964944 | tf_op jit(solution)/shard_map/all_gather | solution.py:204
  194.7 37.8 %all_gather.61 = bf16[352,1408]{0,1:T(8,128)(2,1)} all-gather(bf16[352,176]{0,1:T(8,128)(2,1)S(1)} %copy-done.98), channel_id=1, replica_groups=mesh['dp'=8,'tensor'=4] {'dp'}, dimensions={1}, use_global_device_ids=true | all-gather | bytes 1115136 | tf_op jit(solution)/shard_map/all_gather | solution.py:206
  232.5 19.4 all-gather.22.cloned.1.call-done
  251.9 29.2 %all-gather.20.cloned.1.call-done = bf16[1024,1408]{1,0:T(8,128)(2,1)} async-done(((bf16[256,1408]{1,0:T(8,128)(2,1)}), bf16[1024,1408]{1,0:T(8,128)(2,1)}) %all-gather.20.cloned.1.call-update) | async-done | bytes 2883600 | tf_op jit(solution)/shard_map/all_gather | solution.py:43
  346.9 35.6 %reduce-scatter.17.cloned.1.call-done = bf16[256,1408]{1,0:T(8,128)(2,1)} async-done(((bf16[1024,1408]{1,0:T(8,128)(2,1)}), bf16[256,1408]{1,0:T(8,128)(2,1)}) %reduce-scatter.17.cloned.1.call-update) | async-done | bytes 720912 | tf_op jit(solution)/shard_map/reduce_scatter | solution.py:47
  386.8 36.9 %all_gather.63 = bf16[1408,352]{1,0:T(8,128)(2,1)} all-gather(bf16[176,352]{1,0:T(8,128)(2,1)S(1)} %copy-done.99), channel_id=1, replica_groups=mesh['dp'=8,'tensor'=4] {'dp'}, dimensions={0}, use_global_device_ids=true | all-gather | bytes 1115136 | tf_op jit(solution)/shard_map/all_gather | solution.py:207
  423.6 35.8 %all_gather.65 = bf16[352,1408]{0,1:T(8,128)(2,1)} all-gather(bf16[352,176]{0,1:T(8,128)(2,1)S(1)} %copy-done.100), channel_id=1, replica_groups=mesh['dp'=8,'tensor'=4] {'dp'}, dimensions={1}, use_global_device_ids=true | all-gather | bytes 1115136 | tf_op jit(solution)/shard_map/all_gather | solution.py:209
  511.4 35.8 %reduce-scatter.19.cloned.1.call-done = bf16[256,1408]{1,0:T(8,128)(2,1)} async-done(((bf16[1024,1408]{1,0:T(8,128)(2,1)}), bf16[256,1408]{1,0:T(8,128)(2,1)}) %reduce-scatter.19.cloned.1.call-update) | async-done | bytes 720912 | tf_op jit(solution)/shard_map/reduce_scatter | solution.py:47
  552.4 72.0 %all-gather.30.cloned.1.call-done = bf16[1408,1536]{1,0:T(8,128)(2,1)} async-done(((bf16[176,1536]{1,0:T(8,128)(2,1)}), bf16[1408,1536]{1,0:T(8,128)(2,1)}) %all-gather.30.cloned.1.call-update) | async-done | bytes 4325392 | tf_op jit(solution)/shard_map/all_gather | solution.py:210
  624.4 27.5 %all-gather.28.cloned.1.call-done = bf16[1024,1408]{1,0:T(8,128)(2,1)} async-done(((bf16[256,1408]{1,0:T(8,128)(2,1)}), bf16[1024,1408]{1,0:T(8,128)(2,1)}) %all-gather.28.cloned.1.call-update) | async-done | bytes 2883600 | tf_op jit(solution)/shard_map/all_gather | solution.py:43
  661.3 67.6 %all-gather.32.cloned.1.call-done = bf16[1536,1408]{0,1:T(8,128)(2,1)} async-done(((bf16[1536,176]{0,1:T(8,128)(2,1)}), bf16[1536,1408]{0,1:T(8,128)(2,1)}) %all-gather.32.cloned.1.call-update) | async-done | bytes 4325392 | tf_op jit(solution)/shard_map/all_gather | solution.py:211
  750.7 23.1 reduce-scatter.21.cloned.1.call-done
  778.0 27.2 %all-gather.34.cloned.1.call-done = bf16[1024,1408]{1,0:T(8,128)(2,1)} async-done(((bf16[256,1408]{1,0:T(8,128)(2,1)}), bf16[1024,1408]{1,0:T(8,128)(2,1)}) %all-gather.34.cloned.1.call-update) | async-done | bytes 2883600 | tf_op jit(solution)/shard_map/all_gather | solution.py:43
  828.5 36.5 %reduce-scatter.23.cloned.1.call-done = bf16[256,1408]{1,0:T(8,128)(2,1)} async-done(((bf16[1024,1408]{1,0:T(8,128)(2,1)}), bf16[256,1408]{1,0:T(8,128)(2,1)}) %reduce-scatter.23.cloned.1.call-update) | async-done | bytes 720912 | tf_op jit(solution)/shard_map/reduce_scatter | solution.py:47
  877.0 21.1 all-gather.36.cloned.1.call-done
  907.3 49.9 %while.96 = (s32[]{:T(128)}, f32[333,4,88]{0,2,1:T(8,128)}, f32[333,4,88]{0,2,1:T(8,128)}, f32[2,512,4,88]{1,0,3,2:T(2,128)}, bf16[2,512,4,88]{1,3,2,0:T(8,128)(...) while((s32[]{:T(128)}, f32[333,4,88]{0,2,1:T(8,128)}, ...), condition=%wide.region_33.34_spmd.clone, body=%wide.region_31.33_spmd.clone.sunk | while | flops 606366080 | bytes 28269272 | solution.py:140
  991.6 36.4 %reduce-scatter.25.cloned.1.call-done = bf16[256,1408]{1,0:T(8,128)(2,1)} async-done(((bf16[1024,1408]{1,0:T(8,128)(2,1)}), bf16[256,1408]{1,0:T(8,128)(2,1)}) %reduce-scatter.25.cloned.1.call-update) | async-done | bytes 720912 | tf_op jit(solution)/shard_map/reduce_scatter | solution.py:47
  1034.6 27.0 %all-gather.38.cloned.1.call-done = bf16[1024,1408]{1,0:T(8,128)(2,1)} async-done(((bf16[256,1408]{1,0:T(8,128)(2,1)}), bf16[1024,1408]{1,0:T(8,128)(2,1)}) %all-gather.38.cloned.1.call-update) | async-done | bytes 2883600 | tf_op jit(solution)/shard_map/all_gather | solution.py:43
  1070.0 59.7 %while.97 = (s32[]{:T(128)}, f32[1024,4,88]{0,2,1:T(8,128)S(1)}, f32[1024,4,88]{0,2,1:T(8,128)}, f32[2,512,4,88]{1,0,3,2:T(2,128)}, bf16[2,512,4,88]{1,3,2,0:T(8...) while((s32[]{:T(128)}, f32[1024,4,88]{0,2,1:T(8,128)S(1)}, ...), condition=%wide.region_41.42_spmd.clone, body=%wide.region_39.41_spmd.clone.sunk | while | flops 1872640000 | bytes 84599024 | solution.py:140
  1194.7 30.8 %reduce-scatter.27.cloned.1.call-done = bf16[256,1408]{1,0:T(8,128)(2,1)} async-done(((bf16[1024,1408]{1,0:T(8,128)(2,1)}), bf16[256,1408]{1,0:T(8,128)(2,1)}) %reduce-scatter.27.cloned.1.call-update) | async-done | bytes 720912 | tf_op jit(solution)/shard_map/reduce_scatter | solution.py:47
  1344.4 61.0 %reduce-scatter.43.cloned.1.call-done = f32[352,176]{0,1:T(8,128)} async-done(((f32[352,1408]{0,1:T(8,128)}), f32[352,176]{0,1:T(8,128)}) %reduce-scatter.43.cloned.1.call-update) | async-done | bytes 247824 | tf_op jit(solution)/shard_map/reduce_scatter | solution.py:445
  1405.4 71.2 %reduce-scatter.39.cloned.1.call-done = f32[176,352]{1,0:T(8,128)} async-done(((f32[1408,352]{1,0:T(8,128)}), f32[176,352]{1,0:T(8,128)}) %reduce-scatter.39.cloned.1.call-update) | async-done | bytes 247824 | tf_op jit(solution)/shard_map/reduce_scatter | solution.py:443
  1476.7 75.2 %reduce-scatter.41.cloned.1.call-done = f32[128,2,352]{0,2,1:T(8,128)} async-done(((f32[1024,2,352]{0,2,1:T(8,128)}), f32[128,2,352]{0,2,1:T(8,128)}) %reduce-scatter.41.cloned.1.call-update) | async-done | bytes 360464 | tf_op jit(solution)/shard_map/reduce_scatter | solution.py:444
  1551.9 157.2 %reduce-scatter.47.cloned.1.call-done = f32[1536,176]{0,1:T(8,128)} async-done(((f32[1536,1408]{0,1:T(8,128)}), f32[1536,176]{0,1:T(8,128)}) %reduce-scatter.47.cloned.1.call-update) | async-done | bytes 1081360 | tf_op jit(solution)/shard_map/reduce_scatter | solution.py:447
  1709.1 157.0 %reduce-scatter.45.cloned.1.call-done = f32[176,1536]{1,0:T(8,128)} async-done(((f32[1408,1536]{1,0:T(8,128)}), f32[176,1536]{1,0:T(8,128)}) %reduce-scatter.45.cloned.1.call-update) | async-done | bytes 1081360 | tf_op jit(solution)/shard_map/reduce_scatter | solution.py:446
  1866.1 71.3 %reduce-scatter.37.cloned.1.call-done = f32[352,176]{0,1:T(8,128)} async-done(((f32[352,1408]{0,1:T(8,128)}), f32[352,176]{0,1:T(8,128)}) %reduce-scatter.37.cloned.1.call-update) | async-done | bytes 247824 | tf_op jit(solution)/shard_map/reduce_scatter | solution.py:442
  1937.5 130.5 %all-reduce.17.cloned.1.call-done = (f32[4,1408]{1,0:T(4,128)}, f32[4,1408]{1,0:T(4,128)}, f32[4,88]{1,0:T(4,128)}, f32[4,88]{1,0:T(4,128)}, f32[5,1408]{1,0:T(8,128)}, /*index=5*/f32[6144]{0:T(1024)}, f32[4,1408]{1,0:T(4,128)}) async-done(((f32[4,1408]{1,0:T(4,128)}, f32[4,1408]{1,0:T(4,128)}, f32[4,88]{1,0:T(4,128)}, f32[4,88]{1,0:T(4,128)}, f32[5,1408]{1,0:T(8,128)}, /*index=5*/f32[6144]{0:T(1024)}, ...) | async-done | bytes 123152 | tf_op jit(solution)/shard_map/psum | solution.py:461
  2068.0 129.1 %reduce-scatter.35.cloned.1.call-done = f32[176,3,352]{2,0,1:T(8,128)} async-done(((f32[1408,3,352]{2,0,1:T(8,128)}), f32[176,3,352]{2,0,1:T(8,128)}) %reduce-scatter.35.cloned.1.call-update) | async-done | bytes 743440 | tf_op jit(solution)/shard_map/reduce_scatter | solution.py:441
  2197.0 93.1 %reduce-scatter.31.cloned.1.call-done = f32[352,352]{1,0:T(8,128)} async-done(((f32[2816,352]{1,0:T(8,128)}), f32[352,352]{1,0:T(8,128)}) %reduce-scatter.31.cloned.1.call-update) | async-done | bytes 495632 | tf_op jit(solution)/shard_map/reduce_scatter | solution.py:439
  2290.2 145.8 %reduce-scatter.33.cloned.1.call-done = f32[176,1408]{1,0:T(8,128)} async-done(((f32[1408,1408]{1,0:T(8,128)}), f32[176,1408]{1,0:T(8,128)}) %reduce-scatter.33.cloned.1.call-update) | async-done | bytes 991248 | tf_op jit(solution)/shard_map/reduce_scatter | solution.py:440
  (721 shorter events, 605.4 us)
Async XLA Ops:
  7.2 55.7 %all-gather.16.cloned.1.call-start = ((), (), s32[]{:S(2)}) async-start(), calls=%async_computation.19 | async-start | bytes 2433024 | tf_op jit(solution)/shard_map/all_gather | solution.py:203
  7.9 99.1 %all-gather.14.cloned.1.call-start = ((), (), s32[]{:S(2)}) async-start(), calls=%async_computation.18 | async-start | bytes 7208960 | tf_op jit(solution)/shard_map/all_gather | solution.py:43
  10.5 169.2 %all-gather.18.cloned.1.call-start = ((), (), s32[]{:S(2)}) async-start(), calls=%async_computation.20 | async-start | bytes 4460544 | tf_op jit(solution)/shard_map/all_gather | solution.py:204
  11.3 240.6 %all-gather.22.cloned.1.call-start = ((), (), s32[]{:S(2)}) async-start(), calls=%async_computation.22 | async-start | bytes 3649536 | tf_op jit(solution)/shard_map/all_gather | solution.py:205
  113.5 69.0 %all-to-all-start = ((bf16[4,256,352]{1,2,0:T(8,128)(2,1)}), bf16[4,256,352]{1,2,0:T(8,128)(2,1)S(1)}, u32[]{:S(2)}, u32[]{:S(2)}) async-start(bf16[4,256,352]{1,2,0:T(8,128)(2,1)} %bitcast.352), calls=%async_computation | async-start | bytes 1441792 | tf_op jit(solution)/shard_map/all_to_all | solution.py:236
  117.0 164.1 %all-gather.20.cloned.1.call-start = ((), (), s32[]{:S(2)}) async-start(), calls=%async_computation.21 | async-start | bytes 3604480 | tf_op jit(solution)/shard_map/all_gather | solution.py:43
  189.5 193.0 %reduce-scatter.17.cloned.1.call-start = ((), (), s32[]{:S(2)}) async-start(), calls=%async_computation.23 | async-start | bytes 3604480 | tf_op jit(solution)/shard_map/reduce_scatter | solution.py:47
  346.1 113.4 %all-gather.26.cloned.1.call-start = ((), (), s32[]{:S(2)}) async-start(), calls=%async_computation.25 | async-start | bytes 1622016 | tf_op jit(solution)/shard_map/all_gather | solution.py:208
  346.8 125.2 %all-gather.24.cloned.1.call-start = ((), (), s32[]{:S(2)}) async-start(), calls=%async_computation.24 | async-start | bytes 3604480 | tf_op jit(solution)/shard_map/all_gather | solution.py:43
  386.5 160.8 %reduce-scatter.19.cloned.1.call-start = ((), (), s32[]{:S(2)}) async-start(), calls=%async_computation.26 | async-start | bytes 3604480 | tf_op jit(solution)/shard_map/reduce_scatter | solution.py:47
  510.8 113.6 %all-gather.30.cloned.1.call-start = ((), (), s32[]{:S(2)}) async-start(), calls=%async_computation.28 | async-start | bytes 4866048 | tf_op jit(solution)/shard_map/all_gather | solution.py:210
  511.4 140.4 %all-gather.28.cloned.1.call-start = ((), (), s32[]{:S(2)}) async-start(), calls=%async_computation.27 | async-start | bytes 3604480 | tf_op jit(solution)/shard_map/all_gather | solution.py:43
  551.0 177.9 %all-gather.32.cloned.1.call-start = ((), (), s32[]{:S(2)}) async-start(), calls=%async_computation.29 | async-start | bytes 4866048 | tf_op jit(solution)/shard_map/all_gather | solution.py:211
  551.6 222.3 %reduce-scatter.21.cloned.1.call-start = ((), (), s32[]{:S(2)}) async-start(), calls=%async_computation.30 | async-start | bytes 3604480 | tf_op jit(solution)/shard_map/reduce_scatter | solution.py:47
  739.1 66.1 %all-gather.34.cloned.1.call-start = ((), (), s32[]{:S(2)}) async-start(), calls=%async_computation.31 | async-start | bytes 3604480 | tf_op jit(solution)/shard_map/all_gather | solution.py:43
  778.0 87.0 %reduce-scatter.23.cloned.1.call-start = ((), (), s32[]{:S(2)}) async-start(), calls=%async_computation.32 | async-start | bytes 3604480 | tf_op jit(solution)/shard_map/reduce_scatter | solution.py:47
  828.5 69.7 %all-gather.36.cloned.1.call-start = ((), (), s32[]{:S(2)}) async-start(), calls=%async_computation.33 | async-start | bytes 3604480 | tf_op jit(solution)/shard_map/all_gather | solution.py:43
  870.9 157.1 %reduce-scatter.25.cloned.1.call-start = ((), (), s32[]{:S(2)}) async-start(), calls=%async_computation.34 | async-start | bytes 3604480 | tf_op jit(solution)/shard_map/reduce_scatter | solution.py:47
  991.6 70.0 %all-gather.38.cloned.1.call-start = ((), (), s32[]{:S(2)}) async-start(), calls=%async_computation.35 | async-start | bytes 3604480 | tf_op jit(solution)/shard_map/all_gather | solution.py:43
  1034.4 191.2 %reduce-scatter.27.cloned.1.call-start = ((), (), s32[]{:S(2)}) async-start(), calls=%async_computation.36 | async-start | bytes 3604480 | tf_op jit(solution)/shard_map/reduce_scatter | solution.py:47
  1235.1 103.0 %all-reduce.15.cloned.1.call-start = ((), (), s32[]{:S(2)}) async-start(), calls=%async_computation.38 | async-start | bytes 1376256 | tf_op jit(solution)/shard_map/psum | solution.py:422
  1239.9 101.4 %reduce-scatter.29.cloned.1.call-start = ((), (), s32[]{:S(2)}) async-start(), calls=%async_computation.37 | async-start | bytes 7208960 | tf_op jit(solution)/shard_map/reduce_scatter | solution.py:47
  1253.1 152.3 %reduce-scatter.43.cloned.1.call-start = ((), (), s32[]{:S(2)}) async-start(), calls=%async_computation.45 | async-start | bytes 2433024 | tf_op jit(solution)/shard_map/reduce_scatter | solution.py:445
  1259.1 217.6 %reduce-scatter.39.cloned.1.call-start = ((), (), s32[]{:S(2)}) async-start(), calls=%async_computation.43 | async-start | bytes 2433024 | tf_op jit(solution)/shard_map/reduce_scatter | solution.py:443
  1265.1 286.8 %reduce-scatter.41.cloned.1.call-start = ((), (), s32[]{:S(2)}) async-start(), calls=%async_computation.44 | async-start | bytes 3244032 | tf_op jit(solution)/shard_map/reduce_scatter | solution.py:444
  1268.6 440.5 %reduce-scatter.47.cloned.1.call-start = ((), (), s32[]{:S(2)}) async-start(), calls=%async_computation.47 | async-start | bytes 9732096 | tf_op jit(solution)/shard_map/reduce_scatter | solution.py:447
  1281.2 585.0 %reduce-scatter.45.cloned.1.call-start = ((), (), s32[]{:S(2)}) async-start(), calls=%async_computation.46 | async-start | bytes 9732096 | tf_op jit(solution)/shard_map/reduce_scatter | solution.py:446
  1292.9 644.5 %reduce-scatter.37.cloned.1.call-start = ((), (), s32[]{:S(2)}) async-start(), calls=%async_computation.42 | async-start | bytes 2433024 | tf_op jit(solution)/shard_map/reduce_scatter | solution.py:442
  1299.0 768.9 %all-reduce.17.cloned.1.call-start = ((), (), s32[]{:S(2)}) async-start(), calls=%async_computation.48 | async-start | bytes 282624 | tf_op jit(solution)/shard_map/psum | solution.py:461
  1315.5 881.5 %reduce-scatter.35.cloned.1.call-start = ((), (), s32[]{:S(2)}) async-start(), calls=%async_computation.41 | async-start | bytes 7299072 | tf_op jit(solution)/shard_map/reduce_scatter | solution.py:441
  1324.7 965.4 %reduce-scatter.31.cloned.1.call-start = ((), (), s32[]{:S(2)}) async-start(), calls=%async_computation.39 | async-start | bytes 4866048 | tf_op jit(solution)/shard_map/reduce_scatter | solution.py:439
  1333.7 1102.3 %reduce-scatter.33.cloned.1.call-start = ((), (), s32[]{:S(2)}) async-start(), calls=%async_computation.40 | async-start | bytes 8921088 | tf_op jit(solution)/shard_map/reduce_scatter | solution.py:440
  (157 other events, 3709.0 us)
Sparse Core Ops, SparseCore 0:
  10.2 52.6 all-gather.15
  65.0 41.9 all-gather.13
  109.2 70.4 all-gather.17
  181.8 70.0 all-gather.21
  253.9 27.1 all-gather.19
  346.2 36.3 reduce-scatter.16
  384.8 57.5 all-gather.25
  444.6 27.3 all-gather.23
  510.9 36.3 reduce-scatter.18
  549.3 75.0 all-gather.29
  626.5 25.2 all-gather.27
  653.9 74.9 all-gather.31
  739.2 34.5 reduce-scatter.20
  778.1 27.0 all-gather.33
  828.6 36.3 reduce-scatter.22
  871.0 27.0 all-gather.35
  991.7 36.3 reduce-scatter.24
  1034.5 27.0 all-gather.37
  1189.2 36.3 reduce-scatter.26
  1240.0 35.3 all-reduce.14
  1278.1 55.1 reduce-scatter.28
  1337.3 68.0 reduce-scatter.42
  1409.5 67.1 reduce-scatter.38
  1480.6 71.1 reduce-scatter.40
  1556.1 153.0 reduce-scatter.46
  1713.6 152.4 reduce-scatter.44
  1870.0 67.3 reduce-scatter.36
  1945.0 122.8 all-reduce.16
  2072.6 124.3 reduce-scatter.34
  2201.0 89.0 reduce-scatter.30
  2294.8 141.1 reduce-scatter.32
where the time goes:
time: 2470 us; the launch traced here: 2450 us
  waiting for transfers between devices  1750 us (71%)
  matrix products  207 us (8%)
  local copies, waits for them, and re-layouts  199 us (8%)
  other arithmetic  137 us (6%)
  blocking collectives  127 us (5%)
    reduce_scatter x7, waiting for transfers between devices, collect_rows(): lax.psum_scatter(row_fn(jnp.int32(0), local_rows * lax.axis_size('tensor'...  198 us
    all_gather x7, waiting for transfers between devices, spread_rows(): return lax.all_gather(values, 'tensor', axis=0, tiled=True)  184 us
    reduce_scatter x1, waiting for transfers between devices, body(): lax.psum_scatter(grad_down, 'dp', scatter_dimension=1, tiled=True)  157 us
    reduce_scatter x1, waiting for transfers between devices, body(): lax.psum_scatter(grad_up, 'dp', scatter_dimension=0, tiled=True)  157 us
    reduce_scatter x1, waiting for transfers between devices, body(): lax.psum_scatter(grad_shift_proj, 'dp', scatter_dimension=0, tiled=True)  146 us
    psum x1, waiting for transfers between devices, body(): lax.psum((norm_gain_part, norm_bias_part, head_gain_part, head_bias_part,...  130 us
    reduce_scatter x1, waiting for transfers between devices, body(): lax.psum_scatter(grad_project, 'dp', scatter_dimension=0, tiled=True)  129 us
    reduce_scatter x1, waiting for transfers between devices, body(): lax.psum_scatter(grad_skip_proj, 'dp', scatter_dimension=0, tiled=True)  93.1 us
  transfers between devices with their start and end apart: 33, of which 29 were waited for; matrix products, arithmetic and copies ran while one was open for 6% of the time, Pallas kernels for 0%

commit v1 on v0

v1 whole, which is shorter than its diff:
```python
import functools

import jax
import jax.numpy as jnp
import numpy as np
from jax import lax
from jax.experimental import pallas as pl
from jax.experimental.pallas import tpu as pltpu
from jax.sharding import PartitionSpec as P

EPSILON = 1e-06
MESH = pl.DeviceIdType.MESH
BF16, F32 = jnp.bfloat16, jnp.float32
LANES = 128
CHUNKS = 2
VMEM_BYTES = 56 * 2**20
NEGATIVE = -1e30


def dot_nn(left, right):
    return jnp.dot(left, right, preferred_element_type=F32)


def dot_nt(left, right):
    return lax.dot_general(left, right, (((1,), (1,)), ((), ())), preferred_element_type=F32)


def dot_tn(left, right):
    return lax.dot_general(left, right, (((0,), (0,)), ((), ())), preferred_element_type=F32)


def centre(x):
    cen = x - jnp.mean(x, axis=-1, keepdims=True)
    spread = jnp.mean(cen * cen, axis=-1, keepdims=True)
    return cen, lax.rsqrt(spread + EPSILON)


def norm_back(total, x, gain):
    cen, rstd = centre(x)
    xhat = cen * rstd
    dg = total * gain
    back = rstd * (
        dg - jnp.mean(dg, axis=-1, keepdims=True) - xhat * jnp.mean(dg * xhat, axis=-1, keepdims=True)
    )
    return back, xhat


def remote(src, dst, send_sem, recv_sem, device):
    return pltpu.make_async_remote_copy(
        src_ref=src, dst_ref=dst, send_sem=send_sem, recv_sem=recv_sem, device_id=device, device_id_type=MESH
    )


def tensor_place():
    d, t = lax.axis_index("dp"), lax.axis_index("tensor")
    y, c = t // 2, t % 2
    return d, t, y, c, (d, 2 * y + 1 - c), (d, 2 * (1 - y) + c)


def greet(peers):
    bar = pltpu.get_barrier_semaphore()
    for peer in peers:
        pl.semaphore_signal(bar, inc=1, device_id=peer, device_id_type=MESH)
    return bar


def gather_body(n_rows, n_weights, dp, *refs):
    n = n_rows + n_weights
    ins, outs = refs[:n], refs[n : 2 * n]
    own_sem, core_s, core_r, y_s, y_r, fw_s, fw_r, z_s, z_r, x_s, x_r = refs[2 * n :]
    d, t, y, c, sib, yp = tensor_place()
    line = dp // 2
    zi, par = d // 2, d % 2
    xp = (2 * zi + 1 - par, t)
    zps = [(2 * ((zi + j) % line) + par, t) for j in range(1, line)]
    peers = ([sib, yp] if n_rows else []) + ([xp] + zps if n_weights else [])
    bar = greet(peers)
    locals_ = []
    for i in range(n):
        me = t if i < n_rows else d
        cp = pltpu.make_async_copy(ins[i], outs[i].at[me], own_sem.at[i])
        cp.start()
        locals_.append(cp)
    pl.semaphore_wait(bar, len(peers))
    row_cps = []
    z_cps = [[] for _ in range(n_weights)]
    x_cps = []

    def start_z(w):
        src, dst = ins[n_rows + w], outs[n_rows + w]
        for j in range(1, line):
            cp = remote(src, dst.at[d], z_s.at[w, j], z_r.at[w, j], zps[j - 1])
            cp.start()
            z_cps[w].append(cp)
        cp = remote(src, dst.at[d], x_s.at[w, 0], x_r.at[w, 0], xp)
        cp.start()
        x_cps.append(cp)

    def forward_z(w):
        dst = outs[n_rows + w]
        for j in range(1, line):
            z_cps[w][j - 1].wait_recv()
            source = 2 * ((zi + line - j) % line) + par
            cp = remote(dst.at[source], dst.at[source], x_s.at[w, j], x_r.at[w, j], xp)
            cp.start()
            x_cps.append(cp)

    if n_weights:
        start_z(0)
    for i in range(n_rows):
        a = remote(ins[i], outs[i].at[t], y_s.at[i], y_r.at[i], yp)
        b = remote(ins[i], outs[i].at[t], core_s.at[i], core_r.at[i], sib)
        a.start()
        b.start()
        row_cps.append((a, b))
    for w in range(n_weights):
        forward_z(w)
        if w + 1 < n_weights:
            start_z(w + 1)
    fws = []
    yt = 2 * (1 - y) + c
    for i in range(n_rows):
        row_cps[i][0].wait_recv()
        cp = remote(outs[i].at[yt], outs[i].at[yt], fw_s.at[i], fw_r.at[i], sib)
        cp.start()
        fws.append(cp)
    for cp in locals_:
        cp.wait()
    for i in range(n_rows):
        a, b = row_cps[i]
        b.wait_recv()
        fws[i].wait_recv()
        a.wait_send()
        b.wait_send()
        fws[i].wait_send()
    for cps in z_cps:
        for cp in cps:
            cp.wait_send()
    for cp in x_cps:
        cp.wait_recv()
        cp.wait_send()


def gather_kernel(name, collective_id, dp, rows, weights=()):
    n_rows, n_weights = len(rows), len(weights)
    n = n_rows + n_weights
    dma = pltpu.SemaphoreType.DMA
    r, w, k = max(n_rows, 1), max(n_weights, 1), max(dp // 2, 1)
    outs = [jax.ShapeDtypeStruct((4,) + v.shape, v.dtype) for v in rows]
    outs += [jax.ShapeDtypeStruct((dp,) + v.shape, v.dtype) for v in weights]
    anywhere = pl.BlockSpec(memory_space=pl.ANY)
    return pl.pallas_call(
        functools.partial(gather_body, n_rows, n_weights, dp),
        out_shape=outs,
        in_specs=[anywhere] * n,
        out_specs=[anywhere] * n,
        scratch_shapes=[dma((n,))] + [dma((r,))] * 6 + [dma((w, k))] * 4,
        compiler_params=pltpu.CompilerParams(collective_id=collective_id, has_side_effects=True),
        name=name,
    )(*rows, *weights)


def row_body(mode, rows, n_in, n_out, *refs):
    ins, outs, scr = refs[:n_in], refs[n_in : n_in + n_out], refs[n_in + n_out :]
    lhs, w = ins[0], ins[1]
    far, near, csend, crecv, ysend, yrecv, cs, cr, ys, yr, gcs, gcr, gys, gyr, fs, fr = scr
    d, t, y, c, sib, yp = tensor_place()
    bar = greet((sib, yp))
    ch = rows // CHUNKS

    def partial_rows(base, acc):
        for r in range(2):
            here = pl.ds(pl.multiple_of(base + r * rows, rows), rows)
            acc[pl.ds(r * rows, rows), :] = dot_nt(lhs[here, :], w[...])

    def chunk_of(acc, k):
        return acc[pl.ds(pl.multiple_of(c * rows + k * ch, ch), ch), :]

    other = pl.ds(pl.multiple_of((1 - c) * rows, rows), rows)
    partial_rows((1 - y) * 2 * rows, far)
    csend[0] = far[other, :].astype(BF16)
    pl.semaphore_wait(bar, 2)
    c0 = remote(csend.at[0], crecv.at[0], cs.at[0], cr.at[0], sib)
    c0.start()
    c0.wait_recv()
    ycs = []
    for k in range(CHUNKS):
        sl = pl.ds(k * ch, ch)
        ysend[sl, :] = (chunk_of(far, k) + crecv[0, sl, :].astype(F32)).astype(BF16)
        cp = remote(ysend.at[sl], yrecv.at[sl], ys.at[k], yr.at[k], yp)
        cp.start()
        ycs.append(cp)
    partial_rows(y * 2 * rows, near)
    csend[1] = near[other, :].astype(BF16)
    c1 = remote(csend.at[1], crecv.at[1], cs.at[1], cr.at[1], sib)
    c1.start()
    c1.wait_recv()
    gathers = mode in ("fwd", "final", "bwd")
    sums = None
    ags = []
    for k in range(CHUNKS):
        sl = pl.ds(k * ch, ch)
        ycs[k].wait_recv()
        total = chunk_of(near, k) + crecv[1, sl, :].astype(F32) + yrecv[sl, :].astype(F32)
        parts = []
        if mode == "fwd":
            resid, bias, gain, offset = ins[2:]
            second = resid[sl, :] + (total + bias[...])
            outs[1][sl, :] = second
            cen, rstd = centre(second)
            low = (cen * rstd * gain[...] + offset[...]).astype(BF16)
        elif mode == "final":
            third, bias, teacher, weight = ins[2:]
            final = third[sl, :] + (total + bias[...])
            outs[1][sl, :] = final.astype(BF16)
            grad = weight[sl, :] * (final - teacher[sl, :].astype(F32))
            outs[2][sl, :] = grad
            low = grad.astype(BF16)
            parts = [low.astype(F32)]
        elif mode == "bwd":
            x, gain, before = ins[2:]
            back, xhat = norm_back(total, x[sl, :], gain[...])
            grad = before[sl, :] + back
            outs[1][sl, :] = grad
            low = grad.astype(BF16)
            parts = [low.astype(F32), total * xhat, total]
        elif mode == "first":
            x, gain, before, skipped, gain0 = ins[2:]
            back, xhat = norm_back(total, x[sl, :], gain[...])
            grad = before[sl, :] + back
            back0, xhat0 = norm_back(grad, skipped[sl, :].astype(F32), gain0[...])
            low = back0.astype(BF16)
            outs[0][sl, :] = low
            parts = [low.astype(F32), total * xhat, total, grad * xhat0, grad]
        else:
            outs[0][sl, :] = total
        parts = [jnp.sum(p, axis=0, keepdims=True) for p in parts]
        sums = parts if sums is None else [a + b for a, b in zip(sums, parts)]
        if gathers:
            here = pl.ds(pl.multiple_of(t * rows + k * ch, ch), ch)
            spread = outs[0]
            spread[here, :] = low
            a = remote(spread.at[here], spread.at[here], gys.at[k], gyr.at[k], yp)
            b = remote(spread.at[here], spread.at[here], gcs.at[k], gcr.at[k], sib)
            a.start()
            b.start()
            ags.append((a, b))
    for i, s in enumerate(sums):
        outs[n_out - len(sums) + i][...] = s
    if gathers:
        fws = []
        for k in range(CHUNKS):
            ags[k][0].wait_recv()
            there = pl.ds(pl.multiple_of((2 * (1 - y) + c) * rows + k * ch, ch), ch)
            cp = remote(spread.at[there], spread.at[there], fs.at[k], fr.at[k], sib)
            cp.start()
            fws.append(cp)
        for k in range(CHUNKS):
            a, b = ags[k]
            b.wait_recv()
            fws[k].wait_recv()
            a.wait_send()
            b.wait_send()
            fws[k].wait_send()
    c0.wait_send()
    c1.wait_send()
    for cp in ycs:
        cp.wait_send()


def row_kernel(mode, name, collective_id, lhs, w, *extra):
    rows = lhs.shape[0] // 4
    width = w.shape[0]
    full = jax.ShapeDtypeStruct((4 * rows, width), BF16)
    mine = jax.ShapeDtypeStruct((rows, width), F32)
    mine_low = jax.ShapeDtypeStruct((rows, width), BF16)
    line = jax.ShapeDtypeStruct((1, width), F32)
    outs = {
        "fwd": [full, mine],
        "final": [full, mine_low, mine, line],
        "bwd": [full, mine, line, line, line],
        "first": [mine_low] + [line] * 5,
        "plain": [mine],
    }[mode]
    ins = [lhs, w, *extra]
    vm = pl.BlockSpec(memory_space=pltpu.VMEM)
    dma = pltpu.SemaphoreType.DMA
    return pl.pallas_call(
        functools.partial(row_body, mode, rows, len(ins), len(outs)),
        out_shape=outs,
        in_specs=[vm] * len(ins),
        out_specs=[vm] * len(outs),
        scratch_shapes=[
            pltpu.VMEM((2 * rows, width), F32),
            pltpu.VMEM((2 * rows, width), F32),
            pltpu.VMEM((2, rows, width), BF16),
            pltpu.VMEM((2, rows, width), BF16),
            pltpu.VMEM((rows, width), BF16),
            pltpu.VMEM((rows, width), BF16),
            dma((2,)),
            dma((2,)),
        ]
        + [dma((CHUNKS,))] * 8,
        compiler_params=pltpu.CompilerParams(
            collective_id=collective_id, has_side_effects=True, vmem_limit_bytes=VMEM_BYTES
        ),
        name=name,
    )(*ins)


def head_stats(u, mask, size):
    mean = jnp.sum(u, axis=-1, keepdims=True) * (1.0 / size)
    cen = (u - mean) * mask
    spread = jnp.sum(cen * cen, axis=-1, keepdims=True) * (1.0 / size)
    return cen, lax.rsqrt(spread + EPSILON)


def head_norm(u, mask, gain, offset, size):
    cen, rstd = head_stats(u, mask, size)
    return cen * rstd * gain + offset


def turn(u, cosine, sine):
    return u * cosine + pltpu.roll(u, LANES // 2, 1) * sine


def turn_back(u, cosine, sine):
    return u * cosine - pltpu.roll(u, LANES // 2, 1) * sine


def head_back(grad, u, mask, gain, size):
    cen, rstd = head_stats(u, mask, size)
    xhat = cen * rstd
    dg = grad * gain
    mean = jnp.sum(dg, axis=-1, keepdims=True) * (1.0 / size)
    inner = jnp.sum(dg * xhat, axis=-1, keepdims=True) * (1.0 / size)
    back = rstd * ((dg - mean) * mask - xhat * inner)
    return back, jnp.sum(grad * xhat, axis=0, keepdims=True), jnp.sum(grad, axis=0, keepdims=True)


def head_at(h):
    return pl.ds(h * LANES, LANES)


def attend(q_ref, k_ref, v_ref, out_ref, lse_ref, heads, scale, block, real_keys):
    queries, keys = q_ref.shape[0], k_ref.shape[0]

    def step(i, _):
        here = pl.ds(pl.multiple_of(i * block, block), block)
        for h in range(heads):
            hs = head_at(h)
            scores = dot_nt(k_ref[:, hs], q_ref[here, hs]) * scale
            if real_keys < keys:
                place = lax.broadcasted_iota(jnp.int32, scores.shape, 0)
                scores = jnp.where(place < real_keys, scores, NEGATIVE)
            highest = jnp.max(scores, axis=0, keepdims=True)
            exponent = jnp.exp(scores - highest)
            denominator = jnp.sum(exponent, axis=0, keepdims=True)
            probs = (exponent * (1.0 / denominator)).astype(BF16)
            mixed = dot_tn(v_ref[:, hs], probs)
            out_ref[here, hs] = mixed.T.astype(BF16)
            lse_ref[i, pl.ds(h, 1), :] = highest + jnp.log(denominator)
        return 0

    lax.fori_loop(0, queries // block, step, 0)


def attend_back(q_ref, k_ref, v_ref, do_ref, lse_ref, dq_ref, dk_ref, dv_ref, heads, scale, block, real_keys):
    queries, keys = q_ref.shape[0], k_ref.shape[0]
    dk_ref[...] = jnp.zeros(dk_ref.shape, F32)
    dv_ref[...] = jnp.zeros(dv_ref.shape, F32)

    def step(i, _):
        here = pl.ds(pl.multiple_of(i * block, block), block)
        for h in range(heads):
            hs = head_at(h)
            q, k, v, do = q_ref[here, hs], k_ref[:, hs], v_ref[:, hs], do_ref[here, hs]
            scores = dot_nt(k, q) * scale
            if real_keys < keys:
                place = lax.broadcasted_iota(jnp.int32, scores.shape, 0)
                scores = jnp.where(place < real_keys, scores, NEGATIVE)
            probs = jnp.exp(scores - lse_ref[i, pl.ds(h, 1), :])
            grad_probs = dot_nt(v, do)
            inner = jnp.sum(probs * grad_probs, axis=0, keepdims=True)
            grad_scores = (probs * (grad_probs - inner)).astype(BF16)
            dv_ref[:, hs] += dot_nn(probs.astype(BF16), do)
            dk_ref[:, hs] += dot_nn(grad_scores, q) * scale
            dq_ref[here, hs] = dot_tn(k, grad_scores).T * scale
        return 0

    lax.fori_loop(0, queries // block, step, 0)


def self_fwd_body(size, scale, heads, block, x, w, bias, cosine, sine, gain, offset, mask, fold, pre, low, mixed, lse, padded):
    rows = x.shape[0]
    span = heads * LANES

    def project(i, _):
        here = pl.ds(pl.multiple_of(i * block, block), block)
        for part in range(3):
            cols = pl.ds(part * span, span)
            out = dot_nn(x[here, :], w[part]) + bias[part]
            if part < 2:
                pre[here, cols] = out
                for h in range(heads):
                    u = out[:, h * LANES : (h + 1) * LANES]
                    val = head_norm(u, mask[...], gain[pl.ds(part, 1), :], offset[pl.ds(part, 1), :], size)
                    val = turn(val, cosine[here, :], sine[here, :])
                    low[here, pl.ds(part * span + h * LANES, LANES)] = val.astype(BF16)
            else:
                low[here, cols] = out.astype(BF16)
        return 0

    lax.fori_loop(0, rows // block, project, 0)
    attend(
        low.at[:, pl.ds(0, span)], low.at[:, pl.ds(span, span)], low.at[:, pl.ds(2 * span, span)],
        padded, lse, heads, scale, block, rows,
    )
    mixed[...] = dot_nt(padded[...], fold[...]).astype(BF16)


def self_bwd_body(
    size, scale, heads, block, c_all, w_out, pre, low, lse, cosine, sine, gain, mask, fold,
    p, p_low, gains, offsets, sums, do, dq, dk, dv,
):
    rows = c_all.shape[0]
    span = heads * LANES

    def spread(i, _):
        here = pl.ds(pl.multiple_of(i * block, block), block)
        narrow = dot_nn(c_all[here, :], w_out[...]).astype(BF16)
        do[here, :] = dot_nn(narrow, fold[...]).astype(BF16)
        return 0

    lax.fori_loop(0, rows // block, spread, 0)
    attend_back(
        low.at[:, pl.ds(0, span)], low.at[:, pl.ds(span, span)], low.at[:, pl.ds(2 * span, span)],
        do, lse, dq, dk, dv, heads, scale, block, rows,
    )
    gains[...] = jnp.zeros(gains.shape, F32)
    offsets[...] = jnp.zeros(offsets.shape, F32)
    sums[...] = jnp.zeros(sums.shape, F32)

    def finish(i, _):
        here = pl.ds(pl.multiple_of(i * block, block), block)
        for part, grad_ref in enumerate((dq, dk, dv)):
            for h in range(heads):
                hs = head_at(h)
                wide = pl.ds(part * span + h * LANES, LANES)
                grad = grad_ref[here, hs]
                if part < 2:
                    grad = turn_back(grad, cosine[here, :], sine[here, :])
                    grad, g, o = head_back(grad, pre[here, wide], mask[...], gain[pl.ds(part, 1), :], size)
                    gains[pl.ds(part, 1), :] += g
                    offsets[pl.ds(part, 1), :] += o
                grad_low = grad.astype(BF16)
                p[here, wide] = grad_low
                if part != 1:
                    sums[:, wide] += jnp.sum(grad_low.astype(F32), axis=0, keepdims=True)
            p_low[part, here, :] = dot_nt(p[here, pl.ds(part * span, span)], fold[...]).astype(BF16)
        return 0

    lax.fori_loop(0, rows // block, finish, 0)


def text_body(size, heads, real, x, w, bias, gain, offset, mask, pre, low):
    span = heads * LANES
    for part in range(2):
        out = dot_nn(x[...], w[part]) + bias[part]
        if part == 0:
            pre[...] = out
            for h in range(heads):
                hs = head_at(h)
                val = head_norm(out[:, h * LANES : (h + 1) * LANES], mask[...], gain[...], offset[...], size)
                low[:, hs] = val.astype(BF16)
        else:
            low[:, pl.ds(span, span)] = out.astype(BF16)


def cross_fwd_body(
    size, scale, heads, block, real, x, w, bias, text_low, cosine, sine, gain, offset, mask, fold,
    pre, low, mixed, lse, padded,
):
    rows = x.shape[0]
    span = heads * LANES

    def project(i, _):
        here = pl.ds(pl.multiple_of(i * block, block), block)
        out = dot_nn(x[here, :], w[...]) + bias[...]
        pre[here, :] = out
        for h in range(heads):
            val = head_norm(out[:, h * LANES : (h + 1) * LANES], mask[...], gain[...], offset[...], size)
            low[here, head_at(h)] = turn(val, cosine[here, :], sine[here, :]).astype(BF16)
        return 0

    lax.fori_loop(0, rows // block, project, 0)
    attend(low, text_low.at[:, pl.ds(0, span)], text_low.at[:, pl.ds(span, span)], padded, lse, heads, scale, block, real)
    mixed[...] = dot_nt(padded[...], fold[...]).astype(BF16)


def cross_bwd_body(
    size, scale, heads, block, real, c_all, w_out, pre, low, text_pre, text_low, lse, cosine, sine, gain, text_gain, mask, fold,
    p, p_low, text_p, text_p_low, gains, offsets, sums, text_sums, do, dq, dk, dv,
):
    rows = c_all.shape[0]
    span = heads * LANES

    def spread(i, _):
        here = pl.ds(pl.multiple_of(i * block, block), block)
        narrow = dot_nn(c_all[here, :], w_out[...]).astype(BF16)
        do[here, :] = dot_nn(narrow, fold[...]).astype(BF16)
        return 0

    lax.fori_loop(0, rows // block, spread, 0)
    attend_back(
        low, text_low.at[:, pl.ds(0, span)], text_low.at[:, pl.ds(span, span)],
        do, lse, dq, dk, dv, heads, scale, block, real,
    )
    gains[...] = jnp.zeros(gains.shape, F32)
    offsets[...] = jnp.zeros(offsets.shape, F32)
    sums[...] = jnp.zeros(sums.shape, F32)

    def finish(i, _):
        here = pl.ds(pl.multiple_of(i * block, block), block)
        for h in range(heads):
            hs = head_at(h)
            grad = turn_back(dq[here, hs], cosine[here, :], sine[here, :])
            grad, g, o = head_back(grad, pre[here, hs], mask[...], gain[...], size)
            gains[pl.ds(0, 1), :] += g
            offsets[pl.ds(0, 1), :] += o
            grad_low = grad.astype(BF16)
            p[here, hs] = grad_low
            sums[:, hs] += jnp.sum(grad_low.astype(F32), axis=0, keepdims=True)
        p_low[here, :] = dot_nt(p[here, :], fold[...]).astype(BF16)
        return 0

    lax.fori_loop(0, rows // block, finish, 0)
    for h in range(heads):
        hs = head_at(h)
        grad, g, o = head_back(dk[:, hs], text_pre[:, hs], mask[...], text_gain[...], size)
        gains[pl.ds(1, 1), :] += g
        offsets[pl.ds(1, 1), :] += o
        text_p[:, hs] = grad.astype(BF16)
        low_v = dv[:, hs].astype(BF16)
        text_p[:, pl.ds(span + h * LANES, LANES)] = low_v
        text_sums[:, hs] = jnp.sum(low_v.astype(F32), axis=0, keepdims=True)
    for part in range(2):
        text_p_low[part] = dot_nt(text_p[:, pl.ds(part * span, span)], fold[...]).astype(BF16)


def local_kernel(name, body, ins, outs, scratch=()):
    vm = pl.BlockSpec(memory_space=pltpu.VMEM)
    return pl.pallas_call(
        body,
        out_shape=outs,
        in_specs=[vm] * len(ins),
        out_specs=[vm] * len(outs),
        scratch_shapes=list(scratch),
        compiler_params=pltpu.CompilerParams(vmem_limit_bytes=VMEM_BYTES),
        name=name,
    )(*ins)


def shaped(shape, dtype):
    return jax.ShapeDtypeStruct(shape, dtype)


def fold_matrix(heads, size):
    out = np.zeros((heads * size, heads * LANES), np.float32)
    for h in range(heads):
        for e in range(size):
            out[h * size + e, h * LANES + (e % 2) * (LANES // 2) + e // 2] = 1.0
    return out


def body(
    latent, skip_states, text_states, condition, teacher, loss_mask, true_counts, positions,
    skip_proj, shift_proj, self_project, self_output, cross_query, cross_keyval, cross_output, hidden_up, hidden_down,
    norm_gain, norm_bias, head_gain, head_bias, column_bias, hidden_bias, row_bias,
):
    d, t = lax.axis_index("dp"), lax.axis_index("tensor")
    dp, tensor = lax.axis_size("dp"), lax.axis_size("tensor")
    rows, width = latent.shape
    group = rows * tensor
    size = head_gain.shape[1]
    cols = self_project.shape[2]
    heads = cols // size
    span = heads * LANES
    hidden = hidden_up.shape[1]
    text_len = text_states.shape[1]
    text_pad = -(-text_len // 16) * 16
    scale = size ** (-0.5)
    block = min(256, group)
    fold_np = fold_matrix(heads, size)
    fold = jnp.asarray(fold_np, BF16)
    one_np = fold_np[:size, :LANES]
    mask = jnp.asarray(one_np.sum(0, keepdims=True), F32)

    def widen_head(v):
        return jnp.dot(v, jnp.asarray(one_np), precision=lax.Precision.HIGHEST)

    def widen_cols(v):
        return jnp.dot(v, jnp.asarray(fold_np), precision=lax.Precision.HIGHEST)

    def narrow_head(v):
        return jnp.dot(v, jnp.asarray(one_np.T), precision=lax.Precision.HIGHEST)

    def narrow_cols(v):
        return jnp.dot(v, jnp.asarray(fold_np.T), precision=lax.Precision.HIGHEST)

    small = jnp.concatenate([condition.astype(F32), true_counts.astype(F32)[:, None]], axis=1)
    small_all = lax.all_gather(small, "dp", axis=0, tiled=True)
    counted = jnp.sum(small_all[:, width])
    silu_all = jax.nn.silu(small_all[:, :width]).astype(BF16)
    silu_mine = lax.dynamic_slice_in_dim(silu_all, d * shift_proj.shape[0], shift_proj.shape[0], 1)
    shift_term = lax.psum_scatter(dot_nn(silu_mine, shift_proj), "dp", scatter_dimension=0, tiled=True) + row_bias[3:4]

    project_in = jnp.transpose(self_project, (1, 0, 2))
    joined0, joined1, skip_g, project_g = gather_kernel(
        "gather_joined", 0, dp, (latent, skip_states), (skip_proj, project_in)
    )
    out_t = lax.all_gather(self_output.T, "dp", axis=0, tiled=True)
    query_full = lax.all_gather(cross_query, "dp", axis=0, tiled=True)
    keyval_in = jnp.transpose(cross_keyval, (1, 0, 2))
    keyval_g = lax.all_gather(keyval_in, "dp", axis=0, tiled=False)
    cross_out_t = lax.all_gather(cross_output.T, "dp", axis=0, tiled=True)
    up_full = lax.all_gather(hidden_up, "dp", axis=0, tiled=True)
    down_t = lax.all_gather(hidden_down.T, "dp", axis=0, tiled=True)

    skip_full = skip_g.reshape(2 * width, cols)
    project_full = jnp.transpose(project_g, (1, 0, 2, 3)).reshape(3, width, cols)
    project_wide = jnp.einsum("cdk,kl->cdl", project_full, fold, preferred_element_type=F32).astype(BF16)
    query_wide = dot_nn(query_full, fold).astype(BF16)
    keyval_full = jnp.transpose(keyval_g, (1, 0, 2, 3)).reshape(2, text_states.shape[2], cols)
    keyval_wide = jnp.einsum("cdk,kl->cdl", keyval_full, fold, preferred_element_type=F32).astype(BF16)

    bias_cols = lax.dynamic_slice_in_dim(column_bias, t * cols, cols, 1)
    bias_wide = widen_cols(bias_cols)
    zero_wide = jnp.zeros((1, span), F32)
    self_bias = jnp.stack([bias_wide[0:1], zero_wide, bias_wide[1:2]])
    text_bias = jnp.stack([zero_wide, bias_wide[3:4]])
    hidden_cols_bias = lax.dynamic_slice_in_dim(hidden_bias, t * hidden, hidden, 0)
    gain_wide, offset_wide = widen_head(head_gain), widen_head(head_bias)

    quarter = size // 4
    lane_np = np.zeros((2, LANES), np.float32)
    sign_np = np.zeros((1, LANES), np.float32)
    for i in range(size // 2):
        f = np.float32(10000.0 ** (-(i % quarter) / quarter))
        for half in range(2):
            lane_np[i // quarter, half * (LANES // 2) + i] = f
            sign_np[0, half * (LANES // 2) + i] = 2 * half - 1
    place = positions.astype(F32)
    angles = place[0][:, None] * lane_np[0] + place[1][:, None] * lane_np[1]
    cosine = jnp.cos(angles) * mask
    sine = jnp.sin(angles) * sign_np

    joined0 = joined0.reshape(group, width)
    joined1 = joined1.reshape(group, width)
    skip_pre = dot_nn(joined0, skip_full[:width]) + dot_nn(joined1, skip_full[width:]) + bias_cols[4]
    skipped = lax.all_to_all(skip_pre.astype(BF16), "tensor", split_axis=0, concat_axis=1, tiled=True)
    cen, rstd = centre(skipped.astype(F32))
    residual = cen * rstd * norm_gain[0] + norm_bias[0]
    cen, rstd = centre(residual)
    first_input = (cen * rstd * norm_gain[1] + norm_bias[1] + shift_term).astype(BF16)
    (first_all,) = gather_kernel("gather_first", 1, dp, (first_input,))
    first_all = first_all.reshape(group, width)

    lse_shape = (group // block, heads, block)
    pre, low, mixed, lse = local_kernel(
        "self_fwd",
        functools.partial(self_fwd_body, size, scale, heads, block),
        [first_all, project_wide, self_bias, cosine, sine, gain_wide[0:2], offset_wide[0:2], mask, fold],
        [shaped((group, 2 * span), F32), shaped((group, 3 * span), BF16), shaped((group, cols), BF16), shaped(lse_shape, F32)],
        [pltpu.VMEM((group, span), BF16)],
    )
    third_all, second = row_kernel(
        "fwd", "rows_self", 2, mixed, out_t, residual, row_bias[0:1], norm_gain[2:3], norm_bias[2:3]
    )

    text_rows = jnp.pad(text_states[0], ((0, text_pad - text_len), (0, 0)))
    text_pre, text_low = local_kernel(
        "text_fwd",
        functools.partial(text_body, size, heads, text_len),
        [text_rows, keyval_wide, text_bias, gain_wide[3:4], offset_wide[3:4], mask],
        [shaped((text_pad, span), F32), shaped((text_pad, 2 * span), BF16)],
    )
    cross_pre, cross_low, cross_mixed, cross_lse = local_kernel(
        "cross_fwd",
        functools.partial(cross_fwd_body, size, scale, heads, block, text_len),
        [third_all, query_wide, bias_wide[2:3], text_low, cosine, sine, gain_wide[2:3], offset_wide[2:3], mask, fold],
        [shaped((group, span), F32), shaped((group, span), BF16), shaped((group, cols), BF16), shaped(lse_shape, F32)],
        [pltpu.VMEM((group, span), BF16)],
    )
    fourth_all, third_sum = row_kernel(
        "fwd", "rows_cross", 3, cross_mixed, cross_out_t, second, row_bias[1:2], norm_gain[3:4], norm_bias[3:4]
    )

    upper_pre = dot_nn(fourth_all, up_full) + hidden_cols_bias
    active, pull_gelu = jax.vjp(lambda v: jax.nn.gelu(v, approximate=True), upper_pre)
    active_low = active.astype(BF16)
    row_ids = t * rows + jnp.arange(rows)
    weight = loss_mask.astype(F32) * (row_ids < true_counts[0]).astype(F32)
    loss_scale = dp * group / counted
    grad_all, block_out, grad_final, bias_mlp = row_kernel(
        "final", "rows_mlp", 4, active_low, down_t, third_sum, row_bias[2:3], teacher, (loss_scale * weight)[:, None]
    )

    grad_active = dot_nn(grad_all, down_t)
    (grad_upper,) = pull_gelu(grad_active)
    grad_upper_low = grad_upper.astype(BF16)
    bias_hidden = jnp.sum(grad_upper_low.astype(F32), axis=0)
    grad_down_t = dot_tn(grad_all, active_low).astype(BF16)
    grad_up = dot_tn(fourth_all, grad_upper_low).astype(BF16)
    down_mine = lax.psum_scatter(grad_down_t, "dp", scatter_dimension=0, tiled=True)
    up_mine = lax.psum_scatter(grad_up, "dp", scatter_dimension=0, tiled=True)
    c_all, grad_third, bias_cross_out, gain_fourth, offset_fourth = row_kernel(
        "bwd", "rows_up", 5, grad_upper_low, up_full, third_sum, norm_gain[3:4], grad_final
    )

    qp, qp_low, text_p, text_p_low, cross_gains, cross_offsets, cross_sums, text_sums = local_kernel(
        "cross_bwd",
        functools.partial(cross_bwd_body, size, scale, heads, block, text_len),
        [c_all, cross_out_t, cross_pre, cross_low, text_pre, text_low, cross_lse, cosine, sine,
         gain_wide[2:3], gain_wide[3:4], mask, fold],
        [shaped((group, span), BF16), shaped((group, cols), BF16), shaped((text_pad, 2 * span), BF16),
         shaped((2, text_pad, cols), BF16), shaped((2, LANES), F32), shaped((2, LANES), F32), shaped((1, span), F32), shaped((1, span), F32)],
        [pltpu.VMEM((group, span), BF16), pltpu.VMEM((group, span), F32), pltpu.VMEM((text_pad, span), F32), pltpu.VMEM((text_pad, span), F32)],
    )
    s_all, grad_second, bias_attn, gain_third, offset_third = row_kernel(
        "bwd", "rows_query", 6, qp, query_wide, second, norm_gain[2:3], grad_third
    )
    grad_cross_out_t = dot_tn(c_all, cross_mixed).astype(BF16)
    grad_query = dot_tn(third_all, qp_low).astype(BF16)
    grad_keyval = jnp.stack([dot_tn(text_rows, text_p_low[i]).astype(BF16) for i in range(2)])
    grad_keyval = grad_keyval.reshape(2, dp, -1, cols).transpose(1, 0, 2, 3).reshape(-1, cols)
    text_part = dot_nt(text_p[:, :span], keyval_wide[0]) + dot_nt(text_p[:, span:], keyval_wide[1])
    grad_text = lax.psum(text_part[:text_len].astype(BF16), "tensor").astype(F32)[None]
    cross_out_mine = lax.psum_scatter(grad_cross_out_t, "dp", scatter_dimension=0, tiled=True)
    query_mine = lax.psum_scatter(grad_query, "dp", scatter_dimension=0, tiled=True)
    keyval_mine = lax.psum_scatter(grad_keyval, "dp", scatter_dimension=0, tiled=True)

    p, p_low, self_gains, self_offsets, self_sums = local_kernel(
        "self_bwd",
        functools.partial(self_bwd_body, size, scale, heads, block),
        [s_all, out_t, pre, low, lse, cosine, sine, gain_wide[0:2], mask, fold],
        [shaped((group, 3 * span), BF16), shaped((3, group, cols), BF16), shaped((2, LANES), F32), shaped((2, LANES), F32),
         shaped((1, 3 * span), F32)],
        [pltpu.VMEM((group, span), BF16)] + [pltpu.VMEM((group, span), F32)] * 3,
    )
    project_rows = jnp.transpose(project_wide, (1, 0, 2)).reshape(width, 3 * span)
    k_low, bias_skip, gain_first, offset_first, gain_skip, offset_skip = row_kernel(
        "first", "rows_project", 7, p, project_rows, residual, norm_gain[1:2], grad_second, skipped, norm_gain[0:1]
    )
    grad_out_t = dot_tn(s_all, mixed).astype(BF16)
    grad_project = jnp.stack([dot_tn(first_all, p_low[i]).astype(BF16) for i in range(3)])
    grad_project = grad_project.reshape(3, dp, -1, cols).transpose(1, 0, 2, 3).reshape(-1, cols)
    out_mine = lax.psum_scatter(grad_out_t, "dp", scatter_dimension=0, tiled=True)
    project_mine = lax.psum_scatter(grad_project, "dp", scatter_dimension=0, tiled=True)

    k_cols = lax.all_to_all(k_low, "tensor", split_axis=1, concat_axis=0, tiled=True)
    (grad_latent,) = row_kernel("plain", "rows_latent", 8, k_cols, skip_full[:width])
    (grad_skip,) = row_kernel("plain", "rows_skip", 9, k_cols, skip_full[width:])
    grad_skip_proj = jnp.concatenate([dot_tn(joined0, k_cols).astype(BF16), dot_tn(joined1, k_cols).astype(BF16)])
    skip_mine = lax.psum_scatter(grad_skip_proj, "dp", scatter_dimension=0, tiled=True)

    shift_parts = lax.all_gather(offset_first, ("dp", "tensor"), axis=0, tiled=True)
    shift_low = jnp.sum(shift_parts.reshape(dp, tensor, width), axis=1).astype(BF16)
    grad_shift_proj = dot_tn(silu_mine, shift_low)
    bias_shift = jnp.sum(shift_low.astype(F32), axis=0)

    head_gain_part = narrow_head(jnp.concatenate([self_gains, cross_gains], axis=0))
    head_bias_part = narrow_head(jnp.concatenate([self_offsets, cross_offsets], axis=0))
    column_rows = narrow_cols(
        jnp.concatenate([self_sums[:, :span], self_sums[:, 2 * span :], cross_sums, text_sums], axis=0)
    )
    column_part = lax.dynamic_update_slice_in_dim(jnp.zeros((4, width), F32), column_rows, t * cols, 1)
    hidden_part = lax.dynamic_update_slice_in_dim(jnp.zeros(hidden_bias.shape, F32), bias_hidden, t * hidden, 0)
    sums = lax.psum(
        (
            jnp.concatenate([gain_skip, gain_first, gain_third, gain_fourth]),
            jnp.concatenate([offset_skip, offset_first, offset_third, offset_fourth]),
            head_gain_part,
            head_bias_part,
            jnp.concatenate([column_part, bias_skip]),
            hidden_part,
            jnp.concatenate([bias_attn, bias_cross_out, bias_mlp]),
        ),
        ("dp", "tensor"),
    )
    return (
        block_out,
        grad_latent,
        grad_skip,
        grad_text,
        skip_mine.astype(F32),
        grad_shift_proj,
        jnp.transpose(project_mine.reshape(3, -1, cols), (1, 0, 2)).astype(F32),
        out_mine.T.astype(F32),
        query_mine.astype(F32),
        jnp.transpose(keyval_mine.reshape(2, -1, cols), (1, 0, 2)).astype(F32),
        cross_out_mine.T.astype(F32),
        up_mine.astype(F32),
        down_mine.T.astype(F32),
        sums[0],
        sums[1],
        sums[2],
        sums[3],
        sums[4],
        sums[5],
        jnp.concatenate([sums[6], bias_shift[None]]),
    )


def solution(mesh):
    both = ("dp", "tensor")
    rows2, split2, cross2 = P(both, None), P("dp", "tensor"), P("tensor", "dp")
    middle = P("dp", None, "tensor")
    return jax.shard_map(
        body,
        mesh=mesh,
        in_specs=(
            rows2, rows2, P("dp", None, None), P("dp", None), rows2, P(both), P("dp"), P(None, "dp"),
            split2, P("dp", None), middle, cross2, split2, middle, cross2, split2, cross2,
            P(), P(), P(), P(), P(), P(), P(),
        ),
        out_specs=(
            rows2, rows2, rows2, P("dp", None, None),
            split2, P("dp", None), middle, cross2, split2, middle, cross2, split2, cross2,
            P(), P(), P(), P(), P(), P(), P(),
        ),
        check_vma=False,
    )
```

time: 2470 us -> 1540 us (0.62)
  waiting for transfers between devices: 1750 us -> 553 us
  Pallas kernels: 0 us -> 513 us
  local copies, waits for them, and re-layouts: 199 us -> 77.6 us
  matrix products: 207 us -> 94.3 us
  blocking collectives: 127 us -> 239 us
  other arithmetic: 137 us -> 36.9 us
    reduce_scatter x13 -> x4, waiting for transfers between devices: 884 us -> 307 us  [the longest x1 91.5 us: body(): up_mine = lax.psum_scatter(grad_up, 'dp', scatter_dimension=0, tiled=True)]
    pallas_call x0 -> x15, Pallas kernels: none -> 513 us  [the longest x8 293 us: row_kernel(): pl.pallas_call(functools.partial(row_body, mode, rows, len(ins), len(outs...]
    all_gather x13 -> x3, waiting for transfers between devices: 454 us -> 0.06 us  [the longest x1 0.02 us: body(): keyval_g = lax.all_gather(keyval_in, 'dp', axis=0, tiled=False)]
    dot_general x54 -> x29, matrix products: 207 us -> 94.3 us  [the longest x13 50.4 us: dot_tn(): lax.dot_general(left, right, (((0,), (0,)), ((), ())), preferred_element_...]
    psum x2, waiting for transfers between devices: 130 us -> 18.9 us  [the longest x1 18.9 us: body(): lax.psum(text_part[:text_len].astype(BF16), 'tensor').astype(F32)[None]]
    all_gather x3 -> x5, blocking collectives: 110 us -> 189 us  [the longest x1 42.9 us: body(): small_all = lax.all_gather(small, 'dp', axis=0, tiled=True)]
    unnamed x31 -> x14, waiting for transfers between devices: 4.05 us -> 71 us
    dynamic_update_slice x10 -> x2, local copies, waits for them, and re-layouts: 64.7 us -> 0.48 us  [the longest x1 0.26 us: body(): lax.dynamic_update_slice_in_dim(jnp.zeros((4, width), F32), column_rows,...]
  transfers between devices with their start and end apart: 33 -> 14, of which waited for: 29 -> 9; matrix products, arithmetic and copies ran while one was open for 6% -> 11% of each run, Pallas kernels for 0% -> 19%
where the time goes in v1:
time: 1540 us
  waiting for transfers between devices  553 us (36%)
  Pallas kernels  513 us (33%)
  blocking collectives  239 us (16%)
  matrix products  94.3 us (6%)
  local copies, waits for them, and re-layouts  77.6 us (5%)
  other arithmetic  36.9 us (2%)
  between operations  16.4 us (1%)
    pallas_call x8, Pallas kernels, row_kernel(): pl.pallas_call(functools.partial(row_body, mode, rows, len(ins), len(outs...  293 us
    pallas_call x2, Pallas kernels, gather_kernel(): pl.pallas_call(functools.partial(gather_body, n_rows, n_weights, dp), out...  116 us
    pallas_call x5, Pallas kernels, local_kernel(): pl.pallas_call(body, out_shape=outs, in_specs=[vm] * len(ins), out_specs=...  104 us
    reduce_scatter x1, waiting for transfers between devices, body(): up_mine = lax.psum_scatter(grad_up, 'dp', scatter_dimension=0, tiled=True)  91.5 us
    reduce_scatter x1, waiting for transfers between devices, body(): lax.psum_scatter(grad_down_t, 'dp', scatter_dimension=0, tiled=True)  90.6 us
    reduce_scatter x1, waiting for transfers between devices, body(): lax.psum_scatter(grad_project, 'dp', scatter_dimension=0, tiled=True)  74.9 us
    unnamed x14, waiting for transfers between devices  71 us
    reduce_scatter x1, waiting for transfers between devices, body(): lax.psum_scatter(grad_keyval, 'dp', scatter_dimension=0, tiled=True)  66.9 us
  transfers between devices with their start and end apart: 14, of which 9 were waited for; matrix products, arithmetic and copies ran while one was open for 11% of the time, Pallas kernels for 19%

profile of v1, /device:TPU:0, one launch (start us, length us, event | category | flops | bytes accessed | tf_op | source)
XLA Modules:
  0.0 1535.6 jit_solution(17674467731012855617)
XLA Ops:
  8.7 92.7 %gather_joined.1 = (bf16[4,256,1408]{2,1,0:T(8,128)(2,1)}, bf16[4,256,1408]{2,1,0:T(8,128)(2,1)}, bf16[8,352,352]{2,1,0:T(8,128)(2,1)}, bf16[8,3,176,352]{3,2,1,0:T(8,128)(2,1)}) custom-call(bf16[256,1408]{1,0:T(8,128)(2,1)} %refs_0_.1, bf16[256,1408]{1,0:T(8,128)(2,1)} %refs_1_.1, bf16[352,352]{1,0:T(8,128)(2,1)} %refs_2_.1, bf16[3,176,352]{2,1,0:T(8,128)(2,1)} %bitcast.197), custom_call_target="tpu_custom_call" | custom-call | tf_op jit(solution)/shard_map/gather_joined/pallas_call | solution.py:152
  115.2 42.9 %all-gather.1 = f32[8,1,1409]{2,1,0:T(1,128)S(1)} all-gather(f32[1,1,1409]{2,1,0:T(1,128)S(1)} %maximum_bitcast_fusion.2), channel_id=1, replica_groups=mesh['dp'=8,'tensor'=4] {'dp'}, dimensions={0}, use_global_device_ids=true | all-gather | bytes 50724 | tf_op jit(solution)/shard_map/all_gather | solution.py:612
  159.0 36.9 %all-reduce.2 = f32[8,1408]{1,0:T(8,128)S(1)} all-reduce(f32[8,1408]{1,0:T(8,128)S(1)} %fusion.50), channel_id=3, replica_groups=mesh['dp'=8,'tensor'=4] {'dp'}, use_global_device_ids=true, to_apply=%region_4.5.clone | all-reduce | flops 11264 | bytes 90112
  211.4 36.0 %all_gather.29 = bf16[1408,352]{1,0:T(8,128)(2,1)S(1)} all-gather(bf16[176,352]{1,0:T(8,128)(2,1)S(1)} %copy-done.26), channel_id=1, replica_groups=mesh['dp'=8,'tensor'=4] {'dp'}, dimensions={0}, use_global_device_ids=true | all-gather | bytes 1115136 | tf_op jit(solution)/shard_map/all_gather | solution.py:623
  253.9 36.1 %all_gather.28.refs_1_.w_out = bf16[1408,352]{1,0:T(8,128)(2,1)} all-gather(bf16[176,352]{1,0:T(8,128)(2,1)S(1)} %bitcast.202), channel_id=1, replica_groups=mesh['dp'=8,'tensor'=4] {'dp'}, dimensions={0}, use_global_device_ids=true | all-gather | bytes 1115136 | tf_op jit(solution)/shard_map/all_gather | solution.py:622
  307.6 34.6 %all_gather.32.refs_1_.w_out = bf16[1408,352]{1,0:T(8,128)(2,1)} all-gather(bf16[176,352]{1,0:T(8,128)(2,1)S(1)} %bitcast.203), channel_id=1, replica_groups=mesh['dp'=8,'tensor'=4] {'dp'}, dimensions={0}, use_global_device_ids=true | all-gather | bytes 1115136 | tf_op jit(solution)/shard_map/all_gather | solution.py:626
  346.7 23.2 %gather_first.1 = bf16[4,256,1408]{2,1,0:T(8,128)(2,1)} custom-call(bf16[256,1408]{1,0:T(8,128)(2,1)} %get-tuple-element.218.refs_0_), custom_call_target="tpu_custom_call" | custom-call | tf_op jit(solution)/shard_map/gather_first/pallas_call | solution.py:152
  369.9 25.0 %self_fwd.1 = (f32[1024,1024]{1,0:T(8,128)}, bf16[1024,1536]{1,0:T(8,128)(2,1)}, bf16[1024,352]{1,0:T(8,128)(2,1)}, f32[4,4,256]{2,1,0:T(4,128)}) custom-call(bf16[1024,1408]{1,0:T(8,128)(2,1)} %bitcast.172, bf16[3,1408,512]{2,1,0:T(8,128)(2,1)} %convolution_convert_fusion.2.w, f32[3,1,512]{2,1,0:T(1,128)} %pad_maximum_fusion.8.bias, ...), custom_call_target="tpu_custom_call" | custom-call | tf_op jit(solution)/shard_map/self_fwd/pallas_call | solution.py:553
  394.9 41.8 %rows_self.1 = (bf16[1024,1408]{1,0:T(8,128)(2,1)}, f32[256,1408]{1,0:T(8,128)}) custom-call(bf16[1024,352]{1,0:T(8,128)(2,1)} %get-tuple-element.75.refs_0_, bf16[1408,352]{1,0:T(8,128)(2,1)} %all_gather.28.refs_1_.w_out, f32[256,1408]{1,0:T(8,128)} %get-tuple-element.217.refs_2_, f32[1,1408]{1,0:T(1,128)} %get-tuple-element.222.refs_3_, ...), custom_call_target="tpu_custom_call" | custom-call | tf_op jit(solution)/shard_map/rows_self/pallas_call | solution.py:288
  448.0 16.0 %cross_fwd.1 = (f32[1024,512]{1,0:T(8,128)}, bf16[1024,512]{1,0:T(8,128)(2,1)}, bf16[1024,352]{1,0:T(8,128)(2,1)}, f32[4,4,256]{2,1,0:T(4,128)}) custom-call(bf16[1024,1408]{1,0:T(8,128)(2,1)} %get-tuple-element.76.x, bf16[1408,512]{1,0:T(8,128)(2,1)} %fusion.9.w.refs_1_, f32[1,512]{1,0:T(1,128)} %get-tuple-element.230.bias, ...), custom_call_target="tpu_custom_call" | custom-call | tf_op jit(solution)/shard_map/cross_fwd/pallas_call | solution.py:553
  464.0 41.6 %rows_cross.1 = (bf16[1024,1408]{1,0:T(8,128)(2,1)}, f32[256,1408]{1,0:T(8,128)}) custom-call(bf16[1024,352]{1,0:T(8,128)(2,1)} %get-tuple-element.78.refs_0_, bf16[1408,352]{1,0:T(8,128)(2,1)} %all_gather.32.refs_1_.w_out, f32[256,1408]{1,0:T(8,128)} %get-tuple-element.79.refs_2_, f32[1,1408]{1,0:T(1,128)} %get-tuple-element.224.refs_3_, ...), custom_call_target="tpu_custom_call" | custom-call | tf_op jit(solution)/shard_map/rows_cross/pallas_call | solution.py:288
  505.6 11.1 multiply_convert_fusion
  516.8 45.8 %rows_mlp.1 = (bf16[1024,1408]{1,0:T(8,128)(2,1)}, bf16[256,1408]{1,0:T(8,128)(2,1)}, f32[256,1408]{1,0:T(8,128)}, f32[1,1408]{1,0:T(1,128)}) custom-call(bf16[1024,1536]{1,0:T(8,128)(2,1)} %get-tuple-element.243.refs_0_, bf16[1408,1536]{1,0:T(8,128)(2,1)} %all-gather.9.cloned.1.call-done.refs_1_, f32[256,1408]{1,0:T(8,128)} %get-tuple-element.81.refs_2_, ...), custom_call_target="tpu_custom_call" | custom-call | tf_op jit(solution)/shard_map/rows_mlp/pallas_call | solution.py:288
  562.5 12.7 convert_reduce_fusion
  575.2 45.3 %rows_up.1 = (bf16[1024,1408]{1,0:T(8,128)(2,1)}, f32[256,1408]{1,0:T(8,128)}, f32[1,1408]{1,0:T(1,128)}, f32[1,1408]{1,0:T(1,128)}, f32[1,1408]{1,0:T(1,128)}) custom-call(bf16[1024,1536]{1,0:T(8,128)(2,1)} %get-tuple-element.214.refs_0_, bf16[1408,1536]{1,0:T(8,128)(2,1)} %all-gather.7.cloned.1.call-done.refs_1_, f32[256,1408]{1,0:T(8,128)} %get-tuple-element.81.refs_2_, ...), custom_call_target="tpu_custom_call" | custom-call | tf_op jit(solution)/shard_map/rows_up/pallas_call | solution.py:288
  620.6 22.9 %cross_bwd.1 = (bf16[1024,512]{1,0:T(8,128)(2,1)}, bf16[1024,352]{1,0:T(8,128)(2,1)}, bf16[336,1024]{1,0:T(8,128)(2,1)}, bf16[2,336,352]{2,1,0:T(8,128)(2,1)}, f...) custom-call(bf16[1024,1408]{1,0:T(8,128)(2,1)} %get-tuple-element.85.c_all, ...), custom_call_target="tpu_custom_call" | custom-call | tf_op jit(solution)/shard_map/cross_bwd/pallas_call | solution.py:553
  646.7 42.5 %rows_query.1 = (bf16[1024,1408]{1,0:T(8,128)(2,1)}, f32[256,1408]{1,0:T(8,128)}, f32[1,1408]{1,0:T(1,128)}, f32[1,1408]{1,0:T(1,128)}, f32[1,1408]{1,0:T(1,128)}) custom-call(bf16[1024,512]{1,0:T(8,128)(2,1)} %get-tuple-element.90.refs_0_, bf16[1408,512]{1,0:T(8,128)(2,1)} %fusion.9.w.refs_1_, f32[256,1408]{1,0:T(8,128)} %get-tuple-element.79.refs_2_, ...), custom_call_target="tpu_custom_call" | custom-call | tf_op jit(solution)/shard_map/rows_query/pallas_call | solution.py:288
  689.2 37.1 %self_bwd.1 = (bf16[1024,1536]{1,0:T(8,128)(2,1)}, bf16[3,1024,352]{2,1,0:T(8,128)(2,1)}, f32[2,128]{1,0:T(2,128)}, f32[2,128]{1,0:T(2,128)}, f32[1,1536]{1,0:T(1,128)}) custom-call(bf16[1024,1408]{1,0:T(8,128)(2,1)} %get-tuple-element.92.c_all, bf16[1408,352]{1,0:T(8,128)(2,1)} %all_gather.28.refs_1_.w_out, f32[1024,1024]{1,0:T(8,128)} %get-tuple-element.93.pre, ...), custom_call_target="tpu_custom_call" | custom-call | tf_op jit(solution)/shard_map/self_bwd/pallas_call | solution.py:553
  727.9 29.2 %rows_project.1 = (bf16[256,1408]{1,0:T(8,128)(2,1)}, f32[1,1408]{1,0:T(1,128)}, f32[1,1408]{1,0:T(1,128)}, f32[1,1408]{1,0:T(1,128)}, f32[1,1408]{1,0:T(1,128)}, /*index=5*/f32[1,1408]{1,0:T(1,128)}) custom-call(bf16[1024,1536]{1,0:T(8,128)(2,1)} %get-tuple-element.96.refs_0_, bf16[1408,1536]{1,0:T(8,128)(2,1)} %copy.120.refs_1_, ...), custom_call_target="tpu_custom_call" | custom-call | tf_op jit(solution)/shard_map/rows_project/pallas_call | solution.py:288
  796.3 13.7 all_to_all.38
  863.0 38.9 %all-gather.2 = f32[32,1,1408]{2,1,0:T(1,128)S(1)} all-gather(f32[1,1,1408]{2,1,0:T(1,128)S(1)} %bitcast.204), channel_id=1, replica_groups=mesh['dp'=8,'tensor'=4] {'dp','tensor'}, dimensions={0}, use_global_device_ids=true | all-gather | bytes 185856 | tf_op jit(solution)/shard_map/all_gather | solution.py:767
  905.3 18.9 %all-reduce.7.cloned.1.call-done = bf16[1,333,1024]{2,1,0:T(8,128)(2,1)} async-done(((bf16[1,333,1024]{2,1,0:T(8,128)(2,1)}), bf16[1,333,1024]{2,1,0:T(8,128)(2,1)}) %all-reduce.7.cloned.1.call-update) | async-done | bytes 682000 | tf_op jit(solution)/shard_map/psum | solution.py:738
  928.6 22.2 %rows_skip.1 = f32[256,1408]{1,0:T(8,128)} custom-call(bf16[1024,352]{1,0:T(8,128)(2,1)} %bitcast.176, bf16[1408,352]{1,0:T(8,128)(2,1)} %bitcast.188), custom_call_target="tpu_custom_call" | custom-call | tf_op jit(solution)/shard_map/rows_skip/pallas_call | solution.py:288
  950.7 24.4 %rows_latent.1 = f32[256,1408]{1,0:T(8,128)} custom-call(bf16[1024,352]{1,0:T(8,128)(2,1)} %bitcast.177, bf16[1408,352]{1,0:T(8,128)(2,1)} %bitcast.186), custom_call_target="tpu_custom_call" | custom-call | tf_op jit(solution)/shard_map/rows_latent/pallas_call | solution.py:288
  975.2 14.1 reduce-scatter.15.cloned.1.call-done
  991.0 62.6 %reduce-scatter.19.cloned.1.call-done = bf16[176,352]{1,0:T(8,128)(2,1)} async-done(((bf16[1408,352]{1,0:T(8,128)(2,1)}), bf16[176,352]{1,0:T(8,128)(2,1)}) %reduce-scatter.19.cloned.1.call-update) | async-done | bytes 123920 | tf_op jit(solution)/shard_map/reduce_scatter | solution.py:739
  1055.1 62.6 %reduce-scatter.13.cloned.1.call-done = bf16[176,352]{1,0:T(8,128)(2,1)} async-done(((bf16[1408,352]{1,0:T(8,128)(2,1)}), bf16[176,352]{1,0:T(8,128)(2,1)}) %reduce-scatter.13.cloned.1.call-update) | async-done | bytes 123920 | tf_op jit(solution)/shard_map/reduce_scatter | solution.py:758
  1119.4 66.9 %reduce-scatter.17.cloned.1.call-done = bf16[256,352]{0,1:T(8,128)(2,1)} async-done(((bf16[2048,352]{0,1:T(8,128)(2,1)}), bf16[256,352]{0,1:T(8,128)(2,1)}) %reduce-scatter.17.cloned.1.call-update) | async-done | bytes 180240 | tf_op jit(solution)/shard_map/reduce_scatter | solution.py:741
  1188.1 68.7 %reduce-scatter.25.cloned.1.call-done = bf16[352,352]{1,0:T(8,128)(2,1)} async-done(((bf16[2816,352]{1,0:T(8,128)(2,1)}), bf16[352,352]{1,0:T(8,128)(2,1)}) %reduce-scatter.25.cloned.1.call-update) | async-done | bytes 247824
  1259.0 74.9 %reduce-scatter.11.cloned.1.call-done = bf16[528,352]{1,0:T(8,128)(2,1)} async-done(((bf16[4224,352]{1,0:T(8,128)(2,1)}), bf16[528,352]{1,0:T(8,128)(2,1)}) %reduce-scatter.11.cloned.1.call-update) | async-done | bytes 371728 | tf_op jit(solution)/shard_map/reduce_scatter | solution.py:759
  1335.8 90.6 %reduce-scatter.23.cloned.1.call-done = bf16[176,1536]{1,0:T(8,128)(2,1)} async-done(((bf16[1408,1536]{1,0:T(8,128)(2,1)}), bf16[176,1536]{1,0:T(8,128)(2,1)}) %reduce-scatter.23.cloned.1.call-update) | async-done | bytes 540688 | tf_op jit(solution)/shard_map/reduce_scatter | solution.py:715
  1428.5 91.5 %reduce-scatter.21.cloned.1.call-done = bf16[176,1536]{1,0:T(8,128)(2,1)} async-done(((bf16[1408,1536]{1,0:T(8,128)(2,1)}), bf16[176,1536]{1,0:T(8,128)(2,1)}) %reduce-scatter.21.cloned.1.call-update) | async-done | bytes 540688 | tf_op jit(solution)/shard_map/reduce_scatter | solution.py:716
  (290 shorter events, 196.1 us)
Async XLA Ops:
  7.2 151.5 %copy-start = (bf16[176,1408]{1,0:T(8,128)(2,1)S(1)}, bf16[176,1408]{1,0:T(8,128)(2,1)}, u32[]{:S(2)}) copy-start(bf16[176,1408]{1,0:T(8,128)(2,1)} %param.43) | copy-start | bytes 1486852
  7.2 429.5 %all-gather.11.cloned.1.call-start = ((), (), s32[]{:S(2)}) async-start(), calls=%async_computation.20 | async-start | bytes 1622016 | tf_op jit(solution)/shard_map/all_gather | solution.py:625
  7.9 497.7 %all-gather.7.cloned.1.call-start = ((), (), s32[]{:S(2)}) async-start(), calls=%async_computation.10 | async-start | bytes 4866048 | tf_op jit(solution)/shard_map/all_gather | solution.py:627
  108.2 87.6 %copy-start.21 = (f32[352,512]{1,0:T(8,128)S(1)}, f32[352,512]{1,0:T(8,128)}, u32[]{:S(2)}) copy-start(f32[352,512]{1,0:T(8,128)} %constant.75.clone) | copy-start | bytes 2162692
  108.3 89.4 %copy-start.38 = (s32[2,1024]{1,0:T(2,128)S(1)}, s32[2,1024]{1,0:T(2,128)}, u32[]{:S(2)}) copy-start(s32[2,1024]{1,0:T(2,128)} %param.41) | copy-start | bytes 24580
  109.2 233.0 %all-to-all-start = ((bf16[4,256,352]{1,2,0:T(8,128)(2,1)}), bf16[4,256,352]{1,2,0:T(8,128)(2,1)S(1)}, u32[]{:S(2)}, u32[]{:S(2)}) async-start(bf16[4,256,352]{1,2,0:T(8,128)(2,1)} %bitcast.165), calls=%async_computation | async-start | bytes 1441792 | tf_op jit(solution)/shard_map/all_to_all | solution.py:661
  113.8 403.0 %all-gather.9.cloned.1.call-start = ((), (), s32[]{:S(2)}) async-start(), calls=%async_computation.11 | async-start | bytes 4866048 | tf_op jit(solution)/shard_map/all_gather | solution.py:628
  114.5 789.5 %all-reduce.9.cloned.1.call-start = ((), (), s32[]{:S(2)}) async-start(), calls=%async_computation.22 | async-start | bytes 282624 | tf_op jit(solution)/shard_map/psum | solution.py:779
  201.8 45.6 %copy-start.3 = (bf16[352,512]{1,0:T(8,128)(2,1)S(1)}, bf16[352,512]{1,0:T(8,128)(2,1)}, u32[]{:S(2)}) copy-start(bf16[352,512]{1,0:T(8,128)(2,1)} %constant.73.clone.fold) | copy-start | bytes 1081348
  207.8 41.6 %copy-start.13 = (bf16[3,8,176,352]{3,2,1,0:T(8,128)(2,1)S(1)}, bf16[3,8,176,352]{3,2,1,0:T(8,128)(2,1)}, u32[]{:S(2)}) copy-start(bf16[3,8,176,352]{3,2,1,0:T(8,128)(2,1)} %copy.112) | copy-start | bytes 8921092
  207.8 41.6 %copy-start.67 = (bf16[352,512,1]{1,0,2:T(8,128)(2,1)S(1)}, bf16[352,512,1]{1,0,2:T(8,128)(2,1)}, u32[]{:S(2)}) copy-start(bf16[352,512,1]{1,0,2:T(8,128)(2,1)} %constant.95) | copy-start | bytes 1081348
  249.5 40.6 %copy-start.57 = (s32[256]{0:T(256)S(1)}, s32[256]{0:T(256)}, u32[]{:S(2)}) copy-start(s32[256]{0:T(256)} %param.39) | copy-start | bytes 3076
  516.7 45.8 %copy-start.10 = (bf16[1408,1536]{1,0:T(8,128)(2,1)S(1)}, bf16[1408,1536]{1,0:T(8,128)(2,1)}, u32[]{:S(2)}) copy-start(bf16[1408,1536]{1,0:T(8,128)(2,1)} %all-gather.9.cloned.1.call-done.refs_1_) | copy-start | bytes 12976132
  689.2 37.8 %copy-start.16 = (f32[512,352]{1,0:T(8,128)S(1)}, f32[512,352]{1,0:T(8,128)}, u32[]{:S(2)}) copy-start(f32[512,352]{1,0:T(8,128)} %constant.81.clone) | copy-start | bytes 2162692
  689.2 37.8 %copy-start.47 = (f32[1,512]{1,0:T(1,128)S(1)}, f32[1,512]{1,0:T(1,128)}, u32[]{:S(2)}) copy-start(f32[1,512]{1,0:T(1,128)} %get-tuple-element.116) | copy-start | bytes 6148
  689.2 37.8 %copy-start.48 = (f32[1,512]{1,0:T(1,128)S(1)}, f32[1,512]{1,0:T(1,128)}, u32[]{:S(2)}) copy-start(f32[1,512]{1,0:T(1,128)} %get-tuple-element.117) | copy-start | bytes 6148
  727.9 32.9 %copy-start.43 = (f32[1,1408]{1,0:T(1,128)S(1)}, f32[1,1408]{1,0:T(1,128)}, u32[]{:S(2)}) copy-start(f32[1,1408]{1,0:T(1,128)} %get-tuple-element.107) | copy-start | bytes 16900
  727.9 32.9 %copy-start.44 = (f32[1,1408]{1,0:T(1,128)S(1)}, f32[1,1408]{1,0:T(1,128)}, u32[]{:S(2)}) copy-start(f32[1,1408]{1,0:T(1,128)} %get-tuple-element.110) | copy-start | bytes 16900
  727.9 32.9 %copy-start.45 = (f32[1,1408]{1,0:T(1,128)S(1)}, f32[1,1408]{1,0:T(1,128)}, u32[]{:S(2)}) copy-start(f32[1,1408]{1,0:T(1,128)} %get-tuple-element.106) | copy-start | bytes 16900
  727.9 32.9 %copy-start.46 = (f32[1,1408]{1,0:T(1,128)S(1)}, f32[1,1408]{1,0:T(1,128)}, u32[]{:S(2)}) copy-start(f32[1,1408]{1,0:T(1,128)} %get-tuple-element.109) | copy-start | bytes 16900
  762.2 162.0 %all-reduce.7.cloned.1.call-start = ((), (), s32[]{:S(2)}) async-start(), calls=%async_computation.12 | async-start | bytes 1376256 | tf_op jit(solution)/shard_map/psum | solution.py:738
  764.8 224.5 %reduce-scatter.15.cloned.1.call-start = ((), (), s32[]{:S(2)}) async-start(), calls=%async_computation.15 | async-start | bytes 1216512 | tf_op jit(solution)/shard_map/reduce_scatter | solution.py:740
  769.9 283.6 %reduce-scatter.19.cloned.1.call-start = ((), (), s32[]{:S(2)}) async-start(), calls=%async_computation.17 | async-start | bytes 1216512 | tf_op jit(solution)/shard_map/reduce_scatter | solution.py:739
  774.6 343.1 %reduce-scatter.13.cloned.1.call-start = ((), (), s32[]{:S(2)}) async-start(), calls=%async_computation.14 | async-start | bytes 1216512 | tf_op jit(solution)/shard_map/reduce_scatter | solution.py:758
  779.3 407.0 %reduce-scatter.17.cloned.1.call-start = ((), (), s32[]{:S(2)}) async-start(), calls=%async_computation.16 | async-start | bytes 1622016 | tf_op jit(solution)/shard_map/reduce_scatter | solution.py:741
  795.9 460.9 %reduce-scatter.25.cloned.1.call-start = ((), (), s32[]{:S(2)}) async-start(), calls=%async_computation.21 | async-start | bytes 2433024
  820.3 513.5 %reduce-scatter.11.cloned.1.call-start = ((), (), s32[]{:S(2)}) async-start(), calls=%async_computation.13 | async-start | bytes 3649536 | tf_op jit(solution)/shard_map/reduce_scatter | solution.py:759
  841.6 584.8 %reduce-scatter.23.cloned.1.call-start = ((), (), s32[]{:S(2)}) async-start(), calls=%async_computation.19 | async-start | bytes 4866048 | tf_op jit(solution)/shard_map/reduce_scatter | solution.py:715
  851.9 668.1 %reduce-scatter.21.cloned.1.call-start = ((), (), s32[]{:S(2)}) async-start(), calls=%async_computation.18 | async-start | bytes 4866048 | tf_op jit(solution)/shard_map/reduce_scatter | solution.py:716
  862.3 65.1 %copy-start.15 = (bf16[256,4,352]{0,2,1:T(8,128)(2,1)S(1)}, bf16[256,4,352]{0,2,1:T(8,128)(2,1)}, u32[]{:S(2)}) copy-start(bf16[256,4,352]{0,2,1:T(8,128)(2,1)} %copy-done.14) | copy-start | bytes 2162692
  1259.0 263.2 %copy-start.19 = (bf16[256,1408]{1,0:T(8,128)(2,1)S(1)}, bf16[256,1408]{1,0:T(8,128)(2,1)}, u32[]{:S(2)}) copy-start(bf16[256,1408]{1,0:T(8,128)(2,1)} %get-tuple-element.267) | copy-start | bytes 2162692
  1335.8 187.2 %copy-start.8 = (f32[256,1408]{1,0:T(8,128)S(1)}, f32[256,1408]{1,0:T(8,128)}, u32[]{:S(2)}) copy-start(f32[256,1408]{1,0:T(8,128)} %rows_latent.1) | copy-start | bytes 4325380
  (51 other events, 481.2 us)
Sparse Core Ops, SparseCore 0:
  10.2 72.3 all-gather.10
  84.8 80.4 all-gather.6
  167.5 96.2 all-gather.8
  762.3 122.6 all-reduce.8
  887.3 36.8 all-reduce.6
  927.5 61.8 reduce-scatter.14
  992.7 60.7 reduce-scatter.18
  1056.9 60.7 reduce-scatter.12
  1121.8 64.4 reduce-scatter.16
  1189.6 67.1 reduce-scatter.24
  1260.5 73.3 reduce-scatter.10
  1337.3 89.0 reduce-scatter.22
  1430.4 89.5 reduce-scatter.20

commit v2 on v1

--- a/solution.py
+++ b/solution.py
@@ -64,144 +64,219 @@
     return bar
 
 
-def gather_body(n_rows, n_weights, dp, *refs):
-    n = n_rows + n_weights
-    ins, outs = refs[:n], refs[n : 2 * n]
-    own_sem, core_s, core_r, y_s, y_r, fw_s, fw_r, z_s, z_r, x_s, x_r = refs[2 * n :]
-    d, t, y, c, sib, yp = tensor_place()
-    line = dp // 2
-    zi, par = d // 2, d % 2
-    xp = (2 * zi + 1 - par, t)
-    zps = [(2 * ((zi + j) % line) + par, t) for j in range(1, line)]
-    peers = ([sib, yp] if n_rows else []) + ([xp] + zps if n_weights else [])
-    bar = greet(peers)
-    locals_ = []
-    for i in range(n):
-        me = t if i < n_rows else d
-        cp = pltpu.make_async_copy(ins[i], outs[i].at[me], own_sem.at[i])
+class DpPlace:
+    def __init__(self, dp):
+        self.d, self.t = lax.axis_index("dp"), lax.axis_index("tensor")
+        self.dp, self.line = dp, dp // 2
+        self.zi, self.par = self.d // 2, self.d % 2
+        self.pair = (2 * self.zi + 1 - self.par, self.t)
+
+    def ahead(self, j):
+        return 2 * ((self.zi + j) % self.line) + self.par
+
+    def behind(self, j):
+        return 2 * ((self.zi + self.line - j) % self.line) + self.par
+
+    def others(self):
+        return [((self.d + j) % self.dp, self.t) for j in range(1, self.dp)]
+
+
+class ToAll:
+    def __init__(self, place, source, land, send_sem, recv_sem):
+        self.copies = []
+        for j in range(1, place.dp):
+            q = (place.d + j) % place.dp
+            cp = remote(source(q), land.at[place.d], send_sem.at[j], recv_sem.at[j], (q, place.t))
+            cp.start()
+            self.copies.append(cp)
+
+    def arrived(self):
+        for cp in self.copies:
+            cp.wait_recv()
+
+    def sent(self):
+        for cp in self.copies:
+            cp.wait_send()
+
+
+class WeightGather:
+    def __init__(self, place, shard, land, z_s, z_r, x_s, x_r):
+        self.place, self.land, self.x_s, self.x_r = place, land, x_s, x_r
+        self.z = []
+        for j in range(1, place.line):
+            cp = remote(shard, land.at[place.d], z_s.at[j], z_r.at[j], (place.ahead(j), place.t))
+            cp.start()
+            self.z.append(cp)
+        cp = remote(shard, land.at[place.d], x_s.at[0], x_r.at[0], place.pair)
         cp.start()
-        locals_.append(cp)
-    pl.semaphore_wait(bar, len(peers))
-    row_cps = []
-    z_cps = [[] for _ in range(n_weights)]
-    x_cps = []
-
-    def start_z(w):
-        src, dst = ins[n_rows + w], outs[n_rows + w]
-        for j in range(1, line):
-            cp = remote(src, dst.at[d], z_s.at[w, j], z_r.at[w, j], zps[j - 1])
+        self.x = [cp]
+
+    def forward(self):
+        for j in range(1, self.place.line):
+            self.z[j - 1].wait_recv()
+            source = self.place.behind(j)
+            cp = remote(self.land.at[source], self.land.at[source], self.x_s.at[j], self.x_r.at[j], self.place.pair)
             cp.start()
-            z_cps[w].append(cp)
-        cp = remote(src, dst.at[d], x_s.at[w, 0], x_r.at[w, 0], xp)
+            self.x.append(cp)
+
+    def arrived(self):
+        for cp in self.x:
+            cp.wait_recv()
+
+    def sent(self):
+        for cp in self.z + self.x:
+            cp.wait_send()
+
+
+class GradScatter:
+    def __init__(self, place, source, own, xland, zland, own_sem, z_s, z_r, x_s, x_r):
+        self.place, self.own, self.xland, self.zland, self.z_s, self.z_r = place, own, xland, zland, z_s, z_r
+        self.x, self.local, self.z = [], [], []
+        for i in range(1, place.line + 1):
+            j = (place.zi + i) % place.line
+            cp = remote(source.at[2 * j + 1 - place.par], xland.at[j], x_s.at[i - 1], x_r.at[i - 1], place.pair)
+            cp.start()
+            self.x.append(cp)
+            cp = pltpu.make_async_copy(source.at[2 * j + place.par], own.at[j], own_sem.at[i - 1])
+            cp.start()
+            self.local.append(cp)
+
+    def pass_on(self):
+        for i in range(1, self.place.line):
+            j = (self.place.zi + i) % self.place.line
+            self.local[i - 1].wait()
+            self.x[i - 1].wait_recv()
+            self.own[j] = (self.own[j].astype(F32) + self.xland[j].astype(F32)).astype(BF16)
+            cp = remote(
+                self.own.at[j], self.zland.at[i - 1], self.z_s.at[i], self.z_r.at[i], (self.place.ahead(i), self.place.t)
+            )
+            cp.start()
+            self.z.append(cp)
+
+    def result(self):
+        last = self.place.line - 1
+        self.local[last].wait()
+        self.x[last].wait_recv()
+        total = self.own[self.place.zi].astype(F32) + self.xland[self.place.zi].astype(F32)
+        for i, cp in enumerate(self.z):
+            cp.wait_recv()
+            total = total + self.zland[i].astype(F32)
+        return total
+
+    def sent(self):
+        for cp in self.x + self.z:
+            cp.wait_send()
+
+
+class TensorSum:
+    def __init__(self, near, far, csend, crecv, ysend, yrecv, cs, cr, ys, yr):
+        self.near, self.far, self.csend, self.crecv, self.ysend, self.yrecv = near, far, csend, crecv, ysend, yrecv
+        self.cs, self.cr, self.ys, self.yr = cs, cr, ys, yr
+        _, self.t, self.y, self.c, self.sib, self.yp = tensor_place()
+
+    def core(self, i, value):
+        self.csend[i] = value.astype(BF16)
+        cp = remote(self.csend.at[i], self.crecv.at[i], self.cs.at[i], self.cr.at[i], self.sib)
         cp.start()
-        x_cps.append(cp)
-
-    def forward_z(w):
-        dst = outs[n_rows + w]
-        for j in range(1, line):
-            z_cps[w][j - 1].wait_recv()
-            source = 2 * ((zi + line - j) % line) + par
-            cp = remote(dst.at[source], dst.at[source], x_s.at[w, j], x_r.at[w, j], xp)
+        return cp
+
+    def start(self, product, ready=None):
+        there, here = 2 * (1 - self.y), 2 * self.y
+        first = product(there + 1 - self.c)
+        if ready is not None:
+            ready()
+        self.c0 = self.core(0, first)
+        self.far[...] = product(there + self.c)
+        self.c1 = self.core(1, product(here + 1 - self.c))
+        self.c0.wait_recv()
+        self.ycs = []
+        ch = self.far.shape[0] // CHUNKS
+        for k in range(CHUNKS):
+            sl = pl.ds(k * ch, ch)
+            self.ysend[sl, :] = (self.far[sl, :] + self.crecv[0, sl, :].astype(F32)).astype(BF16)
+            cp = remote(self.ysend.at[sl], self.yrecv.at[sl], self.ys.at[k], self.yr.at[k], self.yp)
             cp.start()
-            x_cps.append(cp)
-
-    if n_weights:
-        start_z(0)
-    for i in range(n_rows):
-        a = remote(ins[i], outs[i].at[t], y_s.at[i], y_r.at[i], yp)
-        b = remote(ins[i], outs[i].at[t], core_s.at[i], core_r.at[i], sib)
+            self.ycs.append(cp)
+        self.near[...] = product(here + self.c)
+        self.c1.wait_recv()
+
+    def chunk(self, k):
+        ch = self.far.shape[0] // CHUNKS
+        sl = pl.ds(k * ch, ch)
+        self.ycs[k].wait_recv()
+        return sl, self.near[sl, :] + self.crecv[1, sl, :].astype(F32) + self.yrecv[sl, :].astype(F32)
+
+    def sent(self):
+        for cp in [self.c0, self.c1] + self.ycs:
+            cp.wait_send()
+
+    @staticmethod
+    def scratch(rows, width):
+        dma = pltpu.SemaphoreType.DMA
+        vm = pltpu.VMEM
+        return [
+            vm((rows, width), F32), vm((rows, width), F32), vm((2, rows, width), BF16), vm((2, rows, width), BF16),
+            vm((rows, width), BF16), vm((rows, width), BF16), dma((2,)), dma((2,)), dma((CHUNKS,)), dma((CHUNKS,)),
+        ]
+
+
+class RowSpread:
+    def __init__(self, spread, rows, ys, yr, cs, cr, fs, fr):
+        self.spread, self.rows = spread, rows
+        self.sems = (ys, yr, cs, cr, fs, fr)
+        _, self.t, self.y, self.c, self.sib, self.yp = tensor_place()
+        self.parts, self.passed = [], []
+
+    def at(self, owner, start, count):
+        return self.spread.at[pl.ds(pl.multiple_of(owner * self.rows + start, 16), count)]
+
+    def send(self, start, count):
+        ys, yr, cs, cr, _, _ = self.sems
+        k = len(self.parts)
+        here = self.at(self.t, start, count)
+        a = remote(here, here, ys.at[k], yr.at[k], self.yp)
+        b = remote(here, here, cs.at[k], cr.at[k], self.sib)
         a.start()
         b.start()
-        row_cps.append((a, b))
-    for w in range(n_weights):
-        forward_z(w)
-        if w + 1 < n_weights:
-            start_z(w + 1)
-    fws = []
-    yt = 2 * (1 - y) + c
-    for i in range(n_rows):
-        row_cps[i][0].wait_recv()
-        cp = remote(outs[i].at[yt], outs[i].at[yt], fw_s.at[i], fw_r.at[i], sib)
-        cp.start()
-        fws.append(cp)
-    for cp in locals_:
-        cp.wait()
-    for i in range(n_rows):
-        a, b = row_cps[i]
-        b.wait_recv()
-        fws[i].wait_recv()
-        a.wait_send()
-        b.wait_send()
-        fws[i].wait_send()
-    for cps in z_cps:
-        for cp in cps:
+        self.parts.append((a, b, start, count))
+
+    def forward(self):
+        fs, fr = self.sems[4:]
+        for k, (a, _, start, count) in enumerate(self.parts):
+            a.wait_recv()
+            there = self.at(2 * (1 - self.y) + self.c, start, count)
+            cp = remote(there, there, fs.at[k], fr.at[k], self.sib)
+            cp.start()
+            self.passed.append(cp)
+
+    def finish(self):
+        for (a, b, _, _), cp in zip(self.parts, self.passed):
+            b.wait_recv()
+            cp.wait_recv()
+            a.wait_send()
+            b.wait_send()
             cp.wait_send()
-    for cp in x_cps:
-        cp.wait_recv()
-        cp.wait_send()
-
-
-def gather_kernel(name, collective_id, dp, rows, weights=()):
-    n_rows, n_weights = len(rows), len(weights)
-    n = n_rows + n_weights
-    dma = pltpu.SemaphoreType.DMA
-    r, w, k = max(n_rows, 1), max(n_weights, 1), max(dp // 2, 1)
-    outs = [jax.ShapeDtypeStruct((4,) + v.shape, v.dtype) for v in rows]
-    outs += [jax.ShapeDtypeStruct((dp,) + v.shape, v.dtype) for v in weights]
-    anywhere = pl.BlockSpec(memory_space=pl.ANY)
-    return pl.pallas_call(
-        functools.partial(gather_body, n_rows, n_weights, dp),
-        out_shape=outs,
-        in_specs=[anywhere] * n,
-        out_specs=[anywhere] * n,
-        scratch_shapes=[dma((n,))] + [dma((r,))] * 6 + [dma((w, k))] * 4,
-        compiler_params=pltpu.CompilerParams(collective_id=collective_id, has_side_effects=True),
-        name=name,
-    )(*rows, *weights)
+
+    @staticmethod
+    def scratch(parts=CHUNKS):
+        return [pltpu.SemaphoreType.DMA((parts,))] * 6
 
 
 def row_body(mode, rows, n_in, n_out, *refs):
     ins, outs, scr = refs[:n_in], refs[n_in : n_in + n_out], refs[n_in + n_out :]
     lhs, w = ins[0], ins[1]
-    far, near, csend, crecv, ysend, yrecv, cs, cr, ys, yr, gcs, gcr, gys, gyr, fs, fr = scr
-    d, t, y, c, sib, yp = tensor_place()
+    _, t, _, _, sib, yp = tensor_place()
     bar = greet((sib, yp))
-    ch = rows // CHUNKS
-
-    def partial_rows(base, acc):
-        for r in range(2):
-            here = pl.ds(pl.multiple_of(base + r * rows, rows), rows)
-            acc[pl.ds(r * rows, rows), :] = dot_nt(lhs[here, :], w[...])
-
-    def chunk_of(acc, k):
-        return acc[pl.ds(pl.multiple_of(c * rows + k * ch, ch), ch), :]
-
-    other = pl.ds(pl.multiple_of((1 - c) * rows, rows), rows)
-    partial_rows((1 - y) * 2 * rows, far)
-    csend[0] = far[other, :].astype(BF16)
-    pl.semaphore_wait(bar, 2)
-    c0 = remote(csend.at[0], crecv.at[0], cs.at[0], cr.at[0], sib)
-    c0.start()
-    c0.wait_recv()
-    ycs = []
+    reduce = TensorSum(*scr[:10])
+    spread = RowSpread(outs[0], rows, *scr[10:])
+
+    def product(b):
+        return dot_nt(lhs[pl.ds(pl.multiple_of(b * rows, rows), rows), :], w[...])
+
+    reduce.start(product, lambda: pl.semaphore_wait(bar, 2))
+    sums = None
     for k in range(CHUNKS):
-        sl = pl.ds(k * ch, ch)
-        ysend[sl, :] = (chunk_of(far, k) + crecv[0, sl, :].astype(F32)).astype(BF16)
-        cp = remote(ysend.at[sl], yrecv.at[sl], ys.at[k], yr.at[k], yp)
-        cp.start()
-        ycs.append(cp)
-    partial_rows(y * 2 * rows, near)
-    csend[1] = near[other, :].astype(BF16)
-    c1 = remote(csend.at[1], crecv.at[1], cs.at[1], cr.at[1], sib)
-    c1.start()
-    c1.wait_recv()
-    gathers = mode in ("fwd", "final", "bwd")
-    sums = None
-    ags = []
-    for k in range(CHUNKS):
-        sl = pl.ds(k * ch, ch)
-        ycs[k].wait_recv()
-        total = chunk_of(near, k) + crecv[1, sl, :].astype(F32) + yrecv[sl, :].astype(F32)
+        sl, total = reduce.chunk(k)
         parts = []
         if mode == "fwd":
             resid, bias, gain, offset = ins[2:]
@@ -217,95 +292,393 @@
             outs[2][sl, :] = grad
             low = grad.astype(BF16)
             parts = [low.astype(F32)]
-        elif mode == "bwd":
+        else:
             x, gain, before = ins[2:]
             back, xhat = norm_back(total, x[sl, :], gain[...])
             grad = before[sl, :] + back
             outs[1][sl, :] = grad
             low = grad.astype(BF16)
             parts = [low.astype(F32), total * xhat, total]
-        elif mode == "first":
-            x, gain, before, skipped, gain0 = ins[2:]
-            back, xhat = norm_back(total, x[sl, :], gain[...])
-            grad = before[sl, :] + back
-            back0, xhat0 = norm_back(grad, skipped[sl, :].astype(F32), gain0[...])
-            low = back0.astype(BF16)
-            outs[0][sl, :] = low
-            parts = [low.astype(F32), total * xhat, total, grad * xhat0, grad]
-        else:
-            outs[0][sl, :] = total
+        ch = rows // CHUNKS
+        outs[0][pl.ds(pl.multiple_of(t * rows + k * ch, ch), ch), :] = low
+        spread.send(k * ch, ch)
         parts = [jnp.sum(p, axis=0, keepdims=True) for p in parts]
         sums = parts if sums is None else [a + b for a, b in zip(sums, parts)]
-        if gathers:
-            here = pl.ds(pl.multiple_of(t * rows + k * ch, ch), ch)
-            spread = outs[0]
-            spread[here, :] = low
-            a = remote(spread.at[here], spread.at[here], gys.at[k], gyr.at[k], yp)
-            b = remote(spread.at[here], spread.at[here], gcs.at[k], gcr.at[k], sib)
-            a.start()
-            b.start()
-            ags.append((a, b))
     for i, s in enumerate(sums):
         outs[n_out - len(sums) + i][...] = s
-    if gathers:
-        fws = []
-        for k in range(CHUNKS):
-            ags[k][0].wait_recv()
-            there = pl.ds(pl.multiple_of((2 * (1 - y) + c) * rows + k * ch, ch), ch)
-            cp = remote(spread.at[there], spread.at[there], fs.at[k], fr.at[k], sib)
-            cp.start()
-            fws.append(cp)
-        for k in range(CHUNKS):
-            a, b = ags[k]
-            b.wait_recv()
-            fws[k].wait_recv()
-            a.wait_send()
-            b.wait_send()
-            fws[k].wait_send()
-    c0.wait_send()
-    c1.wait_send()
-    for cp in ycs:
-        cp.wait_send()
+    spread.forward()
+    spread.finish()
+    reduce.sent()
 
 
 def row_kernel(mode, name, collective_id, lhs, w, *extra):
     rows = lhs.shape[0] // 4
     width = w.shape[0]
-    full = jax.ShapeDtypeStruct((4 * rows, width), BF16)
-    mine = jax.ShapeDtypeStruct((rows, width), F32)
-    mine_low = jax.ShapeDtypeStruct((rows, width), BF16)
-    line = jax.ShapeDtypeStruct((1, width), F32)
+    full = shaped((4 * rows, width), BF16)
+    mine = shaped((rows, width), F32)
+    line = shaped((1, width), F32)
     outs = {
         "fwd": [full, mine],
-        "final": [full, mine_low, mine, line],
+        "final": [full, shaped((rows, width), BF16), mine, line],
         "bwd": [full, mine, line, line, line],
-        "first": [mine_low] + [line] * 5,
-        "plain": [mine],
     }[mode]
     ins = [lhs, w, *extra]
-    vm = pl.BlockSpec(memory_space=pltpu.VMEM)
-    dma = pltpu.SemaphoreType.DMA
+    return talking_kernel(
+        name,
+        collective_id,
+        functools.partial(row_body, mode, rows, len(ins), len(outs)),
+        ins,
+        outs,
+        TensorSum.scratch(rows, width) + RowSpread.scratch(),
+    )
+
+
+def talking_kernel(name, collective_id, body, ins, outs, scratch, in_hbm=(), out_hbm=()):
+    vm, anywhere = pl.BlockSpec(memory_space=pltpu.VMEM), pl.BlockSpec(memory_space=pl.ANY)
     return pl.pallas_call(
-        functools.partial(row_body, mode, rows, len(ins), len(outs)),
+        body,
         out_shape=outs,
-        in_specs=[vm] * len(ins),
-        out_specs=[vm] * len(outs),
-        scratch_shapes=[
-            pltpu.VMEM((2 * rows, width), F32),
-            pltpu.VMEM((2 * rows, width), F32),
-            pltpu.VMEM((2, rows, width), BF16),
-            pltpu.VMEM((2, rows, width), BF16),
-            pltpu.VMEM((rows, width), BF16),
-            pltpu.VMEM((rows, width), BF16),
-            dma((2,)),
-            dma((2,)),
-        ]
-        + [dma((CHUNKS,))] * 8,
+        in_specs=[anywhere if i in in_hbm else vm for i in range(len(ins))],
+        out_specs=[anywhere if i in out_hbm else vm for i in range(len(outs))],
+        scratch_shapes=scratch,
         compiler_params=pltpu.CompilerParams(
             collective_id=collective_id, has_side_effects=True, vmem_limit_bytes=VMEM_BYTES
         ),
         name=name,
     )(*ins)
+
+
+def shaped(shape, dtype):
+    return jax.ShapeDtypeStruct(shape, dtype)
+
+
+def head_body(dp, gather, *refs):
+    (latent, skip_states, skip_in, project_in, small, shift_w, bias, norm_gain, norm_bias, row_bias,
+     j0, j1, skip_full, project_g, skipped, residual, first_all, silu, counted,
+     acc, psend, precv, small_land, part_out, part_land,
+     own_sem, a_s, a_r, b_s, b_r, p_s, p_r, *sems) = refs
+    w_sems, g_sems = sems[:16], sems[16:]
+    _, t, y, c, sib, yp = tensor_place()
+    d = lax.axis_index("dp")
+    rows, cols = latent.shape[0], acc.shape[1]
+    others = [(d, (t + o) % 4) for o in range(1, 4)]
+    place = DpPlace(dp) if gather else None
+    peers = others + (place.others() if gather else [])
+    bar = greet(peers)
+    own = [pltpu.make_async_copy(latent, j0.at[pl.ds(pl.multiple_of(t * rows, rows), rows)], own_sem.at[0]),
+           pltpu.make_async_copy(skip_states, j1.at[pl.ds(pl.multiple_of(t * rows, rows), rows)], own_sem.at[1])]
+    for cp in own:
+        cp.start()
+    if gather:
+        skip_rows = skip_in.shape[0]
+        skip_land = skip_full
+        kept = [pltpu.make_async_copy(skip_in, skip_land.at[d], own_sem.at[2]),
+                pltpu.make_async_copy(project_in, project_g.at[d], own_sem.at[3])]
+        for cp in kept:
+            cp.start()
+    pl.semaphore_wait(bar, len(peers))
+    if gather:
+        small_land[d] = small[d]
+        smalls = ToAll(place, lambda q: small.at[q], small_land, a_s, a_r)
+        skip_g = WeightGather(place, skip_in, skip_land, *w_sems[0:4])
+    for cp in own:
+        cp.wait()
+    spread0 = RowSpread(j0, rows, *g_sems[0:6])
+    spread1 = RowSpread(j1, rows, *g_sems[6:12])
+    spread0.send(0, rows)
+    spread1.send(0, rows)
+    if gather:
+        smalls.arrived()
+        given = small_land[0]
+        for i in range(1, dp):
+            given = given + small_land[i]
+        r = shift_w.shape[0]
+        silu[...] = jax.nn.silu(given[:, :r]).astype(BF16)
+        counted[...] = jnp.sum(given[:, given.shape[1] - LANES :], axis=0, keepdims=True)
+        part_out[...] = dot_nn(silu[...], shift_w[...])
+        part_land[d] = part_out[...]
+        shifts = ToAll(place, lambda q: part_out, part_land, b_s, b_r)
+        skip_g.forward()
+        project_gs = [
+            WeightGather(place, project_in.at[i], project_g.at[:, i], *w_sems[4 * (i + 1) : 4 * (i + 2)]) for i in range(3)
+        ]
+    spread0.forward()
+    if gather:
+        skip_g.arrived()
+        kept[0].wait()
+        half = dp // 2
+        w0 = lambda: skip_full[pl.ds(0, half)].reshape(half * skip_rows, cols)
+        w1 = lambda: skip_full[pl.ds(half, half)].reshape(half * skip_rows, cols)
+    else:
+        half = skip_in.shape[0] // 2
+        w0 = lambda: skip_in[pl.ds(0, half), :]
+        w1 = lambda: skip_in[pl.ds(half, half), :]
+    spread0.finish()
+    for b in range(4):
+        acc[pl.ds(b * rows, rows), :] = dot_nn(j0[pl.ds(b * rows, rows), :], w0())
+    if gather:
+        project_gs[0].forward()
+    spread1.forward()
+    spread1.finish()
+    copies = []
+    for o in (2, 3, 1, 0):
+        b = (t + o) % 4
+        here = pl.ds(pl.multiple_of(b * rows, rows), rows)
+        value = (acc[here, :] + dot_nn(j1[here, :], w1()) + bias[...]).astype(BF16)
+        if o:
+            psend[o] = value
+            cp = remote(psend.at[o], precv.at[t], p_s.at[o], p_r.at[o], (d, b))
+            cp.start()
+            copies.append(cp)
+        else:
+            precv[t] = value
+    if gather:
+        project_gs[1].forward()
+        project_gs[2].forward()
+        shifts.arrived()
+        shift_all = part_land[0]
+        for i in range(1, dp):
+            shift_all = shift_all + part_land[i]
+        place_row = lax.broadcasted_iota(jnp.int32, shift_all.shape, 0)
+        shift = jnp.sum(jnp.where(place_row == d, shift_all, 0.0), axis=0, keepdims=True) + row_bias[pl.ds(3, 1), :]
+    else:
+        shift = shift_w[...]
+    for cp in copies:
+        cp.wait_recv()
+    for s in range(4):
+        skipped[:, s * cols : (s + 1) * cols] = precv[s]
+    spread = RowSpread(first_all, rows, *g_sems[12:18])
+    ch = rows // CHUNKS
+    for k in range(CHUNKS):
+        sl = pl.ds(k * ch, ch)
+        cen, rstd = centre(skipped[sl, :].astype(F32))
+        resid = cen * rstd * norm_gain[pl.ds(0, 1), :] + norm_bias[pl.ds(0, 1), :]
+        residual[sl, :] = resid
+        cen, rstd = centre(resid)
+        first = cen * rstd * norm_gain[pl.ds(1, 1), :] + norm_bias[pl.ds(1, 1), :] + shift
+        first_all[pl.ds(pl.multiple_of(t * rows + k * ch, ch), ch), :] = first.astype(BF16)
+        spread.send(k * ch, ch)
+    spread.forward()
+    spread.finish()
+    for cp in copies:
+        cp.wait_send()
+    if gather:
+        for g in project_gs:
+            g.arrived()
+        kept[1].wait()
+        for g in project_gs + [skip_g, smalls, shifts]:
+            g.sent()
+
+
+def head_kernel(collective_id, dp, gather, latent, skip_states, skip_in, project_in, small, shift_w, bias, norm_gain, norm_bias, row_bias):
+    rows, width = latent.shape
+    cols = bias.shape[1]
+    line = max(dp // 2, 1)
+    dma, vm = pltpu.SemaphoreType.DMA, pltpu.VMEM
+    full = shaped((4 * rows, width), BF16)
+    seats = small.shape[1]
+    outs = [
+        full, full,
+        shaped((dp,) + skip_in.shape if gather else (16, LANES), BF16),
+        shaped((dp,) + project_in.shape if gather else (16, LANES), BF16),
+        shaped((rows, width), BF16), shaped((rows, width), F32), full,
+        shaped((seats, shift_w.shape[0]) if gather else (16, LANES), BF16),
+        shaped((1, LANES), F32),
+    ]
+    scratch = [
+        vm((4 * rows, cols), F32), vm((4, rows, cols), BF16), vm((4, rows, cols), BF16),
+        vm(small.shape, F32), vm((seats, width), F32), vm((dp, seats, width) if gather else (1, seats, width), F32),
+        dma((4,)), dma((dp,)), dma((dp,)), dma((dp,)), dma((dp,)), dma((4,)), dma((4,)),
+    ] + [dma((line,))] * 16 + RowSpread.scratch(1) * 2 + RowSpread.scratch()
+    ins = [latent, skip_states, skip_in, project_in, small, shift_w, bias, norm_gain, norm_bias, row_bias]
+    return talking_kernel(
+        "head", collective_id, functools.partial(head_body, dp, gather), ins, outs, scratch,
+        in_hbm=(0, 1, 2, 3) if gather else (0, 1), out_hbm=(3,),
+    )
+
+
+def tail_body(dp, scatter, *refs):
+    (p, project_rows, residual, grad_second, skipped, norm_gain, skip_w, j0, j1, silu, pack_in, grad_out, grad_project,
+     grad_latent, grad_skip, out_mine, project_mine, skip_mine, shift_grad, shift_bias, pack_sum, pack_cols,
+     klow, ksend, krecv, gskip, tile, tile_land, low_out, low_land, pack, pack_x, pack_z, pack_t,
+     o_own, o_x, o_z, q_own, q_x, q_z, s_own, s_x, s_z,
+     k_s, k_r, t_s, t_r, l_s, l_r, px_s, px_r, pz_s, pz_r, pt_s, pt_r,
+     *rest) = refs
+    sum_refs, half_refs, rs = rest[:10], rest[10:20], rest[20:]
+    _, t, y, c, sib, yp = tensor_place()
+    d = lax.axis_index("dp")
+    rows, cols = residual.shape[0], krecv.shape[2]
+    width = residual.shape[1]
+    others = [(d, (t + o) % 4) for o in range(1, 4)]
+    place = DpPlace(dp) if scatter else None
+    peers = others + (place.others() if scatter else [])
+    bar = greet(peers)
+    if not scatter:
+        place = None
+    reduce = TensorSum(*sum_refs)
+
+    def product(b):
+        return dot_nt(p[pl.ds(pl.multiple_of(b * rows, rows), rows), :], project_rows[...])
+
+    scatters = []
+
+    def ready():
+        pl.semaphore_wait(bar, len(peers))
+        if scatter:
+            scatters.append(GradScatter(place, grad_out, o_own, o_x, o_z, *rs[0:5]))
+            scatters.append(GradScatter(place, grad_project, q_own, q_x, q_z, *rs[5:10]))
+
+    reduce.start(product, ready)
+    sums = None
+    for k in range(CHUNKS):
+        sl, total = reduce.chunk(k)
+        back, xhat = norm_back(total, residual[sl, :], norm_gain[pl.ds(1, 1), :])
+        grad = grad_second[sl, :] + back
+        back0, xhat0 = norm_back(grad, skipped[sl, :].astype(F32), norm_gain[pl.ds(0, 1), :])
+        klow[sl, :] = back0.astype(BF16)
+        parts = [back0.astype(BF16).astype(F32), total * xhat, total, grad * xhat0, grad]
+        parts = [jnp.sum(v, axis=0, keepdims=True) for v in parts]
+        sums = parts if sums is None else [a + b for a, b in zip(sums, parts)]
+    for s in range(4):
+        ksend[s] = klow[:, s * cols : (s + 1) * cols]
+    copies = []
+    for o in (2, 3, 1):
+        b = (t + o) % 4
+        cp = remote(ksend.at[b], krecv.at[t], k_s.at[o], k_r.at[o], (d, b))
+        cp.start()
+        copies.append(cp)
+    krecv[t] = ksend[t]
+    bias_skip, gain_first, offset_first, gain_skip, offset_skip = sums
+    tile[...] = jnp.broadcast_to(offset_first, tile.shape)
+    tile_land[t] = tile[...]
+    tiles = []
+    for o in (1, 2, 3):
+        cp = remote(tile, tile_land.at[t], t_s.at[o], t_r.at[o], (d, (t + o) % 4))
+        cp.start()
+        tiles.append(cp)
+    pack[...] = pack_in[...]
+    for i, v in enumerate((gain_skip, gain_first, offset_skip, offset_first, bias_skip)):
+        pack[pl.ds(i, 1), :] = v
+    if scatter:
+        pack_cp = remote(pack, pack_x, px_s.at[0], px_r.at[0], place.pair)
+        pack_cp.start()
+    for cp in copies:
+        cp.wait_recv()
+    reduce.sent()
+    halves = [TensorSum(*sum_refs), TensorSum(*half_refs)]
+    for h, half in enumerate(halves):
+        half.start(lambda b, h=h: dot_nt(krecv[b], skip_w[pl.ds(h * width, width), :]))
+    for cp in tiles:
+        cp.wait_recv()
+    shift_low = tile_land[0] + tile_land[1] + tile_land[2] + tile_land[3]
+    low_out[...] = shift_low.astype(BF16).astype(F32)
+    if scatter:
+        low_land[d] = low_out[...]
+        lows = ToAll(place, lambda q: low_out, low_land, l_s, l_r)
+        pack_cp.wait_recv()
+        pack_cp.wait_send()
+        pack[...] = pack[...] + pack_x[...]
+        pack_z[place.zi] = pack[...]
+        packs = []
+        for j in range(1, place.line):
+            cp = remote(pack, pack_z.at[place.zi], pz_s.at[j], pz_r.at[j], (place.ahead(j), place.t))
+            cp.start()
+            packs.append(cp)
+        scatters[0].pass_on()
+        scatters[1].pass_on()
+    k_all = krecv[...].reshape(4 * rows, cols)
+    n = gskip.shape[0] // 2
+    for h, joined in enumerate((j0, j1)):
+        gskip[pl.ds(h * n, n)] = dot_tn(joined[...], k_all).astype(BF16).reshape((n,) + gskip.shape[1:])
+    if scatter:
+        scatters.append(GradScatter(place, gskip, s_own, s_x, s_z, *rs[10:15]))
+        lows.arrived()
+        seat = lax.broadcasted_iota(jnp.int32, low_out.shape, 0)
+        low_all = jnp.zeros(low_out.shape, F32)
+        for i in range(dp):
+            low_all = low_all + jnp.where(seat == i, low_land[i], 0.0)
+        shift_grad[...] = dot_tn(silu[...], low_all.astype(BF16))
+        shift_bias[...] = jnp.sum(low_all, axis=0, keepdims=True)
+        for cp in packs:
+            cp.wait_recv()
+            cp.wait_send()
+        total = pack_z[0]
+        for i in range(1, place.line):
+            total = total + pack_z[i]
+        pack[...] = total
+    else:
+        shift_grad[...] = low_out[...]
+        shift_bias[...] = shift_grad[pl.ds(0, 1), :]
+    pack_t[t] = pack[...]
+    ends = []
+    for o in (1, 2, 3):
+        cp = remote(pack, pack_t.at[t], pt_s.at[o], pt_r.at[o], (d, (t + o) % 4))
+        cp.start()
+        ends.append(cp)
+    for half, out in zip(halves, (grad_latent, grad_skip)):
+        for k in range(CHUNKS):
+            sl, total = half.chunk(k)
+            out[sl, :] = total
+        half.sent()
+    if scatter:
+        scatters[2].pass_on()
+    for cp in ends:
+        cp.wait_recv()
+        cp.wait_send()
+    pack_sum[...] = pack_t[0] + pack_t[1] + pack_t[2] + pack_t[3]
+    for s in range(4):
+        pack_cols[s] = pack_t[s, pl.ds(PACK_SUMS, PACK_ROWS - PACK_SUMS), :]
+    if scatter:
+        out_mine[...] = scatters[0].result()
+        project_mine[...] = scatters[1].result()
+        skip_mine[...] = scatters[2].result()
+        for s in scatters:
+            s.sent()
+        lows.sent()
+    else:
+        out_mine[...] = jnp.zeros(out_mine.shape, F32)
+        project_mine[...] = jnp.zeros(project_mine.shape, F32)
+        skip_mine[...] = gskip[...]
+    for cp in copies + tiles:
+        cp.wait_send()
+
+
+PACK_ROWS, PACK_SUMS = 24, 16
+
+
+def tail_kernel(collective_id, dp, scatter, p, project_rows, residual, grad_second, skipped, norm_gain, skip_w, j0, j1, silu, pack_in, grad_out, grad_project):
+    rows, width = residual.shape
+    cols = skip_w.shape[1]
+    line = max(dp // 2, 1)
+    dma, vm = pltpu.SemaphoreType.DMA, pltpu.VMEM
+    seats = max(8, -(-dp // 8) * 8) if scatter else 8
+    skip_rows = skip_w.shape[0] // dp if scatter else skip_w.shape[0] // 2
+    out_shape = grad_out.shape[1:] if scatter else (8, LANES)
+    project_shape = grad_project.shape[1:] if scatter else (8, LANES)
+    gskip = (dp if scatter else 2, skip_rows, cols)
+    skip_shape = gskip[1:]
+    outs = [
+        shaped((rows, width), F32), shaped((rows, width), F32),
+        shaped(out_shape, F32), shaped(project_shape, F32),
+        shaped(skip_shape, F32) if scatter else shaped(gskip, BF16),
+        shaped((silu.shape[1], width) if scatter else (seats, width), F32), shaped((1, width), F32),
+        shaped((PACK_ROWS, width), F32), shaped((4, PACK_ROWS - PACK_SUMS, width), F32),
+    ]
+
+    def bufs(shape):
+        n = line if scatter else 1
+        s = shape if scatter else (16, LANES)
+        return [vm((n,) + s, BF16), vm((n,) + s, BF16), vm((max(n - 1, 1),) + s, BF16)]
+
+    scratch = [
+        vm((rows, width), BF16), vm((4, rows, cols), BF16), vm((4, rows, cols), BF16), vm(gskip, BF16),
+        vm((seats, width), F32), vm((4, seats, width), F32), vm((seats, width), F32), vm((dp if scatter else 1, seats, width), F32),
+        vm((PACK_ROWS, width), F32), vm((PACK_ROWS, width), F32), vm((line if scatter else 1, PACK_ROWS, width), F32), vm((4, PACK_ROWS, width), F32),
+        *bufs(out_shape), *bufs(project_shape), *bufs(skip_shape),
+        dma((4,)), dma((4,)), dma((4,)), dma((4,)), dma((dp,)), dma((dp,)), dma((1,)), dma((1,)), dma((line,)), dma((line,)), dma((4,)), dma((4,)),
+    ] + TensorSum.scratch(rows, width) * 2 + [dma((line,))] * 15
+    ins = [p, project_rows, residual, grad_second, skipped, norm_gain, skip_w, j0, j1, silu, pack_in, grad_out, grad_project]
+    return talking_kernel("tail", collective_id, functools.partial(tail_body, dp, scatter), ins, outs, scratch, in_hbm=(11, 12))
 
 
 def head_stats(u, mask, size):
@@ -420,8 +793,8 @@
 
 
 def self_bwd_body(
-    size, scale, heads, block, c_all, w_out, pre, low, lse, cosine, sine, gain, mask, fold,
-    p, p_low, gains, offsets, sums, do, dq, dk, dv,
+    size, scale, heads, block, c_all, w_out, pre, low, lse, cosine, sine, gain, mask, fold, mixed, x,
+    p, grad_out, grad_project, gains, offsets, sums, do, dq, dk, dv, p_low,
 ):
     rows = c_all.shape[0]
     span = heads * LANES
@@ -461,6 +834,10 @@
         return 0
 
     lax.fori_loop(0, rows // block, finish, 0)
+    by_place = lambda v: v.astype(BF16).reshape(grad_out.shape)
+    grad_out[...] = by_place(dot_tn(c_all[...], mixed[...]))
+    for part in range(3):
+        grad_project[:, part] = by_place(dot_tn(x[...], p_low[part]))
 
 
 def text_body(size, heads, real, x, w, bias, gain, offset, mask, pre, low):
@@ -500,7 +877,8 @@
 
 def cross_bwd_body(
     size, scale, heads, block, real, c_all, w_out, pre, low, text_pre, text_low, lse, cosine, sine, gain, text_gain, mask, fold,
-    p, p_low, text_p, text_p_low, gains, offsets, sums, text_sums, do, dq, dk, dv,
+    mixed, x, text, text_w,
+    p, grads, grad_text, gains, offsets, sums, text_sums, do, dq, dk, dv, p_low, text_p, text_p_low,
 ):
     rows = c_all.shape[0]
     span = heads * LANES
@@ -546,6 +924,20 @@
         text_sums[:, hs] = jnp.sum(low_v.astype(F32), axis=0, keepdims=True)
     for part in range(2):
         text_p_low[part] = dot_nt(text_p[:, pl.ds(part * span, span)], fold[...]).astype(BF16)
+    parts = grads.shape[0]
+
+    def put(start, value):
+        count = value.shape[0] // parts
+        grads[:, pl.ds(start, count)] = value.astype(BF16).reshape(parts, count, value.shape[1])
+        return start + count
+
+    at = put(0, dot_tn(c_all[...], mixed[...]))
+    at = put(at, dot_tn(x[...], p_low[...]))
+    for part in range(2):
+        at = put(at, dot_tn(text[...], text_p_low[part]))
+    grad_text[...] = (
+        dot_nt(text_p[:, pl.ds(0, span)], text_w[0]) + dot_nt(text_p[:, pl.ds(span, span)], text_w[1])
+    ).astype(BF16)
 
 
 def local_kernel(name, body, ins, outs, scratch=()):
@@ -559,10 +951,6 @@
         compiler_params=pltpu.CompilerParams(vmem_limit_bytes=VMEM_BYTES),
         name=name,
     )(*ins)
-
-
-def shaped(shape, dtype):
-    return jax.ShapeDtypeStruct(shape, dtype)
 
 
 def fold_matrix(heads, size):
@@ -608,31 +996,22 @@
     def narrow_cols(v):
         return jnp.dot(v, jnp.asarray(fold_np.T), precision=lax.Precision.HIGHEST)
 
-    small = jnp.concatenate([condition.astype(F32), true_counts.astype(F32)[:, None]], axis=1)
-    small_all = lax.all_gather(small, "dp", axis=0, tiled=True)
-    counted = jnp.sum(small_all[:, width])
-    silu_all = jax.nn.silu(small_all[:, :width]).astype(BF16)
-    silu_mine = lax.dynamic_slice_in_dim(silu_all, d * shift_proj.shape[0], shift_proj.shape[0], 1)
-    shift_term = lax.psum_scatter(dot_nn(silu_mine, shift_proj), "dp", scatter_dimension=0, tiled=True) + row_bias[3:4]
-
-    project_in = jnp.transpose(self_project, (1, 0, 2))
-    joined0, joined1, skip_g, project_g = gather_kernel(
-        "gather_joined", 0, dp, (latent, skip_states), (skip_proj, project_in)
-    )
-    out_t = lax.all_gather(self_output.T, "dp", axis=0, tiled=True)
-    query_full = lax.all_gather(cross_query, "dp", axis=0, tiled=True)
-    keyval_in = jnp.transpose(cross_keyval, (1, 0, 2))
-    keyval_g = lax.all_gather(keyval_in, "dp", axis=0, tiled=False)
-    cross_out_t = lax.all_gather(cross_output.T, "dp", axis=0, tiled=True)
-    up_full = lax.all_gather(hidden_up, "dp", axis=0, tiled=True)
-    down_t = lax.all_gather(hidden_down.T, "dp", axis=0, tiled=True)
-
-    skip_full = skip_g.reshape(2 * width, cols)
-    project_full = jnp.transpose(project_g, (1, 0, 2, 3)).reshape(3, width, cols)
-    project_wide = jnp.einsum("cdk,kl->cdl", project_full, fold, preferred_element_type=F32).astype(BF16)
+    own = shift_proj.shape[0] % 16 == 0 and self_output.shape[1] % 16 == 0 and dp % 2 == 0
+    parts = dp if own else 1
+    text_rows = jnp.pad(text_states[0], ((0, text_pad - text_len), (0, 0)))
+    share, text_share = self_output.shape[1], cross_keyval.shape[0]
+    few = jnp.concatenate(
+        [self_output.T, cross_query, cross_output.T, cross_keyval[:, 0], cross_keyval[:, 1]], axis=0
+    )
+    few_all = lax.all_gather(few, "dp", axis=0, tiled=False)
+    out_t = few_all[:, :share].reshape(width, cols)
+    query_full = few_all[:, share : 2 * share].reshape(width, cols)
+    cross_out_t = few_all[:, 2 * share : 3 * share].reshape(width, cols)
+    keyval_full = [
+        few_all[:, 3 * share + i * text_share : 3 * share + (i + 1) * text_share].reshape(-1, cols) for i in range(2)
+    ]
     query_wide = dot_nn(query_full, fold).astype(BF16)
-    keyval_full = jnp.transpose(keyval_g, (1, 0, 2, 3)).reshape(2, text_states.shape[2], cols)
-    keyval_wide = jnp.einsum("cdk,kl->cdl", keyval_full, fold, preferred_element_type=F32).astype(BF16)
+    keyval_wide = jnp.stack([dot_nn(v, fold).astype(BF16) for v in keyval_full])
 
     bias_cols = lax.dynamic_slice_in_dim(column_bias, t * cols, cols, 1)
     bias_wide = widen_cols(bias_cols)
@@ -655,16 +1034,39 @@
     cosine = jnp.cos(angles) * mask
     sine = jnp.sin(angles) * sign_np
 
-    joined0 = joined0.reshape(group, width)
-    joined1 = joined1.reshape(group, width)
-    skip_pre = dot_nn(joined0, skip_full[:width]) + dot_nn(joined1, skip_full[width:]) + bias_cols[4]
-    skipped = lax.all_to_all(skip_pre.astype(BF16), "tensor", split_axis=0, concat_axis=1, tiled=True)
-    cen, rstd = centre(skipped.astype(F32))
-    residual = cen * rstd * norm_gain[0] + norm_bias[0]
-    cen, rstd = centre(residual)
-    first_input = (cen * rstd * norm_gain[1] + norm_bias[1] + shift_term).astype(BF16)
-    (first_all,) = gather_kernel("gather_first", 1, dp, (first_input,))
-    first_all = first_all.reshape(group, width)
+    project_in = jnp.transpose(self_project, (1, 0, 2))
+    r = shift_proj.shape[0]
+    if own:
+        seats = max(8, -(-dp // 8) * 8)
+        lanes = -(-r // LANES) * LANES
+        slices = jnp.pad(condition.astype(F32).reshape(dp, r), ((0, 0), (0, lanes - r)))
+        slices = jnp.concatenate([slices, jnp.broadcast_to(true_counts.astype(F32)[:, None], (dp, LANES))], axis=1)
+        seat = (jnp.arange(seats) == d).astype(F32)
+        small = slices[:, None, :] * seat[None, :, None]
+        skip_in, shift_in = skip_proj, shift_proj
+    else:
+        small_all = lax.all_gather(
+            jnp.concatenate([condition.astype(F32), true_counts.astype(F32)[:, None]], axis=1), "dp", axis=0, tiled=True
+        )
+        silu_all = jax.nn.silu(small_all[:, :width]).astype(BF16)
+        silu = lax.dynamic_slice_in_dim(silu_all, d * r, r, 1)
+        shift_in = lax.psum_scatter(dot_nn(silu, shift_proj), "dp", scatter_dimension=0, tiled=True) + row_bias[3:4]
+        small = jnp.zeros((1, 8, LANES), F32)
+        skip_in = lax.all_gather(skip_proj, "dp", axis=0, tiled=True)
+        project_in = lax.all_gather(project_in, "dp", axis=0, tiled=False)
+    joined0, joined1, skip_g, project_g, skipped, residual, first_all, silu_k, counted = head_kernel(
+        0, dp, own, latent, skip_states, skip_in, project_in, small, shift_in, bias_cols[4:5], norm_gain, norm_bias, row_bias
+    )
+    if own:
+        silu, counted = silu_k, counted[0, 0]
+        skip_full = skip_g.reshape(2 * width, cols)
+    else:
+        counted, project_g, skip_full = jnp.sum(small_all[:, width]), project_in, skip_in
+    hold, first_hold = lax.optimization_barrier(((hidden_up, hidden_down.T), first_all))
+    up_full = lax.all_gather(hold[0], "dp", axis=0, tiled=True)
+    down_t = lax.all_gather(hold[1], "dp", axis=0, tiled=True)
+    project_full = jnp.transpose(project_g, (1, 0, 2, 3)).reshape(3, width, cols)
+    project_wide = jnp.einsum("cdk,kl->cdl", project_full, fold, preferred_element_type=F32).astype(BF16)
 
     lse_shape = (group // block, heads, block)
     pre, low, mixed, lse = local_kernel(
@@ -678,7 +1080,6 @@
         "fwd", "rows_self", 2, mixed, out_t, residual, row_bias[0:1], norm_gain[2:3], norm_bias[2:3]
     )
 
-    text_rows = jnp.pad(text_states[0], ((0, text_pad - text_len), (0, 0)))
     text_pre, text_low = local_kernel(
         "text_fwd",
         functools.partial(text_body, size, heads, text_len),
@@ -718,97 +1119,86 @@
         "bwd", "rows_up", 5, grad_upper_low, up_full, third_sum, norm_gain[3:4], grad_final
     )
 
-    qp, qp_low, text_p, text_p_low, cross_gains, cross_offsets, cross_sums, text_sums = local_kernel(
+    few_rows = 2 * share + 2 * text_share if own else 2 * width + 2 * text_states.shape[2]
+    qp, few_grads, text_part, cross_gains, cross_offsets, cross_sums, text_sums = local_kernel(
         "cross_bwd",
         functools.partial(cross_bwd_body, size, scale, heads, block, text_len),
         [c_all, cross_out_t, cross_pre, cross_low, text_pre, text_low, cross_lse, cosine, sine,
-         gain_wide[2:3], gain_wide[3:4], mask, fold],
-        [shaped((group, span), BF16), shaped((group, cols), BF16), shaped((text_pad, 2 * span), BF16),
-         shaped((2, text_pad, cols), BF16), shaped((2, LANES), F32), shaped((2, LANES), F32), shaped((1, span), F32), shaped((1, span), F32)],
-        [pltpu.VMEM((group, span), BF16), pltpu.VMEM((group, span), F32), pltpu.VMEM((text_pad, span), F32), pltpu.VMEM((text_pad, span), F32)],
+         gain_wide[2:3], gain_wide[3:4], mask, fold, cross_mixed, third_all, text_rows, keyval_wide],
+        [shaped((group, span), BF16), shaped((parts, few_rows, cols), BF16), shaped((text_pad, text_states.shape[2]), BF16),
+         shaped((2, LANES), F32), shaped((2, LANES), F32), shaped((1, span), F32), shaped((1, span), F32)],
+        [pltpu.VMEM((group, span), BF16), pltpu.VMEM((group, span), F32), pltpu.VMEM((text_pad, span), F32),
+         pltpu.VMEM((text_pad, span), F32), pltpu.VMEM((group, cols), BF16), pltpu.VMEM((text_pad, 2 * span), BF16),
+         pltpu.VMEM((2, text_pad, cols), BF16)],
     )
     s_all, grad_second, bias_attn, gain_third, offset_third = row_kernel(
         "bwd", "rows_query", 6, qp, query_wide, second, norm_gain[2:3], grad_third
     )
-    grad_cross_out_t = dot_tn(c_all, cross_mixed).astype(BF16)
-    grad_query = dot_tn(third_all, qp_low).astype(BF16)
-    grad_keyval = jnp.stack([dot_tn(text_rows, text_p_low[i]).astype(BF16) for i in range(2)])
-    grad_keyval = grad_keyval.reshape(2, dp, -1, cols).transpose(1, 0, 2, 3).reshape(-1, cols)
-    text_part = dot_nt(text_p[:, :span], keyval_wide[0]) + dot_nt(text_p[:, span:], keyval_wide[1])
-    grad_text = lax.psum(text_part[:text_len].astype(BF16), "tensor").astype(F32)[None]
-    cross_out_mine = lax.psum_scatter(grad_cross_out_t, "dp", scatter_dimension=0, tiled=True)
-    query_mine = lax.psum_scatter(grad_query, "dp", scatter_dimension=0, tiled=True)
-    keyval_mine = lax.psum_scatter(grad_keyval, "dp", scatter_dimension=0, tiled=True)
-
-    p, p_low, self_gains, self_offsets, self_sums = local_kernel(
+    if not own:
+        cuts = np.cumsum([0, width, width, text_states.shape[2], text_states.shape[2]])
+        few_grads = jnp.concatenate(
+            [few_grads[0, a:b].reshape(dp, -1, cols) for a, b in zip(cuts[:-1], cuts[1:])], axis=1
+        )
+    grad_text = lax.psum(text_part[:text_len], "tensor").astype(F32)[None]
+    few_mine = lax.psum_scatter(few_grads.reshape(-1, cols), "dp", scatter_dimension=0, tiled=True).astype(F32)
+
+    p, grad_out, grad_project, self_gains, self_offsets, self_sums = local_kernel(
         "self_bwd",
         functools.partial(self_bwd_body, size, scale, heads, block),
-        [s_all, out_t, pre, low, lse, cosine, sine, gain_wide[0:2], mask, fold],
-        [shaped((group, 3 * span), BF16), shaped((3, group, cols), BF16), shaped((2, LANES), F32), shaped((2, LANES), F32),
-         shaped((1, 3 * span), F32)],
-        [pltpu.VMEM((group, span), BF16)] + [pltpu.VMEM((group, span), F32)] * 3,
-    )
-    project_rows = jnp.transpose(project_wide, (1, 0, 2)).reshape(width, 3 * span)
-    k_low, bias_skip, gain_first, offset_first, gain_skip, offset_skip = row_kernel(
-        "first", "rows_project", 7, p, project_rows, residual, norm_gain[1:2], grad_second, skipped, norm_gain[0:1]
-    )
-    grad_out_t = dot_tn(s_all, mixed).astype(BF16)
-    grad_project = jnp.stack([dot_tn(first_all, p_low[i]).astype(BF16) for i in range(3)])
-    grad_project = grad_project.reshape(3, dp, -1, cols).transpose(1, 0, 2, 3).reshape(-1, cols)
-    out_mine = lax.psum_scatter(grad_out_t, "dp", scatter_dimension=0, tiled=True)
-    project_mine = lax.psum_scatter(grad_project, "dp", scatter_dimension=0, tiled=True)
-
-    k_cols = lax.all_to_all(k_low, "tensor", split_axis=1, concat_axis=0, tiled=True)
-    (grad_latent,) = row_kernel("plain", "rows_latent", 8, k_cols, skip_full[:width])
-    (grad_skip,) = row_kernel("plain", "rows_skip", 9, k_cols, skip_full[width:])
-    grad_skip_proj = jnp.concatenate([dot_tn(joined0, k_cols).astype(BF16), dot_tn(joined1, k_cols).astype(BF16)])
-    skip_mine = lax.psum_scatter(grad_skip_proj, "dp", scatter_dimension=0, tiled=True)
-
-    shift_parts = lax.all_gather(offset_first, ("dp", "tensor"), axis=0, tiled=True)
-    shift_low = jnp.sum(shift_parts.reshape(dp, tensor, width), axis=1).astype(BF16)
-    grad_shift_proj = dot_tn(silu_mine, shift_low)
-    bias_shift = jnp.sum(shift_low.astype(F32), axis=0)
-
-    head_gain_part = narrow_head(jnp.concatenate([self_gains, cross_gains], axis=0))
-    head_bias_part = narrow_head(jnp.concatenate([self_offsets, cross_offsets], axis=0))
+        [s_all, out_t, pre, low, lse, cosine, sine, gain_wide[0:2], mask, fold, mixed, first_all],
+        [shaped((group, 3 * span), BF16), shaped((parts, width // parts, cols), BF16), shaped((parts, 3, width // parts, cols), BF16),
+         shaped((2, LANES), F32), shaped((2, LANES), F32), shaped((1, 3 * span), F32)],
+        [pltpu.VMEM((group, span), BF16)] + [pltpu.VMEM((group, span), F32)] * 3 + [pltpu.VMEM((3, group, cols), BF16)],
+    )
+
+    head_part = jnp.concatenate([self_gains, cross_gains, self_offsets, cross_offsets], axis=0).reshape(1, -1)
     column_rows = narrow_cols(
         jnp.concatenate([self_sums[:, :span], self_sums[:, 2 * span :], cross_sums, text_sums], axis=0)
     )
-    column_part = lax.dynamic_update_slice_in_dim(jnp.zeros((4, width), F32), column_rows, t * cols, 1)
-    hidden_part = lax.dynamic_update_slice_in_dim(jnp.zeros(hidden_bias.shape, F32), bias_hidden, t * hidden, 0)
-    sums = lax.psum(
-        (
-            jnp.concatenate([gain_skip, gain_first, gain_third, gain_fourth]),
-            jnp.concatenate([offset_skip, offset_first, offset_third, offset_fourth]),
-            head_gain_part,
-            head_bias_part,
-            jnp.concatenate([column_part, bias_skip]),
-            hidden_part,
-            jnp.concatenate([bias_attn, bias_cross_out, bias_mlp]),
-        ),
-        ("dp", "tensor"),
-    )
+    own_cols = jnp.concatenate([column_rows.reshape(-1), bias_hidden])
+    sums_in = jnp.concatenate(
+        [jnp.zeros((5, width), F32), gain_third, gain_fourth, offset_third, offset_fourth, bias_attn, bias_cross_out, bias_mlp,
+         jnp.pad(head_part, ((0, 0), (0, width - head_part.shape[1]))), jnp.zeros((PACK_SUMS - 13, width), F32),
+         jnp.pad(own_cols, (0, (PACK_ROWS - PACK_SUMS) * width - own_cols.shape[0])).reshape(-1, width)], axis=0
+    )
+    project_rows = jnp.transpose(project_wide, (1, 0, 2)).reshape(width, 3 * span)
+    grad_latent, grad_skip, out_mine, project_mine, skip_mine, shift_grad, shift_bias, pack_sum, pack_cols = tail_kernel(
+        7, dp, own, p, project_rows, residual, grad_second, skipped, norm_gain, skip_full, joined0, joined1,
+        silu if own else jnp.zeros((8, LANES), BF16), sums_in, grad_out, grad_project,
+    )
+    if not own:
+        shift_all = lax.all_gather(shift_grad[:1], "dp", axis=0, tiled=True)
+        shift_bias = jnp.sum(shift_all, axis=0, keepdims=True)
+        shift_grad = dot_tn(silu, shift_all.astype(BF16))
+        pack_sum, pack_cols = lax.psum((pack_sum, pack_cols), "dp")
+        out_mine = lax.psum_scatter(grad_out[0], "dp", scatter_dimension=0, tiled=True)
+        project_mine = lax.psum_scatter(grad_project[0], "dp", scatter_dimension=1, tiled=True)
+        skip_mine = lax.psum_scatter(skip_mine.reshape(-1, cols), "dp", scatter_dimension=0, tiled=True)
+    cols_all = pack_cols.reshape(tensor, -1)
+    column_sums = jnp.transpose(cols_all[:, : 4 * cols].reshape(tensor, 4, cols), (1, 0, 2)).reshape(4, width)
+    hidden_sums = cols_all[:, 4 * cols : 4 * cols + hidden].reshape(-1)
+    head_sums = narrow_head(pack_sum[12, : 8 * LANES].reshape(8, LANES))
     return (
         block_out,
         grad_latent,
         grad_skip,
         grad_text,
         skip_mine.astype(F32),
-        grad_shift_proj,
-        jnp.transpose(project_mine.reshape(3, -1, cols), (1, 0, 2)).astype(F32),
+        shift_grad,
+        jnp.transpose(project_mine, (1, 0, 2)).astype(F32),
         out_mine.T.astype(F32),
-        query_mine.astype(F32),
-        jnp.transpose(keyval_mine.reshape(2, -1, cols), (1, 0, 2)).astype(F32),
-        cross_out_mine.T.astype(F32),
+        few_mine[share : 2 * share],
+        jnp.transpose(few_mine[2 * share :].reshape(2, text_share, cols), (1, 0, 2)),
+        few_mine[:share].T,
         up_mine.astype(F32),
         down_mine.T.astype(F32),
-        sums[0],
-        sums[1],
-        sums[2],
-        sums[3],
-        sums[4],
-        sums[5],
-        jnp.concatenate([sums[6], bias_shift[None]]),
+        jnp.concatenate([pack_sum[0:2], pack_sum[5:7]]),
+        jnp.concatenate([pack_sum[2:4], pack_sum[7:9]]),
+        head_sums[:4],
+        head_sums[4:],
+        jnp.concatenate([column_sums, pack_sum[4:5]]),
+        hidden_sums,
+        jnp.concatenate([pack_sum[9:12], shift_bias]),
     )
 
 

time: 1540 us -> 888 us (0.58)
  waiting for transfers between devices: 553 us -> 23.9 us
  blocking collectives: 239 us -> 0 us
  Pallas kernels: 513 us -> 710 us
  matrix products: 94.3 us -> 51.5 us
  other arithmetic: 36.9 us -> 16.6 us
    reduce_scatter x5 -> x1, waiting for transfers between devices: 281 us -> 0.01 us  [body(): lax.psum_scatter(few_grads.reshape(-1, cols), 'dp', scatter_dimension=0,...]
    all_gather x5 -> x0, blocking collectives: 189 us -> none  [the longest x1 42.9 us: body(): small_all = lax.all_gather(small, 'dp', axis=0, tiled=True)]
    pallas_call x10 -> x7, Pallas kernels: 409 us -> 592 us  [talking_kernel(): pl.pallas_call(body, out_shape=outs, in_specs=[anywhere if i in in_hbm el...]
    reduce_scatter x1, waiting for transfers between devices: 90.6 us -> 0.01 us  [body(): lax.psum_scatter(grad_down_t, 'dp', scatter_dimension=0, tiled=True)]
    unnamed x14 -> x7, waiting for transfers between devices: 71 us -> 1.3 us
    reduce_scatter x1, waiting for transfers between devices: 91.5 us -> 22.6 us  [body(): up_mine = lax.psum_scatter(grad_up, 'dp', scatter_dimension=0, tiled=True)]
    unnamed x1 -> x0, blocking collectives: 36.9 us -> none
    dot_general x13 -> x2, matrix products: 50.4 us -> 16.7 us  [dot_tn(): lax.dot_general(left, right, (((0,), (0,)), ((), ())), preferred_element_...]
  transfers between devices with their start and end apart: 14 -> 7, of which waited for: 9 -> 1; matrix products, arithmetic and copies ran while one was open for 11% -> 11% of each run, Pallas kernels for 19% -> 67%
where the time goes in v2:
time: 888 us; the launch traced here: 881 us
  Pallas kernels  710 us (80%)
  local copies, waits for them, and re-layouts  62.7 us (7%)
  matrix products  51.5 us (6%)
  waiting for transfers between devices  23.9 us (3%)
  other arithmetic  16.6 us (2%)
  between operations  15.7 us (2%)
    pallas_call x7, Pallas kernels, talking_kernel(): pl.pallas_call(body, out_shape=outs, in_specs=[anywhere if i in in_hbm el...  592 us
    pallas_call x5, Pallas kernels, local_kernel(): pl.pallas_call(body, out_shape=outs, in_specs=[vm] * len(ins), out_specs=...  119 us
    dot_general x5, matrix products, dot_nn(): return jnp.dot(left, right, preferred_element_type=F32)  27 us
    reduce_scatter x1, waiting for transfers between devices, body(): up_mine = lax.psum_scatter(grad_up, 'dp', scatter_dimension=0, tiled=True)  22.6 us
  transfers between devices with their start and end apart: 7, of which 1 were waited for; matrix products, arithmetic and copies ran while one was open for 11% of the time, Pallas kernels for 67%

profile of v2, /device:TPU:0, one launch (start us, length us, event | category | flops | bytes accessed | tf_op | source)
XLA Modules:
  0.0 881.2 jit_solution(15994616162210634519)
XLA Ops:
  15.8 148.0 %head.1 = (bf16[1024,1408]{1,0:T(8,128)(2,1)}, bf16[1024,1408]{1,0:T(8,128)(2,1)}, bf16[8,352,352]{2,1,0:T(8,128)(2,1)}, bf16[8,3,176,352]{3,2,1,0:T(8,128)(2,1)...) custom-call(bf16[256,1408]{1,0:T(8,128)(2,1)} %refs_0_.1, ...), custom_call_target="tpu_custom_call" | custom-call | tf_op jit(solution)/shard_map/head/pallas_call | solution.py:338
  165.0 2.3 copy.60
  172.6 2.0 pad.23.x.text
  176.0 3.6 sine_multiply_fusion
  179.6 5.4 convolution_convert_fusion.2.w
  185.0 25.6 %self_fwd.1 = (f32[1024,1024]{1,0:T(8,128)}, bf16[1024,1536]{1,0:T(8,128)(2,1)}, bf16[1024,352]{1,0:T(8,128)(2,1)}, f32[4,4,256]{2,1,0:T(4,128)}) custom-call(bf16[1024,1408]{1,0:T(8,128)(2,1)} %get-tuple-element.81.x, bf16[3,1408,512]{2,1,0:T(8,128)(2,1)} %convolution_convert_fusion.2.w, f32[3,1,512]{2,1,0:T(1,128)} %pad_maximum_fusion.7.bias, ...), custom_call_target="tpu_custom_call" | custom-call | tf_op jit(solution)/shard_map/self_fwd/pallas_call | solution.py:945
  217.3 3.5 text_fwd.1
  220.9 3.5 fusion.16
  224.4 41.7 %rows_self.1 = (bf16[1024,1408]{1,0:T(8,128)(2,1)}, f32[256,1408]{1,0:T(8,128)}) custom-call(bf16[1024,352]{1,0:T(8,128)(2,1)} %get-tuple-element.83.refs_0_.mixed, bf16[1408,352]{1,0:T(8,128)(2,1)} %bitcast.90, f32[256,1408]{1,0:T(8,128)} %get-tuple-element.84.refs_2_, f32[1,1408]{1,0:T(1,128)} %get-tuple-element.196.refs_3_, ...), custom_call_target="tpu_custom_call" | custom-call | tf_op jit(solution)/shard_map/rows_self/pallas_call | solution.py:338
  266.1 2.0 convolution_convert_fusion.3.w.refs_1_
  268.1 15.9 %cross_fwd.1 = (f32[1024,512]{1,0:T(8,128)}, bf16[1024,512]{1,0:T(8,128)(2,1)}, bf16[1024,352]{1,0:T(8,128)(2,1)}, f32[4,4,256]{2,1,0:T(4,128)}) custom-call(bf16[1024,1408]{1,0:T(8,128)(2,1)} %get-tuple-element.85.x, bf16[1408,512]{1,0:T(8,128)(2,1)} %convolution_convert_fusion.3.w.refs_1_, f32[1,512]{1,0:T(1,128)} %get-tuple-element.203.bias, ...), custom_call_target="tpu_custom_call" | custom-call | tf_op jit(solution)/shard_map/cross_fwd/pallas_call | solution.py:945
  284.0 41.7 %rows_cross.1 = (bf16[1024,1408]{1,0:T(8,128)(2,1)}, f32[256,1408]{1,0:T(8,128)}) custom-call(bf16[1024,352]{1,0:T(8,128)(2,1)} %get-tuple-element.87.refs_0_.mixed, bf16[1408,352]{1,0:T(8,128)(2,1)} %bitcast.92, f32[256,1408]{1,0:T(8,128)} %get-tuple-element.88.refs_2_, f32[1,1408]{1,0:T(1,128)} %get-tuple-element.197.refs_3_, ...), custom_call_target="tpu_custom_call" | custom-call | tf_op jit(solution)/shard_map/rows_cross/pallas_call | solution.py:338
  325.7 10.9 %multiply_convert_fusion = (bf16[1024,1536]{1,0:T(8,128)(2,1)}, f32[1024,1536]{1,0:T(8,128)}) fusion(f32[1536]{0:T(1024)S(1)} %dynamic_slice.7, bf16[1024,1408]{1,0:T(8,128)(2,1)} %get-tuple-element.89, bf16[1408,1536]{1,0:T(8,128)(2,1)} %all-gather.5.cloned.1.call-done.refs_1_), kind=kOutput, calls=%fused_computation.12 | convolution fusion | flops 4444913664 | bytes 16652288 | tf_op jit(solution)/shard_map/dot_general | solution.py:21
  336.7 44.6 %rows_mlp.1 = (bf16[1024,1408]{1,0:T(8,128)(2,1)}, bf16[256,1408]{1,0:T(8,128)(2,1)}, f32[256,1408]{1,0:T(8,128)}, f32[1,1408]{1,0:T(1,128)}) custom-call(bf16[1024,1536]{1,0:T(8,128)(2,1)} %get-tuple-element.218.refs_0_, bf16[1408,1536]{1,0:T(8,128)(2,1)} %all-gather.7.cloned.1.call-done.refs_1_, f32[256,1408]{1,0:T(8,128)} %get-tuple-element.92.refs_2_, ...), custom_call_target="tpu_custom_call" | custom-call | tf_op jit(solution)/shard_map/rows_mlp/pallas_call | solution.py:338
  381.3 12.6 %convert_reduce_fusion = (f32[1536]{0:T(1024)S(1)}, bf16[1024,1536]{1,0:T(8,128)(2,1)}) fusion(f32[1024,1536]{1,0:T(8,128)} %get-tuple-element.219, f32[1536]{0:T(1024)S(1)} %dynamic_slice.7, bf16[1024,1408]{1,0:T(8,128)(2,1)} %get-tuple-element.95, bf16[1408,1536]{1,0:T(8,128)(2,1)S(1)} %copy-done.3), kind=kOutput, calls=%fused_computation.11 | convolution fusion | flops 4465359360 | bytes 16658432 | tf_op jit(solution)/shard_map/dot_general | solution.py:21
  393.9 45.5 %rows_up.1 = (bf16[1024,1408]{1,0:T(8,128)(2,1)}, f32[256,1408]{1,0:T(8,128)}, f32[1,1408]{1,0:T(1,128)}, f32[1,1408]{1,0:T(1,128)}, f32[1,1408]{1,0:T(1,128)}) custom-call(bf16[1024,1536]{1,0:T(8,128)(2,1)} %get-tuple-element.183.refs_0_, bf16[1408,1536]{1,0:T(8,128)(2,1)} %all-gather.5.cloned.1.call-done.refs_1_, f32[256,1408]{1,0:T(8,128)} %get-tuple-element.92.refs_2_, ...), custom_call_target="tpu_custom_call" | custom-call | tf_op jit(solution)/shard_map/rows_up/pallas_call | solution.py:338
  439.4 29.6 %cross_bwd.1 = (bf16[1024,512]{1,0:T(8,128)(2,1)}, bf16[8,608,352]{2,1,0:T(8,128)(2,1)}, bf16[336,1024]{1,0:T(8,128)(2,1)}, f32[2,128]{1,0:T(2,128)}, f32[2,128]...) custom-call(bf16[1024,1408]{1,0:T(8,128)(2,1)} %get-tuple-element.97.c_all, bf16[1408,352]{1,0:T(8,128)(2,1)} %bitcast.93, ...), custom_call_target="tpu_custom_call" | custom-call | tf_op jit(solution)/shard_map/cross_bwd/pallas_call | solution.py:945
  469.0 2.1 slice_bitcast_fusion
  471.8 8.2 convolution_convert_fusion
  480.1 1.8 copy-done.5
  481.9 8.4 convolution_convert_fusion.1
  490.4 6.5 copy.66
  496.8 6.6 copy.67.refs_1_
  503.4 42.6 %rows_query.1 = (bf16[1024,1408]{1,0:T(8,128)(2,1)}, f32[256,1408]{1,0:T(8,128)}, f32[1,1408]{1,0:T(1,128)}, f32[1,1408]{1,0:T(1,128)}, f32[1,1408]{1,0:T(1,128)}) custom-call(bf16[1024,512]{1,0:T(8,128)(2,1)} %get-tuple-element.102.refs_0_, bf16[1408,512]{1,0:T(8,128)(2,1)} %convolution_convert_fusion.3.w.refs_1_, f32[256,1408]{1,0:T(8,128)} %get-tuple-element.88.refs_2_, ...), custom_call_target="tpu_custom_call" | custom-call | tf_op jit(solution)/shard_map/rows_query/pallas_call | solution.py:338
  546.2 44.1 %self_bwd.1 = (bf16[1024,1536]{1,0:T(8,128)(2,1)}, bf16[8,176,352]{2,1,0:T(8,128)(2,1)}, bf16[8,3,176,352]{3,2,1,0:T(8,128)(2,1)}, f32[2,128]{1,0:T(2,128)}, f32[2,128]{1,0:T(2,128)}, /*index=5*/f32[1,1536]{1,0:T(1,128)}) custom-call(bf16[1024,1408]{1,0:T(8,128)(2,1)} %get-tuple-element.104.c_all, bf16[1408,352]{1,0:T(8,128)(2,1)} %bitcast.91, ...), custom_call_target="tpu_custom_call" | custom-call | tf_op jit(solution)/shard_map/self_bwd/pallas_call | solution.py:945
  592.4 1.9 concatenate.35.refs_10_
  594.4 227.5 %tail.1 = (f32[256,1408]{1,0:T(8,128)}, f32[256,1408]{1,0:T(8,128)}, f32[176,352]{1,0:T(8,128)}, f32[3,176,352]{2,1,0:T(8,128)}, f32[352,352]{1,0:T(8,128)}, /*i...) custom-call(bf16[1024,1536]{1,0:T(8,128)(2,1)} %get-tuple-element.108.refs_0_, ...), custom_call_target="tpu_custom_call" | custom-call | tf_op jit(solution)/shard_map/tail/pallas_call | solution.py:338
  831.0 3.2 copy.70
  839.6 2.1 convert_bitcast_fusion
  841.8 22.6 %reduce-scatter.6.cloned.1.call-done = bf16[176,1536]{1,0:T(8,128)(2,1)} async-done(((bf16[1408,1536]{1,0:T(8,128)(2,1)}), bf16[176,1536]{1,0:T(8,128)(2,1)}) %reduce-scatter.6.cloned.1.call-update) | async-done | bytes 540688 | tf_op jit(solution)/shard_map/reduce_scatter | solution.py:1117
  864.4 2.1 convert_element_type.82
  866.5 2.1 copy.91
  (169 shorter events, 45.1 us)
Async XLA Ops:
  7.2 160.1 %copy-start = (f32[4,88]{1,0:T(4,128)S(1)}, f32[4,88]{1,0:T(4,128)}, u32[]{:S(2)}) copy-start(f32[4,88]{1,0:T(4,128)} %param.52) | copy-start | bytes 4228
  7.2 205.7 %all-gather.9.cloned.1.call-start = ((), (), s32[]{:S(2)}) async-start(), calls=%async_computation.9 | async-start | bytes 5419008 | tf_op jit(solution)/shard_map/all_gather | solution.py:1006
  12.2 313.6 %all-gather.5.cloned.1.call-start = ((), (), s32[]{:S(2)}) async-start(), calls=%async_computation.3 | async-start | bytes 4866048 | tf_op jit(solution)/shard_map/all_gather | solution.py:1066
  163.8 172.8 %all-gather.7.cloned.1.call-start = ((), (), s32[]{:S(2)}) async-start(), calls=%async_computation.4 | async-start | bytes 4866048 | tf_op jit(solution)/shard_map/all_gather | solution.py:1067
  164.6 666.4 %all-reduce.8.cloned.1.call-start = ((), (), s32[]{:S(2)}) async-start(), calls=%async_computation.5 | async-start | bytes 1376256 | tf_op jit(solution)/shard_map/psum | solution.py:1142
  165.0 11.0 %copy-start.33 = (f32[128]{0:T(128)S(1)}, f32[128]{0:T(128)}, u32[]{:S(2)}) copy-start(f32[128]{0:T(128)} %constant.68.clone) | copy-start | bytes 1540
  165.0 11.0 %copy-start.34 = (f32[128]{0:T(128)S(1)}, f32[128]{0:T(128)}, u32[]{:S(2)}) copy-start(f32[128]{0:T(128)} %constant.69.clone) | copy-start | bytes 1540
  165.0 11.0 %copy-start.35 = (f32[128]{0:T(128)S(1)}, f32[128]{0:T(128)}, u32[]{:S(2)}) copy-start(f32[128]{0:T(128)} %constant.88) | copy-start | bytes 1540
  165.0 11.0 %copy-start.36 = (f32[128]{0:T(128)S(1)}, f32[128]{0:T(128)}, u32[]{:S(2)}) copy-start(f32[128]{0:T(128)} %constant.89) | copy-start | bytes 1540
  185.0 26.6 %copy-start.18 = (f32[4,1408]{1,0:T(4,128)S(1)}, f32[4,1408]{1,0:T(4,128)}, u32[]{:S(2)}) copy-start(f32[4,1408]{1,0:T(4,128)} %refs_8_.1) | copy-start | bytes 67588
  185.0 27.2 %copy-start.15 = (f32[4,1408]{1,0:T(4,128)S(1)}, f32[4,1408]{1,0:T(4,128)}, u32[]{:S(2)}) copy-start(f32[4,1408]{1,0:T(4,128)} %refs_5_.3) | copy-start | bytes 67588
  185.0 27.2 %copy-start.16 = (f32[4,1408]{1,0:T(4,128)S(1)}, f32[4,1408]{1,0:T(4,128)}, u32[]{:S(2)}) copy-start(f32[4,1408]{1,0:T(4,128)} %refs_9_.1) | copy-start | bytes 67588
  336.7 44.6 %copy-start.3 = (bf16[1408,1536]{1,0:T(8,128)(2,1)S(1)}, bf16[1408,1536]{1,0:T(8,128)(2,1)}, u32[]{:S(2)}) copy-start(bf16[1408,1536]{1,0:T(8,128)(2,1)} %all-gather.7.cloned.1.call-done.refs_1_) | copy-start | bytes 12976132
  471.1 363.1 %reduce-scatter.4.cloned.1.call-start = ((), (), s32[]{:S(2)}) async-start(), calls=%async_computation.6 | async-start | bytes 4202496 | tf_op jit(solution)/shard_map/reduce_scatter | solution.py:1143
  471.7 367.9 %reduce-scatter.8.cloned.1.call-start = ((), (), s32[]{:S(2)}) async-start(), calls=%async_computation.8 | async-start | bytes 4866048 | tf_op jit(solution)/shard_map/reduce_scatter | solution.py:1116
  480.0 384.3 %reduce-scatter.6.cloned.1.call-start = ((), (), s32[]{:S(2)}) async-start(), calls=%async_computation.7 | async-start | bytes 4866048 | tf_op jit(solution)/shard_map/reduce_scatter | solution.py:1117
  546.0 44.9 %copy-start.11 = (f32[512,352]{1,0:T(8,128)S(1)}, f32[512,352]{1,0:T(8,128)}, u32[]{:S(2)}) copy-start(f32[512,352]{1,0:T(8,128)} %constant.71.clone) | copy-start | bytes 2162692
  546.0 44.9 %copy-start.27 = (f32[1,512]{1,0:T(1,128)S(1)}, f32[1,512]{1,0:T(1,128)}, u32[]{:S(2)}) copy-start(f32[1,512]{1,0:T(1,128)} %get-tuple-element.127) | copy-start | bytes 6148
  546.1 44.9 %copy-start.28 = (f32[1,512]{1,0:T(1,128)S(1)}, f32[1,512]{1,0:T(1,128)}, u32[]{:S(2)}) copy-start(f32[1,512]{1,0:T(1,128)} %get-tuple-element.128) | copy-start | bytes 6148
  546.1 45.5 %copy-start.31 = (f32[2,128]{1,0:T(2,128)S(1)}, f32[2,128]{1,0:T(2,128)}, u32[]{:S(2)}) copy-start(f32[2,128]{1,0:T(2,128)} %get-tuple-element.123) | copy-start | bytes 3076
  546.1 45.5 %copy-start.32 = (f32[2,128]{1,0:T(2,128)S(1)}, f32[2,128]{1,0:T(2,128)}, u32[]{:S(2)}) copy-start(f32[2,128]{1,0:T(2,128)} %get-tuple-element.125) | copy-start | bytes 3076
  546.1 46.3 %copy-start.20 = (f32[1,1408]{1,0:T(1,128)S(1)}, f32[1,1408]{1,0:T(1,128)}, u32[]{:S(2)}) copy-start(f32[1,1408]{1,0:T(1,128)} %get-tuple-element.121) | copy-start | bytes 16900
  546.1 46.3 %copy-start.21 = (f32[1,1408]{1,0:T(1,128)S(1)}, f32[1,1408]{1,0:T(1,128)}, u32[]{:S(2)}) copy-start(f32[1,1408]{1,0:T(1,128)} %get-tuple-element.120) | copy-start | bytes 16900
  546.1 46.3 %copy-start.22 = (f32[1,1408]{1,0:T(1,128)S(1)}, f32[1,1408]{1,0:T(1,128)}, u32[]{:S(2)}) copy-start(f32[1,1408]{1,0:T(1,128)} %get-tuple-element.116) | copy-start | bytes 16900
  546.1 46.3 %copy-start.23 = (f32[1,1408]{1,0:T(1,128)S(1)}, f32[1,1408]{1,0:T(1,128)}, u32[]{:S(2)}) copy-start(f32[1,1408]{1,0:T(1,128)} %get-tuple-element.118) | copy-start | bytes 16900
  546.1 46.3 %copy-start.24 = (f32[1,1408]{1,0:T(1,128)S(1)}, f32[1,1408]{1,0:T(1,128)}, u32[]{:S(2)}) copy-start(f32[1,1408]{1,0:T(1,128)} %get-tuple-element.119) | copy-start | bytes 16900
  546.1 46.3 %copy-start.25 = (f32[1,1408]{1,0:T(1,128)S(1)}, f32[1,1408]{1,0:T(1,128)}, u32[]{:S(2)}) copy-start(f32[1,1408]{1,0:T(1,128)} %get-tuple-element.115) | copy-start | bytes 16900
  546.2 46.3 %copy-start.26 = (f32[1,1408]{1,0:T(1,128)S(1)}, f32[1,1408]{1,0:T(1,128)}, u32[]{:S(2)}) copy-start(f32[1,1408]{1,0:T(1,128)} %get-tuple-element.117) | copy-start | bytes 16900
  594.4 231.7 %copy-start.17 = (f32[128,88]{1,0:T(8,128)S(1)}, f32[128,88]{1,0:T(8,128)}, u32[]{:S(2)}) copy-start(f32[128,88]{1,0:T(8,128)} %constant.72.clone) | copy-start | bytes 135172
  836.1 32.5 %copy-start.7 = (f32[256,1408]{1,0:T(8,128)S(1)}, f32[256,1408]{1,0:T(8,128)}, u32[]{:S(2)}) copy-start(f32[256,1408]{1,0:T(8,128)} %get-tuple-element.243) | copy-start | bytes 4325380
  841.8 27.9 %copy-start.6 = (f32[256,1408]{1,0:T(8,128)S(1)}, f32[256,1408]{1,0:T(8,128)}, u32[]{:S(2)}) copy-start(f32[256,1408]{1,0:T(8,128)} %get-tuple-element.244) | copy-start | bytes 4325380
  869.7 4.5 copy-start.1
  (13 other events, 39.0 us)
Sparse Core Ops, SparseCore 0:
  12.3 137.8 all-gather.8
  164.0 82.0 all-gather.4
  248.3 73.1 all-gather.6
  471.2 41.4 all-reduce.7
  516.7 81.8 reduce-scatter.3
  602.5 144.5 reduce-scatter.7
  750.7 113.6 reduce-scatter.5

commit v3 on v1

v3 whole, which is shorter than its diff:
```python
import functools
from types import SimpleNamespace

import jax
import jax.numpy as jnp
import numpy as np
from jax import lax
from jax.experimental import pallas as pl
from jax.experimental.pallas import tpu as pltpu
from jax.sharding import PartitionSpec as P

EPSILON = 1e-06
MESH = pl.DeviceIdType.MESH
BF16, F32 = jnp.bfloat16, jnp.float32
LANES = 128
CHUNKS = 2
VMEM_BYTES = 60 * 2**20
NEGATIVE = -1e30


def dot_nn(left, right):
    return jnp.dot(left, right, preferred_element_type=F32)


def dot_nt(left, right):
    return lax.dot_general(left, right, (((1,), (1,)), ((), ())), preferred_element_type=F32)


def dot_tn(left, right):
    return lax.dot_general(left, right, (((0,), (0,)), ((), ())), preferred_element_type=F32)


def centre(x):
    cen = x - jnp.mean(x, axis=-1, keepdims=True)
    spread = jnp.mean(cen * cen, axis=-1, keepdims=True)
    return cen, lax.rsqrt(spread + EPSILON)


def norm_back(total, x, gain):
    cen, rstd = centre(x)
    xhat = cen * rstd
    dg = total * gain
    back = rstd * (
        dg - jnp.mean(dg, axis=-1, keepdims=True) - xhat * jnp.mean(dg * xhat, axis=-1, keepdims=True)
    )
    return back, xhat


def remote(src, dst, send_sem, recv_sem, device):
    return pltpu.make_async_remote_copy(
        src_ref=src, dst_ref=dst, send_sem=send_sem, recv_sem=recv_sem, device_id=device, device_id_type=MESH
    )


def tensor_place():
    d, t = lax.axis_index("dp"), lax.axis_index("tensor")
    y, c = t // 2, t % 2
    return d, t, y, c, (d, 2 * y + 1 - c), (d, 2 * (1 - y) + c)


def greet(peers):
    bar = pltpu.get_barrier_semaphore()
    for peer in peers:
        pl.semaphore_signal(bar, inc=1, device_id=peer, device_id_type=MESH)
    return bar


class DpPlace:
    def __init__(self, dp):
        self.d, self.t = lax.axis_index("dp"), lax.axis_index("tensor")
        self.dp, self.line = dp, dp // 2
        self.zi, self.par = self.d // 2, self.d % 2
        self.pair = (2 * self.zi + 1 - self.par, self.t)
        self.e0, self.e3 = (3 - self.zi) // 3, self.zi // 3
        self.end = self.e0 + self.e3

    def at(self, zi):
        return 2 * zi + self.par

    def ahead(self, j):
        return 2 * ((self.zi + j) % self.line) + self.par

    def behind(self, j):
        return 2 * ((self.zi + self.line - j) % self.line) + self.par

    def near(self):
        return [self.pair] + [(self.ahead(j), self.t) for j in range(1, self.line)]

    def others(self):
        return [((self.d + j) % self.dp, self.t) for j in range(1, self.dp)]


class ToAll:
    def __init__(self, place, source, land, send_sem, recv_sem):
        self.copies = []
        for j in range(1, place.dp):
            q = (place.d + j) % place.dp
            cp = remote(source(q), land.at[place.d], send_sem.at[j], recv_sem.at[j], (q, place.t))
            cp.start()
            self.copies.append(cp)

    def arrived(self):
        for cp in self.copies:
            cp.wait_recv()

    def sent(self):
        for cp in self.copies:
            cp.wait_send()


class WeightGather:
    def __init__(self, place, shard, land, z_s, z_r, x_s, x_r):
        self.place, self.land, self.z_s, self.z_r, self.x_s, self.x_r = place, land, z_s, z_r, x_s, x_r
        self.z = {}
        for j in (2, 1, 3):
            self.z[j] = remote(shard, land.at[place.d], z_s.at[j], z_r.at[j], (place.ahead(j), place.t))
            self.sends(j, self.z[j].start)
        cp = remote(shard, land.at[place.d], x_s.at[0], x_r.at[0], place.pair)
        cp.start()
        self.x = [cp]
        source = place.behind(2)
        self.inner = remote(
            land.at[source], land.at[source], z_s.at[0], z_r.at[1 + 2 * (place.zi // 2)], (place.at(3 * (place.zi // 2)), place.t)
        )

    def sends(self, j, act):
        if j == 2:
            act()
        else:
            pl.when(self.place.zi != (0 if j == 3 else 3))(act)

    def forward(self):
        e0 = self.place.e0
        for j in (2, 1 + 2 * e0, 3 - 2 * e0):
            source = self.place.behind(j)
            here = self.land.at[source]
            remote(here, here, self.z_s.at[j], self.z_r.at[j], self.place.pair).wait_recv()
            if isinstance(j, int):
                pl.when(self.place.end == 0)(self.inner.start)
            cp = remote(here, here, self.x_s.at[j], self.x_r.at[j], self.place.pair)
            cp.start()
            self.x.append(cp)

    def arrived(self):
        for cp in self.x:
            cp.wait_recv()

    def sent(self):
        for j in (1, 2, 3):
            self.sends(j, self.z[j].wait_send)
        pl.when(self.place.end == 0)(self.inner.wait_send)
        for cp in self.x:
            cp.wait_send()


class Gathers:
    def __init__(self, place, z_s, z_r, x_s, x_r):
        self.place, self.sems, self.all, self.passed = place, (z_s, z_r, x_s, x_r), [], 0

    def add(self, shard, land, pieces=1):
        start = 0
        for i in range(pieces):
            count = piece_rows(shard.shape[0], pieces, i) if pieces > 1 else None
            src = shard if count is None else shard.at[pl.ds(start, count)]
            dst = land if count is None else land.at[:, pl.ds(start, count)]
            start += count or 0
            self.all.append(WeightGather(self.place, src, dst, *[v.at[len(self.all)] for v in self.sems]))

    def forward(self, count=1):
        for _ in range(count):
            self.all[self.passed].forward()
            self.passed += 1

    def arrived(self, first, last):
        for g in self.all[first:last]:
            g.arrived()

    def sent(self):
        for g in self.all:
            g.sent()

    @staticmethod
    def scratch(count, line):
        return [pltpu.SemaphoreType.DMA((count, line))] * 4


def piece_rows(rows, pieces, i):
    tiles = rows // 16
    return 16 * (tiles * (i + 1) // pieces - tiles * i // pieces)


class GradScatter:
    def __init__(self, place, source, own, xland, zland, own_sem, x_s, x_r, z_s, z_r):
        self.place, self.own, self.xland, self.zland, self.z_s, self.z_r = place, own, xland, zland, z_s, z_r
        self.at, self.x, self.local, self.z = 0, [], [], []
        zi, e0, e3, end = place.zi, place.e0, place.e3, place.end
        self.order = [1 + 2 * e0, 3 - end, 2 - e0 + e3, 0]
        self.owners = [(zi + i) % 4 for i in self.order]
        self.routes = [
            (zi + 1 - 2 * e3, 3 * end, 1 - end),
            (self.owners[1], self.order[1] - 1, self.order[1]),
            (self.owners[2], self.order[2] - 1, self.order[2]),
        ]
        for k, j in enumerate(self.owners):
            cp = remote(source.at[2 * j + 1 - place.par], xland.at[j], x_s.at[k], x_r.at[k], place.pair)
            cp.start()
            self.x.append(cp)
            cp = pltpu.make_async_copy(source.at[2 * j + place.par], own.at[j], own_sem.at[k])
            cp.start()
            self.local.append(cp)

    def arrival(self, slot, sem):
        return remote(self.own.at[0], self.zland.at[slot], self.z_s.at[0], self.z_r.at[sem], self.place.pair)

    def step(self):
        k = self.at
        self.at += 1
        j = self.owners[k]
        self.local[k].wait()
        self.x[k].wait_recv()
        self.own[j] = (self.own[j].astype(F32) + self.xland[j].astype(F32)).astype(BF16)
        if k == 2:

            @pl.when(self.place.end == 0)
            def _():
                self.arrival(3, 0).wait_recv()
                self.own[j] = (self.own[j].astype(F32) + self.zland[3].astype(F32)).astype(BF16)

        to, slot, sem = self.routes[k]
        cp = remote(self.own.at[j], self.zland.at[slot], self.z_s.at[k], self.z_r.at[sem], (self.place.at(to), self.place.t))
        cp.start()
        self.z.append(cp)

    def steps(self, count=3):
        while self.at < min(3, count):
            self.step()

    def result(self):
        zi = self.place.zi
        self.local[3].wait()
        self.x[3].wait_recv()
        for slot in range(3):
            if slot == 1:
                self.arrival(1, 2).wait_recv()
            else:
                absent = 0 if slot == 0 else 3

                @pl.when(zi == absent)
                def _(slot=slot):
                    self.zland[slot] = jnp.zeros(self.zland.shape[1:], BF16)

                pl.when(zi != absent)(self.arrival(slot, slot + 1).wait_recv)
        total = self.own[zi].astype(F32) + self.xland[zi].astype(F32)
        for slot in range(3):
            total = total + self.zland[slot].astype(F32)
        return total

    def sent(self):
        for cp in self.x + self.z:
            cp.wait_send()

    @staticmethod
    def buffers(shape):
        return [pltpu.VMEM((4,) + shape, BF16)] * 3

    @staticmethod
    def scratch():
        return [pltpu.SemaphoreType.DMA((4,))] * 5


class TensorSum:
    def __init__(self, near, far, csend, crecv, ysend, yrecv, cs, cr, ys, yr):
        self.near, self.far, self.csend, self.crecv, self.ysend, self.yrecv = near, far, csend, crecv, ysend, yrecv
        self.cs, self.cr, self.ys, self.yr = cs, cr, ys, yr
        _, self.t, self.y, self.c, self.sib, self.yp = tensor_place()

    def core(self, i, value):
        self.csend[i] = value.astype(BF16)
        cp = remote(self.csend.at[i], self.crecv.at[i], self.cs.at[i], self.cr.at[i], self.sib)
        cp.start()
        return cp

    def start(self, product, ready=None):
        there, here = 2 * (1 - self.y), 2 * self.y
        first = product(there + 1 - self.c)
        if ready is not None:
            ready()
        self.c0 = self.core(0, first)
        self.far[...] = product(there + self.c)
        self.c1 = self.core(1, product(here + 1 - self.c))
        self.c0.wait_recv()
        self.ycs = []
        ch = self.far.shape[0] // CHUNKS
        for k in range(CHUNKS):
            sl = pl.ds(k * ch, ch)
            self.ysend[sl, :] = (self.far[sl, :] + self.crecv[0, sl, :].astype(F32)).astype(BF16)
            cp = remote(self.ysend.at[sl], self.yrecv.at[sl], self.ys.at[k], self.yr.at[k], self.yp)
            cp.start()
            self.ycs.append(cp)
        self.near[...] = product(here + self.c)
        self.c1.wait_recv()

    def chunk(self, k):
        ch = self.far.shape[0] // CHUNKS
        sl = pl.ds(k * ch, ch)
        self.ycs[k].wait_recv()
        return sl, self.near[sl, :] + self.crecv[1, sl, :].astype(F32) + self.yrecv[sl, :].astype(F32)

    def sent(self):
        for cp in [self.c0, self.c1] + self.ycs:
            cp.wait_send()

    @staticmethod
    def scratch(rows, width):
        dma = pltpu.SemaphoreType.DMA
        vm = pltpu.VMEM
        return [
            vm((rows, width), F32), vm((rows, width), F32), vm((2, rows, width), BF16), vm((2, rows, width), BF16),
            vm((rows, width), BF16), vm((rows, width), BF16), dma((2,)), dma((2,)), dma((CHUNKS,)), dma((CHUNKS,)),
        ]


class RowSpread:
    def __init__(self, spread, rows, ys, yr, cs, cr, fs, fr):
        self.spread, self.rows = spread, rows
        self.sems = (ys, yr, cs, cr, fs, fr)
        _, self.t, self.y, self.c, self.sib, self.yp = tensor_place()
        self.parts, self.passed = [], []

    def at(self, owner, start, count):
        return self.spread.at[pl.ds(pl.multiple_of(owner * self.rows + start, 16), count)]

    def send(self, start, count):
        ys, yr, cs, cr, _, _ = self.sems
        k = len(self.parts)
        here = self.at(self.t, start, count)
        a = remote(here, here, ys.at[k], yr.at[k], self.yp)
        b = remote(here, here, cs.at[k], cr.at[k], self.sib)
        a.start()
        b.start()
        self.parts.append((a, b, start, count))

    def forward(self):
        fs, fr = self.sems[4:]
        for k, (a, _, start, count) in enumerate(self.parts):
            a.wait_recv()
            there = self.at(2 * (1 - self.y) + self.c, start, count)
            cp = remote(there, there, fs.at[k], fr.at[k], self.sib)
            cp.start()
            self.passed.append(cp)

    def finish(self):
        for (a, b, _, _), cp in zip(self.parts, self.passed):
            b.wait_recv()
            cp.wait_recv()
            a.wait_send()
            b.wait_send()
            cp.wait_send()

    @staticmethod
    def scratch(parts=CHUNKS):
        return [pltpu.SemaphoreType.DMA((parts,))] * 6


def shaped(shape, dtype):
    return jax.ShapeDtypeStruct(shape, dtype)


def named_kernel(name, collective_id, body, ins, outs, scratch, hbm=()):
    vm, anywhere = pl.BlockSpec(memory_space=pltpu.VMEM), pl.BlockSpec(memory_space=pl.ANY)
    flat = []
    for v in scratch.values():
        flat.extend(v if isinstance(v, list) else [v])

    def kernel(*refs):
        left = list(refs)
        n = SimpleNamespace()
        for k in [*ins, *outs]:
            setattr(n, k, left.pop(0))
        for k, v in scratch.items():
            if isinstance(v, list):
                setattr(n, k, [left.pop(0) for _ in v])
            else:
                setattr(n, k, left.pop(0))
        body(n)

    talks = {} if collective_id is None else {"collective_id": collective_id, "has_side_effects": True}
    got = pl.pallas_call(
        kernel,
        out_shape=list(outs.values()),
        in_specs=[anywhere if k in hbm else vm for k in ins],
        out_specs=[anywhere if k in hbm else vm for k in outs],
        scratch_shapes=flat,
        compiler_params=pltpu.CompilerParams(vmem_limit_bytes=VMEM_BYTES, **talks),
        name=name,
    )(*ins.values())
    return SimpleNamespace(**dict(zip(outs, got)))


def block_rows(b, rows):
    return pl.ds(pl.multiple_of(b * rows, rows), rows)


def add_sums(sums, parts):
    parts = [jnp.sum(v, axis=0, keepdims=True) for v in parts]
    return parts if sums is None else [a + b for a, b in zip(sums, parts)]


def forward_rows(reduce, spread, spread_ref, resid, bias, gain, offset, out, rows):
    ch = rows // CHUNKS
    for k in range(CHUNKS):
        sl, total = reduce.chunk(k)
        value = resid[sl, :] + (total + bias[...])
        out[sl, :] = value
        cen, rstd = centre(value)
        low = (cen * rstd * gain[...] + offset[...]).astype(BF16)
        spread_ref[pl.ds(pl.multiple_of(reduce.t * rows + k * ch, ch), ch), :] = low
        spread.send(k * ch, ch)


def backward_rows(reduce, spread, spread_ref, x, gain, before, out, sum_refs, rows):
    ch = rows // CHUNKS
    sums = None
    for k in range(CHUNKS):
        sl, total = reduce.chunk(k)
        back, xhat = norm_back(total, x[sl, :], gain[...])
        grad = before[sl, :] + back
        out[sl, :] = grad
        low = grad.astype(BF16)
        spread_ref[pl.ds(pl.multiple_of(reduce.t * rows + k * ch, ch), ch), :] = low
        spread.send(k * ch, ch)
        sums = add_sums(sums, [low.astype(F32), total * xhat, total])
    for ref, v in zip(sum_refs, sums):
        ref[...] = v


def head_stats(u, mask, size):
    mean = jnp.sum(u, axis=-1, keepdims=True) * (1.0 / size)
    cen = (u - mean) * mask
    spread = jnp.sum(cen * cen, axis=-1, keepdims=True) * (1.0 / size)
    return cen, lax.rsqrt(spread + EPSILON)


def head_norm(u, mask, gain, offset, size):
    cen, rstd = head_stats(u, mask, size)
    return cen * rstd * gain + offset


def turn(u, cosine, sine):
    return u * cosine + pltpu.roll(u, LANES // 2, 1) * sine


def turn_back(u, cosine, sine):
    return u * cosine - pltpu.roll(u, LANES // 2, 1) * sine


def head_back(grad, u, mask, gain, size):
    cen, rstd = head_stats(u, mask, size)
    xhat = cen * rstd
    dg = grad * gain
    mean = jnp.sum(dg, axis=-1, keepdims=True) * (1.0 / size)
    inner = jnp.sum(dg * xhat, axis=-1, keepdims=True) * (1.0 / size)
    back = rstd * ((dg - mean) * mask - xhat * inner)
    return back, jnp.sum(grad * xhat, axis=0, keepdims=True), jnp.sum(grad, axis=0, keepdims=True)


def head_at(h):
    return pl.ds(h * LANES, LANES)


def attend(q_ref, k_ref, v_ref, out_ref, lse_ref, heads, scale, block, real_keys):
    queries, keys = q_ref.shape[0], k_ref.shape[0]

    def step(i, _):
        here = pl.ds(pl.multiple_of(i * block, block), block)
        for h in range(heads):
            hs = head_at(h)
            scores = dot_nt(k_ref[:, hs], q_ref[here, hs]) * scale
            if real_keys < keys:
                place = lax.broadcasted_iota(jnp.int32, scores.shape, 0)
                scores = jnp.where(place < real_keys, scores, NEGATIVE)
            highest = jnp.max(scores, axis=0, keepdims=True)
            exponent = jnp.exp(scores - highest)
            denominator = jnp.sum(exponent, axis=0, keepdims=True)
            probs = (exponent * (1.0 / denominator)).astype(BF16)
            mixed = dot_tn(v_ref[:, hs], probs)
            out_ref[here, hs] = mixed.T.astype(BF16)
            lse_ref[i, pl.ds(h, 1), :] = highest + jnp.log(denominator)
        return 0

    lax.fori_loop(0, queries // block, step, 0)


def attend_back(q_ref, k_ref, v_ref, do_ref, lse_ref, dq_ref, dk_ref, dv_ref, heads, scale, block, real_keys):
    queries, keys = q_ref.shape[0], k_ref.shape[0]
    dk_ref[...] = jnp.zeros(dk_ref.shape, F32)
    dv_ref[...] = jnp.zeros(dv_ref.shape, F32)

    def step(i, _):
        here = pl.ds(pl.multiple_of(i * block, block), block)
        for h in range(heads):
            hs = head_at(h)
            q, k, v, do = q_ref[here, hs], k_ref[:, hs], v_ref[:, hs], do_ref[here, hs]
            scores = dot_nt(k, q) * scale
            if real_keys < keys:
                place = lax.broadcasted_iota(jnp.int32, scores.shape, 0)
                scores = jnp.where(place < real_keys, scores, NEGATIVE)
            probs = jnp.exp(scores - lse_ref[i, pl.ds(h, 1), :])
            grad_probs = dot_nt(v, do)
            inner = jnp.sum(probs * grad_probs, axis=0, keepdims=True)
            grad_scores = (probs * (grad_probs - inner)).astype(BF16)
            dv_ref[:, hs] += dot_nn(probs.astype(BF16), do)
            dk_ref[:, hs] += dot_nn(grad_scores, q) * scale
            dq_ref[here, hs] = dot_tn(k, grad_scores).T * scale
        return 0

    lax.fori_loop(0, queries // block, step, 0)


def first_body(dp, own, size, scale, heads, block, n):
    _, t, _, _, _, _ = tensor_place()
    d = lax.axis_index("dp")
    rows, width = n.residual.shape
    cols = n.bias_skip.shape[1]
    span = heads * LANES
    place = DpPlace(dp) if own else None
    peers = [(d, (t + o) % 4) for o in range(1, 4)] + (place.others() if own else [])
    bar = greet(peers)
    mine = block_rows(t, rows)
    kept = [
        pltpu.make_async_copy(n.latent, n.joined0.at[mine], n.own_sem.at[0]),
        pltpu.make_async_copy(n.skip_states, n.joined1.at[mine], n.own_sem.at[1]),
    ]
    if own:
        shards = [(n.skip_in, n.skip_full), (n.project_in, n.p_land), (n.out_in, n.out_land), (n.query_in, n.query_g),
                  (n.key_in, n.key_g), (n.value_in, n.value_g), (n.down_in, n.down_g)]
        kept += [pltpu.make_async_copy(a, b.at[d], n.own_sem.at[2 + i]) for i, (a, b) in enumerate(shards)]
    for cp in kept:
        cp.start()
    pl.semaphore_wait(bar, len(peers))
    spreads = [RowSpread(n.joined0, rows, *n.spread0), RowSpread(n.joined1, rows, *n.spread1)]
    for cp, spread in zip(kept, spreads):
        cp.wait()
        spread.send(0, rows)
    if own:
        n.small_land[d] = n.small[d]
        smalls = ToAll(place, lambda q: n.small.at[q], n.small_land, n.a_s, n.a_r)
        gathers = Gathers(place, *n.gather_sems)
        gathers.add(n.skip_in, n.skip_full, 2)
        smalls.arrived()
        given = jnp.concatenate([n.small_land[i] for i in range(dp)], axis=0)
        n.silu[...] = jax.nn.silu(given[:, : n.shift_in.shape[0]]).astype(BF16)
        n.counted[...] = jnp.sum(given[:, given.shape[1] - LANES :], axis=0, keepdims=True)
        part = dot_nn(n.silu[...], n.shift_in[...])
        for i in range(dp):
            n.shift_part[i] = part[i : i + 1, :]
        n.shift_land[d] = n.shift_part[d]
        shifts = ToAll(place, lambda q: n.shift_part.at[q], n.shift_land, n.b_s, n.b_r)
        for i in range(3):
            gathers.add(n.project_in.at[i], n.p_land.at[:, i])
        gathers.forward()
    spreads[0].forward()
    if own:
        gathers.add(n.out_in, n.out_land)
        gathers.add(n.query_in, n.query_g)
        gathers.add(n.key_in, n.key_g)
        gathers.add(n.value_in, n.value_g)
        gathers.forward()
    spreads[0].finish()
    if own:
        gathers.add(n.down_in, n.down_g, 4)
        gathers.arrived(0, 2)
        kept[2].wait()
        half = dp // 2
        skip_half = lambda i: n.skip_full[pl.ds(i * half, half)].reshape(width, cols)
    else:
        skip_half = lambda i: n.skip_in[pl.ds(i * width, width), :]
    for b in range(4):
        here = pl.ds(b * rows, rows)
        n.pre[here, pl.ds(0, cols)] = dot_nn(n.joined0[here, :], skip_half(0))
    spreads[1].forward()
    if own:
        gathers.forward()
    spreads[1].finish()
    copies = []
    for o in (2, 3, 1, 0):
        b = (t + o) % 4
        here = block_rows(b, rows)
        value = (n.pre[here, pl.ds(0, cols)] + dot_nn(n.joined1[here, :], skip_half(1)) + n.bias_skip[...]).astype(BF16)
        if o:
            n.skip_send[o] = value
            cp = remote(n.skip_send.at[o], n.skip_recv.at[t], n.p_s.at[o], n.p_r.at[o], (d, b))
            cp.start()
            copies.append(cp)
        else:
            n.skip_recv[t] = value
    if own:
        shifts.arrived()
        shift = n.row_bias[pl.ds(3, 1), :] + sum(n.shift_land[i] for i in range(dp))
    else:
        shift = n.shift_in[...]
    for cp in copies:
        cp.wait_recv()
    for s in range(4):
        n.skipped[:, s * cols : (s + 1) * cols] = n.skip_recv[s]
    spread = RowSpread(n.first_all, rows, *n.spread2)
    ch = rows // CHUNKS
    for k in range(CHUNKS):
        sl = pl.ds(k * ch, ch)
        cen, rstd = centre(n.skipped[sl, :].astype(F32))
        resid = cen * rstd * n.norm_gain[pl.ds(0, 1), :] + n.norm_bias[pl.ds(0, 1), :]
        n.residual[sl, :] = resid
        cen, rstd = centre(resid)
        first = cen * rstd * n.norm_gain[pl.ds(1, 1), :] + n.norm_bias[pl.ds(1, 1), :] + shift
        n.first_all[pl.ds(pl.multiple_of(t * rows + k * ch, ch), ch), :] = first.astype(BF16)
        spread.send(k * ch, ch)
    if own:
        gathers.forward()
    spread.forward()
    if own:
        gathers.forward()
    spread.finish()
    for cp in copies:
        cp.wait_send()
    for part in range(3):
        if own:
            gathers.arrived(2 + part, 3 + part)
            if part == 0:
                kept[3].wait()
            narrow = n.p_land[:, part].reshape(width, cols)
        else:
            narrow = n.project_in[part]
        n.project_wide[part] = dot_nn(narrow, n.fold[...]).astype(BF16)
    if own:
        gathers.forward()

    def project(i, _):
        here = pl.ds(pl.multiple_of(i * block, block), block)
        for part in range(3):
            out = dot_nn(n.first_all[here, :], n.project_wide[part]) + n.self_bias[part]
            if part < 2:
                n.pre[here, pl.ds(part * span, span)] = out
                for h in range(heads):
                    u = out[:, h * LANES : (h + 1) * LANES]
                    val = head_norm(u, n.mask[...], n.head_gain[pl.ds(part, 1), :], n.head_bias[pl.ds(part, 1), :], size)
                    val = turn(val, n.cosine[here, :], n.sine[here, :])
                    n.low[here, pl.ds(part * span + h * LANES, LANES)] = val.astype(BF16)
            else:
                n.low[here, pl.ds(part * span, span)] = out.astype(BF16)
        return 0

    lax.fori_loop(0, n.low.shape[0] // block, project, 0)
    if own:
        gathers.forward()
    attend(
        n.low.at[:, pl.ds(0, span)], n.low.at[:, pl.ds(span, span)], n.low.at[:, pl.ds(2 * span, span)],
        n.padded, n.lse, heads, scale, block, n.low.shape[0],
    )
    n.mixed[...] = dot_nt(n.padded[...], n.fold[...]).astype(BF16)
    if own:
        gathers.forward()
        gathers.arrived(5, 6)
        kept[4].wait()
        out_t = lambda: n.out_land[...].reshape(width, cols)
    else:
        out_t = lambda: n.out_in[...]
    reduce = TensorSum(*n.sum)
    reduce.start(lambda b: dot_nt(n.mixed[block_rows(b, rows), :], out_t()))
    if own:
        gathers.forward()
    spread = RowSpread(n.third_all, rows, *n.spread3)
    forward_rows(
        reduce, spread, n.third_all, n.residual, n.row_bias.at[pl.ds(0, 1)], n.norm_gain.at[pl.ds(2, 1)],
        n.norm_bias.at[pl.ds(2, 1)], n.second, rows,
    )
    if own:
        gathers.forward(2)
    spread.forward()
    if own:
        gathers.forward()
    spread.finish()
    reduce.sent()
    if own:
        gathers.forward()
        gathers.arrived(6, len(gathers.all))
        for cp in kept[5:]:
            cp.wait()
        for g in (gathers, smalls, shifts):
            g.sent()


def cross_body(dp, own, size, scale, heads, block, real, n):
    rows, width = n.second.shape
    span = heads * LANES
    d, _, _, _, sib, yp = tensor_place()
    place = DpPlace(dp) if own else None
    peers = [sib, yp] + (place.near() if own else [])
    bar = greet(peers)
    pl.semaphore_wait(bar, len(peers))
    if own:
        gathers = Gathers(place, *n.gather_sems)
        gathers.add(n.cross_out, n.cross_out_land)
        gathers.add(n.up_in, n.up_g, 4)
        kept = [pltpu.make_async_copy(a, b.at[d], n.own_sem.at[i])
                for i, (a, b) in enumerate(((n.cross_out, n.cross_out_land), (n.up_in, n.up_g)))]
        for cp in kept:
            cp.start()
    n.query_wide[...] = dot_nn(n.query[...], n.fold[...]).astype(BF16)
    for part, w in enumerate((n.key, n.value)):
        n.keyval_wide[part] = dot_nn(w[...], n.fold[...]).astype(BF16)
        out = dot_nn(n.text[...], n.keyval_wide[part]) + n.text_bias[part]
        if part == 0:
            n.text_pre[...] = out
            for h in range(heads):
                val = head_norm(out[:, h * LANES : (h + 1) * LANES], n.mask[...], n.head_gain[pl.ds(3, 1), :], n.head_bias[pl.ds(3, 1), :], size)
                n.text_low[:, head_at(h)] = val.astype(BF16)
        else:
            n.text_low[:, pl.ds(span, span)] = out.astype(BF16)
    if own:
        gathers.forward()

    def project(i, _):
        here = pl.ds(pl.multiple_of(i * block, block), block)
        out = dot_nn(n.third_all[here, :], n.query_wide[...]) + n.query_bias[...]
        n.pre[here, :] = out
        for h in range(heads):
            val = head_norm(out[:, h * LANES : (h + 1) * LANES], n.mask[...], n.head_gain[pl.ds(2, 1), :], n.head_bias[pl.ds(2, 1), :], size)
            n.low[here, head_at(h)] = turn(val, n.cosine[here, :], n.sine[here, :]).astype(BF16)
        return 0

    lax.fori_loop(0, n.low.shape[0] // block, project, 0)
    attend(n.low, n.text_low.at[:, pl.ds(0, span)], n.text_low.at[:, pl.ds(span, span)], n.padded, n.lse, heads, scale, block, real)
    n.mixed[...] = dot_nt(n.padded[...], n.fold[...]).astype(BF16)
    if own:
        gathers.forward()
        gathers.arrived(0, 1)
        kept[0].wait()
        out_t = lambda: n.cross_out_land[...].reshape(width, n.mixed.shape[1])
    else:
        out_t = lambda: n.cross_out[...]
    reduce = TensorSum(*n.sum)
    reduce.start(lambda b: dot_nt(n.mixed[block_rows(b, rows), :], out_t()))
    if own:
        gathers.forward()
    spread = RowSpread(n.fourth_all, rows, *n.spread)
    forward_rows(
        reduce, spread, n.fourth_all, n.second, n.row_bias.at[pl.ds(1, 1)], n.norm_gain.at[pl.ds(3, 1)],
        n.norm_bias.at[pl.ds(3, 1)], n.third_sum, rows,
    )
    if own:
        gathers.forward()
    spread.forward()
    if own:
        gathers.forward()
    spread.finish()
    reduce.sent()
    if own:
        gathers.arrived(1, len(gathers.all))
        kept[1].wait()
        gathers.sent()


def feed_body(n):
    rows = n.third_sum.shape[0]
    _, t, _, _, sib, yp = tensor_place()
    bar = greet((sib, yp))
    root, cube = float(np.sqrt(2.0 / np.pi)), 0.044715

    def product(b):
        here = block_rows(b, rows)
        x = dot_nn(n.fourth_all[here, :], n.up[...]) + n.hidden_bias[...]
        square = x * x
        th = jnp.tanh(root * (x + cube * (square * x)))
        cdf = 0.5 * (1.0 + th)
        active = (x * cdf).astype(BF16)
        n.active[here, :] = active
        slope = cdf + (0.5 * root) * x * (1.0 - th * th) * (1.0 + (3.0 * cube) * square)
        n.slope[here, :] = slope.astype(BF16)
        return dot_nt(active, n.down_t[...])

    reduce = TensorSum(*n.sum)
    reduce.start(product, lambda: pl.semaphore_wait(bar, 2))
    spread = RowSpread(n.grad_all, rows, *n.spread)
    ch = rows // CHUNKS
    sums = None
    for k in range(CHUNKS):
        sl, total = reduce.chunk(k)
        final = n.third_sum[sl, :] + (total + n.row_bias[pl.ds(2, 1), :])
        n.block_out[sl, :] = final.astype(BF16)
        grad = n.weight[sl, :] * (final - n.teacher[sl, :].astype(F32))
        n.grad_final[sl, :] = grad
        low = grad.astype(BF16)
        n.grad_all[pl.ds(pl.multiple_of(t * rows + k * ch, ch), ch), :] = low
        spread.send(k * ch, ch)
        sums = add_sums(sums, [low.astype(F32)])
    n.bias_mlp[...] = sums[0]
    spread.forward()
    spread.finish()
    reduce.sent()


def feed_back_body(dp, own, n):
    rows = n.third_sum.shape[0]
    _, _, _, _, sib, yp = tensor_place()
    place = DpPlace(dp) if own else None
    peers = [sib, yp] + (place.near() if own else [])
    bar = greet(peers)
    n.grad_down[...] = dot_tn(n.grad_all[...], n.active[...]).astype(BF16).reshape(n.grad_down.shape)
    pl.semaphore_wait(bar, len(peers))
    if own:
        down = GradScatter(place, n.grad_down, *n.down_bufs, *n.down_sems)

    def product(b):
        here = block_rows(b, rows)
        upper = (dot_nn(n.grad_all[here, :], n.down_t[...]) * n.slope[here, :].astype(F32)).astype(BF16)
        n.upper[here, :] = upper
        return dot_nt(upper, n.up[...])

    reduce = TensorSum(*n.sum)
    reduce.start(product)
    n.bias_hidden[...] = sum(
        jnp.sum(n.upper[pl.ds(b * rows, rows), :].astype(F32), axis=0, keepdims=True) for b in range(4)
    )
    n.grad_up[...] = dot_tn(n.fourth_all[...], n.upper[...]).astype(BF16).reshape(n.grad_up.shape)
    spread = RowSpread(n.c_all, rows, *n.spread)
    if own:
        down.steps(1)
    backward_rows(reduce, spread, n.c_all, n.third_sum, n.gain, n.grad_final, n.grad_third, (n.sum0, n.sum1, n.sum2), rows)
    if own:
        down.steps(2)
    spread.forward()
    if own:
        down.steps()
    spread.finish()
    reduce.sent()
    if own:
        n.down_mine[...] = down.result()
        down.sent()


def spread_heads(n, rows_in, w, do, block):
    def spread(i, _):
        here = pl.ds(pl.multiple_of(i * block, block), block)
        narrow = dot_nn(rows_in[here, :], w[...]).astype(BF16)
        do[here, :] = dot_nn(narrow, n.fold[...]).astype(BF16)
        return 0

    lax.fori_loop(0, do.shape[0] // block, spread, 0)


def cross_back_body(dp, own, size, scale, heads, block, real, n):
    rows = n.second.shape[0]
    span = heads * LANES
    d, t, _, _, sib, yp = tensor_place()
    place = DpPlace(dp) if own else None
    peers = [sib, yp] + (place.near() if own else [])
    bar = greet(peers)
    pl.semaphore_wait(bar, len(peers))
    if own:
        up = GradScatter(place, n.grad_up, *n.up_bufs, *n.up_sems)
    spread_heads(n, n.c_all, n.cross_out, n.do, block)
    attend_back(
        n.low, n.text_low.at[:, pl.ds(0, span)], n.text_low.at[:, pl.ds(span, span)],
        n.do, n.lse, n.dq, n.dk, n.dv, heads, scale, block, real,
    )
    n.gains[...] = jnp.zeros(n.gains.shape, F32)
    n.offsets[...] = jnp.zeros(n.offsets.shape, F32)
    n.sums[...] = jnp.zeros(n.sums.shape, F32)

    def finish(i, _):
        here = pl.ds(pl.multiple_of(i * block, block), block)
        for h in range(heads):
            hs = head_at(h)
            grad = turn_back(n.dq[here, hs], n.cosine[here, :], n.sine[here, :])
            grad, g, o = head_back(grad, n.pre[here, hs], n.mask[...], n.head_gain[pl.ds(2, 1), :], size)
            n.gains[pl.ds(0, 1), :] += g
            n.offsets[pl.ds(0, 1), :] += o
            grad_low = grad.astype(BF16)
            n.p[here, hs] = grad_low
            n.sums[:, hs] += jnp.sum(grad_low.astype(F32), axis=0, keepdims=True)
        return 0

    if own:
        up.steps(1)
    lax.fori_loop(0, n.p.shape[0] // block, finish, 0)
    reduce = TensorSum(*n.sum)
    reduce.start(lambda b: dot_nt(n.p[block_rows(b, rows), :], n.query_wide[...]))
    if own:
        up.steps(2)
    for h in range(heads):
        hs = head_at(h)
        grad, g, o = head_back(n.dk[:, hs], n.text_pre[:, hs], n.mask[...], n.head_gain[pl.ds(3, 1), :], size)
        n.gains[pl.ds(1, 1), :] += g
        n.offsets[pl.ds(1, 1), :] += o
        n.text_p[:, hs] = grad.astype(BF16)
        low_v = n.dv[:, hs].astype(BF16)
        n.text_p[:, pl.ds(span + h * LANES, LANES)] = low_v
        n.text_sums[:, hs] = jnp.sum(low_v.astype(F32), axis=0, keepdims=True)
    parts = n.grads.shape[0]

    def put(start, value):
        count = value.shape[0] // parts
        n.grads[:, pl.ds(start, count)] = value.astype(BF16).reshape(parts, count, value.shape[1])
        return start + count

    at = put(0, dot_tn(n.c_all[...], n.mixed[...]))
    at = put(at, dot_tn(n.third_all[...], dot_nt(n.p[...], n.fold[...]).astype(BF16)))
    for part in range(2):
        narrow = dot_nt(n.text_p[:, pl.ds(part * span, span)], n.fold[...]).astype(BF16)
        at = put(at, dot_tn(n.text[...], narrow))
    n.grad_text[...] = (
        dot_nt(n.text_p[:, pl.ds(0, span)], n.keyval_wide[0]) + dot_nt(n.text_p[:, pl.ds(span, span)], n.keyval_wide[1])
    ).astype(BF16)
    if own:
        up.steps()
    spread = RowSpread(n.s_all, rows, *n.spread)
    backward_rows(reduce, spread, n.s_all, n.second, n.gain, n.grad_third, n.grad_second, (n.sum0, n.sum1, n.sum2), rows)
    spread.forward()
    spread.finish()
    reduce.sent()
    if own:
        n.up_mine[...] = up.result()
        up.sent()


class TextSum:
    def __init__(self, part, total, land, yland, back, sems):
        _, _, _, self.c, self.sib, self.yp = tensor_place()
        self.part, self.total, self.land, self.yland, self.last, self.sems = part, total, land, yland, back, sems
        self.half = piece_rows(part.shape[0], 2, 1)
        self.copies = [remote(part, land, sems.at[0], sems.at[1], self.sib)]
        self.copies[0].start()

    def here(self, c):
        return pl.ds(pl.multiple_of(c * (self.part.shape[0] - self.half), 16), self.half)

    def along(self):
        self.copies[0].wait_recv()
        self.total[...] = (self.part[...].astype(F32) + self.land[...].astype(F32)).astype(BF16)
        cp = remote(self.total.at[self.here(self.c)], self.yland, self.sems.at[2], self.sems.at[3], self.yp)
        cp.start()
        self.copies.append(cp)

    def back(self):
        self.copies[1].wait_recv()
        self.copies[1].wait_send()
        mine = self.here(self.c)
        self.yland[...] = (self.total[mine, :].astype(F32) + self.yland[...].astype(F32)).astype(BF16)
        self.copies[0].wait_send()
        cp = remote(self.yland, self.last, self.sems.at[4], self.sems.at[5], self.sib)
        cp.start()
        self.copies.append(cp)

    def result(self, out):
        self.copies[2].wait_recv()
        out[self.here(self.c), :] = self.yland[...].astype(F32)
        out[self.here(1 - self.c), :] = self.last[...].astype(F32)
        self.copies[2].wait_send()


def self_back_body(dp, own, size, scale, heads, block, n):
    span = heads * LANES
    _, _, _, _, sib, yp = tensor_place()
    place = DpPlace(dp) if own else None
    peers = [sib, yp] + (place.near() if own else [])
    bar = greet(peers)
    pl.semaphore_wait(bar, len(peers))
    text = TextSum(n.text_part, n.text_total, n.text_land, n.text_yland, n.text_back, n.text_sems)
    if own:
        few = GradScatter(place, n.few_grads, *n.few_bufs, *n.few_sems)
    spread_heads(n, n.s_all, n.out_t, n.do, block)
    text.along()
    attend_back(
        n.low.at[:, pl.ds(0, span)], n.low.at[:, pl.ds(span, span)], n.low.at[:, pl.ds(2 * span, span)],
        n.do, n.lse, n.dq, n.dk, n.dv, heads, scale, block, n.low.shape[0],
    )
    text.back()
    if own:
        few.step()
    n.gains[...] = jnp.zeros(n.gains.shape, F32)
    n.offsets[...] = jnp.zeros(n.offsets.shape, F32)
    n.sums[...] = jnp.zeros(n.sums.shape, F32)

    def finish(i, _):
        here = pl.ds(pl.multiple_of(i * block, block), block)
        for part, grad_ref in enumerate((n.dq, n.dk, n.dv)):
            for h in range(heads):
                hs = head_at(h)
                wide = pl.ds(part * span + h * LANES, LANES)
                grad = grad_ref[here, hs]
                if part < 2:
                    grad = turn_back(grad, n.cosine[here, :], n.sine[here, :])
                    grad, g, o = head_back(grad, n.pre[here, wide], n.mask[...], n.head_gain[pl.ds(part, 1), :], size)
                    n.gains[pl.ds(part, 1), :] += g
                    n.offsets[pl.ds(part, 1), :] += o
                grad_low = grad.astype(BF16)
                n.p[here, wide] = grad_low
                if part != 1:
                    n.sums[:, wide] += jnp.sum(grad_low.astype(F32), axis=0, keepdims=True)
            n.p_low[part, here, :] = dot_nt(n.p[here, pl.ds(part * span, span)], n.fold[...]).astype(BF16)
        return 0

    lax.fori_loop(0, n.p.shape[0] // block, finish, 0)
    by_place = lambda v: v.astype(BF16).reshape(n.grad_out.shape)
    if own:
        few.steps()
    n.grad_out[...] = by_place(dot_tn(n.s_all[...], n.mixed[...]))
    for part in range(3):
        n.grad_project[:, part] = by_place(dot_tn(n.first_all[...], n.p_low[part]))
    text.result(n.grad_text)
    if own:
        n.few_mine[...] = few.result()
        few.sent()


PACK_ROWS, PACK_SUMS = 8, 16


def last_body(dp, own, n):
    _, t, _, _, _, _ = tensor_place()
    d = lax.axis_index("dp")
    rows, width = n.residual.shape
    cols = n.krecv.shape[2]
    place = DpPlace(dp) if own else None
    peers = [(d, (t + o) % 4) for o in range(1, 4)] + (place.others() if own else [])
    bar = greet(peers)
    reduce = TensorSum(*n.sum)
    scatters = []

    def scatter(source, buffers):
        i = len(scatters)
        scatters.append(GradScatter(place, source, *buffers, *n.scatter_sems[5 * i : 5 * i + 5]))

    def ready():
        pl.semaphore_wait(bar, len(peers))
        if own:
            scatter(n.grad_out, n.out_bufs)
            for i in range(3):
                scatter(n.grad_project.at[:, i], n.project_bufs[3 * i : 3 * i + 3])

    def product(b):
        here = block_rows(b, rows)
        span = n.project_wide.shape[2]
        total = dot_nt(n.p[here, pl.ds(0, span)], n.project_wide[0])
        for part in range(1, 3):
            total = total + dot_nt(n.p[here, pl.ds(part * span, span)], n.project_wide[part])
        return total

    reduce.start(product, ready)
    if own:
        scatters[0].steps()
    sums = None
    for k in range(CHUNKS):
        sl, total = reduce.chunk(k)
        back, xhat = norm_back(total, n.residual[sl, :], n.norm_gain[pl.ds(1, 1), :])
        grad = n.grad_second[sl, :] + back
        back0, xhat0 = norm_back(grad, n.skipped[sl, :].astype(F32), n.norm_gain[pl.ds(0, 1), :])
        low = back0.astype(BF16)
        for s in range(4):
            n.ksend[s, sl, :] = low[:, s * cols : (s + 1) * cols]
        sums = add_sums(sums, [low.astype(F32), total * xhat, total, grad * xhat0, grad])
    copies = []
    for o in (2, 3, 1):
        b = (t + o) % 4
        cp = remote(n.ksend.at[b], n.krecv.at[t], n.k_s.at[o], n.k_r.at[o], (d, b))
        cp.start()
        copies.append(cp)
    n.krecv[t] = n.ksend[t]
    bias_skip, gain_first, offset_first, gain_skip, offset_skip = sums
    n.tile[...] = offset_first
    n.tile_land[t] = n.tile[...]
    tiles = []
    for o in (1, 2, 3):
        cp = remote(n.tile, n.tile_land.at[t], n.t_s.at[o], n.t_r.at[o], (d, (t + o) % 4))
        cp.start()
        tiles.append(cp)
    n.pack[...] = n.pack_in[...]
    for i, v in enumerate((gain_skip, gain_first, offset_skip, offset_first, bias_skip)):
        n.pack[0, pl.ds(i, 1), :] = v
    shares = []
    for o in (1, 2, 3):
        b = (t + o) % 4
        cp = remote(n.pack.at[b], n.pack_in_land.at[t], n.ps_s.at[o], n.ps_r.at[o], (d, b))
        cp.start()
        shares.append(cp)
    n.pack_in_land[t] = n.pack[t]
    if own:
        scatters[1].steps()
    for cp in copies:
        cp.wait_recv()
    reduce.sent()
    halves = [TensorSum(*n.sum), TensorSum(*n.sum1)]
    for h, half in enumerate(halves):
        half.start(lambda b, h=h: dot_nt(n.krecv[b], n.skip_w[pl.ds(h * width, width), :]))
    k_all = n.krecv[...].reshape(4 * rows, cols)
    count = n.grad_skip_w.shape[0] // 2
    for h, joined in enumerate((n.joined0, n.joined1)):
        n.grad_skip_w[pl.ds(h * count, count)] = (
            dot_tn(joined[...], k_all).astype(BF16).reshape((count,) + n.grad_skip_w.shape[1:])
        )
    if own:
        scatter(n.grad_skip_w, n.skip_bufs)
    for cp in tiles:
        cp.wait_recv()
    shift_low = n.tile_land[0] + n.tile_land[1] + n.tile_land[2] + n.tile_land[3]
    n.low_out[...] = shift_low.astype(BF16).astype(F32)
    if own:
        n.low_land[d] = n.low_out[...]
        lows = ToAll(place, lambda q: n.low_out, n.low_land, n.l_s, n.l_r)
    for cp in shares:
        cp.wait_recv()
    n.pack_mine[...] = n.pack_in_land[0] + n.pack_in_land[1] + n.pack_in_land[2] + n.pack_in_land[3]
    if own:
        pack_cp = remote(n.pack_mine, n.pack_x, n.px_s.at[0], n.px_r.at[0], place.pair)
        pack_cp.start()
        scatters[2].steps()
        pack_cp.wait_recv()
        pack_cp.wait_send()
        n.pack_mine[...] = n.pack_mine[...] + n.pack_x[...]
        n.pack_z[place.zi] = n.pack_mine[...]
        packs = []
        for j in range(1, place.line):
            cp = remote(n.pack_mine, n.pack_z.at[place.zi], n.pz_s.at[j], n.pz_r.at[j], (place.ahead(j), place.t))
            cp.start()
            packs.append(cp)
    for half, out in zip(halves, (n.grad_latent, n.grad_skip)):
        for k in range(CHUNKS):
            sl, total = half.chunk(k)
            out[sl, :] = total
        half.sent()
        if own and out is n.grad_latent:
            scatters[3].steps()
            lows.arrived()
            low_all = jnp.concatenate([n.low_land[i] for i in range(dp)], axis=0)
            n.shift_grad[...] = dot_tn(n.silu[...], low_all.astype(BF16))
            n.shift_bias[...] = jnp.sum(low_all, axis=0, keepdims=True)
            for cp in packs:
                cp.wait_recv()
                cp.wait_send()
            total = n.pack_z[0]
            for i in range(1, place.line):
                total = total + n.pack_z[i]
            n.pack_mine[...] = total
    if not own:
        n.shift_grad[...] = n.low_out[...]
        n.shift_bias[...] = n.low_out[...]
    n.pack_t[t] = n.pack_mine[...]
    ends = []
    for o in (1, 2, 3):
        cp = remote(n.pack_mine, n.pack_t.at[t], n.pt_s.at[o], n.pt_r.at[o], (d, (t + o) % 4))
        cp.start()
        ends.append(cp)
    if own:
        scatters[4].steps()
    for cp in ends:
        cp.wait_recv()
        cp.wait_send()
    n.pack_out[...] = n.pack_t[...]
    if own:
        n.out_mine[...] = scatters[0].result()
        for i in range(3):
            n.project_mine[i] = scatters[1 + i].result()
        n.skip_mine[...] = scatters[4].result()
        for s in scatters:
            s.sent()
        lows.sent()
    for cp in copies + tiles + shares:
        cp.wait_send()


def fold_matrix(heads, size):
    out = np.zeros((heads * size, heads * LANES), np.float32)
    for h in range(heads):
        for e in range(size):
            out[h * size + e, h * LANES + (e % 2) * (LANES // 2) + e // 2] = 1.0
    return out


def body(
    latent, skip_states, text_states, condition, teacher, loss_mask, true_counts, positions,
    skip_proj, shift_proj, self_project, self_output, cross_query, cross_keyval, cross_output, hidden_up, hidden_down,
    norm_gain, norm_bias, head_gain, head_bias, column_bias, hidden_bias, row_bias,
):
    d, t = lax.axis_index("dp"), lax.axis_index("tensor")
    dp, tensor = lax.axis_size("dp"), lax.axis_size("tensor")
    rows, width = latent.shape
    group = rows * tensor
    size = head_gain.shape[1]
    cols = self_project.shape[2]
    heads = cols // size
    span = heads * LANES
    hidden = hidden_up.shape[1]
    text_len, text_width = text_states.shape[1:]
    text_pad = -(-text_len // 16) * 16
    scale = size ** (-0.5)
    block = min(256, group)
    r, text_share = shift_proj.shape[0], cross_keyval.shape[0]
    own = r % 16 == 0 and text_share % 16 == 0 and skip_proj.shape[0] % 32 == 0 and dp == 8
    parts = dp if own else 1
    line = max(dp // 2, 1) if own else 1
    dma, vm = pltpu.SemaphoreType.DMA, pltpu.VMEM
    few = lambda *shape: shape if own else (16, LANES)

    fold_np = fold_matrix(heads, size)
    fold = jnp.asarray(fold_np, BF16)
    one_np = fold_np[:size, :LANES]
    mask = jnp.asarray(one_np.sum(0, keepdims=True), F32)
    exact = functools.partial(jnp.dot, precision=lax.Precision.HIGHEST)
    gain_wide, offset_wide = exact(head_gain, jnp.asarray(one_np)), exact(head_bias, jnp.asarray(one_np))
    bias_cols = lax.dynamic_slice_in_dim(column_bias, t * cols, cols, 1)
    bias_wide = exact(bias_cols, jnp.asarray(fold_np))
    zero_wide = jnp.zeros((1, span), F32)
    self_bias = jnp.stack([bias_wide[0:1], zero_wide, bias_wide[1:2]])
    text_bias = jnp.stack([zero_wide, bias_wide[3:4]])
    hidden_cols_bias = lax.dynamic_slice_in_dim(hidden_bias, t * hidden, hidden, 0)[None]

    quarter = size // 4
    lane_np = np.zeros((2, LANES), np.float32)
    sign_np = np.zeros((1, LANES), np.float32)
    for i in range(size // 2):
        f = np.float32(10000.0 ** (-(i % quarter) / quarter))
        for half in range(2):
            lane_np[i // quarter, half * (LANES // 2) + i] = f
            sign_np[0, half * (LANES // 2) + i] = 2 * half - 1
    place = positions.astype(F32)
    angles = place[0][:, None] * lane_np[0] + place[1][:, None] * lane_np[1]
    cosine = jnp.cos(angles) * mask
    sine = jnp.sin(angles) * sign_np

    project_in = jnp.transpose(self_project, (1, 0, 2))
    shards = [self_output.T, cross_query, cross_output.T, cross_keyval[:, 0], cross_keyval[:, 1], hidden_up, hidden_down.T]
    if own:
        lanes = -(-r // LANES) * LANES
        slices = jnp.pad(condition.astype(F32).reshape(dp, r), ((0, 0), (0, lanes - r)))
        slices = jnp.concatenate([slices, jnp.broadcast_to(true_counts.astype(F32)[:, None], (dp, LANES))], axis=1)
        small = slices[:, None, :]
        skip_in, shift_in = skip_proj, shift_proj
    else:
        small_all = lax.all_gather(
            jnp.concatenate([condition.astype(F32), true_counts.astype(F32)[:, None]], axis=1), "dp", axis=0, tiled=True
        )
        silu_all = jax.nn.silu(small_all[:, :width]).astype(BF16)
        silu = lax.dynamic_slice_in_dim(silu_all, d * r, r, 1)
        shift_in = lax.psum_scatter(dot_nn(silu, shift_proj), "dp", scatter_dimension=0, tiled=True) + row_bias[3:4]
        small = jnp.zeros((1, 8, LANES), F32)
        skip_in = lax.all_gather(skip_proj, "dp", axis=0, tiled=True)
        project_in = lax.all_gather(project_in, "dp", axis=1, tiled=True)
        shards = [lax.all_gather(v, "dp", axis=0, tiled=True) for v in shards]
    full = shaped((group, width), BF16)
    mine = shaped((rows, width), F32)
    mine_low = shaped((rows, width), BF16)
    line_sum = shaped((1, width), F32)
    lse_shape = shaped((group // block, heads, block), F32)
    sum_scratch = TensorSum.scratch(rows, width)
    first = named_kernel(
        "first", 0, functools.partial(first_body, dp, own, size, scale, heads, block),
        dict(
            latent=latent, skip_states=skip_states, skip_in=skip_in, project_in=project_in, out_in=shards[0],
            query_in=shards[1], key_in=shards[3], value_in=shards[4], down_in=shards[6],
            small=small, shift_in=shift_in, bias_skip=bias_cols[4:5], self_bias=self_bias, cosine=cosine, sine=sine,
            norm_gain=norm_gain, norm_bias=norm_bias, row_bias=row_bias, head_gain=gain_wide, head_bias=offset_wide,
            mask=mask, fold=fold,
        ),
        dict(
            joined0=full, joined1=full, skip_full=shaped(few(dp, skip_proj.shape[0], cols), BF16), skipped=mine_low,
            residual=mine, first_all=full, silu=shaped(few(dp, r), BF16), counted=shaped((1, LANES), F32),
            project_wide=shaped((3, width, span), BF16), pre=shaped((group, 2 * span), F32),
            low=shaped((group, 3 * span), BF16), mixed=shaped((group, cols), BF16), lse=lse_shape,
            out_land=shaped(few(dp, r, cols), BF16), query_g=shaped(few(dp, r, cols), BF16),
            key_g=shaped(few(dp, text_share, cols), BF16), value_g=shaped(few(dp, text_share, cols), BF16),
            down_g=shaped(few(dp, r, hidden), BF16), third_all=full, second=mine,
        ),
        dict(
            p_land=vm(few(dp, 3, r, cols), BF16), padded=vm((group, span), BF16), skip_send=vm((4, rows, cols), BF16),
            skip_recv=vm((4, rows, cols), BF16), small_land=vm(small.shape, F32), shift_part=vm((dp, 1, width), F32),
            shift_land=vm((dp, 1, width), F32), sum=sum_scratch, own_sem=dma((9,)), a_s=dma((dp,)),
            a_r=dma((dp,)), b_s=dma((dp,)), b_r=dma((dp,)), p_s=dma((4,)), p_r=dma((4,)), gather_sems=Gathers.scratch(13, line),
            spread0=RowSpread.scratch(1),
            spread1=RowSpread.scratch(1), spread2=RowSpread.scratch(), spread3=RowSpread.scratch(),
        ),
        hbm=("latent", "skip_states", "query_in", "key_in", "value_in", "down_in", "query_g", "key_g", "value_g", "down_g")
        + (("skip_in", "project_in", "out_in") if own else ()),
    )
    if own:
        silu, counted = first.silu, first.counted[0, 0]
        skip_full = first.skip_full.reshape(2 * width, cols)
        out_t, query = [v.reshape(width, cols) for v in (first.out_land, first.query_g)]
        key, value = [v.reshape(text_width, cols) for v in (first.key_g, first.value_g)]
        down_t = first.down_g.reshape(width, hidden)
    else:
        counted, skip_full = jnp.sum(small_all[:, width]), skip_in
        out_t, query, cross_out_t, key, value, up_full, down_t = shards

    text = jnp.pad(text_states[0], ((0, text_pad - text_len), (0, 0)))
    cross = named_kernel(
        "cross", 1, functools.partial(cross_body, dp, own, size, scale, heads, block, text_len),
        dict(
            third_all=first.third_all, query=query, key=key, value=value, cross_out=shards[2], up_in=shards[5], text=text,
            text_bias=text_bias, query_bias=bias_wide[2:3], cosine=cosine, sine=sine, norm_gain=norm_gain,
            norm_bias=norm_bias, row_bias=row_bias, head_gain=gain_wide, head_bias=offset_wide, mask=mask, fold=fold,
            second=first.second,
        ),
        dict(
            query_wide=shaped((width, span), BF16), keyval_wide=shaped((2, text_width, span), BF16),
            text_pre=shaped((text_pad, span), F32), text_low=shaped((text_pad, 2 * span), BF16),
            pre=shaped((group, span), F32), low=shaped((group, span), BF16), mixed=shaped((group, cols), BF16),
            lse=lse_shape, fourth_all=full, third_sum=mine,
            cross_out_land=shaped(few(dp, r, cols), BF16), up_g=shaped(few(dp, r, hidden), BF16),
        ),
        dict(
            padded=vm((group, span), BF16), sum=sum_scratch, spread=RowSpread.scratch(),
            gather_sems=Gathers.scratch(5, line), own_sem=dma((2,)),
        ),
        hbm=("up_in", "up_g") + (("cross_out",) if own else ()),
    )
    if own:
        cross_out_t, up_full = cross.cross_out_land.reshape(width, cols), cross.up_g.reshape(width, hidden)

    row_ids = t * rows + jnp.arange(rows)
    weight = loss_mask.astype(F32) * (row_ids < true_counts[0]).astype(F32)
    loss_scale = dp * group / counted
    feed = named_kernel(
        "feed", 2, feed_body,
        dict(
            fourth_all=cross.fourth_all, up=up_full, hidden_bias=hidden_cols_bias, down_t=down_t, third_sum=cross.third_sum,
            row_bias=row_bias, teacher=teacher, weight=(loss_scale * weight)[:, None],
        ),
        dict(
            active=shaped((group, hidden), BF16), slope=shaped((group, hidden), BF16), grad_all=full, block_out=mine_low,
            grad_final=mine, bias_mlp=line_sum,
        ),
        dict(sum=sum_scratch, spread=RowSpread.scratch()),
    )

    back = named_kernel(
        "feed_back", 3, functools.partial(feed_back_body, dp, own),
        dict(
            grad_all=feed.grad_all, slope=feed.slope, active=feed.active, down_t=down_t, up=up_full,
            fourth_all=cross.fourth_all, third_sum=cross.third_sum, gain=norm_gain[3:4], grad_final=feed.grad_final,
        ),
        dict(
            c_all=full, grad_third=mine, sum0=line_sum, sum1=line_sum, sum2=line_sum, bias_hidden=shaped((1, hidden), F32),
            grad_up=shaped((parts, width // parts, hidden), BF16),
            **(dict(down_mine=shaped((r, hidden), F32)) if own else dict(grad_down=shaped((1, width, hidden), BF16))),
        ),
        dict(
            upper=vm((group, hidden), BF16), sum=sum_scratch, spread=RowSpread.scratch(),
            **(dict(grad_down=vm((dp, r, hidden), BF16), down_bufs=GradScatter.buffers((r, hidden)), down_sems=GradScatter.scratch()) if own else {}),
        ),
    )
    bias_cross_out, gain_fourth, offset_fourth = back.sum0, back.sum1, back.sum2

    few_rows = 2 * r + 2 * text_share if own else 2 * width + 2 * text_width
    cback = named_kernel(
        "cross_back", 4, functools.partial(cross_back_body, dp, own, size, scale, heads, block, text_len),
        dict(
            c_all=back.c_all, cross_out=cross_out_t, pre=cross.pre, low=cross.low, text_pre=cross.text_pre,
            text_low=cross.text_low, lse=cross.lse, cosine=cosine, sine=sine, head_gain=gain_wide, mask=mask, fold=fold,
            mixed=cross.mixed, third_all=first.third_all, text=text, keyval_wide=cross.keyval_wide,
            query_wide=cross.query_wide, second=first.second, gain=norm_gain[2:3], grad_third=back.grad_third,
            **(dict(grad_up=back.grad_up) if own else {}),
        ),
        dict(
            grads=shaped((parts, few_rows, cols), BF16), grad_text=shaped((text_pad, text_width), BF16),
            gains=shaped((2, LANES), F32), offsets=shaped((2, LANES), F32), sums=shaped((1, span), F32),
            text_sums=shaped((1, span), F32), s_all=full, grad_second=mine, sum0=line_sum, sum1=line_sum, sum2=line_sum,
            **(dict(up_mine=shaped((r, hidden), F32)) if own else {}),
        ),
        dict(
            p=vm((group, span), BF16), do=vm((group, span), BF16), dq=vm((group, span), F32), dk=vm((text_pad, span), F32),
            dv=vm((text_pad, span), F32), text_p=vm((text_pad, 2 * span), BF16), sum=sum_scratch, spread=RowSpread.scratch(),
            **(dict(up_bufs=GradScatter.buffers((r, hidden)), up_sems=GradScatter.scratch()) if own else {}),
        ),
        hbm=("grad_up",),
    )
    few_grads = cback.grads
    if not own:
        cuts = np.cumsum([0, width, width, text_width, text_width])
        few_grads = jnp.concatenate(
            [few_grads[0, a:b].reshape(dp, -1, cols) for a, b in zip(cuts[:-1], cuts[1:])], axis=1
        )
        few_mine = lax.psum_scatter(few_grads.reshape(-1, cols), "dp", scatter_dimension=0, tiled=True).astype(F32)
        down_mine = lax.psum_scatter(back.grad_down[0], "dp", scatter_dimension=0, tiled=True).astype(F32)
        up_mine = lax.psum_scatter(back.grad_up[0], "dp", scatter_dimension=0, tiled=True).astype(F32)
    else:
        down_mine, up_mine = back.down_mine, cback.up_mine

    sback = named_kernel(
        "self_back", 6, functools.partial(self_back_body, dp, own, size, scale, heads, block),
        dict(
            text_part=cback.grad_text, **(dict(few_grads=few_grads) if own else {}),
            s_all=cback.s_all, out_t=out_t, pre=first.pre, low=first.low, lse=first.lse, cosine=cosine, sine=sine,
            head_gain=gain_wide, mask=mask, fold=fold, mixed=first.mixed, first_all=first.first_all,
        ),
        dict(
            p=shaped((group, 3 * span), BF16), grad_out=shaped((parts, width // parts, cols), BF16),
            grad_project=shaped((parts, 3, width // parts, cols), BF16), gains=shaped((2, LANES), F32),
            offsets=shaped((2, LANES), F32), sums=shaped((1, 3 * span), F32), grad_text=shaped((text_pad, text_width), F32),
            **(dict(few_mine=shaped((few_rows, cols), F32)) if own else {}),
        ),
        dict(
            do=vm((group, span), BF16), dq=vm((group, span), F32), dk=vm((group, span), F32), dv=vm((group, span), F32),
            p_low=vm((3, group, cols), BF16), text_total=vm((text_pad, text_width), BF16),
            text_land=vm((text_pad, text_width), BF16), text_yland=vm((piece_rows(text_pad, 2, 1), text_width), BF16),
            text_back=vm((piece_rows(text_pad, 2, 1), text_width), BF16),
            text_sems=dma((6,)),
            **(dict(few_bufs=GradScatter.buffers((few_rows, cols)), few_sems=GradScatter.scratch()) if own else {}),
        ),
        hbm=("few_grads",),
    )
    grad_text = sback.grad_text[:text_len][None]
    if own:
        few_mine = sback.few_mine

    head_part = jnp.concatenate([sback.gains, cback.gains, sback.offsets, cback.offsets], axis=0).reshape(1, -1)
    column_rows = exact(
        jnp.concatenate([sback.sums[:, :span], sback.sums[:, 2 * span :], cback.sums, cback.text_sums], axis=0),
        jnp.asarray(fold_np.T),
    )
    own_cols = jnp.concatenate([column_rows.reshape(-1), back.bias_hidden[0]])
    col_rows = (4 * PACK_ROWS - PACK_SUMS) // 4
    own_cols = jnp.pad(own_cols, (0, col_rows * width - own_cols.shape[0])).reshape(1, col_rows, width)
    placed = jnp.where(jnp.arange(tensor)[:, None, None] == t, own_cols, 0.0).reshape(tensor * col_rows, width)
    pack_in = jnp.concatenate(
        [jnp.zeros((5, width), F32), cback.sum1, gain_fourth, cback.sum2, offset_fourth, cback.sum0, bias_cross_out,
         feed.bias_mlp, jnp.pad(head_part, ((0, 0), (0, width - head_part.shape[1]))),
         jnp.zeros((PACK_SUMS - 13, width), F32), placed], axis=0
    ).reshape(4, PACK_ROWS, width)
    skip_rows = 2 * width // dp if own else width
    pack_land = vm((4, PACK_ROWS, width), F32)
    last = named_kernel(
        "last", 5, functools.partial(last_body, dp, own),
        dict(
            p=sback.p, project_wide=first.project_wide, residual=first.residual, grad_second=cback.grad_second,
            skipped=first.skipped, norm_gain=norm_gain, skip_w=skip_full, joined0=first.joined0, joined1=first.joined1,
            silu=silu, pack_in=pack_in, grad_out=sback.grad_out, grad_project=sback.grad_project,
        ),
        dict(
            grad_latent=mine, grad_skip=mine, shift_grad=shaped((r if own else 1, width), F32), shift_bias=line_sum,
            pack_out=shaped((4, PACK_ROWS, width), F32),
            **(dict(out_mine=shaped((r, cols), F32), project_mine=shaped((3, r, cols), F32), skip_mine=shaped((skip_rows, cols), F32))
               if own else dict(grad_skip_w=shaped((2, width, cols), BF16))),
        ),
        dict(
            ksend=vm((4, rows, cols), BF16), krecv=vm((4, rows, cols), BF16), tile=vm((1, width), F32),
            tile_land=vm((4, 1, width), F32), low_out=vm((1, width), F32),
            low_land=vm((dp if own else 1, 1, width), F32), pack=vm((4, PACK_ROWS, width), F32), pack_in_land=pack_land,
            pack_mine=vm((PACK_ROWS, width), F32), pack_x=vm((PACK_ROWS, width), F32), pack_z=pack_land, pack_t=pack_land, sum=sum_scratch, sum1=sum_scratch,
            k_s=dma((4,)), k_r=dma((4,)), t_s=dma((4,)), t_r=dma((4,)), l_s=dma((dp,)), l_r=dma((dp,)), px_s=dma((1,)),
            px_r=dma((1,)), ps_s=dma((4,)), ps_r=dma((4,)), pz_s=dma((line,)), pz_r=dma((line,)), pt_s=dma((4,)), pt_r=dma((4,)),
            **(dict(
                grad_skip_w=vm((dp, skip_rows, cols), BF16), out_bufs=GradScatter.buffers((r, cols)),
                project_bufs=GradScatter.buffers((r, cols)) * 3, skip_bufs=GradScatter.buffers((skip_rows, cols)),
                scatter_sems=GradScatter.scratch() * 5,
            ) if own else {}),
        ),
        hbm=("grad_out", "grad_project"),
    )
    if own:
        out_mine, project_mine, skip_mine = last.out_mine, last.project_mine, last.skip_mine
        shift_grad, shift_bias, pack_sum = last.shift_grad, last.shift_bias, last.pack_out
    else:
        shift_all = lax.all_gather(last.shift_grad[:1], "dp", axis=0, tiled=True)
        shift_bias = jnp.sum(shift_all, axis=0, keepdims=True)
        shift_grad = dot_tn(silu, shift_all.astype(BF16))
        pack_sum = lax.psum(last.pack_out, "dp")
        out_mine = lax.psum_scatter(sback.grad_out[0], "dp", scatter_dimension=0, tiled=True).astype(F32)
        project_mine = lax.psum_scatter(sback.grad_project[0], "dp", scatter_dimension=1, tiled=True).astype(F32)
        skip_mine = lax.psum_scatter(last.grad_skip_w.reshape(-1, cols), "dp", scatter_dimension=0, tiled=True).astype(F32)
    pack_sum = pack_sum.reshape(4 * PACK_ROWS, width)
    cols_all = pack_sum[PACK_SUMS:].reshape(tensor, -1)
    column_sums = jnp.transpose(cols_all[:, : 4 * cols].reshape(tensor, 4, cols), (1, 0, 2)).reshape(4, width)
    hidden_sums = cols_all[:, 4 * cols : 4 * cols + hidden].reshape(-1)
    head_sums = exact(pack_sum[12, : 8 * LANES].reshape(8, LANES), jnp.asarray(one_np.T))
    return (
        feed.block_out,
        last.grad_latent,
        last.grad_skip,
        grad_text,
        skip_mine,
        shift_grad,
        jnp.transpose(project_mine, (1, 0, 2)),
        out_mine.T,
        few_mine[r : 2 * r],
        jnp.transpose(few_mine[2 * r :].reshape(2, text_share, cols), (1, 0, 2)),
        few_mine[:r].T,
        up_mine,
        down_mine.T,
        jnp.concatenate([pack_sum[0:2], pack_sum[5:7]]),
        jnp.concatenate([pack_sum[2:4], pack_sum[7:9]]),
        head_sums[:4],
        head_sums[4:],
        jnp.concatenate([column_sums, pack_sum[4:5]]),
        hidden_sums,
        jnp.concatenate([pack_sum[9:12], shift_bias]),
    )


def solution(mesh):
    both = ("dp", "tensor")
    rows2, split2, cross2 = P(both, None), P("dp", "tensor"), P("tensor", "dp")
    middle = P("dp", None, "tensor")
    return jax.shard_map(
        body,
        mesh=mesh,
        in_specs=(
            rows2, rows2, P("dp", None, None), P("dp", None), rows2, P(both), P("dp"), P(None, "dp"),
            split2, P("dp", None), middle, cross2, split2, middle, cross2, split2, cross2,
            P(), P(), P(), P(), P(), P(), P(),
        ),
        out_specs=(
            rows2, rows2, rows2, P("dp", None, None),
            split2, P("dp", None), middle, cross2, split2, middle, cross2, split2, cross2,
            P(), P(), P(), P(), P(), P(), P(),
        ),
        check_vma=False,
    )
```

time: 1540 us -> 743 us (0.48)
  waiting for transfers between devices: 553 us -> 0 us
  blocking collectives: 239 us -> 0 us
  Pallas kernels: 513 us -> 688 us
  matrix products: 94.3 us -> 3.75 us
  local copies, waits for them, and re-layouts: 77.6 us -> 31.2 us
  other arithmetic: 36.9 us -> 8.71 us
    reduce_scatter x7 -> x0, waiting for transfers between devices: 463 us -> none  [the longest x1 91.5 us: body(): up_mine = lax.psum_scatter(grad_up, 'dp', scatter_dimension=0, tiled=True)]
    all_gather x5 -> x0, blocking collectives: 189 us -> none  [the longest x1 42.9 us: body(): small_all = lax.all_gather(small, 'dp', axis=0, tiled=True)]
    pallas_call x15 -> x7, Pallas kernels: 513 us -> 688 us  [named_kernel(): pl.pallas_call(kernel, out_shape=list(outs.values()), in_specs=[anywhere...]
    dot_general x29 -> x5, matrix products: 94.3 us -> 3.75 us  [the longest x1 1.68 us: body(): bias_wide = exact(bias_cols, jnp.asarray(fold_np))]
    unnamed x14 -> x0, waiting for transfers between devices: 71 us -> none
    unnamed x1 -> x0, blocking collectives: 36.9 us -> none
    psum x2 -> x0, waiting for transfers between devices: 18.9 us -> none  [the longest x1 18.9 us: body(): lax.psum(text_part[:text_len].astype(BF16), 'tensor').astype(F32)[None]]
  transfers between devices with their start and end apart: 14 -> 0, of which waited for: 9 -> 0; matrix products, arithmetic and copies ran while one was open for 11% -> 0% of each run, Pallas kernels for 19% -> 0%
where the time goes in v3:
time: 743 us; the launch traced here: 734 us
  Pallas kernels  688 us (93%)
  local copies, waits for them, and re-layouts  31.2 us (4%)
  other arithmetic  8.71 us (1%)
    pallas_call x7, Pallas kernels, named_kernel(): pl.pallas_call(kernel, out_shape=list(outs.values()), in_specs=[anywhere...  688 us

profile of v3, /device:TPU:0, one launch (start us, length us, event | category | flops | bytes accessed | tf_op | source)
XLA Modules:
  0.0 734.4 jit_solution(16016568361799733901)
XLA Ops:
  0.7 1.7 fusion
  3.7 1.4 dynamic-slice.refs_11_
  5.8 3.9 sine_multiply_fusion
  14.1 200.2 %first.1 = (bf16[1024,1408]{1,0:T(8,128)(2,1)}, bf16[1024,1408]{1,0:T(8,128)(2,1)}, bf16[8,352,352]{2,1,0:T(8,128)(2,1)}, bf16[256,1408]{1,0:T(8,128)(2,1)}, f32...) custom-call(bf16[256,1408]{1,0:T(8,128)(2,1)} %refs_0_.1, ...), custom_call_target="tpu_custom_call" | custom-call | tf_op jit(solution)/shard_map/first/pallas_call | solution.py:388
  214.9 0.9 pad.23.refs_6_.refs_14_
  215.8 96.7 %cross.1 = (bf16[1408,512]{1,0:T(8,128)(2,1)}, bf16[2,1024,512]{2,1,0:T(8,128)(2,1)}, f32[336,512]{1,0:T(8,128)}, bf16[336,1024]{1,0:T(8,128)(2,1)}, f32[1024,51...) custom-call(bf16[1024,1408]{1,0:T(8,128)(2,1)} %get-tuple-element.94, ...), custom_call_target="tpu_custom_call" | custom-call | tf_op jit(solution)/shard_map/cross/pallas_call | solution.py:388
  312.6 0.8 copy.60.refs_7_
  313.4 0.8 dynamic_slice.7
  314.8 52.4 %feed.1 = (bf16[1024,1536]{1,0:T(8,128)(2,1)}, bf16[1024,1536]{1,0:T(8,128)(2,1)}, bf16[1024,1408]{1,0:T(8,128)(2,1)}, bf16[256,1408]{1,0:T(8,128)(2,1)}, f32[256,1408]{1,0:T(8,128)}, /*index=5*/f32[1,1408]{1,0:T(1,128)}) custom-call(bf16[1024,1408]{1,0:T(8,128)(2,1)} %get-tuple-element.99.refs_0_.refs_5_, bf16[1408,1536]{1,0:T(8,128)(2,1)} %bitcast.60, ...), custom_call_target="tpu_custom_call" | custom-call | tf_op jit(solution)/shard_map/feed/pallas_call | solution.py:388
  367.8 76.5 %feed_back.1 = (bf16[1024,1408]{1,0:T(8,128)(2,1)}, f32[256,1408]{1,0:T(8,128)}, f32[1,1408]{1,0:T(1,128)}, f32[1,1408]{1,0:T(1,128)}, f32[1,1408]{1,0:T(1,128)}...) custom-call(bf16[1024,1408]{1,0:T(8,128)(2,1)} %get-tuple-element.105.refs_0_, ...), custom_call_target="tpu_custom_call" | custom-call | tf_op jit(solution)/shard_map/feed_back/pallas_call | solution.py:388
  444.3 73.6 %cross_back.1 = (bf16[8,608,352]{2,1,0:T(8,128)(2,1)}, bf16[336,1024]{1,0:T(8,128)(2,1)}, f32[2,128]{1,0:T(2,128)}, f32[2,128]{1,0:T(2,128)}, f32[1,512]{1,0:T(1...) custom-call(bf16[1024,1408]{1,0:T(8,128)(2,1)} %get-tuple-element.10, ...), custom_call_target="tpu_custom_call" | custom-call | tf_op jit(solution)/shard_map/cross_back/pallas_call | solution.py:388
  518.0 73.4 %self_back.1 = (bf16[1024,1536]{1,0:T(8,128)(2,1)}, bf16[8,176,352]{2,1,0:T(8,128)(2,1)}, bf16[8,3,176,352]{3,2,1,0:T(8,128)(2,1)}, f32[2,128]{1,0:T(2,128)}, f3...) custom-call(bf16[336,1024]{1,0:T(8,128)(2,1)} %get-tuple-element.121.refs_0_, ...), custom_call_target="tpu_custom_call" | custom-call | tf_op jit(solution)/shard_map/self_back/pallas_call | solution.py:388
  594.1 2.0 concatenate.31
  596.1 115.5 %last.1 = (f32[256,1408]{1,0:T(8,128)}, f32[256,1408]{1,0:T(8,128)}, f32[176,1408]{1,0:T(8,128)}, f32[1,1408]{1,0:T(1,128)}, f32[4,8,1408]{2,1,0:T(8,128)}, /*in...) custom-call(bf16[1024,1536]{1,0:T(8,128)(2,1)} %get-tuple-element.130.refs_0_, ...), custom_call_target="tpu_custom_call" | custom-call | tf_op jit(solution)/shard_map/last/pallas_call | solution.py:388
  711.6 0.8 slice.135
  712.4 1.3 pad_maximum_fusion.3
  713.7 0.9 slice.116
  714.8 0.8 slice.133
  716.3 1.0 fusion.6
  718.5 0.8 slice.131
  720.2 2.5 copy.63
  722.7 0.9 copy.61
  723.6 0.8 slice_bitcast_fusion.1
  724.4 0.9 copy.78
  725.3 1.1 copy.79
  726.4 0.8 copy-done.2
  727.2 1.1 copy.80
  728.6 0.8 copy.81
  729.4 0.9 copy.82
  730.3 0.9 copy.83
  731.9 1.0 copy.85
  732.9 1.0 copy.86
  (118 shorter events, 14.1 us)
Async XLA Ops:
  0.7 9.0 %copy-start = (f32[4,88]{1,0:T(4,128)S(1)}, f32[4,88]{1,0:T(4,128)}, u32[]{:S(2)}) copy-start(f32[4,88]{1,0:T(4,128)} %param.52) | copy-start | bytes 4228
  0.7 9.0 %copy-start.17 = (f32[88,128]{1,0:T(8,128)S(1)}, f32[88,128]{1,0:T(8,128)}, u32[]{:S(2)}) copy-start(f32[88,128]{1,0:T(8,128)} %constant.49.clone) | copy-start | bytes 135172
  0.7 9.7 %copy-start.16 = (bf16[128,2,352]{0,2,1:T(8,128)(2,1)S(1)}, bf16[128,2,352]{0,2,1:T(8,128)(2,1)}, u32[]{:S(2)}) copy-start(bf16[128,2,352]{0,2,1:T(8,128)(2,1)} %param.46) | copy-start | bytes 540676
  0.7 11.9 %copy-start.20 = (bf16[1,1408]{1,0:T(2,128)(2,1)S(1)}, bf16[1,1408]{1,0:T(2,128)(2,1)}, u32[]{:S(2)}) copy-start(bf16[1,1408]{1,0:T(2,128)(2,1)} %param.36) | copy-start | bytes 8452
  0.7 12.7 %copy-start.30 = (f32[4,88]{1,0:T(4,128)S(1)}, f32[4,88]{1,0:T(4,128)}, u32[]{:S(2)}) copy-start(f32[4,88]{1,0:T(4,128)} %param.53) | copy-start | bytes 4228
  14.1 200.8 %copy-start.12 = (bf16[1,333,1024]{2,1,0:T(8,128)(2,1)S(1)}, bf16[1,333,1024]{2,1,0:T(8,128)(2,1)}, u32[]{:S(2)}) copy-start(bf16[1,333,1024]{2,1,0:T(8,128)(2,1)} %param.35) | copy-start | bytes 2045956
  215.8 96.7 %copy-start.34 = (f32[1,128]{1,0:T(1,128)S(1)}, f32[1,128]{1,0:T(1,128)}, u32[]{:S(2)}) copy-start(f32[1,128]{1,0:T(1,128)} %get-tuple-element.103) | copy-start | bytes 1540
  215.8 96.8 %copy-start.31 = (s32[256]{0:T(256)S(1)}, s32[256]{0:T(256)}, u32[]{:S(2)}) copy-start(s32[256]{0:T(256)} %param.38) | copy-start | bytes 3076
  314.8 52.4 %copy-start.14 = (f32[4,1408]{1,0:T(4,128)S(1)}, f32[4,1408]{1,0:T(4,128)}, u32[]{:S(2)}) copy-start(f32[4,1408]{1,0:T(4,128)} %refs_5_.7) | copy-start | bytes 67588
  518.0 74.3 %copy-start.10 = (f32[512,352]{1,0:T(8,128)S(1)}, f32[512,352]{1,0:T(8,128)}, u32[]{:S(2)}) copy-start(f32[512,352]{1,0:T(8,128)} %constant.54.clone) | copy-start | bytes 2162692
  518.0 74.3 %copy-start.28 = (f32[1,512]{1,0:T(1,128)S(1)}, f32[1,512]{1,0:T(1,128)}, u32[]{:S(2)}) copy-start(f32[1,512]{1,0:T(1,128)} %get-tuple-element.151) | copy-start | bytes 6148
  518.0 74.3 %copy-start.29 = (f32[1,512]{1,0:T(1,128)S(1)}, f32[1,512]{1,0:T(1,128)}, u32[]{:S(2)}) copy-start(f32[1,512]{1,0:T(1,128)} %get-tuple-element.152) | copy-start | bytes 6148
  518.0 74.9 %copy-start.19 = (f32[1,1536]{1,0:T(1,128)S(1)}, f32[1,1536]{1,0:T(1,128)}, u32[]{:S(2)}) copy-start(f32[1,1536]{1,0:T(1,128)} %get-tuple-element.153) | copy-start | bytes 18436
  518.0 75.2 %copy-start.32 = (f32[2,128]{1,0:T(2,128)S(1)}, f32[2,128]{1,0:T(2,128)}, u32[]{:S(2)}) copy-start(f32[2,128]{1,0:T(2,128)} %get-tuple-element.147) | copy-start | bytes 3076
  518.0 75.2 %copy-start.33 = (f32[2,128]{1,0:T(2,128)S(1)}, f32[2,128]{1,0:T(2,128)}, u32[]{:S(2)}) copy-start(f32[2,128]{1,0:T(2,128)} %get-tuple-element.149) | copy-start | bytes 3076
  591.5 2.5 copy-start.21
  591.5 2.5 copy-start.22
  591.5 2.5 copy-start.23
  591.5 2.5 copy-start.24
  591.5 2.5 copy-start.25
  591.5 2.5 copy-start.26
  591.6 2.5 copy-start.27
  596.1 123.2 %copy-start.18 = (f32[128,88]{1,0:T(8,128)S(1)}, f32[128,88]{1,0:T(8,128)}, u32[]{:S(2)}) copy-start(f32[128,88]{1,0:T(8,128)} %constant.55.clone) | copy-start | bytes 135172
  596.1 124.0 %copy-start.4 = (f32[336,1024]{1,0:T(8,128)S(1)}, f32[336,1024]{1,0:T(8,128)}, u32[]{:S(2)}) copy-start(f32[336,1024]{1,0:T(8,128)} %get-tuple-element.158) | copy-start | bytes 4128772
  720.2 2.5 copy-start.8
  722.7 1.8 copy-start.11
  725.3 1.9 copy-start.2
  727.2 2.2 copy-start.7
  728.6 1.8 copy-start.9
  729.4 1.8 copy-start.15
  731.2 1.7 copy-start.5
  731.9 2.0 copy-start.1
  (3 other events, 4.7 us)

commit v4 on v3

--- a/solution.py
+++ b/solution.py
@@ -108,76 +108,58 @@
             cp.wait_send()
 
 
-class WeightGather:
-    def __init__(self, place, shard, land, z_s, z_r, x_s, x_r):
-        self.place, self.land, self.z_s, self.z_r, self.x_s, self.x_r = place, land, z_s, z_r, x_s, x_r
-        self.z = {}
-        for j in (2, 1, 3):
-            self.z[j] = remote(shard, land.at[place.d], z_s.at[j], z_r.at[j], (place.ahead(j), place.t))
-            self.sends(j, self.z[j].start)
-        cp = remote(shard, land.at[place.d], x_s.at[0], x_r.at[0], place.pair)
-        cp.start()
-        self.x = [cp]
-        source = place.behind(2)
-        self.inner = remote(
-            land.at[source], land.at[source], z_s.at[0], z_r.at[1 + 2 * (place.zi // 2)], (place.at(3 * (place.zi // 2)), place.t)
-        )
-
-    def sends(self, j, act):
-        if j == 2:
-            act()
-        else:
-            pl.when(self.place.zi != (0 if j == 3 else 3))(act)
-
-    def forward(self):
-        e0 = self.place.e0
-        for j in (2, 1 + 2 * e0, 3 - 2 * e0):
-            source = self.place.behind(j)
-            here = self.land.at[source]
-            remote(here, here, self.z_s.at[j], self.z_r.at[j], self.place.pair).wait_recv()
-            if isinstance(j, int):
-                pl.when(self.place.end == 0)(self.inner.start)
-            cp = remote(here, here, self.x_s.at[j], self.x_r.at[j], self.place.pair)
-            cp.start()
-            self.x.append(cp)
-
-    def arrived(self):
-        for cp in self.x:
-            cp.wait_recv()
-
-    def sent(self):
-        for j in (1, 2, 3):
-            self.sends(j, self.z[j].wait_send)
-        pl.when(self.place.end == 0)(self.inner.wait_send)
-        for cp in self.x:
-            cp.wait_send()
-
-
 class Gathers:
-    def __init__(self, place, z_s, z_r, x_s, x_r):
-        self.place, self.sems, self.all, self.passed = place, (z_s, z_r, x_s, x_r), [], 0
+    def __init__(self, place, ahead, z_s, z_r, x_s, x_r):
+        self.place, self.ahead, self.sems = place, ahead, (z_s, z_r, x_s, x_r)
+        self.pieces, self.z, self.x, self.passed = [], [], [], 0
 
     def add(self, shard, land, pieces=1):
         start = 0
         for i in range(pieces):
-            count = piece_rows(shard.shape[0], pieces, i) if pieces > 1 else None
-            src = shard if count is None else shard.at[pl.ds(start, count)]
-            dst = land if count is None else land.at[:, pl.ds(start, count)]
-            start += count or 0
-            self.all.append(WeightGather(self.place, src, dst, *[v.at[len(self.all)] for v in self.sems]))
+            if pieces == 1:
+                self.pieces.append((shard, land))
+            else:
+                count = piece_rows(shard.shape[0], pieces, i)
+                self.pieces.append((shard.at[pl.ds(start, count)], land.at[:, pl.ds(start, count)]))
+                start += count
+        self.fill()
+
+    def fill(self):
+        place = self.place
+        while len(self.z) < min(len(self.pieces), self.passed + self.ahead):
+            k = len(self.z)
+            shard, land = self.pieces[k]
+            z_s, z_r, x_s, x_r = [v.at[k] for v in self.sems]
+            self.z.append([
+                remote(shard, land.at[place.d], z_s.at[j], z_r.at[j], (place.ahead(j), place.t)) for j in range(1, place.line)
+            ])
+            self.x.append([remote(shard, land.at[place.d], x_s.at[0], x_r.at[0], place.pair)])
+            for cp in self.z[k] + self.x[k]:
+                cp.start()
 
     def forward(self, count=1):
         for _ in range(count):
-            self.all[self.passed].forward()
+            k = self.passed
+            _, land = self.pieces[k]
+            _, _, x_s, x_r = [v.at[k] for v in self.sems]
+            for j in range(1, self.place.line):
+                self.z[k][j - 1].wait_recv()
+                here = land.at[self.place.behind(j)]
+                cp = remote(here, here, x_s.at[j], x_r.at[j], self.place.pair)
+                cp.start()
+                self.x[k].append(cp)
             self.passed += 1
+            self.fill()
 
     def arrived(self, first, last):
-        for g in self.all[first:last]:
-            g.arrived()
+        for cps in self.x[first:last]:
+            for cp in cps:
+                cp.wait_recv()
 
     def sent(self):
-        for g in self.all:
-            g.sent()
+        for cps in self.z + self.x:
+            for cp in cps:
+                cp.wait_send()
 
     @staticmethod
     def scratch(count, line):
@@ -280,14 +262,15 @@
         cp.start()
         return cp
 
-    def start(self, product, ready=None):
+    def start(self, product, ready=None, long=False):
         there, here = 2 * (1 - self.y), 2 * self.y
         first = product(there + 1 - self.c)
         if ready is not None:
             ready()
         self.c0 = self.core(0, first)
         self.far[...] = product(there + self.c)
-        self.c1 = self.core(1, product(here + 1 - self.c))
+        if not long:
+            self.c1 = self.core(1, product(here + 1 - self.c))
         self.c0.wait_recv()
         self.ycs = []
         ch = self.far.shape[0] // CHUNKS
@@ -297,6 +280,8 @@
             cp = remote(self.ysend.at[sl], self.yrecv.at[sl], self.ys.at[k], self.yr.at[k], self.yp)
             cp.start()
             self.ycs.append(cp)
+        if long:
+            self.c1 = self.core(1, product(here + 1 - self.c))
         self.near[...] = product(here + self.c)
         self.c1.wait_recv()
 
@@ -366,11 +351,15 @@
     return jax.ShapeDtypeStruct(shape, dtype)
 
 
-def named_kernel(name, collective_id, body, ins, outs, scratch, hbm=()):
+def named_kernel(name, collective_id, body, ins, outs, scratch, hbm=(), late=(), early=()):
     vm, anywhere = pl.BlockSpec(memory_space=pltpu.VMEM), pl.BlockSpec(memory_space=pl.ANY)
     flat = []
     for v in scratch.values():
         flat.extend(v if isinstance(v, list) else [v])
+    buffers = [pltpu.VMEM(ins[k].shape, ins[k].dtype) for k in late] + [pltpu.VMEM(outs[k].shape, outs[k].dtype) for k in early]
+    moved = len(buffers)
+    if moved:
+        buffers.append(pltpu.SemaphoreType.DMA((moved,)))
 
     def kernel(*refs):
         left = list(refs)
@@ -382,15 +371,40 @@
                 setattr(n, k, [left.pop(0) for _ in v])
             else:
                 setattr(n, k, left.pop(0))
+        loads, stores, going = {}, {}, []
+        for i, k in enumerate([*late, *early]):
+            if k in ins:
+                loads[k] = pltpu.make_async_copy(getattr(n, k), left[i], left[-1].at[i])
+                loads[k].start()
+            else:
+                stores[k] = pltpu.make_async_copy(left[i], getattr(n, k), left[-1].at[i])
+            setattr(n, k, left[i])
+
+        def need(*names):
+            for k in names:
+                if k in loads:
+                    loads.pop(k).wait()
+
+        def done(*names):
+            for k in names:
+                if k in stores:
+                    going.append(stores.pop(k))
+                    going[-1].start()
+
+        n.need, n.done = need, done
         body(n)
+        need(*list(loads))
+        done(*list(stores))
+        for cp in going:
+            cp.wait()
 
     talks = {} if collective_id is None else {"collective_id": collective_id, "has_side_effects": True}
     got = pl.pallas_call(
         kernel,
         out_shape=list(outs.values()),
-        in_specs=[anywhere if k in hbm else vm for k in ins],
-        out_specs=[anywhere if k in hbm else vm for k in outs],
-        scratch_shapes=flat,
+        in_specs=[anywhere if k in hbm or k in late else vm for k in ins],
+        out_specs=[anywhere if k in hbm or k in early else vm for k in outs],
+        scratch_shapes=flat + buffers,
         compiler_params=pltpu.CompilerParams(vmem_limit_bytes=VMEM_BYTES, **talks),
         name=name,
     )(*ins.values())
@@ -468,7 +482,16 @@
     return pl.ds(h * LANES, LANES)
 
 
-def attend(q_ref, k_ref, v_ref, out_ref, lse_ref, heads, scale, block, real_keys):
+def in_halves(count, step, between):
+    if between is None:
+        lax.fori_loop(0, count, step, 0)
+    else:
+        for i in range(2):
+            lax.fori_loop(i * count // 2, (i + 1) * count // 2, step, 0)
+            between()
+
+
+def attend(q_ref, k_ref, v_ref, out_ref, lse_ref, heads, scale, block, real_keys, between=None):
     queries, keys = q_ref.shape[0], k_ref.shape[0]
 
     def step(i, _):
@@ -488,10 +511,10 @@
             lse_ref[i, pl.ds(h, 1), :] = highest + jnp.log(denominator)
         return 0
 
-    lax.fori_loop(0, queries // block, step, 0)
-
-
-def attend_back(q_ref, k_ref, v_ref, do_ref, lse_ref, dq_ref, dk_ref, dv_ref, heads, scale, block, real_keys):
+    in_halves(queries // block, step, between)
+
+
+def attend_back(q_ref, k_ref, v_ref, do_ref, lse_ref, dq_ref, dk_ref, dv_ref, heads, scale, block, real_keys, between=None):
     queries, keys = q_ref.shape[0], k_ref.shape[0]
     dk_ref[...] = jnp.zeros(dk_ref.shape, F32)
     dv_ref[...] = jnp.zeros(dv_ref.shape, F32)
@@ -514,14 +537,34 @@
             dq_ref[here, hs] = dot_tn(k, grad_scores).T * scale
         return 0
 
-    lax.fori_loop(0, queries // block, step, 0)
+    in_halves(queries // block, step, between)
+
+
+def exact(left, right):
+    return jnp.dot(left, right, precision=lax.Precision.HIGHEST, preferred_element_type=F32)
+
+
+def my_cols(whole, t, cols):
+    return sum(jnp.where(t == s, whole[:, s * cols : (s + 1) * cols], 0.0) for s in range(4))
+
+
+def prepare(t, cols, n):
+    n.gain_wide[...] = exact(n.head_gain[...], n.one[...])
+    n.offset_wide[...] = exact(n.head_bias[...], n.one[...])
+    mine = my_cols(n.column_bias[...], t, cols)
+    n.bias_wide[...] = exact(mine, n.fold_f32[...])
+    angles = n.positions[:, 0:1] * n.lanes[0:1, :] + n.positions[:, 1:2] * n.lanes[1:2, :]
+    n.cosine[...] = jnp.cos(angles) * n.mask[...]
+    n.sine[...] = jnp.sin(angles) * n.lanes[2:3, :]
+    n.done("cosine", "sine")
+    return mine[4:5, :]
 
 
 def first_body(dp, own, size, scale, heads, block, n):
     _, t, _, _, _, _ = tensor_place()
     d = lax.axis_index("dp")
     rows, width = n.residual.shape
-    cols = n.bias_skip.shape[1]
+    cols = n.skip_send.shape[2]
     span = heads * LANES
     place = DpPlace(dp) if own else None
     peers = [(d, (t + o) % 4) for o in range(1, 4)] + (place.others() if own else [])
@@ -533,7 +576,7 @@
     ]
     if own:
         shards = [(n.skip_in, n.skip_full), (n.project_in, n.p_land), (n.out_in, n.out_land), (n.query_in, n.query_g),
-                  (n.key_in, n.key_g), (n.value_in, n.value_g), (n.down_in, n.down_g)]
+                  (n.key_in, n.key_g), (n.value_in, n.value_g), (n.cross_out_in, n.cross_out_g), (n.down_in, n.down_g)]
         kept += [pltpu.make_async_copy(a, b.at[d], n.own_sem.at[2 + i]) for i, (a, b) in enumerate(shards)]
     for cp in kept:
         cp.start()
@@ -545,7 +588,7 @@
     if own:
         n.small_land[d] = n.small[d]
         smalls = ToAll(place, lambda q: n.small.at[q], n.small_land, n.a_s, n.a_r)
-        gathers = Gathers(place, *n.gather_sems)
+        gathers = Gathers(place, 2, *n.gather_sems)
         gathers.add(n.skip_in, n.skip_full, 2)
         smalls.arrived()
         given = jnp.concatenate([n.small_land[i] for i in range(dp)], axis=0)
@@ -558,6 +601,8 @@
         shifts = ToAll(place, lambda q: n.shift_part.at[q], n.shift_land, n.b_s, n.b_r)
         for i in range(3):
             gathers.add(n.project_in.at[i], n.p_land.at[:, i])
+    bias_skip = prepare(t, cols, n)
+    if own:
         gathers.forward()
     spreads[0].forward()
     if own:
@@ -565,10 +610,11 @@
         gathers.add(n.query_in, n.query_g)
         gathers.add(n.key_in, n.key_g)
         gathers.add(n.value_in, n.value_g)
+        gathers.add(n.cross_out_in, n.cross_out_g)
         gathers.forward()
     spreads[0].finish()
     if own:
-        gathers.add(n.down_in, n.down_g, 4)
+        gathers.add(n.down_in, n.down_g, 3)
         gathers.arrived(0, 2)
         kept[2].wait()
         half = dp // 2
@@ -586,7 +632,7 @@
     for o in (2, 3, 1, 0):
         b = (t + o) % 4
         here = block_rows(b, rows)
-        value = (n.pre[here, pl.ds(0, cols)] + dot_nn(n.joined1[here, :], skip_half(1)) + n.bias_skip[...]).astype(BF16)
+        value = (n.pre[here, pl.ds(0, cols)] + dot_nn(n.joined1[here, :], skip_half(1)) + bias_skip).astype(BF16)
         if o:
             n.skip_send[o] = value
             cp = remote(n.skip_send.at[o], n.skip_recv.at[t], n.p_s.at[o], n.p_r.at[o], (d, b))
@@ -622,6 +668,7 @@
     spread.finish()
     for cp in copies:
         cp.wait_send()
+    n.done("joined0", "joined1", "skip_full", "skipped", "residual", "first_all")
     for part in range(3):
         if own:
             gathers.arrived(2 + part, 3 + part)
@@ -637,12 +684,14 @@
     def project(i, _):
         here = pl.ds(pl.multiple_of(i * block, block), block)
         for part in range(3):
-            out = dot_nn(n.first_all[here, :], n.project_wide[part]) + n.self_bias[part]
+            out = dot_nn(n.first_all[here, :], n.project_wide[part])
+            if part != 1:
+                out = out + n.bias_wide[pl.ds(part // 2, 1), :]
             if part < 2:
                 n.pre[here, pl.ds(part * span, span)] = out
                 for h in range(heads):
                     u = out[:, h * LANES : (h + 1) * LANES]
-                    val = head_norm(u, n.mask[...], n.head_gain[pl.ds(part, 1), :], n.head_bias[pl.ds(part, 1), :], size)
+                    val = head_norm(u, n.mask[...], n.gain_wide[pl.ds(part, 1), :], n.offset_wide[pl.ds(part, 1), :], size)
                     val = turn(val, n.cosine[here, :], n.sine[here, :])
                     n.low[here, pl.ds(part * span + h * LANES, LANES)] = val.astype(BF16)
             else:
@@ -650,15 +699,16 @@
         return 0
 
     lax.fori_loop(0, n.low.shape[0] // block, project, 0)
+    n.done("project_wide", "pre", "low")
     if own:
         gathers.forward()
     attend(
         n.low.at[:, pl.ds(0, span)], n.low.at[:, pl.ds(span, span)], n.low.at[:, pl.ds(2 * span, span)],
-        n.padded, n.lse, heads, scale, block, n.low.shape[0],
+        n.padded, n.lse, heads, scale, block, n.low.shape[0], gathers.forward if own else None,
     )
     n.mixed[...] = dot_nt(n.padded[...], n.fold[...]).astype(BF16)
-    if own:
-        gathers.forward()
+    n.done("mixed")
+    if own:
         gathers.arrived(5, 6)
         kept[4].wait()
         out_t = lambda: n.out_land[...].reshape(width, cols)
@@ -673,8 +723,9 @@
         reduce, spread, n.third_all, n.residual, n.row_bias.at[pl.ds(0, 1)], n.norm_gain.at[pl.ds(2, 1)],
         n.norm_bias.at[pl.ds(2, 1)], n.second, rows,
     )
-    if own:
-        gathers.forward(2)
+    n.done("second")
+    if own:
+        gathers.forward()
     spread.forward()
     if own:
         gathers.forward()
@@ -682,7 +733,7 @@
     reduce.sent()
     if own:
         gathers.forward()
-        gathers.arrived(6, len(gathers.all))
+        gathers.arrived(6, len(gathers.pieces))
         for cp in kept[5:]:
             cp.wait()
         for g in (gathers, smalls, shifts):
@@ -698,30 +749,30 @@
     bar = greet(peers)
     pl.semaphore_wait(bar, len(peers))
     if own:
-        gathers = Gathers(place, *n.gather_sems)
-        gathers.add(n.cross_out, n.cross_out_land)
+        gathers = Gathers(place, 2, *n.gather_sems)
         gathers.add(n.up_in, n.up_g, 4)
+        gathers.add(n.down_in, n.down_g)
         kept = [pltpu.make_async_copy(a, b.at[d], n.own_sem.at[i])
-                for i, (a, b) in enumerate(((n.cross_out, n.cross_out_land), (n.up_in, n.up_g)))]
+                for i, (a, b) in enumerate(((n.up_in, n.up_g), (n.down_in, n.down_g)))]
         for cp in kept:
             cp.start()
+    n.need("query", "key", "value", "text")
     n.query_wide[...] = dot_nn(n.query[...], n.fold[...]).astype(BF16)
     for part, w in enumerate((n.key, n.value)):
         n.keyval_wide[part] = dot_nn(w[...], n.fold[...]).astype(BF16)
-        out = dot_nn(n.text[...], n.keyval_wide[part]) + n.text_bias[part]
+        out = dot_nn(n.text[...], n.keyval_wide[part])
         if part == 0:
             n.text_pre[...] = out
             for h in range(heads):
                 val = head_norm(out[:, h * LANES : (h + 1) * LANES], n.mask[...], n.head_gain[pl.ds(3, 1), :], n.head_bias[pl.ds(3, 1), :], size)
                 n.text_low[:, head_at(h)] = val.astype(BF16)
         else:
-            n.text_low[:, pl.ds(span, span)] = out.astype(BF16)
-    if own:
-        gathers.forward()
+            n.text_low[:, pl.ds(span, span)] = (out + n.bias_wide[pl.ds(3, 1), :]).astype(BF16)
+    n.need("third_all", "cosine", "sine")
 
     def project(i, _):
         here = pl.ds(pl.multiple_of(i * block, block), block)
-        out = dot_nn(n.third_all[here, :], n.query_wide[...]) + n.query_bias[...]
+        out = dot_nn(n.third_all[here, :], n.query_wide[...]) + n.bias_wide[pl.ds(2, 1), :]
         n.pre[here, :] = out
         for h in range(heads):
             val = head_norm(out[:, h * LANES : (h + 1) * LANES], n.mask[...], n.head_gain[pl.ds(2, 1), :], n.head_bias[pl.ds(2, 1), :], size)
@@ -729,19 +780,15 @@
         return 0
 
     lax.fori_loop(0, n.low.shape[0] // block, project, 0)
+    n.done("query_wide", "keyval_wide", "pre", "low")
     attend(n.low, n.text_low.at[:, pl.ds(0, span)], n.text_low.at[:, pl.ds(span, span)], n.padded, n.lse, heads, scale, block, real)
     n.mixed[...] = dot_nt(n.padded[...], n.fold[...]).astype(BF16)
-    if own:
-        gathers.forward()
-        gathers.arrived(0, 1)
-        kept[0].wait()
-        out_t = lambda: n.cross_out_land[...].reshape(width, n.mixed.shape[1])
-    else:
-        out_t = lambda: n.cross_out[...]
+    n.need("cross_out", "second")
     reduce = TensorSum(*n.sum)
-    reduce.start(lambda b: dot_nt(n.mixed[block_rows(b, rows), :], out_t()))
-    if own:
-        gathers.forward()
+    reduce.start(lambda b: dot_nt(n.mixed[block_rows(b, rows), :], n.cross_out[...]))
+    n.done("mixed")
+    if own:
+        gathers.forward(2)
     spread = RowSpread(n.fourth_all, rows, *n.spread)
     forward_rows(
         reduce, spread, n.fourth_all, n.second, n.row_bias.at[pl.ds(1, 1)], n.norm_gain.at[pl.ds(3, 1)],
@@ -755,20 +802,42 @@
     spread.finish()
     reduce.sent()
     if own:
-        gathers.arrived(1, len(gathers.all))
-        kept[1].wait()
+        gathers.forward()
+        gathers.arrived(0, len(gathers.pieces))
+        for cp in kept:
+            cp.wait()
         gathers.sent()
 
 
-def feed_body(n):
+def load_down(own, n):
+    if not own:
+        return [], lambda: n.down_t[...]
+    first = n.down_a.shape[1]
+    copies = [
+        pltpu.make_async_copy(n.down_a, n.down_t.at[:, pl.ds(0, first)], n.down_sem.at[0]),
+        pltpu.make_async_copy(n.down_b, n.down_t.at[:, pl.ds(first, n.down_b.shape[1])], n.down_sem.at[1]),
+    ]
+    for cp in copies:
+        cp.start()
+    return copies, lambda: n.down_t[...].reshape(-1, n.down_t.shape[2])
+
+
+def feed_body(own, n):
     rows = n.third_sum.shape[0]
     _, t, _, _, sib, yp = tensor_place()
     bar = greet((sib, yp))
+    down_copies, down_t = load_down(own, n)
+    hidden = n.up.shape[1]
+    my_hidden = pl.ds(pl.multiple_of(t * hidden, LANES), hidden)
+    seat = t * rows + lax.broadcasted_iota(jnp.int32, (rows, 1), 0)
+    weight = n.loss_mask[...].astype(F32) * (seat < n.true_count[...]).astype(F32)
+    weight = (n.total[...] / n.counted[:, 0:1]) * weight
+    n.need("fourth_all", "up")
     root, cube = float(np.sqrt(2.0 / np.pi)), 0.044715
 
     def product(b):
         here = block_rows(b, rows)
-        x = dot_nn(n.fourth_all[here, :], n.up[...]) + n.hidden_bias[...]
+        x = dot_nn(n.fourth_all[here, :], n.up[...]) + n.hidden_bias[:, my_hidden]
         square = x * x
         th = jnp.tanh(root * (x + cube * (square * x)))
         cdf = 0.5 * (1.0 + th)
@@ -776,10 +845,14 @@
         n.active[here, :] = active
         slope = cdf + (0.5 * root) * x * (1.0 - th * th) * (1.0 + (3.0 * cube) * square)
         n.slope[here, :] = slope.astype(BF16)
-        return dot_nt(active, n.down_t[...])
+        while down_copies:
+            down_copies.pop().wait()
+        return dot_nt(active, down_t())
 
     reduce = TensorSum(*n.sum)
-    reduce.start(product, lambda: pl.semaphore_wait(bar, 2))
+    reduce.start(product, lambda: pl.semaphore_wait(bar, 2), long=True)
+    n.done("active", "slope")
+    n.need("third_sum", "teacher")
     spread = RowSpread(n.grad_all, rows, *n.spread)
     ch = rows // CHUNKS
     sums = None
@@ -787,13 +860,14 @@
         sl, total = reduce.chunk(k)
         final = n.third_sum[sl, :] + (total + n.row_bias[pl.ds(2, 1), :])
         n.block_out[sl, :] = final.astype(BF16)
-        grad = n.weight[sl, :] * (final - n.teacher[sl, :].astype(F32))
+        grad = weight[k * ch : (k + 1) * ch, :] * (final - n.teacher[sl, :].astype(F32))
         n.grad_final[sl, :] = grad
         low = grad.astype(BF16)
         n.grad_all[pl.ds(pl.multiple_of(t * rows + k * ch, ch), ch), :] = low
         spread.send(k * ch, ch)
         sums = add_sums(sums, [low.astype(F32)])
     n.bias_mlp[...] = sums[0]
+    n.done("block_out", "grad_final")
     spread.forward()
     spread.finish()
     reduce.sent()
@@ -805,6 +879,8 @@
     place = DpPlace(dp) if own else None
     peers = [sib, yp] + (place.near() if own else [])
     bar = greet(peers)
+    down_copies, down_t = load_down(own, n)
+    n.need("grad_all", "active")
     n.grad_down[...] = dot_tn(n.grad_all[...], n.active[...]).astype(BF16).reshape(n.grad_down.shape)
     pl.semaphore_wait(bar, len(peers))
     if own:
@@ -812,16 +888,21 @@
 
     def product(b):
         here = block_rows(b, rows)
-        upper = (dot_nn(n.grad_all[here, :], n.down_t[...]) * n.slope[here, :].astype(F32)).astype(BF16)
+        upper = (dot_nn(n.grad_all[here, :], down_t()) * n.slope[here, :].astype(F32)).astype(BF16)
         n.upper[here, :] = upper
         return dot_nt(upper, n.up[...])
 
+    for cp in down_copies:
+        cp.wait()
+    n.need("slope", "up")
     reduce = TensorSum(*n.sum)
-    reduce.start(product)
+    reduce.start(product, long=True)
+    n.need("fourth_all", "third_sum", "grad_final")
     n.bias_hidden[...] = sum(
         jnp.sum(n.upper[pl.ds(b * rows, rows), :].astype(F32), axis=0, keepdims=True) for b in range(4)
     )
     n.grad_up[...] = dot_tn(n.fourth_all[...], n.upper[...]).astype(BF16).reshape(n.grad_up.shape)
+    n.done("grad_up")
     spread = RowSpread(n.c_all, rows, *n.spread)
     if own:
         down.steps(1)
@@ -858,7 +939,9 @@
     pl.semaphore_wait(bar, len(peers))
     if own:
         up = GradScatter(place, n.grad_up, *n.up_bufs, *n.up_sems)
+    n.need("c_all", "cross_out")
     spread_heads(n, n.c_all, n.cross_out, n.do, block)
+    n.need("low", "text_low")
     attend_back(
         n.low, n.text_low.at[:, pl.ds(0, span)], n.text_low.at[:, pl.ds(span, span)],
         n.do, n.lse, n.dq, n.dk, n.dv, heads, scale, block, real,
@@ -882,11 +965,14 @@
 
     if own:
         up.steps(1)
+    n.need("pre", "cosine", "sine")
     lax.fori_loop(0, n.p.shape[0] // block, finish, 0)
+    n.need("query_wide")
     reduce = TensorSum(*n.sum)
     reduce.start(lambda b: dot_nt(n.p[block_rows(b, rows), :], n.query_wide[...]))
     if own:
         up.steps(2)
+    n.need("text_pre", "mixed", "third_all", "text", "keyval_wide", "second", "grad_third")
     for h in range(heads):
         hs = head_at(h)
         grad, g, o = head_back(n.dk[:, hs], n.text_pre[:, hs], n.mask[...], n.head_gain[pl.ds(3, 1), :], size)
@@ -908,6 +994,7 @@
     for part in range(2):
         narrow = dot_nt(n.text_p[:, pl.ds(part * span, span)], n.fold[...]).astype(BF16)
         at = put(at, dot_tn(n.text[...], narrow))
+    n.done("grads")
     n.grad_text[...] = (
         dot_nt(n.text_p[:, pl.ds(0, span)], n.keyval_wide[0]) + dot_nt(n.text_p[:, pl.ds(span, span)], n.keyval_wide[1])
     ).astype(BF16)
@@ -968,15 +1055,16 @@
     text = TextSum(n.text_part, n.text_total, n.text_land, n.text_yland, n.text_back, n.text_sems)
     if own:
         few = GradScatter(place, n.few_grads, *n.few_bufs, *n.few_sems)
+    n.need("s_all", "out_t")
     spread_heads(n, n.s_all, n.out_t, n.do, block)
     text.along()
+    n.need("low")
     attend_back(
         n.low.at[:, pl.ds(0, span)], n.low.at[:, pl.ds(span, span)], n.low.at[:, pl.ds(2 * span, span)],
-        n.do, n.lse, n.dq, n.dk, n.dv, heads, scale, block, n.low.shape[0],
+        n.do, n.lse, n.dq, n.dk, n.dv, heads, scale, block, n.low.shape[0], few.step if own else None,
     )
     text.back()
-    if own:
-        few.step()
+    n.need("pre", "cosine", "sine")
     n.gains[...] = jnp.zeros(n.gains.shape, F32)
     n.offsets[...] = jnp.zeros(n.offsets.shape, F32)
     n.sums[...] = jnp.zeros(n.sums.shape, F32)
@@ -1004,9 +1092,12 @@
     by_place = lambda v: v.astype(BF16).reshape(n.grad_out.shape)
     if own:
         few.steps()
+    n.done("p")
+    n.need("mixed", "first_all")
     n.grad_out[...] = by_place(dot_tn(n.s_all[...], n.mixed[...]))
     for part in range(3):
         n.grad_project[:, part] = by_place(dot_tn(n.first_all[...], n.p_low[part]))
+    n.done("grad_out", "grad_project")
     text.result(n.grad_text)
     if own:
         n.few_mine[...] = few.result()
@@ -1046,7 +1137,9 @@
             total = total + dot_nt(n.p[here, pl.ds(part * span, span)], n.project_wide[part])
         return total
 
+    n.need("p", "project_wide")
     reduce.start(product, ready)
+    n.need("residual", "grad_second", "skipped")
     if own:
         scatters[0].steps()
     sums = None
@@ -1074,9 +1167,26 @@
         cp = remote(n.tile, n.tile_land.at[t], n.t_s.at[o], n.t_r.at[o], (d, (t + o) % 4))
         cp.start()
         tiles.append(cp)
-    n.pack[...] = n.pack_in[...]
-    for i, v in enumerate((gain_skip, gain_first, offset_skip, offset_first, bias_skip)):
-        n.pack[0, pl.ds(i, 1), :] = v
+    n.pack[...] = jnp.zeros(n.pack.shape, F32)
+    lines = [gain_skip, gain_first, offset_skip, offset_first, bias_skip, n.gain_third[...], n.gain_fourth[...],
+             n.offset_third[...], n.offset_fourth[...], n.bias_attn[...], n.bias_cross_out[...], n.bias_mlp[...]]
+    for i, v in enumerate(lines):
+        n.pack[i // PACK_ROWS, pl.ds(i % PACK_ROWS, 1), :] = v
+    heads_at = len(lines)
+    for i, v in enumerate((n.self_gains, n.cross_gains, n.self_offsets, n.cross_offsets)):
+        for r in range(2):
+            n.pack[heads_at // PACK_ROWS, pl.ds(heads_at % PACK_ROWS, 1), pl.ds((2 * i + r) * LANES, LANES)] = v[pl.ds(r, 1), :]
+    span = n.project_wide.shape[2]
+    wide = [n.self_sums[:, pl.ds(0, span)], n.self_sums[:, pl.ds(2 * span, span)], n.cross_sums[...], n.text_sums[...]]
+    hidden = n.bias_hidden.shape[1]
+    for s in range(4):
+        seat = (t == s).astype(F32)
+        block, row = divmod(PACK_SUMS + 4 * s, PACK_ROWS)
+        for i, v in enumerate(wide):
+            n.pack[block, pl.ds(row, 1), pl.ds(i * cols, cols)] = seat * exact(v, n.unfold[...])
+        for i, start in enumerate(range(0, hidden, width)):
+            count = min(width, hidden - start)
+            n.pack[block, pl.ds(row + 1 + i, 1), pl.ds(0, count)] = seat * n.bias_hidden[:, pl.ds(start, count)]
     shares = []
     for o in (1, 2, 3):
         b = (t + o) % 4
@@ -1089,31 +1199,22 @@
     for cp in copies:
         cp.wait_recv()
     reduce.sent()
+    for cp in tiles:
+        cp.wait_recv()
+    n.low_out[...] = (n.tile_land[0] + n.tile_land[1] + n.tile_land[2] + n.tile_land[3]).astype(BF16).astype(F32)
+    for cp in shares:
+        cp.wait_recv()
+    n.pack_mine[...] = n.pack_in_land[0] + n.pack_in_land[1] + n.pack_in_land[2] + n.pack_in_land[3]
+    if own:
+        n.low_land[d] = n.low_out[...]
+        lows = ToAll(place, lambda q: n.low_out, n.low_land, n.l_s, n.l_r)
+        pack_cp = remote(n.pack_mine, n.pack_x, n.px_s.at[0], n.px_r.at[0], place.pair)
+        pack_cp.start()
+    n.need("skip_w")
     halves = [TensorSum(*n.sum), TensorSum(*n.sum1)]
     for h, half in enumerate(halves):
         half.start(lambda b, h=h: dot_nt(n.krecv[b], n.skip_w[pl.ds(h * width, width), :]))
-    k_all = n.krecv[...].reshape(4 * rows, cols)
-    count = n.grad_skip_w.shape[0] // 2
-    for h, joined in enumerate((n.joined0, n.joined1)):
-        n.grad_skip_w[pl.ds(h * count, count)] = (
-            dot_tn(joined[...], k_all).astype(BF16).reshape((count,) + n.grad_skip_w.shape[1:])
-        )
-    if own:
-        scatter(n.grad_skip_w, n.skip_bufs)
-    for cp in tiles:
-        cp.wait_recv()
-    shift_low = n.tile_land[0] + n.tile_land[1] + n.tile_land[2] + n.tile_land[3]
-    n.low_out[...] = shift_low.astype(BF16).astype(F32)
-    if own:
-        n.low_land[d] = n.low_out[...]
-        lows = ToAll(place, lambda q: n.low_out, n.low_land, n.l_s, n.l_r)
-    for cp in shares:
-        cp.wait_recv()
-    n.pack_mine[...] = n.pack_in_land[0] + n.pack_in_land[1] + n.pack_in_land[2] + n.pack_in_land[3]
-    if own:
-        pack_cp = remote(n.pack_mine, n.pack_x, n.px_s.at[0], n.px_r.at[0], place.pair)
-        pack_cp.start()
-        scatters[2].steps()
+    if own:
         pack_cp.wait_recv()
         pack_cp.wait_send()
         n.pack_mine[...] = n.pack_mine[...] + n.pack_x[...]
@@ -1123,27 +1224,21 @@
             cp = remote(n.pack_mine, n.pack_z.at[place.zi], n.pz_s.at[j], n.pz_r.at[j], (place.ahead(j), place.t))
             cp.start()
             packs.append(cp)
-    for half, out in zip(halves, (n.grad_latent, n.grad_skip)):
-        for k in range(CHUNKS):
-            sl, total = half.chunk(k)
-            out[sl, :] = total
-        half.sent()
-        if own and out is n.grad_latent:
-            scatters[3].steps()
-            lows.arrived()
-            low_all = jnp.concatenate([n.low_land[i] for i in range(dp)], axis=0)
-            n.shift_grad[...] = dot_tn(n.silu[...], low_all.astype(BF16))
-            n.shift_bias[...] = jnp.sum(low_all, axis=0, keepdims=True)
-            for cp in packs:
-                cp.wait_recv()
-                cp.wait_send()
-            total = n.pack_z[0]
-            for i in range(1, place.line):
-                total = total + n.pack_z[i]
-            n.pack_mine[...] = total
-    if not own:
-        n.shift_grad[...] = n.low_out[...]
-        n.shift_bias[...] = n.low_out[...]
+        scatters[2].steps()
+    n.need("joined0", "joined1")
+    k_all = n.krecv[...].reshape(4 * rows, cols)
+    count = n.grad_skip_w.shape[0] // 2
+    for h, joined in enumerate((n.joined0, n.joined1)):
+        n.grad_skip_w[pl.ds(h * count, count)] = (
+            dot_tn(joined[...], k_all).astype(BF16).reshape((count,) + n.grad_skip_w.shape[1:])
+        )
+    if own:
+        scatters[3].steps()
+        scatter(n.grad_skip_w, n.skip_bufs)
+        for cp in packs:
+            cp.wait_recv()
+            cp.wait_send()
+        n.pack_mine[...] = sum(n.pack_z[i] for i in range(place.line))
     n.pack_t[t] = n.pack_mine[...]
     ends = []
     for o in (1, 2, 3):
@@ -1152,20 +1247,63 @@
         ends.append(cp)
     if own:
         scatters[4].steps()
+        lows.arrived()
+        low_all = jnp.concatenate([n.low_land[i] for i in range(dp)], axis=0)
+        n.shift_grad[...] = dot_tn(n.silu[...], low_all.astype(BF16))
+        n.shift_bias[...] = jnp.sum(low_all, axis=0, keepdims=True)
+        n.out_mine[...] = scatters[0].result()
+        for i in range(3):
+            n.project_mine[i] = scatters[1 + i].result()
+    else:
+        n.shift_grad[...] = n.low_out[...]
+        n.shift_bias[...] = n.low_out[...]
+    for half, out in zip(halves, (n.grad_latent, n.grad_skip)):
+        for k in range(CHUNKS):
+            sl, total = half.chunk(k)
+            out[sl, :] = total
+        half.sent()
+        n.done("grad_latent" if out is n.grad_latent else "grad_skip")
     for cp in ends:
         cp.wait_recv()
         cp.wait_send()
     n.pack_out[...] = n.pack_t[...]
     if own:
-        n.out_mine[...] = scatters[0].result()
-        for i in range(3):
-            n.project_mine[i] = scatters[1 + i].result()
         n.skip_mine[...] = scatters[4].result()
         for s in scatters:
             s.sent()
         lows.sent()
     for cp in copies + tiles + shares:
         cp.wait_send()
+
+
+def finish_body(cols, hidden, n):
+    pairs = [(n.block_out, n.o_block), (n.grad_latent, n.o_latent), (n.grad_skip, n.o_skip), (n.skip_mine, n.o_skip_mine),
+             (n.shift_grad, n.o_shift), (n.up_mine, n.o_up)]
+    r = n.o_query.shape[0]
+    for source, out in pairs:
+        out[...] = source[...]
+    n.o_query[...] = n.query_mine[pl.ds(n.query_mine.shape[0] - r if n.query_mine.shape[0] == r else r, r), :]
+    n.o_text[...] = n.text_part[pl.ds(0, n.o_text.shape[0]), :]
+    row = lambda i: n.pack[i // PACK_ROWS, pl.ds(i % PACK_ROWS, 1), :]
+    for out, places in ((n.norm_gain, (0, 1, 5, 6)), (n.norm_bias, (2, 3, 7, 8)), (n.row_bias, (9, 10, 11))):
+        for i, at in enumerate(places):
+            out[pl.ds(i, 1), :] = row(at)
+    n.row_bias[pl.ds(3, 1), :] = n.shift_bias[...]
+    packed = row(12)
+    for k, out in enumerate((n.head_gain, n.head_bias)):
+        for i in range(4):
+            at = (4 * k + i) * LANES
+            out[pl.ds(i, 1), :] = exact(packed[:, at : at + LANES], n.unfold[...])
+    width = packed.shape[1]
+    for s in range(4):
+        at = PACK_SUMS + 4 * s
+        columns = row(at)
+        for i in range(4):
+            n.column_bias[pl.ds(i, 1), pl.ds(s * cols, cols)] = columns[:, i * cols : (i + 1) * cols]
+        for i, start in enumerate(range(0, hidden, width)):
+            count = min(width, hidden - start)
+            n.hidden_bias[:, pl.ds(s * hidden + start, count)] = row(at + 1 + i)[:, :count]
+    n.column_bias[pl.ds(4, 1), :] = row(4)
 
 
 def fold_matrix(heads, size):
@@ -1205,15 +1343,6 @@
     fold = jnp.asarray(fold_np, BF16)
     one_np = fold_np[:size, :LANES]
     mask = jnp.asarray(one_np.sum(0, keepdims=True), F32)
-    exact = functools.partial(jnp.dot, precision=lax.Precision.HIGHEST)
-    gain_wide, offset_wide = exact(head_gain, jnp.asarray(one_np)), exact(head_bias, jnp.asarray(one_np))
-    bias_cols = lax.dynamic_slice_in_dim(column_bias, t * cols, cols, 1)
-    bias_wide = exact(bias_cols, jnp.asarray(fold_np))
-    zero_wide = jnp.zeros((1, span), F32)
-    self_bias = jnp.stack([bias_wide[0:1], zero_wide, bias_wide[1:2]])
-    text_bias = jnp.stack([zero_wide, bias_wide[3:4]])
-    hidden_cols_bias = lax.dynamic_slice_in_dim(hidden_bias, t * hidden, hidden, 0)[None]
-
     quarter = size // 4
     lane_np = np.zeros((2, LANES), np.float32)
     sign_np = np.zeros((1, LANES), np.float32)
@@ -1222,10 +1351,8 @@
         for half in range(2):
             lane_np[i // quarter, half * (LANES // 2) + i] = f
             sign_np[0, half * (LANES // 2) + i] = 2 * half - 1
-    place = positions.astype(F32)
-    angles = place[0][:, None] * lane_np[0] + place[1][:, None] * lane_np[1]
-    cosine = jnp.cos(angles) * mask
-    sine = jnp.sin(angles) * sign_np
+    lanes_in = jnp.asarray(np.concatenate([lane_np, sign_np]))
+    one = jnp.asarray(one_np)
 
     project_in = jnp.transpose(self_project, (1, 0, 2))
     shards = [self_output.T, cross_query, cross_output.T, cross_keyval[:, 0], cross_keyval[:, 1], hidden_up, hidden_down.T]
@@ -1246,6 +1373,8 @@
         skip_in = lax.all_gather(skip_proj, "dp", axis=0, tiled=True)
         project_in = lax.all_gather(project_in, "dp", axis=1, tiled=True)
         shards = [lax.all_gather(v, "dp", axis=0, tiled=True) for v in shards]
+    early_rows = 128 if own else r
+    down_parts = [shards[6][:early_rows], shards[6][early_rows:]] if own else [shards[6], shards[6]]
     full = shaped((group, width), BF16)
     mine = shaped((rows, width), F32)
     mine_low = shaped((rows, width), BF16)
@@ -1256,10 +1385,10 @@
         "first", 0, functools.partial(first_body, dp, own, size, scale, heads, block),
         dict(
             latent=latent, skip_states=skip_states, skip_in=skip_in, project_in=project_in, out_in=shards[0],
-            query_in=shards[1], key_in=shards[3], value_in=shards[4], down_in=shards[6],
-            small=small, shift_in=shift_in, bias_skip=bias_cols[4:5], self_bias=self_bias, cosine=cosine, sine=sine,
-            norm_gain=norm_gain, norm_bias=norm_bias, row_bias=row_bias, head_gain=gain_wide, head_bias=offset_wide,
-            mask=mask, fold=fold,
+            query_in=shards[1], cross_out_in=shards[2], key_in=shards[3], value_in=shards[4], down_in=down_parts[0],
+            small=small, shift_in=shift_in, column_bias=column_bias, positions=positions.T.astype(F32), lanes=lanes_in,
+            norm_gain=norm_gain, norm_bias=norm_bias, row_bias=row_bias, head_gain=head_gain, head_bias=head_bias,
+            one=one, fold_f32=jnp.asarray(fold_np), mask=mask, fold=fold,
         ),
         dict(
             joined0=full, joined1=full, skip_full=shaped(few(dp, skip_proj.shape[0], cols), BF16), skipped=mine_low,
@@ -1268,36 +1397,38 @@
             low=shaped((group, 3 * span), BF16), mixed=shaped((group, cols), BF16), lse=lse_shape,
             out_land=shaped(few(dp, r, cols), BF16), query_g=shaped(few(dp, r, cols), BF16),
             key_g=shaped(few(dp, text_share, cols), BF16), value_g=shaped(few(dp, text_share, cols), BF16),
-            down_g=shaped(few(dp, r, hidden), BF16), third_all=full, second=mine,
+            cross_out_g=shaped(few(dp, r, cols), BF16), down_g=shaped(few(dp, early_rows, hidden), BF16), third_all=full, second=mine,
+            gain_wide=shaped((4, LANES), F32), offset_wide=shaped((4, LANES), F32), bias_wide=shaped((column_bias.shape[0], span), F32),
+            cosine=shaped((group, LANES), F32), sine=shaped((group, LANES), F32),
         ),
         dict(
             p_land=vm(few(dp, 3, r, cols), BF16), padded=vm((group, span), BF16), skip_send=vm((4, rows, cols), BF16),
             skip_recv=vm((4, rows, cols), BF16), small_land=vm(small.shape, F32), shift_part=vm((dp, 1, width), F32),
-            shift_land=vm((dp, 1, width), F32), sum=sum_scratch, own_sem=dma((9,)), a_s=dma((dp,)),
+            shift_land=vm((dp, 1, width), F32), sum=sum_scratch, own_sem=dma((10,)), a_s=dma((dp,)),
             a_r=dma((dp,)), b_s=dma((dp,)), b_r=dma((dp,)), p_s=dma((4,)), p_r=dma((4,)), gather_sems=Gathers.scratch(13, line),
             spread0=RowSpread.scratch(1),
             spread1=RowSpread.scratch(1), spread2=RowSpread.scratch(), spread3=RowSpread.scratch(),
         ),
-        hbm=("latent", "skip_states", "query_in", "key_in", "value_in", "down_in", "query_g", "key_g", "value_g", "down_g")
-        + (("skip_in", "project_in", "out_in") if own else ()),
-    )
-    if own:
-        silu, counted = first.silu, first.counted[0, 0]
+        hbm=("latent", "skip_states", "query_in", "cross_out_in", "key_in", "value_in", "down_in",
+             "query_g", "cross_out_g", "key_g", "value_g", "down_g") + (("skip_in", "project_in", "out_in") if own else ()),
+        early=("cosine", "sine", "joined0", "joined1", "skip_full", "skipped", "residual", "first_all", "project_wide", "pre", "low", "mixed", "second"),
+    )
+    if own:
+        silu, counted = first.silu, first.counted
         skip_full = first.skip_full.reshape(2 * width, cols)
-        out_t, query = [v.reshape(width, cols) for v in (first.out_land, first.query_g)]
+        out_t, query, cross_out_t = [v.reshape(width, cols) for v in (first.out_land, first.query_g, first.cross_out_g)]
         key, value = [v.reshape(text_width, cols) for v in (first.key_g, first.value_g)]
-        down_t = first.down_g.reshape(width, hidden)
     else:
-        counted, skip_full = jnp.sum(small_all[:, width]), skip_in
+        counted, skip_full = jnp.full((1, LANES), jnp.sum(small_all[:, width])), skip_in
         out_t, query, cross_out_t, key, value, up_full, down_t = shards
 
     text = jnp.pad(text_states[0], ((0, text_pad - text_len), (0, 0)))
     cross = named_kernel(
         "cross", 1, functools.partial(cross_body, dp, own, size, scale, heads, block, text_len),
         dict(
-            third_all=first.third_all, query=query, key=key, value=value, cross_out=shards[2], up_in=shards[5], text=text,
-            text_bias=text_bias, query_bias=bias_wide[2:3], cosine=cosine, sine=sine, norm_gain=norm_gain,
-            norm_bias=norm_bias, row_bias=row_bias, head_gain=gain_wide, head_bias=offset_wide, mask=mask, fold=fold,
+            third_all=first.third_all, query=query, key=key, value=value, cross_out=cross_out_t, up_in=shards[5], down_in=down_parts[1], text=text,
+            bias_wide=first.bias_wide, cosine=first.cosine, sine=first.sine, norm_gain=norm_gain,
+            norm_bias=norm_bias, row_bias=row_bias, head_gain=first.gain_wide, head_bias=first.offset_wide, mask=mask, fold=fold,
             second=first.second,
         ),
         dict(
@@ -1305,37 +1436,44 @@
             text_pre=shaped((text_pad, span), F32), text_low=shaped((text_pad, 2 * span), BF16),
             pre=shaped((group, span), F32), low=shaped((group, span), BF16), mixed=shaped((group, cols), BF16),
             lse=lse_shape, fourth_all=full, third_sum=mine,
-            cross_out_land=shaped(few(dp, r, cols), BF16), up_g=shaped(few(dp, r, hidden), BF16),
+            up_g=shaped(few(dp, r, hidden), BF16), down_g=shaped(few(dp, r - early_rows, hidden), BF16),
         ),
         dict(
             padded=vm((group, span), BF16), sum=sum_scratch, spread=RowSpread.scratch(),
             gather_sems=Gathers.scratch(5, line), own_sem=dma((2,)),
         ),
-        hbm=("up_in", "up_g") + (("cross_out",) if own else ()),
-    )
-    if own:
-        cross_out_t, up_full = cross.cross_out_land.reshape(width, cols), cross.up_g.reshape(width, hidden)
-
-    row_ids = t * rows + jnp.arange(rows)
-    weight = loss_mask.astype(F32) * (row_ids < true_counts[0]).astype(F32)
-    loss_scale = dp * group / counted
+        hbm=("up_in", "up_g", "down_in", "down_g"),
+        late=("query", "key", "value", "text", "third_all", "cosine", "sine", "cross_out", "second"),
+        early=("query_wide", "keyval_wide", "pre", "low", "mixed"),
+    )
+    if own:
+        up_full = cross.up_g.reshape(width, hidden)
+        down_ins = dict(down_a=first.down_g, down_b=cross.down_g)
+        down_scratch = dict(down_t=vm((dp, r, hidden), BF16), down_sem=dma((2,)))
+    else:
+        down_ins, down_scratch = dict(down_t=down_t), {}
+
     feed = named_kernel(
-        "feed", 2, feed_body,
-        dict(
-            fourth_all=cross.fourth_all, up=up_full, hidden_bias=hidden_cols_bias, down_t=down_t, third_sum=cross.third_sum,
-            row_bias=row_bias, teacher=teacher, weight=(loss_scale * weight)[:, None],
+        "feed", 2, functools.partial(feed_body, own),
+        dict(
+            fourth_all=cross.fourth_all, up=up_full, hidden_bias=hidden_bias[None], **down_ins, third_sum=cross.third_sum,
+            row_bias=row_bias, teacher=teacher, loss_mask=loss_mask[:, None], true_count=true_counts[:, None],
+            counted=counted, total=jnp.full((1, 1), dp * group, F32),
         ),
         dict(
             active=shaped((group, hidden), BF16), slope=shaped((group, hidden), BF16), grad_all=full, block_out=mine_low,
             grad_final=mine, bias_mlp=line_sum,
         ),
-        dict(sum=sum_scratch, spread=RowSpread.scratch()),
+        dict(sum=sum_scratch, spread=RowSpread.scratch(), **down_scratch),
+        hbm=("down_a", "down_b"),
+        late=("fourth_all", "up", "third_sum", "teacher"),
+        early=("active", "slope", "block_out", "grad_final"),
     )
 
     back = named_kernel(
         "feed_back", 3, functools.partial(feed_back_body, dp, own),
         dict(
-            grad_all=feed.grad_all, slope=feed.slope, active=feed.active, down_t=down_t, up=up_full,
+            grad_all=feed.grad_all, slope=feed.slope, active=feed.active, **down_ins, up=up_full,
             fourth_all=cross.fourth_all, third_sum=cross.third_sum, gain=norm_gain[3:4], grad_final=feed.grad_final,
         ),
         dict(
@@ -1344,9 +1482,12 @@
             **(dict(down_mine=shaped((r, hidden), F32)) if own else dict(grad_down=shaped((1, width, hidden), BF16))),
         ),
         dict(
-            upper=vm((group, hidden), BF16), sum=sum_scratch, spread=RowSpread.scratch(),
+            upper=vm((group, hidden), BF16), sum=sum_scratch, spread=RowSpread.scratch(), **down_scratch,
             **(dict(grad_down=vm((dp, r, hidden), BF16), down_bufs=GradScatter.buffers((r, hidden)), down_sems=GradScatter.scratch()) if own else {}),
         ),
+        hbm=("down_a", "down_b"),
+        late=("grad_all", "active", "slope", "up", "fourth_all", "third_sum", "grad_final"),
+        early=("grad_up",),
     )
     bias_cross_out, gain_fourth, offset_fourth = back.sum0, back.sum1, back.sum2
 
@@ -1355,7 +1496,7 @@
         "cross_back", 4, functools.partial(cross_back_body, dp, own, size, scale, heads, block, text_len),
         dict(
             c_all=back.c_all, cross_out=cross_out_t, pre=cross.pre, low=cross.low, text_pre=cross.text_pre,
-            text_low=cross.text_low, lse=cross.lse, cosine=cosine, sine=sine, head_gain=gain_wide, mask=mask, fold=fold,
+            text_low=cross.text_low, lse=cross.lse, cosine=first.cosine, sine=first.sine, head_gain=first.gain_wide, mask=mask, fold=fold,
             mixed=cross.mixed, third_all=first.third_all, text=text, keyval_wide=cross.keyval_wide,
             query_wide=cross.query_wide, second=first.second, gain=norm_gain[2:3], grad_third=back.grad_third,
             **(dict(grad_up=back.grad_up) if own else {}),
@@ -1372,6 +1513,9 @@
             **(dict(up_bufs=GradScatter.buffers((r, hidden)), up_sems=GradScatter.scratch()) if own else {}),
         ),
         hbm=("grad_up",),
+        late=("c_all", "cross_out", "low", "text_low", "pre", "cosine", "sine", "query_wide", "text_pre", "mixed", "third_all",
+              "text", "keyval_wide", "second", "grad_third"),
+        early=("grads",),
     )
     few_grads = cback.grads
     if not own:
@@ -1389,8 +1533,8 @@
         "self_back", 6, functools.partial(self_back_body, dp, own, size, scale, heads, block),
         dict(
             text_part=cback.grad_text, **(dict(few_grads=few_grads) if own else {}),
-            s_all=cback.s_all, out_t=out_t, pre=first.pre, low=first.low, lse=first.lse, cosine=cosine, sine=sine,
-            head_gain=gain_wide, mask=mask, fold=fold, mixed=first.mixed, first_all=first.first_all,
+            s_all=cback.s_all, out_t=out_t, pre=first.pre, low=first.low, lse=first.lse, cosine=first.cosine, sine=first.sine,
+            head_gain=first.gain_wide, mask=mask, fold=fold, mixed=first.mixed, first_all=first.first_all,
         ),
         dict(
             p=shaped((group, 3 * span), BF16), grad_out=shaped((parts, width // parts, cols), BF16),
@@ -1407,25 +1551,12 @@
             **(dict(few_bufs=GradScatter.buffers((few_rows, cols)), few_sems=GradScatter.scratch()) if own else {}),
         ),
         hbm=("few_grads",),
-    )
-    grad_text = sback.grad_text[:text_len][None]
+        late=("s_all", "out_t", "low", "pre", "cosine", "sine", "mixed", "first_all"),
+        early=("p", "grad_out", "grad_project"),
+    )
     if own:
         few_mine = sback.few_mine
 
-    head_part = jnp.concatenate([sback.gains, cback.gains, sback.offsets, cback.offsets], axis=0).reshape(1, -1)
-    column_rows = exact(
-        jnp.concatenate([sback.sums[:, :span], sback.sums[:, 2 * span :], cback.sums, cback.text_sums], axis=0),
-        jnp.asarray(fold_np.T),
-    )
-    own_cols = jnp.concatenate([column_rows.reshape(-1), back.bias_hidden[0]])
-    col_rows = (4 * PACK_ROWS - PACK_SUMS) // 4
-    own_cols = jnp.pad(own_cols, (0, col_rows * width - own_cols.shape[0])).reshape(1, col_rows, width)
-    placed = jnp.where(jnp.arange(tensor)[:, None, None] == t, own_cols, 0.0).reshape(tensor * col_rows, width)
-    pack_in = jnp.concatenate(
-        [jnp.zeros((5, width), F32), cback.sum1, gain_fourth, cback.sum2, offset_fourth, cback.sum0, bias_cross_out,
-         feed.bias_mlp, jnp.pad(head_part, ((0, 0), (0, width - head_part.shape[1]))),
-         jnp.zeros((PACK_SUMS - 13, width), F32), placed], axis=0
-    ).reshape(4, PACK_ROWS, width)
     skip_rows = 2 * width // dp if own else width
     pack_land = vm((4, PACK_ROWS, width), F32)
     last = named_kernel(
@@ -1433,7 +1564,11 @@
         dict(
             p=sback.p, project_wide=first.project_wide, residual=first.residual, grad_second=cback.grad_second,
             skipped=first.skipped, norm_gain=norm_gain, skip_w=skip_full, joined0=first.joined0, joined1=first.joined1,
-            silu=silu, pack_in=pack_in, grad_out=sback.grad_out, grad_project=sback.grad_project,
+            silu=silu, gain_third=cback.sum1, gain_fourth=gain_fourth, offset_third=cback.sum2, offset_fourth=offset_fourth,
+            bias_attn=cback.sum0, bias_cross_out=bias_cross_out, bias_mlp=feed.bias_mlp, self_gains=sback.gains,
+            cross_gains=cback.gains, self_offsets=sback.offsets, cross_offsets=cback.offsets, self_sums=sback.sums,
+            cross_sums=cback.sums, text_sums=cback.text_sums, bias_hidden=back.bias_hidden, unfold=jnp.asarray(fold_np.T),
+            grad_out=sback.grad_out, grad_project=sback.grad_project,
         ),
         dict(
             grad_latent=mine, grad_skip=mine, shift_grad=shaped((r if own else 1, width), F32), shift_bias=line_sum,
@@ -1455,6 +1590,8 @@
             ) if own else {}),
         ),
         hbm=("grad_out", "grad_project"),
+        late=("p", "project_wide", "residual", "grad_second", "skipped", "skip_w", "joined0", "joined1"),
+        early=("grad_latent", "grad_skip"),
     )
     if own:
         out_mine, project_mine, skip_mine = last.out_mine, last.project_mine, last.skip_mine
@@ -1467,32 +1604,43 @@
         out_mine = lax.psum_scatter(sback.grad_out[0], "dp", scatter_dimension=0, tiled=True).astype(F32)
         project_mine = lax.psum_scatter(sback.grad_project[0], "dp", scatter_dimension=1, tiled=True).astype(F32)
         skip_mine = lax.psum_scatter(last.grad_skip_w.reshape(-1, cols), "dp", scatter_dimension=0, tiled=True).astype(F32)
-    pack_sum = pack_sum.reshape(4 * PACK_ROWS, width)
-    cols_all = pack_sum[PACK_SUMS:].reshape(tensor, -1)
-    column_sums = jnp.transpose(cols_all[:, : 4 * cols].reshape(tensor, 4, cols), (1, 0, 2)).reshape(4, width)
-    hidden_sums = cols_all[:, 4 * cols : 4 * cols + hidden].reshape(-1)
-    head_sums = exact(pack_sum[12, : 8 * LANES].reshape(8, LANES), jnp.asarray(one_np.T))
+    end = named_kernel(
+        "finish", None, functools.partial(finish_body, cols, hidden),
+        dict(
+            pack=pack_sum, shift_bias=shift_bias, unfold=jnp.asarray(one_np.T), block_out=feed.block_out,
+            grad_latent=last.grad_latent, grad_skip=last.grad_skip, skip_mine=skip_mine, shift_grad=shift_grad,
+            up_mine=up_mine, query_mine=few_mine[r : 2 * r] if not own else few_mine, text_part=sback.grad_text,
+        ),
+        dict(
+            norm_gain=shaped(norm_gain.shape, F32), norm_bias=shaped(norm_bias.shape, F32), head_gain=shaped(head_gain.shape, F32),
+            head_bias=shaped(head_bias.shape, F32), column_bias=shaped(column_bias.shape, F32), hidden_bias=shaped((1, 4 * hidden), F32),
+            row_bias=shaped(row_bias.shape, F32), o_block=mine_low, o_latent=mine, o_skip=mine, o_skip_mine=shaped(skip_mine.shape, F32),
+            o_shift=shaped(shift_grad.shape, F32), o_up=shaped(up_mine.shape, F32), o_query=shaped((r, cols), F32),
+            o_text=shaped((text_len, text_width), F32),
+        ),
+        {},
+    )
     return (
-        feed.block_out,
-        last.grad_latent,
-        last.grad_skip,
-        grad_text,
-        skip_mine,
-        shift_grad,
+        end.o_block,
+        end.o_latent,
+        end.o_skip,
+        end.o_text[None],
+        end.o_skip_mine,
+        end.o_shift,
         jnp.transpose(project_mine, (1, 0, 2)),
         out_mine.T,
-        few_mine[r : 2 * r],
+        end.o_query,
         jnp.transpose(few_mine[2 * r :].reshape(2, text_share, cols), (1, 0, 2)),
         few_mine[:r].T,
-        up_mine,
+        end.o_up,
         down_mine.T,
-        jnp.concatenate([pack_sum[0:2], pack_sum[5:7]]),
-        jnp.concatenate([pack_sum[2:4], pack_sum[7:9]]),
-        head_sums[:4],
-        head_sums[4:],
-        jnp.concatenate([column_sums, pack_sum[4:5]]),
-        hidden_sums,
-        jnp.concatenate([pack_sum[9:12], shift_bias]),
+        end.norm_gain,
+        end.norm_bias,
+        end.head_gain,
+        end.head_bias,
+        end.column_bias,
+        end.hidden_bias[0],
+        end.row_bias,
     )
 
 

time: 743 us -> 639 us (0.86)
  Pallas kernels: 688 us -> 611 us
  local copies, waits for them, and re-layouts: 31.2 us -> 17.3 us
    pallas_call x7 -> x8, Pallas kernels: 688 us -> 611 us  [named_kernel(): pl.pallas_call(kernel, out_shape=list(outs.values()), in_specs=[anywhere...]
where the time goes in v4:
time: 639 us; the launch traced here: 631 us
  Pallas kernels  611 us (96%)
  local copies, waits for them, and re-layouts  17.3 us (3%)
    pallas_call x8, Pallas kernels, named_kernel(): pl.pallas_call(kernel, out_shape=list(outs.values()), in_specs=[anywhere...  611 us

profile of v4, /device:TPU:0, one launch (start us, length us, event | category | flops | bytes accessed | tf_op | source)
XLA Modules:
  0.0 631.1 jit_solution(4037176794053559608)
XLA Ops:
  0.7 0.0 copy-start.5
  0.7 0.0 copy-start.4
  1.4 0.7 reduce
  2.1 0.1 reshape.69
  2.3 0.6 broadcast_in_dim.22.refs_10_
  2.9 0.7 convert_element_type.14
  3.6 1.4 fusion.1
  5.0 1.5 copy.59.refs_8_
  6.5 1.6 slice.33.refs_6_
  8.0 0.9 fusion
  9.0 0.8 copy.63
  9.7 0.8 copy.62
  10.5 0.8 slice.32.refs_9_
  11.3 1.0 copy.58
  12.3 0.9 pad.14.refs_7_.refs_14_
  13.2 175.0 %first.1 = (bf16[1024,1408]{1,0:T(8,128)(2,1)}, bf16[1024,1408]{1,0:T(8,128)(2,1)}, bf16[8,352,352]{2,1,0:T(8,128)(2,1)}, bf16[256,1408]{1,0:T(8,128)(2,1)}, f32...) custom-call(bf16[256,1408]{1,0:T(8,128)(2,1)} %refs_0_.1, ...), custom_call_target="tpu_custom_call" | custom-call | tf_op jit(solution)/shard_map/first/pallas_call | solution.py:402
  188.2 85.1 %cross.1 = (bf16[1408,512]{1,0:T(8,128)(2,1)}, bf16[2,1024,512]{2,1,0:T(8,128)(2,1)}, f32[336,512]{1,0:T(8,128)}, bf16[336,1024]{1,0:T(8,128)(2,1)}, f32[1024,51...) custom-call(bf16[1024,1408]{1,0:T(8,128)(2,1)} %get-tuple-element.11, ...), custom_call_target="tpu_custom_call" | custom-call | tf_op jit(solution)/shard_map/cross/pallas_call | solution.py:402
  273.4 47.6 %feed.1 = (bf16[1024,1536]{1,0:T(8,128)(2,1)}, bf16[1024,1536]{1,0:T(8,128)(2,1)}, bf16[1024,1408]{1,0:T(8,128)(2,1)}, bf16[256,1408]{1,0:T(8,128)(2,1)}, f32[256,1408]{1,0:T(8,128)}, /*index=5*/f32[1,1408]{1,0:T(1,128)}) custom-call(bf16[1024,1408]{1,0:T(8,128)(2,1)} %get-tuple-element.126.refs_0_.refs_6_, bf16[1408,1536]{1,0:T(8,128)(2,1)} %bitcast.29, ...), custom_call_target="tpu_custom_call" | custom-call | tf_op jit(solution)/shard_map/feed/pallas_call | solution.py:402
  320.9 74.4 %feed_back.1 = (bf16[1024,1408]{1,0:T(8,128)(2,1)}, f32[256,1408]{1,0:T(8,128)}, f32[1,1408]{1,0:T(1,128)}, f32[1,1408]{1,0:T(1,128)}, f32[1,1408]{1,0:T(1,128)}...) custom-call(bf16[1024,1408]{1,0:T(8,128)(2,1)} %get-tuple-element.132.refs_0_, ...), custom_call_target="tpu_custom_call" | custom-call | tf_op jit(solution)/shard_map/feed_back/pallas_call | solution.py:402
  395.3 65.7 %cross_back.1 = (bf16[8,608,352]{2,1,0:T(8,128)(2,1)}, bf16[336,1024]{1,0:T(8,128)(2,1)}, f32[2,128]{1,0:T(2,128)}, f32[2,128]{1,0:T(2,128)}, f32[1,512]{1,0:T(1...) custom-call(bf16[1024,1408]{1,0:T(8,128)(2,1)} %get-tuple-element.13, ...), custom_call_target="tpu_custom_call" | custom-call | tf_op jit(solution)/shard_map/cross_back/pallas_call | solution.py:402
  461.0 57.5 %self_back.1 = (bf16[1024,1536]{1,0:T(8,128)(2,1)}, bf16[8,176,352]{2,1,0:T(8,128)(2,1)}, bf16[8,3,176,352]{3,2,1,0:T(8,128)(2,1)}, f32[2,128]{1,0:T(2,128)}, f3...) custom-call(bf16[336,1024]{1,0:T(8,128)(2,1)} %get-tuple-element.147.refs_0_, ...), custom_call_target="tpu_custom_call" | custom-call | tf_op jit(solution)/shard_map/self_back/pallas_call | solution.py:402
  518.5 98.1 %last.1 = (f32[256,1408]{1,0:T(8,128)}, f32[256,1408]{1,0:T(8,128)}, f32[176,1408]{1,0:T(8,128)}, f32[1,1408]{1,0:T(1,128)}, f32[4,8,1408]{2,1,0:T(8,128)}, /*in...) custom-call(bf16[1024,1536]{1,0:T(8,128)(2,1)} %get-tuple-element.156.refs_0_, ...), custom_call_target="tpu_custom_call" | custom-call | tf_op jit(solution)/shard_map/last/pallas_call | solution.py:402
  616.6 7.4 %finish.1 = (f32[4,1408]{1,0:T(4,128)}, f32[4,1408]{1,0:T(4,128)}, f32[4,88]{1,0:T(4,128)}, f32[4,88]{1,0:T(4,128)}, f32[5,1408]{1,0:T(8,128)}, /*index=5*/f32[1...) custom-call(f32[4,8,1408]{2,1,0:T(8,128)} %get-tuple-element.182.ref, ...), custom_call_target="tpu_custom_call" | custom-call | tf_op jit(solution)/shard_map/finish/pallas_call | solution.py:402
  624.0 0.0 copy-done
  624.0 0.7 slice_bitcast_fusion
  624.8 0.9 copy.60
  625.7 0.0 copy-done.1
  625.7 2.5 copy.61
  628.2 0.9 copy.68
  629.1 0.2 copy-done.6
  629.3 0.7 copy.69
  630.0 1.0 copy.70
  (12 shorter events, 0.1 us)
Async XLA Ops:
  0.7 9.8 %copy-start.5 = (bf16[1536,176]{0,1:T(8,128)(2,1)S(1)}, bf16[1536,176]{0,1:T(8,128)(2,1)}, u32[]{:S(2)}) copy-start(bf16[1536,176]{0,1:T(8,128)(2,1)} %param.47) | copy-start | bytes 1622020
  0.7 11.6 %copy-start.4 = (bf16[1,333,1024]{2,1,0:T(8,128)(2,1)S(1)}, bf16[1,333,1024]{2,1,0:T(8,128)(2,1)}, u32[]{:S(2)}) copy-start(bf16[1,333,1024]{2,1,0:T(8,128)(2,1)} %param.33) | copy-start | bytes 2045956
  616.6 7.4 %copy-start = (f32[608,352]{1,0:T(8,128)S(1)}, f32[608,352]{1,0:T(8,128)}, u32[]{:S(2)}) copy-start(f32[608,352]{1,0:T(8,128)} %get-tuple-element.190.refs_9_) | copy-start | bytes 2568196
  624.0 1.7 copy-start.1
  625.7 2.5 copy-start.3
  628.2 1.1 copy-start.6
  628.2 1.8 copy-start.2

commit v5 on v4

--- a/solution.py
+++ b/solution.py
@@ -256,34 +256,51 @@
         self.cs, self.cr, self.ys, self.yr = cs, cr, ys, yr
         _, self.t, self.y, self.c, self.sib, self.yp = tensor_place()
 
-    def core(self, i, value):
-        self.csend[i] = value.astype(BF16)
-        cp = remote(self.csend.at[i], self.crecv.at[i], self.cs.at[i], self.cr.at[i], self.sib)
+    def core(self, i, value, k=0):
+        sl = pl.ds(k * value.shape[0], value.shape[0])
+        self.csend[i, sl, :] = value.astype(BF16)
+        at = CHUNKS * i + k
+        cp = remote(self.csend.at[i, sl], self.crecv.at[i, sl], self.cs.at[at], self.cr.at[at], self.sib)
         cp.start()
         return cp
 
     def start(self, product, ready=None, long=False):
         there, here = 2 * (1 - self.y), 2 * self.y
-        first = product(there + 1 - self.c)
-        if ready is not None:
-            ready()
-        self.c0 = self.core(0, first)
-        self.far[...] = product(there + self.c)
-        if not long:
-            self.c1 = self.core(1, product(here + 1 - self.c))
-        self.c0.wait_recv()
-        self.ycs = []
+        rows = self.far.shape[0]
+        ch = rows // CHUNKS
+        part = lambda b, k: product(pl.ds(pl.multiple_of(b * rows + k * ch, ch), ch))
+        self.ycs, self.c0 = [], []
+        if long:
+            for k in range(CHUNKS):
+                sl = pl.ds(k * ch, ch)
+                value = part(there + 1 - self.c, k)
+                if ready is not None and k == 0:
+                    ready()
+                self.c0.append(self.core(0, value, k))
+                self.far[sl, :] = part(there + self.c, k)
+                self.along(k)
+            self.c1 = self.core(1, product(block_rows(here + 1 - self.c, rows)))
+        else:
+            value = product(block_rows(there + 1 - self.c, rows))
+            if ready is not None:
+                ready()
+            for k in range(CHUNKS):
+                self.c0.append(self.core(0, value[k * ch : (k + 1) * ch, :], k))
+            self.far[...] = product(block_rows(there + self.c, rows))
+            self.c1 = self.core(1, product(block_rows(here + 1 - self.c, rows)))
+            for k in range(CHUNKS):
+                self.along(k)
+        self.near[...] = product(block_rows(here + self.c, rows))
+        self.c1.wait_recv()
+
+    def along(self, k):
         ch = self.far.shape[0] // CHUNKS
-        for k in range(CHUNKS):
-            sl = pl.ds(k * ch, ch)
-            self.ysend[sl, :] = (self.far[sl, :] + self.crecv[0, sl, :].astype(F32)).astype(BF16)
-            cp = remote(self.ysend.at[sl], self.yrecv.at[sl], self.ys.at[k], self.yr.at[k], self.yp)
-            cp.start()
-            self.ycs.append(cp)
-        if long:
-            self.c1 = self.core(1, product(here + 1 - self.c))
-        self.near[...] = product(here + self.c)
-        self.c1.wait_recv()
+        sl = pl.ds(k * ch, ch)
+        self.c0[k].wait_recv()
+        self.ysend[sl, :] = (self.far[sl, :] + self.crecv[0, sl, :].astype(F32)).astype(BF16)
+        cp = remote(self.ysend.at[sl], self.yrecv.at[sl], self.ys.at[k], self.yr.at[k], self.yp)
+        cp.start()
+        self.ycs.append(cp)
 
     def chunk(self, k):
         ch = self.far.shape[0] // CHUNKS
@@ -292,7 +309,7 @@
         return sl, self.near[sl, :] + self.crecv[1, sl, :].astype(F32) + self.yrecv[sl, :].astype(F32)
 
     def sent(self):
-        for cp in [self.c0, self.c1] + self.ycs:
+        for cp in self.c0 + [self.c1] + self.ycs:
             cp.wait_send()
 
     @staticmethod
@@ -301,7 +318,7 @@
         vm = pltpu.VMEM
         return [
             vm((rows, width), F32), vm((rows, width), F32), vm((2, rows, width), BF16), vm((2, rows, width), BF16),
-            vm((rows, width), BF16), vm((rows, width), BF16), dma((2,)), dma((2,)), dma((CHUNKS,)), dma((CHUNKS,)),
+            vm((rows, width), BF16), vm((rows, width), BF16), dma((CHUNKS + 1,)), dma((CHUNKS + 1,)), dma((CHUNKS,)), dma((CHUNKS,)),
         ]
 
 
@@ -351,15 +368,31 @@
     return jax.ShapeDtypeStruct(shape, dtype)
 
 
-def named_kernel(name, collective_id, body, ins, outs, scratch, hbm=(), late=(), early=()):
+class Placed:
+    def __init__(self, value, moves):
+        self.value, self.moves = value, moves
+
+
+def hbm(value):
+    return Placed(value, False)
+
+
+def late(value):
+    return Placed(value, True)
+
+
+def named_kernel(name, collective_id, body, ins, outs, scratch):
     vm, anywhere = pl.BlockSpec(memory_space=pltpu.VMEM), pl.BlockSpec(memory_space=pl.ANY)
     flat = []
     for v in scratch.values():
         flat.extend(v if isinstance(v, list) else [v])
-    buffers = [pltpu.VMEM(ins[k].shape, ins[k].dtype) for k in late] + [pltpu.VMEM(outs[k].shape, outs[k].dtype) for k in early]
-    moved = len(buffers)
-    if moved:
-        buffers.append(pltpu.SemaphoreType.DMA((moved,)))
+    placed = {k: v for k, v in [*ins.items(), *outs.items()] if isinstance(v, Placed)}
+    bare = lambda v: v.value if isinstance(v, Placed) else v
+    specs = lambda group: [anywhere if k in placed else vm for k in group]
+    moving = [k for k, v in placed.items() if v.moves]
+    buffers = [pltpu.VMEM(placed[k].value.shape, placed[k].value.dtype) for k in moving]
+    if moving:
+        buffers.append(pltpu.SemaphoreType.DMA((len(moving),)))
 
     def kernel(*refs):
         left = list(refs)
@@ -372,42 +405,45 @@
             else:
                 setattr(n, k, left.pop(0))
         loads, stores, going = {}, {}, []
-        for i, k in enumerate([*late, *early]):
+        for i, k in enumerate(moving):
+            outer, inner, sem = getattr(n, k), left[i], left[-1].at[i]
             if k in ins:
-                loads[k] = pltpu.make_async_copy(getattr(n, k), left[i], left[-1].at[i])
-                loads[k].start()
+                loads[id(inner)] = pltpu.make_async_copy(outer, inner, sem)
+                loads[id(inner)].start()
             else:
-                stores[k] = pltpu.make_async_copy(left[i], getattr(n, k), left[-1].at[i])
-            setattr(n, k, left[i])
-
-        def need(*names):
-            for k in names:
-                if k in loads:
-                    loads.pop(k).wait()
-
-        def done(*names):
-            for k in names:
-                if k in stores:
-                    going.append(stores.pop(k))
+                stores[id(inner)] = pltpu.make_async_copy(inner, outer, sem)
+            setattr(n, k, inner)
+
+        def need(*wanted):
+            for ref in wanted:
+                if id(ref) in loads:
+                    loads.pop(id(ref)).wait()
+
+        def done(*ready):
+            for ref in ready:
+                if id(ref) in stores:
+                    going.append(stores.pop(id(ref)))
                     going[-1].start()
 
         n.need, n.done = need, done
         body(n)
-        need(*list(loads))
-        done(*list(stores))
-        for cp in going:
+        for cp in loads.values():
             cp.wait()
-
-    talks = {} if collective_id is None else {"collective_id": collective_id, "has_side_effects": True}
+        for cp in stores.values():
+            cp.start()
+        for cp in going + list(stores.values()):
+            cp.wait()
+
+    talks = {} if collective_id is None else dict(collective_id=collective_id, has_side_effects=True)
     got = pl.pallas_call(
         kernel,
-        out_shape=list(outs.values()),
-        in_specs=[anywhere if k in hbm or k in late else vm for k in ins],
-        out_specs=[anywhere if k in hbm or k in early else vm for k in outs],
+        out_shape=[bare(v) for v in outs.values()],
+        in_specs=specs(ins),
+        out_specs=specs(outs),
         scratch_shapes=flat + buffers,
         compiler_params=pltpu.CompilerParams(vmem_limit_bytes=VMEM_BYTES, **talks),
         name=name,
-    )(*ins.values())
+    )(*[bare(v) for v in ins.values()])
     return SimpleNamespace(**dict(zip(outs, got)))
 
 
@@ -553,10 +589,13 @@
     n.offset_wide[...] = exact(n.head_bias[...], n.one[...])
     mine = my_cols(n.column_bias[...], t, cols)
     n.bias_wide[...] = exact(mine, n.fold_f32[...])
-    angles = n.positions[:, 0:1] * n.lanes[0:1, :] + n.positions[:, 1:2] * n.lanes[1:2, :]
+    angles = lax.dot_general(
+        n.positions[...].astype(F32), n.lanes[0:2, :], (((0,), (0,)), ((), ())), precision=lax.Precision.HIGHEST,
+        preferred_element_type=F32,
+    )
     n.cosine[...] = jnp.cos(angles) * n.mask[...]
     n.sine[...] = jnp.sin(angles) * n.lanes[2:3, :]
-    n.done("cosine", "sine")
+    n.done(n.cosine, n.sine)
     return mine[4:5, :]
 
 
@@ -576,7 +615,8 @@
     ]
     if own:
         shards = [(n.skip_in, n.skip_full), (n.project_in, n.p_land), (n.out_in, n.out_land), (n.query_in, n.query_g),
-                  (n.key_in, n.key_g), (n.value_in, n.value_g), (n.cross_out_in, n.cross_out_g), (n.down_in, n.down_g)]
+                  (n.keyval_in.at[0], n.key_g), (n.keyval_in.at[1], n.value_g), (n.cross_out_in, n.cross_out_g),
+                  (n.down_in.at[pl.ds(0, n.down_g.shape[1])], n.down_g)]
         kept += [pltpu.make_async_copy(a, b.at[d], n.own_sem.at[2 + i]) for i, (a, b) in enumerate(shards)]
     for cp in kept:
         cp.start()
@@ -586,6 +626,11 @@
         cp.wait()
         spread.send(0, rows)
     if own:
+        count = jnp.broadcast_to(n.true_count[...].astype(F32), (1, LANES))
+        share = n.shift_in.shape[0]
+        for q in range(dp):
+            n.small[q, :, pl.ds(0, share)] = n.condition[:, pl.ds(q * share, share)].astype(F32)
+            n.small[q, :, pl.ds(n.small.shape[2] - LANES, LANES)] = count
         n.small_land[d] = n.small[d]
         smalls = ToAll(place, lambda q: n.small.at[q], n.small_land, n.a_s, n.a_r)
         gathers = Gathers(place, 2, *n.gather_sems)
@@ -608,13 +653,13 @@
     if own:
         gathers.add(n.out_in, n.out_land)
         gathers.add(n.query_in, n.query_g)
-        gathers.add(n.key_in, n.key_g)
-        gathers.add(n.value_in, n.value_g)
+        gathers.add(n.keyval_in.at[0], n.key_g)
+        gathers.add(n.keyval_in.at[1], n.value_g)
         gathers.add(n.cross_out_in, n.cross_out_g)
         gathers.forward()
     spreads[0].finish()
     if own:
-        gathers.add(n.down_in, n.down_g, 3)
+        gathers.add(n.down_in.at[pl.ds(0, n.down_g.shape[1])], n.down_g, 3)
         gathers.arrived(0, 2)
         kept[2].wait()
         half = dp // 2
@@ -668,7 +713,7 @@
     spread.finish()
     for cp in copies:
         cp.wait_send()
-    n.done("joined0", "joined1", "skip_full", "skipped", "residual", "first_all")
+    n.done(n.joined0, n.joined1, n.skip_full, n.skipped, n.residual, n.first_all)
     for part in range(3):
         if own:
             gathers.arrived(2 + part, 3 + part)
@@ -699,7 +744,7 @@
         return 0
 
     lax.fori_loop(0, n.low.shape[0] // block, project, 0)
-    n.done("project_wide", "pre", "low")
+    n.done(n.project_wide, n.pre, n.low)
     if own:
         gathers.forward()
     attend(
@@ -707,7 +752,7 @@
         n.padded, n.lse, heads, scale, block, n.low.shape[0], gathers.forward if own else None,
     )
     n.mixed[...] = dot_nt(n.padded[...], n.fold[...]).astype(BF16)
-    n.done("mixed")
+    n.done(n.mixed)
     if own:
         gathers.arrived(5, 6)
         kept[4].wait()
@@ -715,7 +760,7 @@
     else:
         out_t = lambda: n.out_in[...]
     reduce = TensorSum(*n.sum)
-    reduce.start(lambda b: dot_nt(n.mixed[block_rows(b, rows), :], out_t()))
+    reduce.start(lambda here: dot_nt(n.mixed[here, :], out_t()))
     if own:
         gathers.forward()
     spread = RowSpread(n.third_all, rows, *n.spread3)
@@ -723,7 +768,7 @@
         reduce, spread, n.third_all, n.residual, n.row_bias.at[pl.ds(0, 1)], n.norm_gain.at[pl.ds(2, 1)],
         n.norm_bias.at[pl.ds(2, 1)], n.second, rows,
     )
-    n.done("second")
+    n.done(n.second)
     if own:
         gathers.forward()
     spread.forward()
@@ -751,12 +796,13 @@
     if own:
         gathers = Gathers(place, 2, *n.gather_sems)
         gathers.add(n.up_in, n.up_g, 4)
-        gathers.add(n.down_in, n.down_g)
+        down_in = n.down_in.at[pl.ds(n.down_in.shape[0] - n.down_g.shape[1], n.down_g.shape[1])]
+        gathers.add(down_in, n.down_g)
         kept = [pltpu.make_async_copy(a, b.at[d], n.own_sem.at[i])
-                for i, (a, b) in enumerate(((n.up_in, n.up_g), (n.down_in, n.down_g)))]
+                for i, (a, b) in enumerate(((n.up_in, n.up_g), (down_in, n.down_g)))]
         for cp in kept:
             cp.start()
-    n.need("query", "key", "value", "text")
+    n.need(n.query, n.key, n.value, n.text)
     n.query_wide[...] = dot_nn(n.query[...], n.fold[...]).astype(BF16)
     for part, w in enumerate((n.key, n.value)):
         n.keyval_wide[part] = dot_nn(w[...], n.fold[...]).astype(BF16)
@@ -768,7 +814,7 @@
                 n.text_low[:, head_at(h)] = val.astype(BF16)
         else:
             n.text_low[:, pl.ds(span, span)] = (out + n.bias_wide[pl.ds(3, 1), :]).astype(BF16)
-    n.need("third_all", "cosine", "sine")
+    n.need(n.third_all, n.cosine, n.sine)
 
     def project(i, _):
         here = pl.ds(pl.multiple_of(i * block, block), block)
@@ -780,13 +826,13 @@
         return 0
 
     lax.fori_loop(0, n.low.shape[0] // block, project, 0)
-    n.done("query_wide", "keyval_wide", "pre", "low")
+    n.done(n.query_wide, n.keyval_wide, n.pre, n.low)
     attend(n.low, n.text_low.at[:, pl.ds(0, span)], n.text_low.at[:, pl.ds(span, span)], n.padded, n.lse, heads, scale, block, real)
     n.mixed[...] = dot_nt(n.padded[...], n.fold[...]).astype(BF16)
-    n.need("cross_out", "second")
+    n.need(n.cross_out, n.second)
     reduce = TensorSum(*n.sum)
-    reduce.start(lambda b: dot_nt(n.mixed[block_rows(b, rows), :], n.cross_out[...]))
-    n.done("mixed")
+    reduce.start(lambda here: dot_nt(n.mixed[here, :], n.cross_out[...]))
+    n.done(n.mixed)
     if own:
         gathers.forward(2)
     spread = RowSpread(n.fourth_all, rows, *n.spread)
@@ -828,16 +874,20 @@
     bar = greet((sib, yp))
     down_copies, down_t = load_down(own, n)
     hidden = n.up.shape[1]
-    my_hidden = pl.ds(pl.multiple_of(t * hidden, LANES), hidden)
+    tiles = hidden // LANES
+    mine = sum(jnp.where(t == s, n.hidden_bias[pl.ds(s * tiles, tiles), :], 0.0) for s in range(4))
+    hidden_bias = jnp.concatenate([mine[i : i + 1, :] for i in range(tiles)], axis=1)
     seat = t * rows + lax.broadcasted_iota(jnp.int32, (rows, 1), 0)
-    weight = n.loss_mask[...].astype(F32) * (seat < n.true_count[...]).astype(F32)
+    mask = lax.dot_general(
+        n.loss_mask[...].astype(F32), jnp.ones((1, LANES), F32), (((0,), (0,)), ((), ())), preferred_element_type=F32
+    )[:, 0:1]
+    weight = mask * (seat < n.true_count[...]).astype(F32)
     weight = (n.total[...] / n.counted[:, 0:1]) * weight
-    n.need("fourth_all", "up")
+    n.need(n.fourth_all, n.up)
     root, cube = float(np.sqrt(2.0 / np.pi)), 0.044715
 
-    def product(b):
-        here = block_rows(b, rows)
-        x = dot_nn(n.fourth_all[here, :], n.up[...]) + n.hidden_bias[:, my_hidden]
+    def product(here):
+        x = dot_nn(n.fourth_all[here, :], n.up[...]) + hidden_bias
         square = x * x
         th = jnp.tanh(root * (x + cube * (square * x)))
         cdf = 0.5 * (1.0 + th)
@@ -851,8 +901,8 @@
 
     reduce = TensorSum(*n.sum)
     reduce.start(product, lambda: pl.semaphore_wait(bar, 2), long=True)
-    n.done("active", "slope")
-    n.need("third_sum", "teacher")
+    n.done(n.active, n.slope)
+    n.need(n.third_sum, n.teacher)
     spread = RowSpread(n.grad_all, rows, *n.spread)
     ch = rows // CHUNKS
     sums = None
@@ -867,7 +917,7 @@
         spread.send(k * ch, ch)
         sums = add_sums(sums, [low.astype(F32)])
     n.bias_mlp[...] = sums[0]
-    n.done("block_out", "grad_final")
+    n.done(n.block_out, n.grad_final)
     spread.forward()
     spread.finish()
     reduce.sent()
@@ -880,33 +930,32 @@
     peers = [sib, yp] + (place.near() if own else [])
     bar = greet(peers)
     down_copies, down_t = load_down(own, n)
-    n.need("grad_all", "active")
+    n.need(n.grad_all, n.active)
     n.grad_down[...] = dot_tn(n.grad_all[...], n.active[...]).astype(BF16).reshape(n.grad_down.shape)
     pl.semaphore_wait(bar, len(peers))
     if own:
         down = GradScatter(place, n.grad_down, *n.down_bufs, *n.down_sems)
 
-    def product(b):
-        here = block_rows(b, rows)
+    def product(here):
         upper = (dot_nn(n.grad_all[here, :], down_t()) * n.slope[here, :].astype(F32)).astype(BF16)
         n.upper[here, :] = upper
         return dot_nt(upper, n.up[...])
 
     for cp in down_copies:
         cp.wait()
-    n.need("slope", "up")
+    n.need(n.slope, n.up)
     reduce = TensorSum(*n.sum)
     reduce.start(product, long=True)
-    n.need("fourth_all", "third_sum", "grad_final")
+    n.need(n.fourth_all, n.third_sum, n.grad_final)
     n.bias_hidden[...] = sum(
         jnp.sum(n.upper[pl.ds(b * rows, rows), :].astype(F32), axis=0, keepdims=True) for b in range(4)
     )
     n.grad_up[...] = dot_tn(n.fourth_all[...], n.upper[...]).astype(BF16).reshape(n.grad_up.shape)
-    n.done("grad_up")
+    n.done(n.grad_up)
     spread = RowSpread(n.c_all, rows, *n.spread)
     if own:
         down.steps(1)
-    backward_rows(reduce, spread, n.c_all, n.third_sum, n.gain, n.grad_final, n.grad_third, (n.sum0, n.sum1, n.sum2), rows)
+    backward_rows(reduce, spread, n.c_all, n.third_sum, n.norm_gain.at[pl.ds(3, 1)], n.grad_final, n.grad_third, (n.sum0, n.sum1, n.sum2), rows)
     if own:
         down.steps(2)
     spread.forward()
@@ -939,9 +988,9 @@
     pl.semaphore_wait(bar, len(peers))
     if own:
         up = GradScatter(place, n.grad_up, *n.up_bufs, *n.up_sems)
-    n.need("c_all", "cross_out")
+    n.need(n.c_all, n.cross_out)
     spread_heads(n, n.c_all, n.cross_out, n.do, block)
-    n.need("low", "text_low")
+    n.need(n.low, n.text_low)
     attend_back(
         n.low, n.text_low.at[:, pl.ds(0, span)], n.text_low.at[:, pl.ds(span, span)],
         n.do, n.lse, n.dq, n.dk, n.dv, heads, scale, block, real,
@@ -965,14 +1014,14 @@
 
     if own:
         up.steps(1)
-    n.need("pre", "cosine", "sine")
+    n.need(n.pre, n.cosine, n.sine)
     lax.fori_loop(0, n.p.shape[0] // block, finish, 0)
-    n.need("query_wide")
+    n.need(n.query_wide)
     reduce = TensorSum(*n.sum)
-    reduce.start(lambda b: dot_nt(n.p[block_rows(b, rows), :], n.query_wide[...]))
+    reduce.start(lambda here: dot_nt(n.p[here, :], n.query_wide[...]))
     if own:
         up.steps(2)
-    n.need("text_pre", "mixed", "third_all", "text", "keyval_wide", "second", "grad_third")
+    n.need(n.text_pre, n.mixed, n.third_all, n.text, n.keyval_wide, n.second, n.grad_third)
     for h in range(heads):
         hs = head_at(h)
         grad, g, o = head_back(n.dk[:, hs], n.text_pre[:, hs], n.mask[...], n.head_gain[pl.ds(3, 1), :], size)
@@ -994,14 +1043,14 @@
     for part in range(2):
         narrow = dot_nt(n.text_p[:, pl.ds(part * span, span)], n.fold[...]).astype(BF16)
         at = put(at, dot_tn(n.text[...], narrow))
-    n.done("grads")
+    n.done(n.grads)
     n.grad_text[...] = (
         dot_nt(n.text_p[:, pl.ds(0, span)], n.keyval_wide[0]) + dot_nt(n.text_p[:, pl.ds(span, span)], n.keyval_wide[1])
     ).astype(BF16)
     if own:
         up.steps()
     spread = RowSpread(n.s_all, rows, *n.spread)
-    backward_rows(reduce, spread, n.s_all, n.second, n.gain, n.grad_third, n.grad_second, (n.sum0, n.sum1, n.sum2), rows)
+    backward_rows(reduce, spread, n.s_all, n.second, n.norm_gain.at[pl.ds(2, 1)], n.grad_third, n.grad_second, (n.sum0, n.sum1, n.sum2), rows)
     spread.forward()
     spread.finish()
     reduce.sent()
@@ -1055,16 +1104,16 @@
     text = TextSum(n.text_part, n.text_total, n.text_land, n.text_yland, n.text_back, n.text_sems)
     if own:
         few = GradScatter(place, n.few_grads, *n.few_bufs, *n.few_sems)
-    n.need("s_all", "out_t")
+    n.need(n.s_all, n.out_t)
     spread_heads(n, n.s_all, n.out_t, n.do, block)
     text.along()
-    n.need("low")
+    n.need(n.low)
     attend_back(
         n.low.at[:, pl.ds(0, span)], n.low.at[:, pl.ds(span, span)], n.low.at[:, pl.ds(2 * span, span)],
         n.do, n.lse, n.dq, n.dk, n.dv, heads, scale, block, n.low.shape[0], few.step if own else None,
     )
     text.back()
-    n.need("pre", "cosine", "sine")
+    n.need(n.pre, n.cosine, n.sine)
     n.gains[...] = jnp.zeros(n.gains.shape, F32)
     n.offsets[...] = jnp.zeros(n.offsets.shape, F32)
     n.sums[...] = jnp.zeros(n.sums.shape, F32)
@@ -1092,12 +1141,12 @@
     by_place = lambda v: v.astype(BF16).reshape(n.grad_out.shape)
     if own:
         few.steps()
-    n.done("p")
-    n.need("mixed", "first_all")
+    n.done(n.p)
+    n.need(n.mixed, n.first_all)
     n.grad_out[...] = by_place(dot_tn(n.s_all[...], n.mixed[...]))
     for part in range(3):
         n.grad_project[:, part] = by_place(dot_tn(n.first_all[...], n.p_low[part]))
-    n.done("grad_out", "grad_project")
+    n.done(n.grad_out, n.grad_project)
     text.result(n.grad_text)
     if own:
         n.few_mine[...] = few.result()
@@ -1111,7 +1160,7 @@
     _, t, _, _, _, _ = tensor_place()
     d = lax.axis_index("dp")
     rows, width = n.residual.shape
-    cols = n.krecv.shape[2]
+    cols = n.krecv.shape[1]
     place = DpPlace(dp) if own else None
     peers = [(d, (t + o) % 4) for o in range(1, 4)] + (place.others() if own else [])
     bar = greet(peers)
@@ -1129,17 +1178,16 @@
             for i in range(3):
                 scatter(n.grad_project.at[:, i], n.project_bufs[3 * i : 3 * i + 3])
 
-    def product(b):
-        here = block_rows(b, rows)
+    def product(here):
         span = n.project_wide.shape[2]
         total = dot_nt(n.p[here, pl.ds(0, span)], n.project_wide[0])
         for part in range(1, 3):
             total = total + dot_nt(n.p[here, pl.ds(part * span, span)], n.project_wide[part])
         return total
 
-    n.need("p", "project_wide")
+    n.need(n.p, n.project_wide)
     reduce.start(product, ready)
-    n.need("residual", "grad_second", "skipped")
+    n.need(n.residual, n.grad_second, n.skipped)
     if own:
         scatters[0].steps()
     sums = None
@@ -1155,10 +1203,10 @@
     copies = []
     for o in (2, 3, 1):
         b = (t + o) % 4
-        cp = remote(n.ksend.at[b], n.krecv.at[t], n.k_s.at[o], n.k_r.at[o], (d, b))
+        cp = remote(n.ksend.at[b], n.krecv.at[block_rows(t, rows)], n.k_s.at[o], n.k_r.at[o], (d, b))
         cp.start()
         copies.append(cp)
-    n.krecv[t] = n.ksend[t]
+    n.krecv[block_rows(t, rows), :] = n.ksend[t]
     bias_skip, gain_first, offset_first, gain_skip, offset_skip = sums
     n.tile[...] = offset_first
     n.tile_land[t] = n.tile[...]
@@ -1210,10 +1258,10 @@
         lows = ToAll(place, lambda q: n.low_out, n.low_land, n.l_s, n.l_r)
         pack_cp = remote(n.pack_mine, n.pack_x, n.px_s.at[0], n.px_r.at[0], place.pair)
         pack_cp.start()
-    n.need("skip_w")
+    n.need(n.skip_w)
     halves = [TensorSum(*n.sum), TensorSum(*n.sum1)]
     for h, half in enumerate(halves):
-        half.start(lambda b, h=h: dot_nt(n.krecv[b], n.skip_w[pl.ds(h * width, width), :]))
+        half.start(lambda here, h=h: dot_nt(n.krecv[here, :], n.skip_w[pl.ds(h * width, width), :]))
     if own:
         pack_cp.wait_recv()
         pack_cp.wait_send()
@@ -1225,8 +1273,8 @@
             cp.start()
             packs.append(cp)
         scatters[2].steps()
-    n.need("joined0", "joined1")
-    k_all = n.krecv[...].reshape(4 * rows, cols)
+    n.need(n.joined0, n.joined1)
+    k_all = n.krecv[...]
     count = n.grad_skip_w.shape[0] // 2
     for h, joined in enumerate((n.joined0, n.joined1)):
         n.grad_skip_w[pl.ds(h * count, count)] = (
@@ -1235,6 +1283,7 @@
     if own:
         scatters[3].steps()
         scatter(n.grad_skip_w, n.skip_bufs)
+        scatters[4].steps()
         for cp in packs:
             cp.wait_recv()
             cp.wait_send()
@@ -1246,7 +1295,6 @@
         cp.start()
         ends.append(cp)
     if own:
-        scatters[4].steps()
         lows.arrived()
         low_all = jnp.concatenate([n.low_land[i] for i in range(dp)], axis=0)
         n.shift_grad[...] = dot_tn(n.silu[...], low_all.astype(BF16))
@@ -1262,7 +1310,7 @@
             sl, total = half.chunk(k)
             out[sl, :] = total
         half.sent()
-        n.done("grad_latent" if out is n.grad_latent else "grad_skip")
+        n.done(out)
     for cp in ends:
         cp.wait_recv()
         cp.wait_send()
@@ -1276,13 +1324,17 @@
         cp.wait_send()
 
 
-def finish_body(cols, hidden, n):
-    pairs = [(n.block_out, n.o_block), (n.grad_latent, n.o_latent), (n.grad_skip, n.o_skip), (n.skip_mine, n.o_skip_mine),
+def finish_body(hidden, n):
+    r, cols = n.o_query.shape
+    pairs = [(n.out_mine, n.o_out), (n.down_mine, n.o_down), (n.project_mine, n.o_project), (n.block_out, n.o_block), (n.grad_latent, n.o_latent), (n.grad_skip, n.o_skip), (n.skip_mine, n.o_skip_mine),
              (n.shift_grad, n.o_shift), (n.up_mine, n.o_up)]
-    r = n.o_query.shape[0]
     for source, out in pairs:
         out[...] = source[...]
-    n.o_query[...] = n.query_mine[pl.ds(n.query_mine.shape[0] - r if n.query_mine.shape[0] == r else r, r), :]
+    n.o_query[...] = n.few_mine[pl.ds(r, r), :]
+    n.o_cross_out[...] = n.few_mine[pl.ds(0, r), :]
+    for i in range(2):
+        count = n.o_keyval.shape[2]
+        n.o_keyval[i] = n.few_mine[pl.ds(2 * r + i * count, count), :].T
     n.o_text[...] = n.text_part[pl.ds(0, n.o_text.shape[0]), :]
     row = lambda i: n.pack[i // PACK_ROWS, pl.ds(i % PACK_ROWS, 1), :]
     for out, places in ((n.norm_gain, (0, 1, 5, 6)), (n.norm_bias, (2, 3, 7, 8)), (n.row_bias, (9, 10, 11))):
@@ -1355,12 +1407,9 @@
     one = jnp.asarray(one_np)
 
     project_in = jnp.transpose(self_project, (1, 0, 2))
-    shards = [self_output.T, cross_query, cross_output.T, cross_keyval[:, 0], cross_keyval[:, 1], hidden_up, hidden_down.T]
-    if own:
-        lanes = -(-r // LANES) * LANES
-        slices = jnp.pad(condition.astype(F32).reshape(dp, r), ((0, 0), (0, lanes - r)))
-        slices = jnp.concatenate([slices, jnp.broadcast_to(true_counts.astype(F32)[:, None], (dp, LANES))], axis=1)
-        small = slices[:, None, :]
+    shards = [self_output.T, cross_query, cross_output.T, jnp.transpose(cross_keyval, (1, 0, 2)), hidden_up, hidden_down.T]
+    if own:
+        small_shape = (dp, 1, -(-r // LANES) * LANES + LANES)
         skip_in, shift_in = skip_proj, shift_proj
     else:
         small_all = lax.all_gather(
@@ -1369,12 +1418,11 @@
         silu_all = jax.nn.silu(small_all[:, :width]).astype(BF16)
         silu = lax.dynamic_slice_in_dim(silu_all, d * r, r, 1)
         shift_in = lax.psum_scatter(dot_nn(silu, shift_proj), "dp", scatter_dimension=0, tiled=True) + row_bias[3:4]
-        small = jnp.zeros((1, 8, LANES), F32)
+        small_shape = (1, 8, LANES)
         skip_in = lax.all_gather(skip_proj, "dp", axis=0, tiled=True)
         project_in = lax.all_gather(project_in, "dp", axis=1, tiled=True)
-        shards = [lax.all_gather(v, "dp", axis=0, tiled=True) for v in shards]
+        shards = [lax.all_gather(v, "dp", axis=v.ndim - 2, tiled=True) for v in shards]
     early_rows = 128 if own else r
-    down_parts = [shards[6][:early_rows], shards[6][early_rows:]] if own else [shards[6], shards[6]]
     full = shaped((group, width), BF16)
     mine = shaped((rows, width), F32)
     mine_low = shaped((rows, width), BF16)
@@ -1384,34 +1432,31 @@
     first = named_kernel(
         "first", 0, functools.partial(first_body, dp, own, size, scale, heads, block),
         dict(
-            latent=latent, skip_states=skip_states, skip_in=skip_in, project_in=project_in, out_in=shards[0],
-            query_in=shards[1], cross_out_in=shards[2], key_in=shards[3], value_in=shards[4], down_in=down_parts[0],
-            small=small, shift_in=shift_in, column_bias=column_bias, positions=positions.T.astype(F32), lanes=lanes_in,
+            latent=hbm(latent), skip_states=hbm(skip_states), skip_in=hbm(skip_in) if own else skip_in, project_in=hbm(project_in) if own else project_in, out_in=hbm(shards[0]) if own else shards[0],
+            query_in=hbm(shards[1]), cross_out_in=hbm(shards[2]), keyval_in=hbm(shards[3]), down_in=hbm(shards[5]),
+            condition=condition, true_count=true_counts[:, None], shift_in=shift_in, column_bias=column_bias, positions=positions, lanes=lanes_in,
             norm_gain=norm_gain, norm_bias=norm_bias, row_bias=row_bias, head_gain=head_gain, head_bias=head_bias,
             one=one, fold_f32=jnp.asarray(fold_np), mask=mask, fold=fold,
         ),
         dict(
-            joined0=full, joined1=full, skip_full=shaped(few(dp, skip_proj.shape[0], cols), BF16), skipped=mine_low,
-            residual=mine, first_all=full, silu=shaped(few(dp, r), BF16), counted=shaped((1, LANES), F32),
-            project_wide=shaped((3, width, span), BF16), pre=shaped((group, 2 * span), F32),
-            low=shaped((group, 3 * span), BF16), mixed=shaped((group, cols), BF16), lse=lse_shape,
-            out_land=shaped(few(dp, r, cols), BF16), query_g=shaped(few(dp, r, cols), BF16),
-            key_g=shaped(few(dp, text_share, cols), BF16), value_g=shaped(few(dp, text_share, cols), BF16),
-            cross_out_g=shaped(few(dp, r, cols), BF16), down_g=shaped(few(dp, early_rows, hidden), BF16), third_all=full, second=mine,
+            joined0=late(full), joined1=late(full), skip_full=late(shaped(few(dp, skip_proj.shape[0], cols), BF16)), skipped=late(mine_low),
+            residual=late(mine), first_all=late(full), silu=shaped(few(dp, r), BF16), counted=shaped((1, LANES), F32),
+            project_wide=late(shaped((3, width, span), BF16)), pre=late(shaped((group, 2 * span), F32)),
+            low=late(shaped((group, 3 * span), BF16)), mixed=late(shaped((group, cols), BF16)), lse=lse_shape,
+            out_land=shaped(few(dp, r, cols), BF16), query_g=hbm(shaped(few(dp, r, cols), BF16)),
+            key_g=hbm(shaped(few(dp, text_share, cols), BF16)), value_g=hbm(shaped(few(dp, text_share, cols), BF16)),
+            cross_out_g=hbm(shaped(few(dp, r, cols), BF16)), down_g=hbm(shaped(few(dp, early_rows, hidden), BF16)), third_all=full, second=late(mine),
             gain_wide=shaped((4, LANES), F32), offset_wide=shaped((4, LANES), F32), bias_wide=shaped((column_bias.shape[0], span), F32),
-            cosine=shaped((group, LANES), F32), sine=shaped((group, LANES), F32),
+            cosine=late(shaped((group, LANES), F32)), sine=late(shaped((group, LANES), F32)),
         ),
         dict(
             p_land=vm(few(dp, 3, r, cols), BF16), padded=vm((group, span), BF16), skip_send=vm((4, rows, cols), BF16),
-            skip_recv=vm((4, rows, cols), BF16), small_land=vm(small.shape, F32), shift_part=vm((dp, 1, width), F32),
+            skip_recv=vm((4, rows, cols), BF16), small=vm(small_shape, F32), small_land=vm(small_shape, F32), shift_part=vm((dp, 1, width), F32),
             shift_land=vm((dp, 1, width), F32), sum=sum_scratch, own_sem=dma((10,)), a_s=dma((dp,)),
             a_r=dma((dp,)), b_s=dma((dp,)), b_r=dma((dp,)), p_s=dma((4,)), p_r=dma((4,)), gather_sems=Gathers.scratch(13, line),
             spread0=RowSpread.scratch(1),
             spread1=RowSpread.scratch(1), spread2=RowSpread.scratch(), spread3=RowSpread.scratch(),
         ),
-        hbm=("latent", "skip_states", "query_in", "cross_out_in", "key_in", "value_in", "down_in",
-             "query_g", "cross_out_g", "key_g", "value_g", "down_g") + (("skip_in", "project_in", "out_in") if own else ()),
-        early=("cosine", "sine", "joined0", "joined1", "skip_full", "skipped", "residual", "first_all", "project_wide", "pre", "low", "mixed", "second"),
     )
     if own:
         silu, counted = first.silu, first.counted
@@ -1420,35 +1465,32 @@
         key, value = [v.reshape(text_width, cols) for v in (first.key_g, first.value_g)]
     else:
         counted, skip_full = jnp.full((1, LANES), jnp.sum(small_all[:, width])), skip_in
-        out_t, query, cross_out_t, key, value, up_full, down_t = shards
+        out_t, query, cross_out_t, (key, value), up_full, down_t = shards
 
     text = jnp.pad(text_states[0], ((0, text_pad - text_len), (0, 0)))
     cross = named_kernel(
         "cross", 1, functools.partial(cross_body, dp, own, size, scale, heads, block, text_len),
         dict(
-            third_all=first.third_all, query=query, key=key, value=value, cross_out=cross_out_t, up_in=shards[5], down_in=down_parts[1], text=text,
-            bias_wide=first.bias_wide, cosine=first.cosine, sine=first.sine, norm_gain=norm_gain,
+            query=late(query), key=late(key), value=late(value), cross_out=late(cross_out_t), up_in=hbm(shards[4]), down_in=hbm(shards[5]), text=late(text), third_all=late(first.third_all),
+            bias_wide=first.bias_wide, cosine=late(first.cosine), sine=late(first.sine), norm_gain=norm_gain,
             norm_bias=norm_bias, row_bias=row_bias, head_gain=first.gain_wide, head_bias=first.offset_wide, mask=mask, fold=fold,
-            second=first.second,
-        ),
-        dict(
-            query_wide=shaped((width, span), BF16), keyval_wide=shaped((2, text_width, span), BF16),
+            second=late(first.second),
+        ),
+        dict(
+            query_wide=late(shaped((width, span), BF16)), keyval_wide=late(shaped((2, text_width, span), BF16)),
             text_pre=shaped((text_pad, span), F32), text_low=shaped((text_pad, 2 * span), BF16),
-            pre=shaped((group, span), F32), low=shaped((group, span), BF16), mixed=shaped((group, cols), BF16),
+            pre=late(shaped((group, span), F32)), low=late(shaped((group, span), BF16)), mixed=late(shaped((group, cols), BF16)),
             lse=lse_shape, fourth_all=full, third_sum=mine,
-            up_g=shaped(few(dp, r, hidden), BF16), down_g=shaped(few(dp, r - early_rows, hidden), BF16),
+            up_g=hbm(shaped(few(dp, r, hidden), BF16)), down_g=hbm(shaped(few(dp, r - early_rows, hidden), BF16)),
         ),
         dict(
             padded=vm((group, span), BF16), sum=sum_scratch, spread=RowSpread.scratch(),
             gather_sems=Gathers.scratch(5, line), own_sem=dma((2,)),
         ),
-        hbm=("up_in", "up_g", "down_in", "down_g"),
-        late=("query", "key", "value", "text", "third_all", "cosine", "sine", "cross_out", "second"),
-        early=("query_wide", "keyval_wide", "pre", "low", "mixed"),
     )
     if own:
         up_full = cross.up_g.reshape(width, hidden)
-        down_ins = dict(down_a=first.down_g, down_b=cross.down_g)
+        down_ins = dict(down_a=hbm(first.down_g), down_b=hbm(cross.down_g))
         down_scratch = dict(down_t=vm((dp, r, hidden), BF16), down_sem=dma((2,)))
     else:
         down_ins, down_scratch = dict(down_t=down_t), {}
@@ -1456,38 +1498,32 @@
     feed = named_kernel(
         "feed", 2, functools.partial(feed_body, own),
         dict(
-            fourth_all=cross.fourth_all, up=up_full, hidden_bias=hidden_bias[None], **down_ins, third_sum=cross.third_sum,
-            row_bias=row_bias, teacher=teacher, loss_mask=loss_mask[:, None], true_count=true_counts[:, None],
+            fourth_all=late(cross.fourth_all), up=late(up_full), hidden_bias=hidden_bias.reshape(-1, LANES), **down_ins, third_sum=late(cross.third_sum),
+            row_bias=row_bias, teacher=late(teacher), loss_mask=loss_mask[None], true_count=true_counts[:, None],
             counted=counted, total=jnp.full((1, 1), dp * group, F32),
         ),
         dict(
-            active=shaped((group, hidden), BF16), slope=shaped((group, hidden), BF16), grad_all=full, block_out=mine_low,
-            grad_final=mine, bias_mlp=line_sum,
+            active=late(shaped((group, hidden), BF16)), slope=late(shaped((group, hidden), BF16)), grad_all=full, block_out=late(mine_low),
+            grad_final=late(mine), bias_mlp=line_sum,
         ),
         dict(sum=sum_scratch, spread=RowSpread.scratch(), **down_scratch),
-        hbm=("down_a", "down_b"),
-        late=("fourth_all", "up", "third_sum", "teacher"),
-        early=("active", "slope", "block_out", "grad_final"),
     )
 
     back = named_kernel(
         "feed_back", 3, functools.partial(feed_back_body, dp, own),
         dict(
-            grad_all=feed.grad_all, slope=feed.slope, active=feed.active, **down_ins, up=up_full,
-            fourth_all=cross.fourth_all, third_sum=cross.third_sum, gain=norm_gain[3:4], grad_final=feed.grad_final,
+            grad_all=late(feed.grad_all), active=late(feed.active), **down_ins, slope=late(feed.slope), up=late(up_full),
+            fourth_all=late(cross.fourth_all), third_sum=late(cross.third_sum), norm_gain=norm_gain, grad_final=late(feed.grad_final),
         ),
         dict(
             c_all=full, grad_third=mine, sum0=line_sum, sum1=line_sum, sum2=line_sum, bias_hidden=shaped((1, hidden), F32),
-            grad_up=shaped((parts, width // parts, hidden), BF16),
+            grad_up=late(shaped((parts, width // parts, hidden), BF16)),
             **(dict(down_mine=shaped((r, hidden), F32)) if own else dict(grad_down=shaped((1, width, hidden), BF16))),
         ),
         dict(
             upper=vm((group, hidden), BF16), sum=sum_scratch, spread=RowSpread.scratch(), **down_scratch,
             **(dict(grad_down=vm((dp, r, hidden), BF16), down_bufs=GradScatter.buffers((r, hidden)), down_sems=GradScatter.scratch()) if own else {}),
         ),
-        hbm=("down_a", "down_b"),
-        late=("grad_all", "active", "slope", "up", "fourth_all", "third_sum", "grad_final"),
-        early=("grad_up",),
     )
     bias_cross_out, gain_fourth, offset_fourth = back.sum0, back.sum1, back.sum2
 
@@ -1495,14 +1531,14 @@
     cback = named_kernel(
         "cross_back", 4, functools.partial(cross_back_body, dp, own, size, scale, heads, block, text_len),
         dict(
-            c_all=back.c_all, cross_out=cross_out_t, pre=cross.pre, low=cross.low, text_pre=cross.text_pre,
-            text_low=cross.text_low, lse=cross.lse, cosine=first.cosine, sine=first.sine, head_gain=first.gain_wide, mask=mask, fold=fold,
-            mixed=cross.mixed, third_all=first.third_all, text=text, keyval_wide=cross.keyval_wide,
-            query_wide=cross.query_wide, second=first.second, gain=norm_gain[2:3], grad_third=back.grad_third,
-            **(dict(grad_up=back.grad_up) if own else {}),
-        ),
-        dict(
-            grads=shaped((parts, few_rows, cols), BF16), grad_text=shaped((text_pad, text_width), BF16),
+            c_all=late(back.c_all), cross_out=late(cross_out_t), low=late(cross.low), text_low=late(cross.text_low), pre=late(cross.pre),
+            text_pre=late(cross.text_pre), lse=cross.lse, cosine=late(first.cosine), sine=late(first.sine), head_gain=first.gain_wide, mask=mask, fold=fold,
+            mixed=late(cross.mixed), third_all=late(first.third_all), text=late(text), keyval_wide=late(cross.keyval_wide),
+            query_wide=late(cross.query_wide), second=late(first.second), norm_gain=norm_gain, grad_third=late(back.grad_third),
+            **(dict(grad_up=hbm(back.grad_up)) if own else {}),
+        ),
+        dict(
+            grads=late(shaped((parts, few_rows, cols), BF16)), grad_text=shaped((text_pad, text_width), BF16),
             gains=shaped((2, LANES), F32), offsets=shaped((2, LANES), F32), sums=shaped((1, span), F32),
             text_sums=shaped((1, span), F32), s_all=full, grad_second=mine, sum0=line_sum, sum1=line_sum, sum2=line_sum,
             **(dict(up_mine=shaped((r, hidden), F32)) if own else {}),
@@ -1512,10 +1548,6 @@
             dv=vm((text_pad, span), F32), text_p=vm((text_pad, 2 * span), BF16), sum=sum_scratch, spread=RowSpread.scratch(),
             **(dict(up_bufs=GradScatter.buffers((r, hidden)), up_sems=GradScatter.scratch()) if own else {}),
         ),
-        hbm=("grad_up",),
-        late=("c_all", "cross_out", "low", "text_low", "pre", "cosine", "sine", "query_wide", "text_pre", "mixed", "third_all",
-              "text", "keyval_wide", "second", "grad_third"),
-        early=("grads",),
     )
     few_grads = cback.grads
     if not own:
@@ -1532,13 +1564,13 @@
     sback = named_kernel(
         "self_back", 6, functools.partial(self_back_body, dp, own, size, scale, heads, block),
         dict(
-            text_part=cback.grad_text, **(dict(few_grads=few_grads) if own else {}),
-            s_all=cback.s_all, out_t=out_t, pre=first.pre, low=first.low, lse=first.lse, cosine=first.cosine, sine=first.sine,
-            head_gain=first.gain_wide, mask=mask, fold=fold, mixed=first.mixed, first_all=first.first_all,
-        ),
-        dict(
-            p=shaped((group, 3 * span), BF16), grad_out=shaped((parts, width // parts, cols), BF16),
-            grad_project=shaped((parts, 3, width // parts, cols), BF16), gains=shaped((2, LANES), F32),
+            text_part=cback.grad_text, **(dict(few_grads=hbm(few_grads)) if own else {}),
+            s_all=late(cback.s_all), out_t=late(out_t), low=late(first.low), pre=late(first.pre), lse=first.lse, cosine=late(first.cosine), sine=late(first.sine),
+            head_gain=first.gain_wide, mask=mask, fold=fold, mixed=late(first.mixed), first_all=late(first.first_all),
+        ),
+        dict(
+            p=late(shaped((group, 3 * span), BF16)), grad_out=late(shaped((parts, width // parts, cols), BF16)),
+            grad_project=late(shaped((parts, 3, width // parts, cols), BF16)), gains=shaped((2, LANES), F32),
             offsets=shaped((2, LANES), F32), sums=shaped((1, 3 * span), F32), grad_text=shaped((text_pad, text_width), F32),
             **(dict(few_mine=shaped((few_rows, cols), F32)) if own else {}),
         ),
@@ -1550,9 +1582,6 @@
             text_sems=dma((6,)),
             **(dict(few_bufs=GradScatter.buffers((few_rows, cols)), few_sems=GradScatter.scratch()) if own else {}),
         ),
-        hbm=("few_grads",),
-        late=("s_all", "out_t", "low", "pre", "cosine", "sine", "mixed", "first_all"),
-        early=("p", "grad_out", "grad_project"),
     )
     if own:
         few_mine = sback.few_mine
@@ -1562,22 +1591,22 @@
     last = named_kernel(
         "last", 5, functools.partial(last_body, dp, own),
         dict(
-            p=sback.p, project_wide=first.project_wide, residual=first.residual, grad_second=cback.grad_second,
-            skipped=first.skipped, norm_gain=norm_gain, skip_w=skip_full, joined0=first.joined0, joined1=first.joined1,
+            p=late(sback.p), project_wide=late(first.project_wide), residual=late(first.residual), grad_second=late(cback.grad_second),
+            skipped=late(first.skipped), norm_gain=norm_gain, skip_w=late(skip_full), joined0=late(first.joined0), joined1=late(first.joined1),
             silu=silu, gain_third=cback.sum1, gain_fourth=gain_fourth, offset_third=cback.sum2, offset_fourth=offset_fourth,
             bias_attn=cback.sum0, bias_cross_out=bias_cross_out, bias_mlp=feed.bias_mlp, self_gains=sback.gains,
             cross_gains=cback.gains, self_offsets=sback.offsets, cross_offsets=cback.offsets, self_sums=sback.sums,
             cross_sums=cback.sums, text_sums=cback.text_sums, bias_hidden=back.bias_hidden, unfold=jnp.asarray(fold_np.T),
-            grad_out=sback.grad_out, grad_project=sback.grad_project,
-        ),
-        dict(
-            grad_latent=mine, grad_skip=mine, shift_grad=shaped((r if own else 1, width), F32), shift_bias=line_sum,
+            grad_out=hbm(sback.grad_out), grad_project=hbm(sback.grad_project),
+        ),
+        dict(
+            grad_latent=late(mine), grad_skip=late(mine), shift_grad=shaped((r if own else 1, width), F32), shift_bias=line_sum,
             pack_out=shaped((4, PACK_ROWS, width), F32),
             **(dict(out_mine=shaped((r, cols), F32), project_mine=shaped((3, r, cols), F32), skip_mine=shaped((skip_rows, cols), F32))
                if own else dict(grad_skip_w=shaped((2, width, cols), BF16))),
         ),
         dict(
-            ksend=vm((4, rows, cols), BF16), krecv=vm((4, rows, cols), BF16), tile=vm((1, width), F32),
+            ksend=vm((4, rows, cols), BF16), krecv=vm((group, cols), BF16), tile=vm((1, width), F32),
             tile_land=vm((4, 1, width), F32), low_out=vm((1, width), F32),
             low_land=vm((dp if own else 1, 1, width), F32), pack=vm((4, PACK_ROWS, width), F32), pack_in_land=pack_land,
             pack_mine=vm((PACK_ROWS, width), F32), pack_x=vm((PACK_ROWS, width), F32), pack_z=pack_land, pack_t=pack_land, sum=sum_scratch, sum1=sum_scratch,
@@ -1589,9 +1618,6 @@
                 scatter_sems=GradScatter.scratch() * 5,
             ) if own else {}),
         ),
-        hbm=("grad_out", "grad_project"),
-        late=("p", "project_wide", "residual", "grad_second", "skipped", "skip_w", "joined0", "joined1"),
-        early=("grad_latent", "grad_skip"),
     )
     if own:
         out_mine, project_mine, skip_mine = last.out_mine, last.project_mine, last.skip_mine
@@ -1605,18 +1631,20 @@
         project_mine = lax.psum_scatter(sback.grad_project[0], "dp", scatter_dimension=1, tiled=True).astype(F32)
         skip_mine = lax.psum_scatter(last.grad_skip_w.reshape(-1, cols), "dp", scatter_dimension=0, tiled=True).astype(F32)
     end = named_kernel(
-        "finish", None, functools.partial(finish_body, cols, hidden),
+        "finish", None, functools.partial(finish_body, hidden),
         dict(
             pack=pack_sum, shift_bias=shift_bias, unfold=jnp.asarray(one_np.T), block_out=feed.block_out,
             grad_latent=last.grad_latent, grad_skip=last.grad_skip, skip_mine=skip_mine, shift_grad=shift_grad,
-            up_mine=up_mine, query_mine=few_mine[r : 2 * r] if not own else few_mine, text_part=sback.grad_text,
+            up_mine=up_mine, few_mine=few_mine, text_part=sback.grad_text,
+            out_mine=out_mine, down_mine=down_mine, project_mine=project_mine,
         ),
         dict(
             norm_gain=shaped(norm_gain.shape, F32), norm_bias=shaped(norm_bias.shape, F32), head_gain=shaped(head_gain.shape, F32),
             head_bias=shaped(head_bias.shape, F32), column_bias=shaped(column_bias.shape, F32), hidden_bias=shaped((1, 4 * hidden), F32),
             row_bias=shaped(row_bias.shape, F32), o_block=mine_low, o_latent=mine, o_skip=mine, o_skip_mine=shaped(skip_mine.shape, F32),
             o_shift=shaped(shift_grad.shape, F32), o_up=shaped(up_mine.shape, F32), o_query=shaped((r, cols), F32),
-            o_text=shaped((text_len, text_width), F32),
+            o_text=shaped((text_len, text_width), F32), o_out=shaped((r, cols), F32), o_cross_out=shaped((r, cols), F32),
+            o_down=shaped((r, hidden), F32), o_project=shaped((3, r, cols), F32), o_keyval=shaped((2, cols, text_share), F32),
         ),
         {},
     )
@@ -1627,13 +1655,13 @@
         end.o_text[None],
         end.o_skip_mine,
         end.o_shift,
-        jnp.transpose(project_mine, (1, 0, 2)),
-        out_mine.T,
+        jnp.transpose(end.o_project, (1, 0, 2)),
+        end.o_out.T,
         end.o_query,
-        jnp.transpose(few_mine[2 * r :].reshape(2, text_share, cols), (1, 0, 2)),
-        few_mine[:r].T,
+        jnp.transpose(end.o_keyval, (2, 0, 1)),
+        end.o_cross_out.T,
         end.o_up,
-        down_mine.T,
+        end.o_down.T,
         end.norm_gain,
         end.norm_bias,
         end.head_gain,

time: 639 us -> 625 us (0.978)
  local copies, waits for them, and re-layouts: 17.3 us -> 7.55 us
where the time goes in v5:
time: 625 us; the launch traced here: 617 us
  Pallas kernels  608 us (97%)
  local copies, waits for them, and re-layouts  7.55 us (1%)
    pallas_call x8, Pallas kernels, named_kernel(): pl.pallas_call(kernel, out_shape=[bare(v) for v in outs.values()], in_spe...  608 us

profile of v5, /device:TPU:0, one launch (start us, length us, event | category | flops | bytes accessed | tf_op | source)
XLA Modules:
  0.0 616.9 jit_solution(13326491322718854849)
XLA Ops:
  1.3 1.7 copy.51
  3.0 2.0 pad.4.refs_6_.refs_14_
  5.0 175.4 %first.1 = (bf16[1024,1408]{1,0:T(8,128)(2,1)}, bf16[1024,1408]{1,0:T(8,128)(2,1)}, bf16[8,352,352]{2,1,0:T(8,128)(2,1)}, bf16[256,1408]{1,0:T(8,128)(2,1)}, f32...) custom-call(bf16[256,1408]{1,0:T(8,128)(2,1)} %refs_0_.1, ...), custom_call_target="tpu_custom_call" | custom-call | tf_op jit(solution)/shard_map/first/pallas_call | solution.py:438
  180.5 84.3 %cross.1 = (bf16[1408,512]{1,0:T(8,128)(2,1)}, bf16[2,1024,512]{2,1,0:T(8,128)(2,1)}, f32[336,512]{1,0:T(8,128)}, bf16[336,1024]{1,0:T(8,128)(2,1)}, f32[1024,51...) custom-call(bf16[1408,352]{1,0:T(8,128)(2,1)} %bitcast.33, ...), custom_call_target="tpu_custom_call" | custom-call | tf_op jit(solution)/shard_map/cross/pallas_call | solution.py:438
  264.8 46.3 %feed.1 = (bf16[1024,1536]{1,0:T(8,128)(2,1)}, bf16[1024,1536]{1,0:T(8,128)(2,1)}, bf16[1024,1408]{1,0:T(8,128)(2,1)}, bf16[256,1408]{1,0:T(8,128)(2,1)}, f32[256,1408]{1,0:T(8,128)}, /*index=5*/f32[1,1408]{1,0:T(1,128)}) custom-call(bf16[1024,1408]{1,0:T(8,128)(2,1)} %get-tuple-element.131.refs_0_.refs_6_, bf16[1408,1536]{1,0:T(8,128)(2,1)} %bitcast.25, ...), custom_call_target="tpu_custom_call" | custom-call | tf_op jit(solution)/shard_map/feed/pallas_call | solution.py:438
  311.1 73.0 %feed_back.1 = (bf16[1024,1408]{1,0:T(8,128)(2,1)}, f32[256,1408]{1,0:T(8,128)}, f32[1,1408]{1,0:T(1,128)}, f32[1,1408]{1,0:T(1,128)}, f32[1,1408]{1,0:T(1,128)}...) custom-call(bf16[1024,1408]{1,0:T(8,128)(2,1)} %get-tuple-element.137.refs_0_, ...), custom_call_target="tpu_custom_call" | custom-call | tf_op jit(solution)/shard_map/feed_back/pallas_call | solution.py:438
  384.1 67.1 %cross_back.1 = (bf16[8,608,352]{2,1,0:T(8,128)(2,1)}, bf16[336,1024]{1,0:T(8,128)(2,1)}, f32[2,128]{1,0:T(2,128)}, f32[2,128]{1,0:T(2,128)}, f32[1,512]{1,0:T(1...) custom-call(bf16[1024,1408]{1,0:T(8,128)(2,1)} %get-tuple-element.14, ...), custom_call_target="tpu_custom_call" | custom-call | tf_op jit(solution)/shard_map/cross_back/pallas_call | solution.py:438
  451.1 56.2 %self_back.1 = (bf16[1024,1536]{1,0:T(8,128)(2,1)}, bf16[8,176,352]{2,1,0:T(8,128)(2,1)}, bf16[8,3,176,352]{3,2,1,0:T(8,128)(2,1)}, f32[2,128]{1,0:T(2,128)}, f3...) custom-call(bf16[336,1024]{1,0:T(8,128)(2,1)} %get-tuple-element.152.refs_0_, ...), custom_call_target="tpu_custom_call" | custom-call | tf_op jit(solution)/shard_map/self_back/pallas_call | solution.py:438
  507.4 96.8 %last.1 = (f32[256,1408]{1,0:T(8,128)}, f32[256,1408]{1,0:T(8,128)}, f32[176,1408]{1,0:T(8,128)}, f32[1,1408]{1,0:T(1,128)}, f32[4,8,1408]{2,1,0:T(8,128)}, /*in...) custom-call(bf16[1024,1536]{1,0:T(8,128)(2,1)} %get-tuple-element.161.refs_0_, ...), custom_call_target="tpu_custom_call" | custom-call | tf_op jit(solution)/shard_map/last/pallas_call | solution.py:438
  604.2 8.7 %finish.1 = (f32[4,1408]{1,0:T(4,128)}, f32[4,1408]{1,0:T(4,128)}, f32[4,88]{1,0:T(4,128)}, f32[4,88]{1,0:T(4,128)}, f32[5,1408]{1,0:T(8,128)}, /*index=5*/f32[1...) custom-call(f32[4,8,1408]{2,1,0:T(8,128)} %get-tuple-element.187.ref, ...), custom_call_target="tpu_custom_call" | custom-call | tf_op jit(solution)/shard_map/finish/pallas_call | solution.py:438
  612.9 3.8 copy.52

commit v6 on v5

--- a/solution.py
+++ b/solution.py
@@ -108,62 +108,150 @@
             cp.wait_send()
 
 
+class LineSpread:
+    def __init__(self, place, shard, land, owner_par, z_s, z_r):
+        self.place, self.land, self.z_s, self.z_r, self.par = place, land, z_s, z_r, owner_par
+        here = land.at[2 * place.zi + owner_par]
+        self.direct = {j: remote(shard, here, z_s.at[j], z_r.at[j], (place.ahead(j), place.t)) for j in (2, 1, 3)}
+        for j, cp in self.direct.items():
+            self.when(j, cp.start)
+        self.order = (2, 1 + 2 * place.e0, 3 - 2 * place.e0)
+        source = land.at[self.owner(2)]
+        end = 3 * (place.zi // 2)
+        self.inner = remote(source, source, z_s.at[0], z_r.at[1 + 2 * (place.zi // 2)], (place.at(end), place.t))
+
+    def owner(self, j):
+        return 2 * ((self.place.zi + 4 - j) % 4) + self.par
+
+    def when(self, j, act):
+        if j == 2:
+            act()
+        else:
+            pl.when(self.place.zi != (0 if j == 3 else 3))(act)
+
+    def arrival(self, i):
+        j = self.order[i]
+        here = self.land.at[self.owner(j)]
+        remote(here, here, self.z_s.at[j], self.z_r.at[j], self.place.pair).wait_recv()
+        if i == 0:
+            pl.when(self.place.end == 0)(self.inner.start)
+        return self.owner(j), j
+
+    def sent(self):
+        for j, cp in self.direct.items():
+            self.when(j, cp.wait_send)
+        pl.when(self.place.end == 0)(self.inner.wait_send)
+
+
+class LineFirst:
+    def __init__(self, place, shard, land, z_s, z_r, x_s, x_r):
+        self.place, self.land, self.x_s, self.x_r = place, land, x_s, x_r
+        self.line = LineSpread(place, shard, land, place.par, z_s.at[0], z_r.at[0])
+        self.x = []
+        self.cross(shard, place.d, 0)
+
+    def cross(self, source, owner, j):
+        cp = remote(source, self.land.at[owner], self.x_s.at[j], self.x_r.at[j], self.place.pair)
+        cp.start()
+        self.x.append(cp)
+
+    def pass_on(self, arrivals):
+        for i in arrivals:
+            owner, j = self.line.arrival(i)
+            self.cross(self.land.at[owner], owner, j)
+
+    def early(self):
+        self.pass_on((0, 1))
+
+    def later(self):
+        self.pass_on((2,))
+
+    def arrived(self):
+        for cp in self.x:
+            cp.wait_recv()
+
+    def sent(self):
+        self.line.sent()
+        for cp in self.x:
+            cp.wait_send()
+
+
+class PairFirst:
+    def __init__(self, place, shard, land, z_s, z_r, x_s, x_r):
+        self.place, self.land, self.sems = place, land, (z_s, z_r)
+        self.lines = [LineSpread(place, shard, land, place.par, z_s.at[0], z_r.at[0])]
+        self.x = remote(shard, land.at[place.d], x_s.at[0], x_r.at[0], place.pair)
+        self.x.start()
+
+    def early(self):
+        self.x.wait_recv()
+        z_s, z_r = self.sems
+        par = 1 - self.place.par
+        other = self.land.at[2 * self.place.zi + par]
+        self.lines.append(LineSpread(self.place, other, self.land, par, z_s.at[1], z_r.at[1]))
+
+    def later(self):
+        for line in self.lines:
+            line.arrival(0)
+
+    def arrived(self):
+        for line in self.lines:
+            line.arrival(1)
+            line.arrival(2)
+
+    def sent(self):
+        self.x.wait_send()
+        for line in self.lines:
+            line.sent()
+
+
 class Gathers:
     def __init__(self, place, ahead, z_s, z_r, x_s, x_r):
         self.place, self.ahead, self.sems = place, ahead, (z_s, z_r, x_s, x_r)
-        self.pieces, self.z, self.x, self.passed = [], [], [], 0
-
-    def add(self, shard, land, pieces=1):
+        self.pieces, self.going, self.passed, self.ended = [], [], 0, 0
+
+    def add(self, shard, land, pieces=1, kind=LineFirst):
         start = 0
         for i in range(pieces):
             if pieces == 1:
-                self.pieces.append((shard, land))
+                self.pieces.append((kind, shard, land))
             else:
                 count = piece_rows(shard.shape[0], pieces, i)
-                self.pieces.append((shard.at[pl.ds(start, count)], land.at[:, pl.ds(start, count)]))
+                self.pieces.append((kind, shard.at[pl.ds(start, count)], land.at[:, pl.ds(start, count)]))
                 start += count
         self.fill()
 
     def fill(self):
-        place = self.place
-        while len(self.z) < min(len(self.pieces), self.passed + self.ahead):
-            k = len(self.z)
-            shard, land = self.pieces[k]
-            z_s, z_r, x_s, x_r = [v.at[k] for v in self.sems]
-            self.z.append([
-                remote(shard, land.at[place.d], z_s.at[j], z_r.at[j], (place.ahead(j), place.t)) for j in range(1, place.line)
-            ])
-            self.x.append([remote(shard, land.at[place.d], x_s.at[0], x_r.at[0], place.pair)])
-            for cp in self.z[k] + self.x[k]:
-                cp.start()
+        while len(self.going) < min(len(self.pieces), self.passed + self.ahead):
+            k = len(self.going)
+            kind, shard, land = self.pieces[k]
+            self.going.append(kind(self.place, shard, land, *[v.at[k] for v in self.sems]))
 
     def forward(self, count=1):
         for _ in range(count):
-            k = self.passed
-            _, land = self.pieces[k]
-            _, _, x_s, x_r = [v.at[k] for v in self.sems]
-            for j in range(1, self.place.line):
-                self.z[k][j - 1].wait_recv()
-                here = land.at[self.place.behind(j)]
-                cp = remote(here, here, x_s.at[j], x_r.at[j], self.place.pair)
-                cp.start()
-                self.x[k].append(cp)
+            self.end(self.passed)
+            self.going[self.passed].early()
             self.passed += 1
             self.fill()
 
+    def end(self, last):
+        while self.ended < last:
+            self.going[self.ended].later()
+            self.ended += 1
+
     def arrived(self, first, last):
-        for cps in self.x[first:last]:
-            for cp in cps:
-                cp.wait_recv()
+        self.end(last)
+        for g in self.going[first:last]:
+            g.arrived()
 
     def sent(self):
-        for cps in self.z + self.x:
-            for cp in cps:
-                cp.wait_send()
+        for g in self.going:
+            g.sent()
 
     @staticmethod
-    def scratch(count, line):
-        return [pltpu.SemaphoreType.DMA((count, line))] * 4
+    def scratch(count):
+        dma = pltpu.SemaphoreType.DMA
+        return [dma((count, 2, 4)), dma((count, 2, 4)), dma((count, 4)), dma((count, 4))]
 
 
 def piece_rows(rows, pieces, i):
@@ -633,7 +721,7 @@
             n.small[q, :, pl.ds(n.small.shape[2] - LANES, LANES)] = count
         n.small_land[d] = n.small[d]
         smalls = ToAll(place, lambda q: n.small.at[q], n.small_land, n.a_s, n.a_r)
-        gathers = Gathers(place, 2, *n.gather_sems)
+        gathers = Gathers(place, 3, *n.gather_sems)
         gathers.add(n.skip_in, n.skip_full, 2)
         smalls.arrived()
         given = jnp.concatenate([n.small_land[i] for i in range(dp)], axis=0)
@@ -659,7 +747,7 @@
         gathers.forward()
     spreads[0].finish()
     if own:
-        gathers.add(n.down_in.at[pl.ds(0, n.down_g.shape[1])], n.down_g, 3)
+        gathers.add(n.down_in.at[pl.ds(0, n.down_g.shape[1])], n.down_g, 3, PairFirst)
         gathers.arrived(0, 2)
         kept[2].wait()
         half = dp // 2
@@ -724,7 +812,7 @@
             narrow = n.project_in[part]
         n.project_wide[part] = dot_nn(narrow, n.fold[...]).astype(BF16)
     if own:
-        gathers.forward()
+        gathers.forward(2)
 
     def project(i, _):
         here = pl.ds(pl.multiple_of(i * block, block), block)
@@ -746,7 +834,7 @@
     lax.fori_loop(0, n.low.shape[0] // block, project, 0)
     n.done(n.project_wide, n.pre, n.low)
     if own:
-        gathers.forward()
+        gathers.forward(2)
     attend(
         n.low.at[:, pl.ds(0, span)], n.low.at[:, pl.ds(span, span)], n.low.at[:, pl.ds(2 * span, span)],
         n.padded, n.lse, heads, scale, block, n.low.shape[0], gathers.forward if own else None,
@@ -773,11 +861,10 @@
         gathers.forward()
     spread.forward()
     if own:
-        gathers.forward()
+        gathers.end(len(gathers.pieces))
     spread.finish()
     reduce.sent()
     if own:
-        gathers.forward()
         gathers.arrived(6, len(gathers.pieces))
         for cp in kept[5:]:
             cp.wait()
@@ -794,10 +881,10 @@
     bar = greet(peers)
     pl.semaphore_wait(bar, len(peers))
     if own:
-        gathers = Gathers(place, 2, *n.gather_sems)
+        gathers = Gathers(place, 3, *n.gather_sems)
         gathers.add(n.up_in, n.up_g, 4)
         down_in = n.down_in.at[pl.ds(n.down_in.shape[0] - n.down_g.shape[1], n.down_g.shape[1])]
-        gathers.add(down_in, n.down_g)
+        gathers.add(down_in, n.down_g, 1, PairFirst)
         kept = [pltpu.make_async_copy(a, b.at[d], n.own_sem.at[i])
                 for i, (a, b) in enumerate(((n.up_in, n.up_g), (down_in, n.down_g)))]
         for cp in kept:
@@ -1258,6 +1345,15 @@
         lows = ToAll(place, lambda q: n.low_out, n.low_land, n.l_s, n.l_r)
         pack_cp = remote(n.pack_mine, n.pack_x, n.px_s.at[0], n.px_r.at[0], place.pair)
         pack_cp.start()
+    n.need(n.joined0, n.joined1)
+    k_all = n.krecv[...]
+    count = n.grad_skip_w.shape[0] // 2
+    for h, joined in enumerate((n.joined0, n.joined1)):
+        n.grad_skip_w[pl.ds(h * count, count)] = (
+            dot_tn(joined[...], k_all).astype(BF16).reshape((count,) + n.grad_skip_w.shape[1:])
+        )
+    if own:
+        scatter(n.grad_skip_w, n.skip_bufs)
     n.need(n.skip_w)
     halves = [TensorSum(*n.sum), TensorSum(*n.sum1)]
     for h, half in enumerate(halves):
@@ -1273,16 +1369,7 @@
             cp.start()
             packs.append(cp)
         scatters[2].steps()
-    n.need(n.joined0, n.joined1)
-    k_all = n.krecv[...]
-    count = n.grad_skip_w.shape[0] // 2
-    for h, joined in enumerate((n.joined0, n.joined1)):
-        n.grad_skip_w[pl.ds(h * count, count)] = (
-            dot_tn(joined[...], k_all).astype(BF16).reshape((count,) + n.grad_skip_w.shape[1:])
-        )
-    if own:
         scatters[3].steps()
-        scatter(n.grad_skip_w, n.skip_bufs)
         scatters[4].steps()
         for cp in packs:
             cp.wait_recv()
@@ -1453,7 +1540,7 @@
             p_land=vm(few(dp, 3, r, cols), BF16), padded=vm((group, span), BF16), skip_send=vm((4, rows, cols), BF16),
             skip_recv=vm((4, rows, cols), BF16), small=vm(small_shape, F32), small_land=vm(small_shape, F32), shift_part=vm((dp, 1, width), F32),
             shift_land=vm((dp, 1, width), F32), sum=sum_scratch, own_sem=dma((10,)), a_s=dma((dp,)),
-            a_r=dma((dp,)), b_s=dma((dp,)), b_r=dma((dp,)), p_s=dma((4,)), p_r=dma((4,)), gather_sems=Gathers.scratch(13, line),
+            a_r=dma((dp,)), b_s=dma((dp,)), b_r=dma((dp,)), p_s=dma((4,)), p_r=dma((4,)), gather_sems=Gathers.scratch(13),
             spread0=RowSpread.scratch(1),
             spread1=RowSpread.scratch(1), spread2=RowSpread.scratch(), spread3=RowSpread.scratch(),
         ),
@@ -1485,7 +1572,7 @@
         ),
         dict(
             padded=vm((group, span), BF16), sum=sum_scratch, spread=RowSpread.scratch(),
-            gather_sems=Gathers.scratch(5, line), own_sem=dma((2,)),
+            gather_sems=Gathers.scratch(5), own_sem=dma((2,)),
         ),
     )
     if own:

time: 625 us -> 611 us (0.978)
  Pallas kernels: 608 us -> 594 us
    pallas_call x8, Pallas kernels: 608 us -> 594 us  [named_kernel(): pl.pallas_call(kernel, out_shape=[bare(v) for v in outs.values()], in_spe...]
where the time goes in v6:
time: 611 us; the launch traced here: 603 us
  Pallas kernels  594 us (97%)
  local copies, waits for them, and re-layouts  7.55 us (1%)
    pallas_call x8, Pallas kernels, named_kernel(): pl.pallas_call(kernel, out_shape=[bare(v) for v in outs.values()], in_spe...  594 us

profile of v6, /device:TPU:0, one launch (start us, length us, event | category | flops | bytes accessed | tf_op | source)
XLA Modules:
  0.0 603.2 jit_solution(7968596005196868504)
XLA Ops:
  1.3 1.7 copy.51
  3.0 2.0 pad.4.refs_6_.refs_14_
  5.0 172.6 %first.1 = (bf16[1024,1408]{1,0:T(8,128)(2,1)}, bf16[1024,1408]{1,0:T(8,128)(2,1)}, bf16[8,352,352]{2,1,0:T(8,128)(2,1)}, bf16[256,1408]{1,0:T(8,128)(2,1)}, f32...) custom-call(bf16[256,1408]{1,0:T(8,128)(2,1)} %refs_0_.1, ...), custom_call_target="tpu_custom_call" | custom-call | tf_op jit(solution)/shard_map/first/pallas_call | solution.py:526
  177.6 75.4 %cross.1 = (bf16[1408,512]{1,0:T(8,128)(2,1)}, bf16[2,1024,512]{2,1,0:T(8,128)(2,1)}, f32[336,512]{1,0:T(8,128)}, bf16[336,1024]{1,0:T(8,128)(2,1)}, f32[1024,51...) custom-call(bf16[1408,352]{1,0:T(8,128)(2,1)} %bitcast.33, ...), custom_call_target="tpu_custom_call" | custom-call | tf_op jit(solution)/shard_map/cross/pallas_call | solution.py:526
  253.1 45.0 %feed.1 = (bf16[1024,1536]{1,0:T(8,128)(2,1)}, bf16[1024,1536]{1,0:T(8,128)(2,1)}, bf16[1024,1408]{1,0:T(8,128)(2,1)}, bf16[256,1408]{1,0:T(8,128)(2,1)}, f32[256,1408]{1,0:T(8,128)}, /*index=5*/f32[1,1408]{1,0:T(1,128)}) custom-call(bf16[1024,1408]{1,0:T(8,128)(2,1)} %get-tuple-element.131.refs_0_.refs_6_, bf16[1408,1536]{1,0:T(8,128)(2,1)} %bitcast.25, ...), custom_call_target="tpu_custom_call" | custom-call | tf_op jit(solution)/shard_map/feed/pallas_call | solution.py:526
  298.0 74.6 %feed_back.1 = (bf16[1024,1408]{1,0:T(8,128)(2,1)}, f32[256,1408]{1,0:T(8,128)}, f32[1,1408]{1,0:T(1,128)}, f32[1,1408]{1,0:T(1,128)}, f32[1,1408]{1,0:T(1,128)}...) custom-call(bf16[1024,1408]{1,0:T(8,128)(2,1)} %get-tuple-element.137.refs_0_, ...), custom_call_target="tpu_custom_call" | custom-call | tf_op jit(solution)/shard_map/feed_back/pallas_call | solution.py:526
  372.6 66.7 %cross_back.1 = (bf16[8,608,352]{2,1,0:T(8,128)(2,1)}, bf16[336,1024]{1,0:T(8,128)(2,1)}, f32[2,128]{1,0:T(2,128)}, f32[2,128]{1,0:T(2,128)}, f32[1,512]{1,0:T(1...) custom-call(bf16[1024,1408]{1,0:T(8,128)(2,1)} %get-tuple-element.14, ...), custom_call_target="tpu_custom_call" | custom-call | tf_op jit(solution)/shard_map/cross_back/pallas_call | solution.py:526
  439.3 56.6 %self_back.1 = (bf16[1024,1536]{1,0:T(8,128)(2,1)}, bf16[8,176,352]{2,1,0:T(8,128)(2,1)}, bf16[8,3,176,352]{3,2,1,0:T(8,128)(2,1)}, f32[2,128]{1,0:T(2,128)}, f3...) custom-call(bf16[336,1024]{1,0:T(8,128)(2,1)} %get-tuple-element.152.refs_0_, ...), custom_call_target="tpu_custom_call" | custom-call | tf_op jit(solution)/shard_map/self_back/pallas_call | solution.py:526
  495.9 94.6 %last.1 = (f32[256,1408]{1,0:T(8,128)}, f32[256,1408]{1,0:T(8,128)}, f32[176,1408]{1,0:T(8,128)}, f32[1,1408]{1,0:T(1,128)}, f32[4,8,1408]{2,1,0:T(8,128)}, /*in...) custom-call(bf16[1024,1536]{1,0:T(8,128)(2,1)} %get-tuple-element.161.refs_0_, ...), custom_call_target="tpu_custom_call" | custom-call | tf_op jit(solution)/shard_map/last/pallas_call | solution.py:526
  590.5 8.7 %finish.1 = (f32[4,1408]{1,0:T(4,128)}, f32[4,1408]{1,0:T(4,128)}, f32[4,88]{1,0:T(4,128)}, f32[4,88]{1,0:T(4,128)}, f32[5,1408]{1,0:T(8,128)}, /*index=5*/f32[1...) custom-call(f32[4,8,1408]{2,1,0:T(8,128)} %get-tuple-element.187.ref, ...), custom_call_target="tpu_custom_call" | custom-call | tf_op jit(solution)/shard_map/finish/pallas_call | solution.py:526
  599.2 3.8 copy.52
